TPU v7x, 32 devices: a whole 2x2x4 slice. The times are simulated.
32 devices in a mesh: section: 8 (over z, y), expert: 4 (over x, core).
Axes of the slice: x: 2, y: 2, z: 4, core: 2. Of those that a mesh axis runs over, the one named last changes fastest.
Arguments:
- x_fwd: bfloat16 [8, 256, 3584], P('section', 'expert'), may hold values from -6 to 6
- saved_gate: bfloat16 [8, 4, 34, 2048], P('section', None, None, 'expert'), may hold values from -6 to 6
- saved_up: bfloat16 [8, 4, 34, 2048], P('section', None, None, 'expert'), may hold values from -6 to 6
- grad_next: bfloat16 [8, 256, 3584], P('section', 'expert'), may hold values from -6 to 6
- routes_fwd: int32 [8, 256, 1], P('section', 'expert'), may hold values from 0 to 1; in each aligned block of 64 rows (0 to 63, 64 to 127, ..., all dimensions but the last counted through in order) at most 34 rows name the same one
- routes_bwd: int32 [8, 256, 1], P('section', 'expert'), may hold values from 0 to 1; in each aligned block of 64 rows (0 to 63, 64 to 127, ..., all dimensions but the last counted through in order) at most 34 rows name the same one
- scores_fwd: float32 [8, 256, 1], P('section', 'expert'), may hold values from 0.05 to 1
- scores_bwd: float32 [8, 256, 1], P('section', 'expert'), may hold values from 0.05 to 1
- w_gate: bfloat16 [8, 3584, 2048], P('section', None, 'expert'), may hold values from -0.09375 to 0.09375
- w_up: bfloat16 [8, 3584, 2048], P('section', None, 'expert'), may hold values from -0.09375 to 0.09375
- w_down: bfloat16 [8, 2048, 3584], P('section', 'expert'), may hold values from -0.1875 to 0.1875
Outputs:
- next_input: bfloat16 [8, 256, 3584], P('section', 'expert')
- input_grad: bfloat16 [8, 256, 3584], P('section', 'expert')
- score_grad: float32 [8, 256, 1], P('section', 'expert')
Inputs may be any that keep to these rules, and one draw needn't show every extreme that they name: `routes_fwd`: among the tokens of one device no expert is named by more than 34 of them, and in every draw some expert is named by exactly 34. `routes_bwd`: as for routes_fwd.
All inputs are finite; a program needn't handle non-finite values.
Results may differ from a plain program's by a relative error of at most 0.0052.
Values may be sent and summed in bfloat16 or wider, within the bound.
No kernel may reach another device: no remote copies, remote signals or barrier semaphores. Data moves between devices by JAX's collectives and lax.ppermute only.
A program may use at most 64 MiB of HBM per device.

v0:
```python
import jax
import jax.numpy as jnp
from jax import lax
from jax.sharding import PartitionSpec as P

EXPERTS = 2


def from_behind(block, axis, distance):
    devices = range(lax.axis_size(axis))
    route = [((i - distance) % len(devices), i) for i in devices]
    return lax.ppermute(block, axis, route)


def gates_of(scores):
    return 2.5 * scores


def slot_ids(routes, count, capacity):
    flat = routes.reshape(-1)
    hits = (flat[:, None] == jnp.arange(count, dtype=jnp.int32)[None, :]).astype(jnp.int32)
    before = jnp.cumsum(hits, axis=0) - hits
    return flat * capacity + jnp.sum(before * hits, axis=1)


def dispatch(slots, tokens, count, capacity, slices):
    width = count * capacity
    picks = slots.reshape(tokens.shape[0], -1)
    table = jnp.sum(
        (picks[:, :, None] == jnp.arange(width, dtype=jnp.int32)[None, None, :]).astype(
            jnp.bfloat16
        ),
        axis=1,
    )
    moved = lax.dot_general(
        table, tokens, (((0,), (0,)), ((), ())), preferred_element_type=jnp.float32
    )
    moved = moved.astype(jnp.bfloat16).reshape(count, 1, capacity, tokens.shape[1])
    spread = jnp.broadcast_to(moved, (count, slices, capacity, tokens.shape[1]))
    return spread.reshape(count * slices, capacity, tokens.shape[1])


def body(
    x_fwd,
    saved_gate,
    saved_up,
    grad_next,
    routes_fwd,
    routes_bwd,
    scores_fwd,
    scores_bwd,
    w_gate,
    w_up,
    w_down,
):
    groups = lax.axis_size("expert")
    count = EXPERTS
    slices = groups // count
    wg = w_gate[0]
    wu = w_up[0]
    wd = w_down[0]
    capacity = saved_gate.shape[2]
    width = count * capacity
    tokens = x_fwd[0]
    tok = tokens.shape[0]
    depth = tokens.shape[1]
    slots_a = slot_ids(routes_fwd[0], count, capacity)
    slots_b = slot_ids(routes_bwd[0], count, capacity)
    send = dispatch(slots_a, tokens, count, capacity, slices)
    recv = lax.all_to_all(send, "expert", split_axis=0, concat_axis=0, tiled=True)
    flat = recv.reshape(-1, depth)
    g = jnp.dot(flat, wg, preferred_element_type=jnp.float32)
    u = jnp.dot(flat, wu, preferred_element_type=jnp.float32)
    hidden = (jax.nn.silu(g) * u).astype(jnp.bfloat16)
    result = jnp.dot(hidden, wd, preferred_element_type=jnp.float32).astype(jnp.bfloat16)
    back = lax.all_to_all(
        result.reshape(groups, capacity, depth), "expert", split_axis=0, concat_axis=0, tiled=True
    )
    summed = jnp.sum(
        back.reshape(count, slices, capacity, depth).astype(jnp.float32), axis=1
    ).reshape(width, depth)
    rows = jnp.take(summed, slots_a, axis=0).reshape(tok, -1, depth)
    gate_a = gates_of(scores_fwd[0])
    layer_out = (tokens.astype(jnp.float32) + jnp.sum(gate_a[:, :, None] * rows, axis=1)).astype(
        jnp.bfloat16
    )
    next_input = from_behind(layer_out[None], "section", 1)
    upstream = from_behind(grad_next, "section", -1)[0]
    send_d = dispatch(slots_b, upstream, count, capacity, slices)
    recv_d = lax.all_to_all(send_d, "expert", split_axis=0, concat_axis=0, tiled=True)
    upstream, recv_d = (upstream, recv_d)
    g = saved_gate[0].astype(jnp.float32)
    u = saved_up[0].astype(jnp.float32)
    sig = jax.nn.sigmoid(g)
    hidden = (jax.nn.silu(g) * u).astype(jnp.bfloat16)
    pulled = jnp.einsum("scd,fd->scf", recv_d, wd, preferred_element_type=jnp.float32)
    dgp = (pulled * u * sig * (1.0 + g * (1.0 - sig))).astype(jnp.bfloat16)
    dup = (pulled * g * sig).astype(jnp.bfloat16)
    dxe = (
        jnp.einsum("scf,df->scd", dgp, wg, preferred_element_type=jnp.float32)
        + jnp.einsum("scf,df->scd", dup, wu, preferred_element_type=jnp.float32)
    ).astype(jnp.bfloat16)
    inner = jnp.sum(pulled * hidden.astype(jnp.float32), axis=-1)
    back_grad = lax.all_to_all(dxe, "expert", split_axis=0, concat_axis=0, tiled=True)
    back_inner = lax.all_to_all(inner, "expert", split_axis=0, concat_axis=0, tiled=True)
    inner_sum = jnp.sum(back_inner.reshape(count, slices, capacity), axis=1).reshape(width)
    grad_sum = jnp.sum(
        back_grad.reshape(count, slices, capacity, depth).astype(jnp.float32), axis=1
    ).reshape(width, depth)
    dgate = jnp.take(inner_sum, slots_b, axis=0).reshape(tok, -1)
    grad_rows = jnp.take(grad_sum, slots_b, axis=0).reshape(tok, -1, depth)
    gate_b = gates_of(scores_bwd[0])
    input_grad = (
        upstream.astype(jnp.float32) + jnp.sum(gate_b[:, :, None] * grad_rows, axis=1)
    ).astype(jnp.bfloat16)
    score_grad = 2.5 * dgate
    input_grad, score_grad = (input_grad, score_grad)
    return (next_input, input_grad[None], score_grad[None])


def solution(mesh):
    placed = (
        P("section", "expert", None),
        P("section", None, None, "expert"),
        P("section", None, None, "expert"),
        P("section", "expert", None),
        P("section", "expert", None),
        P("section", "expert", None),
        P("section", "expert", None),
        P("section", "expert", None),
        P("section", None, "expert"),
        P("section", None, "expert"),
        P("section", "expert", None),
    )
    return jax.shard_map(
        body,
        mesh=mesh,
        in_specs=placed,
        out_specs=(
            P("section", "expert", None),
            P("section", "expert", None),
            P("section", "expert", None),
        ),
        check_vma=False,
    )
```

profile of v0, /device:TPU:0, one launch (start us, length us, event | category | flops | bytes accessed | tf_op | source)
XLA Modules:
  0.0 108.6 jit_solution(4276122955413636175)
XLA Ops:
  0.6 6.1 %collective-permute-start.1 = (bf16[1,64,3584]{2,1,0:T(8,128)(2,1)}, bf16[1,64,3584]{2,1,0:T(8,128)(2,1)S(1)}, u32[]{:S(2)}, u32[]{:S(2)}) collective-permute-start(bf16[1,64,3584]{2,1,0:T(8,128)(2,1)} %param.16), channel_id=1, source_target_pairs={{4,0},{8,4},{12,8},{16,12},{20,16},{24,20},{28,24},{0,28},{5,1},{9... | collective-permute-start | bytes 1376264 | tf_op jit(solution)/shard_map/ppermute | solution.py:12
  9.0 1.4 %convolution_convert_fusion.2 = bf16[68,3584]{1,0:T(8,128)(2,1)S(1)} fusion(bf16[1,64,3584]{2,1,0:T(8,128)(2,1)} %param.13, s32[64]{0:T(128)S(1)} %get-tuple-element.7), kind=kOutput, calls=%fused_computation.7 | convolution fusion | flops 31443200 | bytes 946432 | tf_op jit(solution)/shard_map/dot_general | solution.py:35
  10.6 1.1 %broadcast_in_dim.24 = bf16[2,2,34,3584]{3,2,1,0:T(8,128)(2,1)} broadcast(bf16[2,34,3584]{2,1,0:T(8,128)(2,1)S(1)} %broadcast_in_dim.23), dimensions={0,2,3} | broadcast | bytes 1462272 | tf_op jit(solution)/shard_map/broadcast_in_dim | solution.py:39
  11.7 3.5 %all-to-all-start = ((bf16[4,34,3584]{2,1,0:T(8,128)(2,1)}), bf16[4,34,3584]{2,1,0:T(8,128)(2,1)S(1)}, u32[]{:S(2)}, u32[]{:S(2)}) async-start(bf16[4,34,3584]{2,1,0:T(8,128)(2,1)} %bitcast.4), calls=%async_computation | async-start | bytes 2293760 | tf_op jit(solution)/shard_map/all_to_all | solution.py:70
  15.7 1.1 %collective-permute-done.1 = bf16[1,64,3584]{2,1,0:T(8,128)(2,1)S(1)} collective-permute-done((bf16[1,64,3584]{2,1,0:T(8,128)(2,1)}, bf16[1,64,3584]{2,1,0:T(8,128)(2,1)S(1)}, u32[]{:S(2)}, u32[]{:S(2)}) %collective-permute-start.1) | collective-permute-done | bytes 458784 | tf_op jit(solution)/shard_map/ppermute | solution.py:12
  17.3 13.4 %all-to-all-done = bf16[4,34,3584]{2,1,0:T(8,128)(2,1)S(1)} async-done(((bf16[4,34,3584]{2,1,0:T(8,128)(2,1)}), bf16[4,34,3584]{2,1,0:T(8,128)(2,1)S(1)}, u32[]{:S(2)}, u32[]{:S(2)}) %all-to-all-start) | async-done | bytes 974880 | tf_op jit(solution)/shard_map/all_to_all | solution.py:70
  30.7 1.1 %broadcast_in_dim.41 = bf16[2,2,34,3584]{3,2,1,0:T(8,128)(2,1)} broadcast(bf16[2,34,3584]{2,1,0:T(8,128)(2,1)S(1)} %broadcast_in_dim.40), dimensions={0,2,3} | broadcast | bytes 1462272 | tf_op jit(solution)/shard_map/broadcast_in_dim | solution.py:39
  31.8 4.3 %all-to-all-start.2 = ((bf16[4,34,3584]{2,1,0:T(8,128)(2,1)}), bf16[4,34,3584]{2,1,0:T(8,128)(2,1)}, u32[]{:S(2)}, u32[]{:S(2)}) async-start(bf16[4,34,3584]{2,1,0:T(8,128)(2,1)} %bitcast.14), calls=%async_computation.2 | async-start | bytes 2293760 | tf_op jit(solution)/shard_map/all_to_all | solution.py:90
  36.5 2.8 %fusion.9 = f32[136,512]{1,0:T(8,128)S(1)} fusion(bf16[136,3584]{1,0:T(8,128)(2,1)S(1)} %reshape.245, bf16[1,3584,512]{2,1,0:T(8,128)(2,1)} %param.21), kind=kOutput, calls=%fused_computation.16 | convolution fusion | flops 499122176 | bytes 4923392 | tf_op jit(solution)/shard_map/dot_general | solution.py:72
  39.2 12.4 %all-to-all-done.2 = bf16[4,34,3584]{2,1,0:T(8,128)(2,1)} async-done(((bf16[4,34,3584]{2,1,0:T(8,128)(2,1)}), bf16[4,34,3584]{2,1,0:T(8,128)(2,1)}, u32[]{:S(2)}, u32[]{:S(2)}) %all-to-all-start.2) | async-done | bytes 974880 | tf_op jit(solution)/shard_map/all_to_all | solution.py:90
  51.7 4.4 %multiply_reduce_fusion = (f32[4,34]{1,0:T(4,128)}, f32[4,34,512]{2,1,0:T(8,128)S(1)}) fusion(bf16[1,4,34,512]{3,1,2,0:T(4,128)(2,1)S(1)} %copy-done.4, bf16[1,4,34,512]{3,1,2,0:T(4,128)(2,1)S(1)} %copy-done.3, bf16[4,34,3584]{2,1,0:T(8,128)(2,1)} %all-to-all-done.2, bf16[1,512,3584]{2,1,0:T(8,128)(2,1)} %param.23), kind=kOutput, calls=%fused_computation.46 | convolution fusion | flops 499888000 | bytes 5202464 | tf_op jit(solution)/shard_map/scd,fd->scf/dot_general | solution.py:96
  56.1 3.2 %all-to-all-start.4 = ((f32[4,1,34]{2,1,0:T(1,128)}), f32[4,1,34]{2,1,0:T(1,128)S(1)}, u32[]{:S(2)}, u32[]{:S(2)}) async-start(f32[4,1,34]{2,1,0:T(1,128)} %bitcast.25), calls=%async_computation.4 | async-start | bytes 4096 | tf_op jit(solution)/shard_map/all_to_all | solution.py:105
  59.3 4.5 %convolution_convert_fusion = bf16[136,3584]{1,0:T(8,128)(2,1)S(1)} fusion(bf16[1,512,3584]{2,1,0:T(8,128)(2,1)} %param.23, bf16[136,3584]{1,0:T(8,128)(2,1)S(1)} %reshape.245, bf16[1,3584,512]{2,1,0:T(8,128)(2,1)} %param.22, f32[136,512]{1,0:T(8,128)S(1)} %fusion.9), kind=kOutput, calls=%fused_computation.5 | convolution fusion | flops 999149568 | bytes 9568256 | tf_op jit(solution)/shard_map/dot_general | solution.py:75
  63.8 1.3 %reshape.246 = bf16[4,34,3584]{2,1,0:T(8,128)(2,1)} reshape(bf16[136,3584]{1,0:T(8,128)(2,1)S(1)} %convolution_convert_fusion) | data formatting | bytes 1949696 | tf_op jit(solution)/shard_map/reshape | solution.py:77
  65.1 3.5 %all-to-all-start.1 = ((bf16[4,34,3584]{2,1,0:T(8,128)(2,1)}), bf16[4,34,3584]{2,1,0:T(8,128)(2,1)S(1)}, u32[]{:S(2)}, u32[]{:S(2)}) async-start(bf16[4,34,3584]{2,1,0:T(8,128)(2,1)} %reshape.246), calls=%async_computation.1 | async-start | bytes 2293760 | tf_op jit(solution)/shard_map/all_to_all | solution.py:76
  68.6 3.5 %fusion.2 = f32[4,34,3584]{2,1,0:T(8,128)S(1)} fusion(bf16[1,3584,512]{2,1,0:T(8,128)(2,1)} %param.21, f32[4,34,512]{2,1,0:T(8,128)S(1)} %get-tuple-element.9, bf16[1,4,34,512]{3,1,2,0:T(4,128)(2,1)S(1)} %copy-done.4, bf16[1,4,34,512]{3,1,2,0:T(4,128)(2,1)S(1)} %copy-done.3), kind=kOutput, calls=%fused_computation.9 | convolution fusion | flops 499957760 | bytes 6176768 | tf_op jit(solution)/shard_map/scf,df->scd/dot_general | solution.py:100
  72.1 2.4 %fusion = bf16[4,34,3584]{2,1,0:T(8,128)(2,1)} fusion(f32[4,34,3584]{2,1,0:T(8,128)S(1)} %fusion.2, bf16[1,3584,512]{2,1,0:T(8,128)(2,1)S(1)} %copy-done, f32[4,34,512]{2,1,0:T(8,128)S(1)} %get-tuple-element.9, bf16[1,4,34,512]{3,1,2,0:T(4,128)(2,1)S(1)} %copy-done.3), kind=kOutput, calls=%fused_computation.4 | convolution fusion | flops 500584448 | bytes 7012352 | tf_op jit(solution)/shard_map/scf,df->scd/dot_general | solution.py:101
  75.9 8.2 %all-to-all-done.1 = bf16[4,34,3584]{2,1,0:T(8,128)(2,1)S(1)} async-done(((bf16[4,34,3584]{2,1,0:T(8,128)(2,1)}), bf16[4,34,3584]{2,1,0:T(8,128)(2,1)S(1)}, u32[]{:S(2)}, u32[]{:S(2)}) %all-to-all-start.1) | async-done | bytes 974880 | tf_op jit(solution)/shard_map/all_to_all | solution.py:76
  84.1 3.5 %all-to-all-start.3 = ((bf16[4,34,3584]{2,1,0:T(8,128)(2,1)}), bf16[4,34,3584]{2,1,0:T(8,128)(2,1)S(1)}, u32[]{:S(2)}, u32[]{:S(2)}) async-start(bf16[4,34,3584]{2,1,0:T(8,128)(2,1)} %fusion), calls=%async_computation.3 | async-start | bytes 2293760 | tf_op jit(solution)/shard_map/all_to_all | solution.py:104
  88.8 2.0 %fusion.20 = bf16[1,64,3584]{2,1,0:T(8,128)(2,1)} fusion(f32[64,3584]{1,0:T(8,128)S(1)} %gather_fusion.1, bf16[1,64,3584]{2,1,0:T(8,128)(2,1)} %param.13, f32[64]{0:T(128)S(1)} %multiply_bitcast_fusion.1, pred[64]{0:T(512)(128)(4,1)S(1)} %get-tuple-element.6), kind=kLoop, calls=%fused_computation.25 | loop fusion | flops 1146880 | bytes 1835328 | tf_op jit(solution)/shard_map/convert_element_type | solution.py:84
  90.9 12.3 %all-to-all-done.3 = bf16[4,34,3584]{2,1,0:T(8,128)(2,1)S(1)} async-done(((bf16[4,34,3584]{2,1,0:T(8,128)(2,1)}), bf16[4,34,3584]{2,1,0:T(8,128)(2,1)S(1)}, u32[]{:S(2)}, u32[]{:S(2)}) %all-to-all-start.3) | async-done | bytes 974880 | tf_op jit(solution)/shard_map/all_to_all | solution.py:104
  104.5 1.0 fusion.19
  105.4 1.3 %collective-permute-done = bf16[1,64,3584]{2,1,0:T(8,128)(2,1)} collective-permute-done((bf16[1,64,3584]{2,1,0:T(8,128)(2,1)}, bf16[1,64,3584]{2,1,0:T(8,128)(2,1)}, u32[]{:S(2)}, u32[]{:S(2)}) %collective-permute-start) | collective-permute-done | bytes 458784 | tf_op jit(solution)/shard_map/ppermute | solution.py:12
  106.8 1.8 %copy.35 = bf16[1,64,3584]{2,1,0:T(8,128)(2,1)} copy(bf16[1,64,3584]{2,1,0:T(8,128)(2,1)} %collective-permute-done) | data formatting | bytes 917504
  (48 shorter events, 7.6 us)
Async XLA Ops:
  0.6 16.2 %collective-permute-start.1 = (bf16[1,64,3584]{2,1,0:T(8,128)(2,1)}, bf16[1,64,3584]{2,1,0:T(8,128)(2,1)S(1)}, u32[]{:S(2)}, u32[]{:S(2)}) collective-permute-start(bf16[1,64,3584]{2,1,0:T(8,128)(2,1)} %param.16), channel_id=1, source_target_pairs={{4,0},{8,4},{12,8},{16,12},{20,16},{24,20},{28,24},{0,28},{5,1},{9... | collective-permute-start | bytes 1376264 | tf_op jit(solution)/shard_map/ppermute | solution.py:12
  10.4 4.8 %copy-start.5 = (s32[1,64,1]{1,2,0:T(1,128)S(1)}, s32[1,64,1]{1,2,0:T(1,128)}, u32[]{:S(2)}) copy-start(s32[1,64,1]{1,2,0:T(1,128)} %param.18) | copy-start | bytes 772
  10.6 5.0 %copy-start.6 = (f32[1,64,1]{1,2,0:T(1,128)S(1)}, f32[1,64,1]{1,2,0:T(1,128)}, u32[]{:S(2)}) copy-start(f32[1,64,1]{1,2,0:T(1,128)} %param.20) | copy-start | bytes 772
  11.7 19.0 %all-to-all-start = ((bf16[4,34,3584]{2,1,0:T(8,128)(2,1)}), bf16[4,34,3584]{2,1,0:T(8,128)(2,1)S(1)}, u32[]{:S(2)}, u32[]{:S(2)}) async-start(bf16[4,34,3584]{2,1,0:T(8,128)(2,1)} %bitcast.4), calls=%async_computation | async-start | bytes 2293760 | tf_op jit(solution)/shard_map/all_to_all | solution.py:70
  16.8 15.0 %copy-start.1 = (bf16[1,64,3584]{2,1,0:T(8,128)(2,1)}, bf16[1,64,3584]{2,1,0:T(8,128)(2,1)S(1)}, u32[]{:S(2)}) copy-start(bf16[1,64,3584]{2,1,0:T(8,128)(2,1)S(1)} %collective-permute-done.1) | copy-start | bytes 1376260
  17.2 18.9 %copy-start.7 = (f32[1,64,1]{1,2,0:T(1,128)S(1)}, f32[1,64,1]{1,2,0:T(1,128)}, u32[]{:S(2)}) copy-start(f32[1,64,1]{1,2,0:T(1,128)} %param.19) | copy-start | bytes 772
  31.8 19.8 %all-to-all-start.2 = ((bf16[4,34,3584]{2,1,0:T(8,128)(2,1)}), bf16[4,34,3584]{2,1,0:T(8,128)(2,1)}, u32[]{:S(2)}, u32[]{:S(2)}) async-start(bf16[4,34,3584]{2,1,0:T(8,128)(2,1)} %bitcast.14), calls=%async_computation.2 | async-start | bytes 2293760 | tf_op jit(solution)/shard_map/all_to_all | solution.py:90
  36.4 15.2 %copy-start.3 = (bf16[1,4,34,512]{3,1,2,0:T(4,128)(2,1)S(1)}, bf16[1,4,34,512]{3,1,2,0:T(4,128)(2,1)}, u32[]{:S(2)}) copy-start(bf16[1,4,34,512]{3,1,2,0:T(4,128)(2,1)} %param.14) | copy-start | bytes 417796
  36.4 15.2 %copy-start.4 = (bf16[1,4,34,512]{3,1,2,0:T(4,128)(2,1)S(1)}, bf16[1,4,34,512]{3,1,2,0:T(4,128)(2,1)}, u32[]{:S(2)}) copy-start(bf16[1,4,34,512]{3,1,2,0:T(4,128)(2,1)} %param.15) | copy-start | bytes 417796
  56.1 9.0 %all-to-all-start.4 = ((f32[4,1,34]{2,1,0:T(1,128)}), f32[4,1,34]{2,1,0:T(1,128)S(1)}, u32[]{:S(2)}, u32[]{:S(2)}) async-start(f32[4,1,34]{2,1,0:T(1,128)} %bitcast.25), calls=%async_computation.4 | async-start | bytes 4096 | tf_op jit(solution)/shard_map/all_to_all | solution.py:105
  65.1 19.0 %all-to-all-start.1 = ((bf16[4,34,3584]{2,1,0:T(8,128)(2,1)}), bf16[4,34,3584]{2,1,0:T(8,128)(2,1)S(1)}, u32[]{:S(2)}, u32[]{:S(2)}) async-start(bf16[4,34,3584]{2,1,0:T(8,128)(2,1)} %reshape.246), calls=%async_computation.1 | async-start | bytes 2293760 | tf_op jit(solution)/shard_map/all_to_all | solution.py:76
  68.6 3.5 %copy-start = (bf16[1,3584,512]{2,1,0:T(8,128)(2,1)S(1)}, bf16[1,3584,512]{2,1,0:T(8,128)(2,1)}, u32[]{:S(2)}) copy-start(bf16[1,3584,512]{2,1,0:T(8,128)(2,1)} %param.22) | copy-start | bytes 11010052
  84.1 19.0 %all-to-all-start.3 = ((bf16[4,34,3584]{2,1,0:T(8,128)(2,1)}), bf16[4,34,3584]{2,1,0:T(8,128)(2,1)S(1)}, u32[]{:S(2)}, u32[]{:S(2)}) async-start(bf16[4,34,3584]{2,1,0:T(8,128)(2,1)} %fusion), calls=%async_computation.3 | async-start | bytes 2293760 | tf_op jit(solution)/shard_map/all_to_all | solution.py:104
  90.9 15.9 %collective-permute-start = (bf16[1,64,3584]{2,1,0:T(8,128)(2,1)}, bf16[1,64,3584]{2,1,0:T(8,128)(2,1)}, u32[]{:S(2)}, u32[]{:S(2)}) collective-permute-start(bf16[1,64,3584]{2,1,0:T(8,128)(2,1)} %fusion.20), channel_id=1, source_target_pairs={{28,0},{0,4},{4,8},{8,12},{12,16},{16,20},{20,24},{24,28},{29,1},{... | collective-permute-start | bytes 1376264 | tf_op jit(solution)/shard_map/ppermute | solution.py:12
  103.4 1.0 copy-start.2
where the time goes:
time: 109 us
  waiting for transfers between devices  48.7 us (45%)
  starting transfers between devices  24.1 us (22%)
  matrix products  19.3 us (18%)
  local copies, waits for them, and re-layouts  8.86 us (8%)
  other arithmetic  6.62 us (6%)
    all_to_all x1, waiting for transfers between devices, body(): lax.all_to_all(send, 'expert', split_axis=0, concat_axis=0, tiled=True)  13.4 us
    all_to_all x1, waiting for transfers between devices, body(): lax.all_to_all(send_d, 'expert', split_axis=0, concat_axis=0, tiled=True)  12.4 us
    all_to_all x1, waiting for transfers between devices, body(): lax.all_to_all(dxe, 'expert', split_axis=0, concat_axis=0, tiled=True)  12.3 us
    all_to_all x1, waiting for transfers between devices, body(): lax.all_to_all(result.reshape(groups, capacity, depth), 'expert', split_a...  8.21 us
    ppermute x2, starting transfers between devices, from_behind(): return lax.ppermute(block, axis, route)  6.06 us
    dot_general x1, matrix products, body(): jnp.dot(hidden, wd, preferred_element_type=jnp.float32).astype(jnp.bfloat16)  4.46 us
    dot_general x1, matrix products, body(): jnp.einsum('scd,fd->scf', recv_d, wd, preferred_element_type=jnp.float32)  4.4 us
    all_to_all x1, starting transfers between devices, body(): lax.all_to_all(send_d, 'expert', split_axis=0, concat_axis=0, tiled=True)  4.26 us
  transfers between devices with their start and end apart: 7, of which 6 were waited for; matrix products, arithmetic and copies ran while one was open for 25% of the time, Pallas kernels for 0%

commit v1 on v0

v1 whole, which is shorter than its diff:
```python
import jax
import jax.numpy as jnp
from jax import lax
from jax.sharding import PartitionSpec as P

EXPERTS = 2


def from_behind(block, axis, distance):
    devices = range(lax.axis_size(axis))
    route = [((i - distance) % len(devices), i) for i in devices]
    return lax.ppermute(block, axis, route)


def across(block, distance, count, slices):
    route = [
        (e * slices + j, (e + distance) % count * slices + j)
        for e in range(count)
        for j in range(slices)
    ]
    return lax.ppermute(block, "expert", route)


def beside(block, distance, count, slices):
    route = [
        (e * slices + j, e * slices + (j + distance) % slices)
        for e in range(count)
        for j in range(slices)
    ]
    return lax.ppermute(block, "expert", route)


def ranks_of(routes, count):
    flat = routes.reshape(-1)
    tok = flat.shape[0]
    same = flat[:, None] == flat[None, :]
    earlier = jnp.arange(tok)[None, :] < jnp.arange(tok)[:, None]
    return flat, jnp.sum((same & earlier).astype(jnp.int32), axis=1)


def table_of(flat, rank, expert, capacity):
    return (
        (flat[None, :] == expert)
        & (rank[None, :] == jnp.arange(capacity, dtype=jnp.int32)[:, None])
    ).astype(jnp.bfloat16)


def body(
    x_fwd,
    saved_gate,
    saved_up,
    grad_next,
    routes_fwd,
    routes_bwd,
    scores_fwd,
    scores_bwd,
    w_gate,
    w_up,
    w_down,
):
    groups = lax.axis_size("expert")
    count = EXPERTS
    slices = groups // count
    me = lax.axis_index("expert")
    mine_e = me // slices
    mine_j = me % slices
    wg = w_gate[0]
    wu = w_up[0]
    wd = w_down[0]
    capacity = saved_gate.shape[2]
    depth = x_fwd.shape[2]
    f32 = jnp.float32

    def tables(routes):
        flat, rank = ranks_of(routes, count)
        return [table_of(flat, rank, (mine_e + d) % count, capacity) for d in range(count)]

    def pick(table, tokens):
        return jnp.dot(table, tokens, preferred_element_type=f32).astype(jnp.bfloat16)

    def dispatch(tabs, tokens):
        sent = [pick(tabs[d], tokens) for d in range(count)]
        got = [sent[0]] + [across(sent[d], d, count, slices) for d in range(1, count)]
        out = [got]
        for k in range(1, slices):
            out.append([beside(b, k, count, slices) for b in got])
        return jnp.concatenate([b for row in out for b in row], axis=0)

    def combine(parts):
        total = parts[0]
        for k in range(1, slices):
            total = total + beside(
                parts[k].astype(jnp.bfloat16), -k, count, slices
            ).astype(f32)
        back = [total[0]]
        for d in range(1, count):
            back.append(across(total[d].astype(jnp.bfloat16), -d, count, slices).astype(f32))
        return back

    def give(tabs, back, gate):
        rows = sum(
            lax.dot_general(
                t, b.astype(jnp.bfloat16), (((0,), (0,)), ((), ())), preferred_element_type=f32
            )
            for t, b in zip(tabs, back)
        )
        return gate * rows

    tokens = x_fwd[0]
    tabs_a = tables(routes_fwd[0])
    tabs_b = tables(routes_bwd[0])
    upstream = from_behind(grad_next, "section", -1)[0]

    flat = dispatch(tabs_a, tokens)
    g = jnp.dot(flat, wg, preferred_element_type=f32)
    u = jnp.dot(flat, wu, preferred_element_type=f32)
    hidden = (jax.nn.silu(g) * u).astype(jnp.bfloat16)
    parts = jnp.dot(hidden, wd, preferred_element_type=f32)
    back = combine(parts.reshape(slices, count, capacity, depth))
    gate_a = 2.5 * scores_fwd[0]
    layer_out = (tokens.astype(f32) + give(tabs_a, back, gate_a)).astype(jnp.bfloat16)
    next_input = from_behind(layer_out[None], "section", 1)

    recv_d = dispatch(tabs_b, upstream)
    order = [
        (mine_e - d) % count * slices + (mine_j - k) % slices
        for k in range(slices)
        for d in range(count)
    ]
    g = jnp.concatenate([saved_gate[0, q] for q in order], axis=0).astype(f32)
    u = jnp.concatenate([saved_up[0, q] for q in order], axis=0).astype(f32)
    sig = jax.nn.sigmoid(g)
    hidden = (jax.nn.silu(g) * u).astype(jnp.bfloat16)
    pulled = lax.dot_general(recv_d, wd, (((1,), (1,)), ((), ())), preferred_element_type=f32)
    dgp = (pulled * u * sig * (1.0 + g * (1.0 - sig))).astype(jnp.bfloat16)
    dup = (pulled * g * sig).astype(jnp.bfloat16)
    nt = (((1,), (1,)), ((), ()))
    dxe = lax.dot_general(dgp, wg, nt, preferred_element_type=f32) + lax.dot_general(
        dup, wu, nt, preferred_element_type=f32
    )
    inner = jnp.sum(pulled * hidden.astype(f32), axis=-1).reshape(slices, count, capacity)
    total = inner[0]
    for k in range(1, slices):
        total = total + beside(inner[k], -k, count, slices)
    home = [total[0]] + [across(total[d], -d, count, slices) for d in range(1, count)]
    dgate = sum(
        jnp.sum(t.astype(f32) * h[:, None], axis=0) for t, h in zip(tabs_b, home)
    )
    back = combine(dxe.reshape(slices, count, capacity, depth))
    gate_b = 2.5 * scores_bwd[0]
    input_grad = (upstream.astype(f32) + give(tabs_b, back, gate_b)).astype(jnp.bfloat16)
    score_grad = 2.5 * dgate
    return (next_input, input_grad[None], score_grad[None, :, None])


def solution(mesh):
    placed = (
        P("section", "expert", None),
        P("section", None, None, "expert"),
        P("section", None, None, "expert"),
        P("section", "expert", None),
        P("section", "expert", None),
        P("section", "expert", None),
        P("section", "expert", None),
        P("section", "expert", None),
        P("section", None, "expert"),
        P("section", None, "expert"),
        P("section", "expert", None),
    )
    return jax.shard_map(
        body,
        mesh=mesh,
        in_specs=placed,
        out_specs=(
            P("section", "expert", None),
            P("section", "expert", None),
            P("section", "expert", None),
        ),
        check_vma=False,
    )
```

time: 109 us -> 81.3 us (0.75)
  waiting for transfers between devices: 48.7 us -> 24.8 us
  starting transfers between devices: 24.1 us -> 15 us
  matrix products: 19.3 us -> 23 us
  local copies, waits for them, and re-layouts: 8.86 us -> 12 us
  other arithmetic: 6.62 us -> 4.95 us
    all_to_all x5 -> x0, waiting for transfers between devices: 46.3 us -> none  [the longest x1 13.4 us: body(): lax.all_to_all(send, 'expert', split_axis=0, concat_axis=0, tiled=True)]
    all_to_all x5 -> x0, starting transfers between devices: 18.1 us -> none  [the longest x1 4.26 us: body(): lax.all_to_all(send_d, 'expert', split_axis=0, concat_axis=0, tiled=True)]
    ppermute x0 -> x12, waiting for transfers between devices: none -> 13.3 us  [the longest x5 13.3 us: across(): return lax.ppermute(block, 'expert', route)]
    ppermute x2, waiting for transfers between devices: 2.44 us -> 11.5 us  [from_behind(): return lax.ppermute(block, axis, route)]
    ppermute x0 -> x12, starting transfers between devices: none -> 8.9 us  [the longest x5 7.78 us: across(): return lax.ppermute(block, 'expert', route)]
    slice x0 -> x5, local copies, waits for them, and re-layouts: none -> 4.6 us  [the longest x2 2.32 us: combine(): total = parts[0]]
    convert_element_type x4 -> x0, other arithmetic: 3.77 us -> none  [the longest x1 2 us: body(): (tokens.astype(jnp.float32) + jnp.sum(gate_a[:, :, None] * rows, axis=1))...]
    dot_general x7 -> x13, matrix products: 19.3 us -> 23 us  [the longest x1 5.83 us: body(): parts = jnp.dot(hidden, wd, preferred_element_type=f32)]
  transfers between devices with their start and end apart: 7 -> 14, of which waited for: 6 -> 5; matrix products, arithmetic and copies ran while one was open for 25% -> 47% of each run, Pallas kernels for 0% -> 0%
where the time goes in v1:
time: 81.3 us; the launch traced here: 80.8 us
  waiting for transfers between devices  24.8 us (31%)
  matrix products  23 us (28%)
  starting transfers between devices  15 us (18%)
  local copies, waits for them, and re-layouts  12 us (15%)
  other arithmetic  4.95 us (6%)
  between operations  1.01 us (1%)
    ppermute x5, waiting for transfers between devices, across(): return lax.ppermute(block, 'expert', route)  13.3 us
    ppermute x2, waiting for transfers between devices, from_behind(): return lax.ppermute(block, axis, route)  11.5 us
    ppermute x5, starting transfers between devices, across(): return lax.ppermute(block, 'expert', route)  7.78 us
    ppermute x2, starting transfers between devices, from_behind(): return lax.ppermute(block, axis, route)  6.12 us
    dot_general x1, matrix products, body(): parts = jnp.dot(hidden, wd, preferred_element_type=f32)  5.83 us
    dot_general x1, matrix products, body(): lax.dot_general(recv_d, wd, (((1,), (1,)), ((), ())), preferred_element_t...  3.87 us
    dot_general x4, matrix products, pick(): jnp.dot(table, tokens, preferred_element_type=f32).astype(jnp.bfloat16)  3.62 us
    dot_general x1, matrix products, body(): lax.dot_general(dgp, wg, nt, preferred_element_type=f32)  3.49 us
  transfers between devices with their start and end apart: 14, of which 5 were waited for; matrix products, arithmetic and copies ran while one was open for 47% of the time, Pallas kernels for 0%

profile of v1, /device:TPU:0, one launch (start us, length us, event | category | flops | bytes accessed | tf_op | source)
XLA Modules:
  0.0 80.8 jit_solution(5525711721865011561)
XLA Ops:
  0.6 6.1 %collective-permute-start.6 = (bf16[1,64,3584]{2,1,0:T(8,128)(2,1)}, bf16[1,64,3584]{2,1,0:T(8,128)(2,1)S(1)}, u32[]{:S(2)}, u32[]{:S(2)}) collective-permute-start(bf16[1,64,3584]{2,1,0:T(8,128)(2,1)} %param.14), channel_id=1, source_target_pairs={{4,0},{8,4},{12,8},{16,12},{20,16},{24,20},{28,24},{0,28},{5,1},{9... | collective-permute-start | bytes 1376264 | tf_op jit(solution)/shard_map/ppermute | solution.py:12
  8.3 1.2 %convolution_convert_fusion.2 = bf16[34,3584]{1,0:T(8,128)(2,1)S(1)} fusion(bf16[1,64,3584]{2,1,0:T(8,128)(2,1)} %param.11, s32[64]{0:T(128)S(1)} %convert_reduce_fusion.1, pred[64]{0:T(512)(128)(4,1)S(1)} %get-tuple-element.20), kind=kOutput, calls=%fused_computation.10 | convolution fusion | flops 15723776 | bytes 702784 | tf_op jit(solution)/shard_map/dot_general | solution.py:79
  9.5 1.6 %collective-permute-start = (bf16[34,3584]{1,0:T(8,128)(2,1)S(1)}, bf16[34,3584]{1,0:T(8,128)(2,1)S(1)}, u32[]{:S(2)}, u32[]{:S(2)}) collective-permute-start(bf16[34,3584]{1,0:T(8,128)(2,1)S(1)} %convolution_convert_fusion.2), channel_id=1, source_target_pairs={{0,2},{1,3},{2,0},{3,1},{4,6},{5,7},{6,4},{7,5},{8,10},{9,11},{10,... | collective-permute-start | bytes 731144 | tf_op jit(solution)/shard_map/ppermute | solution.py:21
  11.1 1.2 %convolution_convert_fusion.3 = bf16[34,3584]{1,0:T(8,128)(2,1)S(1)} fusion(bf16[1,64,3584]{2,1,0:T(8,128)(2,1)} %param.11, s32[64]{0:T(128)S(1)} %convert_reduce_fusion.1, pred[64]{0:T(512)(128)(4,1)S(1)} %get-tuple-element.19), kind=kOutput, calls=%fused_computation.11 | convolution fusion | flops 15723776 | bytes 702784 | tf_op jit(solution)/shard_map/dot_general | solution.py:79
  13.8 2.1 %constant_dynamic-slice_fusion.3 = (bf16[1,1,34,512]{3,1,2,0:T(2,128)(2,1)S(1)}, bf16[1,1,34,512]{3,1,2,0:T(2,128)(2,1)S(1)}, bf16[1,1,34,512]{3,1,2,0:T(2,128)(...) fusion(bf16[1,4,34,512]{3,1,2,0:T(4,128)(2,1)} %param.12, ...), kind=kLoop, calls=%fused_computation.112 | loop fusion | bytes 557072 | tf_op jit(solution)/shard_map/dynamic_slice | solution.py:130
  16.2 1.7 %collective-permute-done = bf16[34,3584]{1,0:T(8,128)(2,1)S(1)} collective-permute-done((bf16[34,3584]{1,0:T(8,128)(2,1)S(1)}, bf16[34,3584]{1,0:T(8,128)(2,1)S(1)}, u32[]{:S(2)}, u32[]{:S(2)}) %collective-permute-start) | collective-permute-done | bytes 243744 | tf_op jit(solution)/shard_map/ppermute | solution.py:21
  18.1 1.6 %collective-permute-start.7 = (bf16[34,3584]{1,0:T(8,128)(2,1)S(1)}, bf16[34,3584]{1,0:T(8,128)(2,1)}, u32[]{:S(2)}, u32[]{:S(2)}) collective-permute-start(bf16[34,3584]{1,0:T(8,128)(2,1)S(1)} %convolution_convert_fusion), channel_id=1, source_target_pairs={{0,2},{1,3},{2,0},{3,1},{4,6},{5,7},{6,4},{7,5},{8,10},{9,11},{10,... | collective-permute-start | bytes 731144 | tf_op jit(solution)/shard_map/ppermute | solution.py:21
  20.8 2.7 %fusion.10 = f32[136,512]{1,0:T(8,128)S(1)} fusion(bf16[1,3584,512]{2,1,0:T(8,128)(2,1)} %param.20, bf16[34,3584]{1,0:T(8,128)(2,1)S(1)} %collective-permute-done.2, bf16[34,3584]{1,0:T(8,128)(2,1)S(1)} %collective-permute-done.1, bf16[34,3584]{1,0:T(8,128)(2,1)S(1)} %collective-permute-done, bf16[34,3584]{1,0:T(8,128)(2,1)S(1)} %convolution_convert_fusion.3), kind=kOutput, calls=%fused_computation.17 | convolution fusion | flops 503021568 | bytes 4923392 | tf_op jit(solution)/shard_map/dot_general | solution.py:116
  23.6 4.0 %collective-permute-done.7 = bf16[34,3584]{1,0:T(8,128)(2,1)} collective-permute-done((bf16[34,3584]{1,0:T(8,128)(2,1)S(1)}, bf16[34,3584]{1,0:T(8,128)(2,1)}, u32[]{:S(2)}, u32[]{:S(2)}) %collective-permute-start.7) | collective-permute-done | bytes 243744 | tf_op jit(solution)/shard_map/ppermute | solution.py:21
  27.5 5.8 %fusion.7 = f32[136,3584]{1,0:T(8,128)} fusion(bf16[1,512,3584]{2,1,0:T(8,128)(2,1)} %param.21, f32[136,512]{1,0:T(8,128)S(1)} %fusion.10, bf16[1,3584,512]{2,1,0:T(8,128)(2,1)} %param.19, bf16[34,3584]{1,0:T(8,128)(2,1)S(1)} %collective-permute-done.2, bf16[34,3584]{1,0:T(8,128)(2,1)S(1)} %collective-permute-done.1, ...), kind=kOutput, calls=%fused_computation.14 | convolution fusion | flops 1002561536 | bytes 10543104 | tf_op jit(solution)/shard_map/dot_general | solution.py:118
  33.4 1.3 %slice.76 = f32[68,3584]{1,0:T(8,128)S(1)} slice(f32[136,3584]{1,0:T(8,128)} %fusion.7), slice={[0:68], [0:3584]} | slice | bytes 1949696 | tf_op jit(solution)/shard_map/slice | solution.py:90
  34.7 1.3 %slice.95 = bf16[68,3584]{1,0:T(8,128)(2,1)S(1)} slice(f32[136,3584]{1,0:T(8,128)} %fusion.7), slice={[68:136], [0:3584]} | slice | bytes 974848 | tf_op jit(solution)/shard_map/slice | solution.py:93
  36.2 1.2 %copy.34 = bf16[2,34,3584]{2,0,1:T(2,128)(2,1)} copy(bf16[2,34,3584]{2,1,0:T(8,128)(2,1)S(1)} %convert_element_type.104) | data formatting | bytes 974848 | tf_op jit(solution)/shard_map/convert_element_type | solution.py:93
  37.9 3.9 %multiply_reduce_fusion = (f32[136]{0:T(256)S(1)}, f32[136,512]{1,0:T(8,128)S(1)}) fusion(bf16[34,512]{1,0:T(8,128)(2,1)S(1)} %bitcast.101, bf16[34,512]{1,0:T(8,128)(2,1)S(1)} %bitcast.103, bf16[34,512]{1,0:T(8,128)(2,1)S(1)} %bitcast.105, bf16[34,512]{1,0:T(8,128)(2,1)S(1)} %bitcast.107, bf16[34,512]{1,0:T(8,128)(2,1)S(1)} %bitcast.89, ...), kind=kOutput, calls=%fused_computation.63 | convolution fusion | flops 504762240 | bytes 5202464 | tf_op jit(solution)/shard_map/dot_general | solution.py:134
  41.9 3.5 %fusion.12 = f32[136,3584]{1,0:T(8,128)S(1)} fusion(bf16[1,3584,512]{2,1,0:T(8,128)(2,1)} %param.19, f32[136,512]{1,0:T(8,128)S(1)} %get-tuple-element.22, bf16[34,512]{1,0:T(8,128)(2,1)S(1)} %bitcast.102, bf16[34,512]{1,0:T(8,128)(2,1)S(1)} %bitcast.104, bf16[34,512]{1,0:T(8,128)(2,1)S(1)} %bitcast.106, bf16[34,512]{1,0:T(8,128)(2,1)S(1)} %bitcast.108, ...), kind=kOutput, calls=%fused_computation.19 | convolution fusion | flops 500932608 | bytes 6176768 | tf_op jit(solution)/shard_map/dot_general | solution.py:138
  45.4 1.3 %convolution_add_fusion = f32[136,3584]{1,0:T(8,128)S(1)} fusion(f32[136,3584]{1,0:T(8,128)S(1)} %fusion.12, bf16[1,3584,512]{2,1,0:T(8,128)(2,1)S(1)} %copy-done.1, f32[136,512]{1,0:T(8,128)S(1)} %get-tuple-element.22, bf16[34,512]{1,0:T(8,128)(2,1)S(1)} %bitcast.91, bf16[34,512]{1,0:T(8,128)(2,1)S(1)} %bitcast.94, bf16[34,512]{1,0:T(8,128)(2,1)S(1)} %bitcast.97, ...), kind=kOutput, calls=%fused_computation | convolution fusion | flops 500584448 | bytes 7987200 | tf_op jit(solution)/shard_map/dot_general | solution.py:138
  48.8 1.3 %squeeze.76 = f32[2,34,3584]{2,1,0:T(8,128)S(1)} reshape(f32[68,3584]{1,0:T(8,128)} %slice.80) | data formatting | bytes 1949696 | tf_op jit(solution)/shard_map/squeeze | solution.py:90
  51.3 1.6 %collective-permute-start.13 = (f32[34]{0:T(128)S(1)}, f32[34]{0:T(128)S(1)}, u32[]{:S(2)}, u32[]{:S(2)}) collective-permute-start(f32[34]{0:T(128)S(1)} %get-tuple-element.14), channel_id=1, source_target_pairs={{0,2},{1,3},{2,0},{3,1},{4,6},{5,7},{6,4},{7,5},{8,10},{9,11},{10,... | collective-permute-start | bytes 416 | tf_op jit(solution)/shard_map/ppermute | solution.py:21
  53.5 1.4 %collective-permute-done.13 = f32[34]{0:T(128)S(1)} collective-permute-done((f32[34]{0:T(128)S(1)}, f32[34]{0:T(128)S(1)}, u32[]{:S(2)}, u32[]{:S(2)}) %collective-permute-start.13) | collective-permute-done | bytes 168 | tf_op jit(solution)/shard_map/ppermute | solution.py:21
  55.5 1.2 %add_convert_fusion.1 = bf16[2,34,3584]{2,1,0:T(8,128)(2,1)S(1)} fusion(f32[2,34,3584]{2,1,0:T(8,128)S(1)} %squeeze.66, bf16[2,34,3584]{2,0,1:T(2,128)(2,1)} %collective-permute-done.3), kind=kLoop, calls=%fused_computation.24 | loop fusion | flops 731136 | bytes 1949696 | tf_op jit(solution)/shard_map/convert.4
  56.7 1.6 %collective-permute-start.4 = (bf16[34,3584]{1,0:T(8,128)(2,1)S(1)}, bf16[34,3584]{1,0:T(8,128)(2,1)S(1)}, u32[]{:S(2)}, u32[]{:S(2)}) collective-permute-start(bf16[34,3584]{1,0:T(8,128)(2,1)S(1)} %slice_bitcast_fusion.3), channel_id=1, source_target_pairs={{0,2},{1,3},{2,0},{3,1},{4,6},{5,7},{6,4},{7,5},{8,10},{9,11},{10,... | collective-permute-start | bytes 731144 | tf_op jit(solution)/shard_map/ppermute | solution.py:21
  58.6 6.3 %collective-permute-done.4 = bf16[34,3584]{1,0:T(8,128)(2,1)S(1)} collective-permute-done((bf16[34,3584]{1,0:T(8,128)(2,1)S(1)}, bf16[34,3584]{1,0:T(8,128)(2,1)S(1)}, u32[]{:S(2)}, u32[]{:S(2)}) %collective-permute-start.4) | collective-permute-done | bytes 243744 | tf_op jit(solution)/shard_map/ppermute | solution.py:21
  65.5 1.6 %collective-permute-start.11 = (bf16[34,3584]{1,0:T(8,128)(2,1)S(1)}, bf16[34,3584]{1,0:T(8,128)(2,1)S(1)}, u32[]{:S(2)}, u32[]{:S(2)}) collective-permute-start(bf16[34,3584]{1,0:T(8,128)(2,1)S(1)} %slice_bitcast_fusion), channel_id=1, source_target_pairs={{0,2},{1,3},{2,0},{3,1},{4,6},{5,7},{6,4},{7,5},{8,10},{9,11},{10,... | collective-permute-start | bytes 731144 | tf_op jit(solution)/shard_map/ppermute | solution.py:21
  67.4 11.5 %collective-permute-done.5 = bf16[1,64,3584]{2,1,0:T(8,128)(2,1)S(1)} collective-permute-done((bf16[1,64,3584]{2,1,0:T(8,128)(2,1)S(1)}, bf16[1,64,3584]{2,1,0:T(8,128)(2,1)S(1)}, u32[]{:S(2)}, u32[]{:S(2)}) %collective-permute-start.5) | collective-permute-done | bytes 458784 | tf_op jit(solution)/shard_map/ppermute | solution.py:12
  (60 shorter events, 13.1 us)
Async XLA Ops:
  0.6 15.2 %copy-start.2 = (s32[1,64,1]{1,2,0:T(1,128)S(1)}, s32[1,64,1]{1,2,0:T(1,128)}, u32[]{:S(2)}) copy-start(s32[1,64,1]{1,2,0:T(1,128)} %param.16) | copy-start | bytes 772
  0.6 17.3 %collective-permute-start.6 = (bf16[1,64,3584]{2,1,0:T(8,128)(2,1)}, bf16[1,64,3584]{2,1,0:T(8,128)(2,1)S(1)}, u32[]{:S(2)}, u32[]{:S(2)}) collective-permute-start(bf16[1,64,3584]{2,1,0:T(8,128)(2,1)} %param.14), channel_id=1, source_target_pairs={{4,0},{8,4},{12,8},{16,12},{20,16},{24,20},{28,24},{0,28},{5,1},{9... | collective-permute-start | bytes 1376264 | tf_op jit(solution)/shard_map/ppermute | solution.py:12
  9.5 8.4 %collective-permute-start = (bf16[34,3584]{1,0:T(8,128)(2,1)S(1)}, bf16[34,3584]{1,0:T(8,128)(2,1)S(1)}, u32[]{:S(2)}, u32[]{:S(2)}) collective-permute-start(bf16[34,3584]{1,0:T(8,128)(2,1)S(1)} %convolution_convert_fusion.2), channel_id=1, source_target_pairs={{0,2},{1,3},{2,0},{3,1},{4,6},{5,7},{6,4},{7,5},{8,10},{9,11},{10,... | collective-permute-start | bytes 731144 | tf_op jit(solution)/shard_map/ppermute | solution.py:21
  12.3 8.5 %collective-permute-start.1 = (bf16[34,3584]{1,0:T(8,128)(2,1)S(1)}, bf16[34,3584]{1,0:T(8,128)(2,1)S(1)}, u32[]{:S(2)}, u32[]{:S(2)}) collective-permute-start(bf16[34,3584]{1,0:T(8,128)(2,1)S(1)} %convolution_convert_fusion.3), channel_id=1, source_target_pairs={{0,1},{1,0},{2,3},{3,2},{4,5},{5,4},{6,7},{7,6},{8,9},{9,8},{10,11... | collective-permute-start | bytes 731144 | tf_op jit(solution)/shard_map/ppermute | solution.py:30
  17.9 3.0 %collective-permute-start.2 = (bf16[34,3584]{1,0:T(8,128)(2,1)S(1)}, bf16[34,3584]{1,0:T(8,128)(2,1)S(1)}, u32[]{:S(2)}, u32[]{:S(2)}) collective-permute-start(bf16[34,3584]{1,0:T(8,128)(2,1)S(1)} %collective-permute-done), channel_id=1, source_target_pairs={{0,1},{1,0},{2,3},{3,2},{4,5},{5,4},{6,7},{7,6},{8,9},{9,8},{10,11... | collective-permute-start | bytes 731144 | tf_op jit(solution)/shard_map/ppermute | solution.py:30
  18.1 9.4 %collective-permute-start.7 = (bf16[34,3584]{1,0:T(8,128)(2,1)S(1)}, bf16[34,3584]{1,0:T(8,128)(2,1)}, u32[]{:S(2)}, u32[]{:S(2)}) collective-permute-start(bf16[34,3584]{1,0:T(8,128)(2,1)S(1)} %convolution_convert_fusion), channel_id=1, source_target_pairs={{0,2},{1,3},{2,0},{3,1},{4,6},{5,7},{6,4},{7,5},{8,10},{9,11},{10,... | collective-permute-start | bytes 731144 | tf_op jit(solution)/shard_map/ppermute | solution.py:21
  20.6 17.3 %collective-permute-start.8 = (bf16[34,3584]{1,0:T(8,128)(2,1)}, bf16[34,3584]{1,0:T(8,128)(2,1)}, u32[]{:S(2)}, u32[]{:S(2)}) collective-permute-start(bf16[34,3584]{1,0:T(8,128)(2,1)} %convolution_convert_fusion.1), channel_id=1, source_target_pairs={{0,1},{1,0},{2,3},{3,2},{4,5},{5,4},{6,7},{7,6},{8,9},{9,8},{10,11... | collective-permute-start | bytes 731144 | tf_op jit(solution)/shard_map/ppermute | solution.py:30
  27.5 10.3 %collective-permute-start.9 = (bf16[34,3584]{1,0:T(8,128)(2,1)}, bf16[34,3584]{1,0:T(8,128)(2,1)}, u32[]{:S(2)}, u32[]{:S(2)}) collective-permute-start(bf16[34,3584]{1,0:T(8,128)(2,1)} %collective-permute-done.7), channel_id=1, source_target_pairs={{0,1},{1,0},{2,3},{3,2},{4,5},{5,4},{6,7},{7,6},{8,9},{9,8},{10,11... | collective-permute-start | bytes 731144 | tf_op jit(solution)/shard_map/ppermute | solution.py:30
  37.4 18.2 %collective-permute-start.3 = (bf16[2,34,3584]{2,0,1:T(2,128)(2,1)}, bf16[2,34,3584]{2,0,1:T(2,128)(2,1)}, u32[]{:S(2)}, u32[]{:S(2)}) collective-permute-start(bf16[2,34,3584]{2,0,1:T(2,128)(2,1)} %copy.34), channel_id=1, source_target_pairs={{0,1},{1,0},{2,3},{3,2},{4,5},{5,4},{6,7},{7,6},{8,9},{9,8},{10,11... | collective-permute-start | bytes 1462280 | tf_op jit(solution)/shard_map/ppermute | solution.py:30
  41.9 9.4 %collective-permute-start.12 = (f32[2,34]{1,0:T(2,128)S(1)}, f32[2,34]{1,0:T(2,128)S(1)}, u32[]{:S(2)}, u32[]{:S(2)}) collective-permute-start(f32[2,34]{1,0:T(2,128)S(1)} %squeeze.78), channel_id=1, source_target_pairs={{0,1},{1,0},{2,3},{3,2},{4,5},{5,4},{6,7},{7,6},{8,9},{9,8},{10,11... | collective-permute-start | bytes 824 | tf_op jit(solution)/shard_map/ppermute | solution.py:30
  41.9 3.5 %copy-start.1 = (bf16[1,3584,512]{2,1,0:T(8,128)(2,1)S(1)}, bf16[1,3584,512]{2,1,0:T(8,128)(2,1)}, u32[]{:S(2)}) copy-start(bf16[1,3584,512]{2,1,0:T(8,128)(2,1)} %param.20) | copy-start | bytes 11010052
  51.3 3.6 %collective-permute-start.13 = (f32[34]{0:T(128)S(1)}, f32[34]{0:T(128)S(1)}, u32[]{:S(2)}, u32[]{:S(2)}) collective-permute-start(f32[34]{0:T(128)S(1)} %get-tuple-element.14), channel_id=1, source_target_pairs={{0,2},{1,3},{2,0},{3,1},{4,6},{5,7},{6,4},{7,5},{8,10},{9,11},{10,... | collective-permute-start | bytes 416 | tf_op jit(solution)/shard_map/ppermute | solution.py:21
  53.2 12.1 %collective-permute-start.10 = (bf16[2,34,3584]{2,0,1:T(2,128)(2,1)S(1)}, bf16[2,34,3584]{2,0,1:T(2,128)(2,1)S(1)}, u32[]{:S(2)}, u32[]{:S(2)}) collective-permute-start(bf16[2,34,3584]{2,0,1:T(2,128)(2,1)S(1)} %copy.44), channel_id=1, source_target_pairs={{0,1},{1,0},{2,3},{3,2},{4,5},{5,4},{6,7},{7,6},{8,9},{9,8},{10,11... | collective-permute-start | bytes 1462280 | tf_op jit(solution)/shard_map/ppermute | solution.py:30
  55.5 9.4 %copy-start = (bf16[1,64,3584]{2,1,0:T(8,128)(2,1)S(1)}, bf16[1,64,3584]{2,1,0:T(8,128)(2,1)}, u32[]{:S(2)}) copy-start(bf16[1,64,3584]{2,1,0:T(8,128)(2,1)} %param.11) | copy-start | bytes 1376260
  56.7 8.2 %collective-permute-start.4 = (bf16[34,3584]{1,0:T(8,128)(2,1)S(1)}, bf16[34,3584]{1,0:T(8,128)(2,1)S(1)}, u32[]{:S(2)}, u32[]{:S(2)}) collective-permute-start(bf16[34,3584]{1,0:T(8,128)(2,1)S(1)} %slice_bitcast_fusion.3), channel_id=1, source_target_pairs={{0,2},{1,3},{2,0},{3,1},{4,6},{5,7},{6,4},{7,5},{8,10},{9,11},{10,... | collective-permute-start | bytes 731144 | tf_op jit(solution)/shard_map/ppermute | solution.py:21
  65.3 13.6 %collective-permute-start.5 = (bf16[1,64,3584]{2,1,0:T(8,128)(2,1)S(1)}, bf16[1,64,3584]{2,1,0:T(8,128)(2,1)S(1)}, u32[]{:S(2)}, u32[]{:S(2)}) collective-permute-start(bf16[1,64,3584]{2,1,0:T(8,128)(2,1)S(1)} %fusion.4), channel_id=1, source_target_pairs={{28,0},{0,4},{4,8},{8,12},{12,16},{16,20},{20,24},{24,28},{29,1},{... | collective-permute-start | bytes 1376264 | tf_op jit(solution)/shard_map/ppermute | solution.py:12
  65.5 13.4 %collective-permute-start.11 = (bf16[34,3584]{1,0:T(8,128)(2,1)S(1)}, bf16[34,3584]{1,0:T(8,128)(2,1)S(1)}, u32[]{:S(2)}, u32[]{:S(2)}) collective-permute-start(bf16[34,3584]{1,0:T(8,128)(2,1)S(1)} %slice_bitcast_fusion), channel_id=1, source_target_pairs={{0,2},{1,3},{2,0},{3,1},{4,6},{5,7},{6,4},{7,5},{8,10},{9,11},{10,... | collective-permute-start | bytes 731144 | tf_op jit(solution)/shard_map/ppermute | solution.py:21

commit v2 on v0

v2 whole, which is shorter than its diff:
```python
import functools

import jax
import jax.numpy as jnp
from jax import lax
from jax.experimental import pallas as pl
from jax.experimental.pallas import tpu as pltpu
from jax.sharding import PartitionSpec as P

EXPERTS = 2
LANES = 128
F32 = jnp.float32
BF16 = jnp.bfloat16
NT = (((1,), (1,)), ((), ()))


class Sizes:
    def __init__(self, cap, depth, count, slices, tok):
        self.cap, self.depth, self.count, self.slices, self.tok = cap, depth, count, slices, tok
        self.main = cap // 16 * 16
        self.extra = cap - self.main
        self.folds = depth // LANES
        assert self.folds < self.main and depth % LANES == 0
        self.width = depth + LANES * self.extra
        self.blocks = count * slices
        self.tail_rows = -(-(self.blocks * self.extra) // 16) * 16
        self.rows = self.blocks * self.main + self.tail_rows


def from_behind(block, axis, distance):
    devices = range(lax.axis_size(axis))
    route = [((i - distance) % len(devices), i) for i in devices]
    return lax.ppermute(block, axis, route)


def across(block, distance, s):
    route = [
        (e * s.slices + j, (e + distance) % s.count * s.slices + j)
        for e in range(s.count)
        for j in range(s.slices)
    ]
    return lax.ppermute(block, "expert", route)


def beside(block, distance, s):
    route = [
        (e * s.slices + j, e * s.slices + (j + distance) % s.slices)
        for e in range(s.count)
        for j in range(s.slices)
    ]
    return lax.ppermute(block, "expert", route)


def iota(shape, dim):
    return lax.broadcasted_iota(jnp.int32, shape, dim).astype(F32)


def as_column(row):
    n = row.shape[1]
    return jnp.sum(
        jnp.where(iota((n, n), 0) == iota((n, n), 1), row, 0.0), axis=1, keepdims=True
    )


def own_expert(s):
    return lax.axis_index("expert") // s.slices


def expert_at(s, distance):
    return ((own_expert(s) + distance) % s.count).astype(F32)


def slot_rows(route_row, s):
    col = as_column(route_row)
    n = s.tok
    same = (col == route_row) & (iota((n, n), 0) < iota((n, n), 1))
    return jnp.sum(jnp.where(same, 1.0, 0.0), axis=0, keepdims=True)


def slot_columns(route_row, s):
    col = as_column(route_row)
    n = s.tok
    same = (col == route_row) & (iota((n, n), 1) < iota((n, n), 0))
    return col, jnp.sum(jnp.where(same, 1.0, 0.0), axis=1, keepdims=True)


def fold(values_ref, first, tail_ref, s):
    for j in range(s.extra):
        for r in range(s.folds):
            tail_ref[r : r + 1, j * LANES : (j + 1) * LANES] = values_ref[
                first + j : first + j + 1, r * LANES : (r + 1) * LANES
            ]


def unfold(tail_ref, values_ref, first, s):
    for j in range(s.extra):
        for r in range(s.folds):
            values_ref[first + j : first + j + 1, r * LANES : (r + 1) * LANES] = tail_ref[
                r : r + 1, j * LANES : (j + 1) * LANES
            ]


def slot_values(route_row, value_row, expert, s):
    rank = slot_rows(route_row, s)
    hit = route_row == expert
    main = jnp.sum(
        jnp.where(hit & (rank == iota((s.main, s.tok), 0)), value_row, 0.0), axis=1, keepdims=True
    )
    extra = [
        jnp.sum(jnp.where(hit & (rank == float(s.main + j)), value_row, 0.0), axis=1, keepdims=True)
        for j in range(s.extra)
    ]
    return main, extra


def add_gated(out_ref, base_ref, main, extra, total, s):
    d = s.depth
    out_ref[:, :d] = (base_ref[:, :d].astype(F32) + main * total[:, :d]).astype(BF16)
    for j in range(s.extra):
        at = slice(d + j * LANES, d + (j + 1) * LANES)
        out_ref[:, at] = (base_ref[:, at].astype(F32) + extra[j] * total[:, at]).astype(BF16)


def pack_kernel(s, route_ref, x_ref, *rest):
    outs, (extra_ref, tail_ref) = rest[: s.count], rest[s.count :]
    route_row = route_ref[...].astype(F32)
    rank = slot_rows(route_row, s)
    high = s.main + 16
    slots = iota((high, s.tok), 0)
    tail_ref[...] = jnp.zeros_like(tail_ref)
    for d in range(s.count):
        hit = route_row == expert_at(s, d)
        table = jnp.where(hit & (rank == slots), 1.0, 0.0).astype(BF16)
        rows = jnp.dot(table, x_ref[...], preferred_element_type=F32)
        outs[d][:, : s.depth] = rows[: s.main].astype(BF16)
        extra_ref[...] = rows[s.main :]
        fold(extra_ref, 0, tail_ref, s)
        outs[d][:, s.depth :] = tail_ref[...].astype(BF16)


def gather_packs(packs, rows_ref, extra_ref, tail_ref, s):
    extra_ref[...] = jnp.zeros_like(extra_ref)
    for i, pack in enumerate(packs):
        rows_ref[i * s.main : (i + 1) * s.main, :] = pack[:, : s.depth]
        tail_ref[...] = pack[:, s.depth : s.width].astype(F32)
        unfold(tail_ref, extra_ref, i * s.extra, s)
    rows_ref[s.blocks * s.main :, :] = extra_ref[...].astype(BF16)


def scatter_chunk(value, outs, extra_ref, at, s):
    for i in range(s.blocks):
        outs[i // s.count][i % s.count, :, at] = value[i * s.main : (i + 1) * s.main].astype(BF16)
    extra_ref[:, at] = value[s.blocks * s.main :]


def scatter_tails(outs, extra_ref, tail_ref, s):
    for i in range(s.blocks):
        fold(extra_ref, i * s.extra, tail_ref, s)
        outs[i // s.count][i % s.count, :, s.depth : s.width] = tail_ref[...].astype(BF16)


def chunk_of(depth):
    for chunk in (512, 256, 128):
        if depth % chunk == 0:
            return chunk


def forward_kernel(s, *refs):
    packs = refs[: s.blocks]
    wg, wu, wd = refs[s.blocks : s.blocks + 3]
    outs = refs[s.blocks + 3 : s.blocks + 3 + s.slices]
    wg_v, wu_v, wd_v, rows_ref, extra_ref, tail_ref, sems = refs[s.blocks + 3 + s.slices :]
    chunk = wd_v.shape[2]
    steps = s.depth // chunk
    up, down = [], []
    for c in range(steps):
        at = pl.ds(c * chunk, chunk)
        up.append(
            (
                pltpu.make_async_copy(wg.at[at, :], wg_v.at[c], sems.at[0, c]),
                pltpu.make_async_copy(wu.at[at, :], wu_v.at[c], sems.at[1, c]),
            )
        )
        down.append(pltpu.make_async_copy(wd.at[:, at], wd_v.at[c], sems.at[2, c]))
    for pair in up:
        for copy in pair:
            copy.start()
    for copy in down:
        copy.start()
    gather_packs(packs, rows_ref, extra_ref, tail_ref, s)
    g = u = None
    for c in range(steps):
        for copy in up[c]:
            copy.wait()
        lhs = rows_ref[:, c * chunk : (c + 1) * chunk]
        more_g = jnp.dot(lhs, wg_v[c], preferred_element_type=F32)
        more_u = jnp.dot(lhs, wu_v[c], preferred_element_type=F32)
        g = more_g if g is None else g + more_g
        u = more_u if u is None else u + more_u
    hidden = (g * jax.nn.sigmoid(g) * u).astype(BF16)
    tail_ref[...] = jnp.zeros_like(tail_ref)
    for c in range(steps):
        down[c].wait()
        part = jnp.dot(hidden, wd_v[c], preferred_element_type=F32)
        scatter_chunk(part, outs, extra_ref, slice(c * chunk, (c + 1) * chunk), s)
    scatter_tails(outs, extra_ref, tail_ref, s)


def saved_kernel(s, gate_ref, up_ref, c1_ref, c2_ref, hb_ref, g_ref, u_ref):
    me = lax.axis_index("expert")
    e, j = me // s.slices, me % s.slices
    g_ref[...] = jnp.zeros_like(g_ref)
    u_ref[...] = jnp.zeros_like(u_ref)
    for i in range(s.blocks):
        k, d = i // s.count, i % s.count
        source = (e + s.count - d) % s.count * s.slices + (j + s.slices - k) % s.slices
        for src, dst in ((gate_ref, g_ref), (up_ref, u_ref)):
            rows = src[source].astype(F32)
            dst[i * s.main : (i + 1) * s.main, :] = rows[: s.main]
            first = s.blocks * s.main + i * s.extra
            dst[first : first + s.extra, :] = rows[s.main :]
    g = g_ref[...]
    u = u_ref[...]
    sig = jax.nn.sigmoid(g)
    c1_ref[...] = u * sig * (1.0 + g * (1.0 - sig))
    c2_ref[...] = g * sig
    hb_ref[...] = (g * sig * u).astype(BF16).astype(F32)


def split_three(value):
    high = value.astype(BF16).astype(F32)
    rest = value - high
    mid = rest.astype(BF16).astype(F32)
    return high, mid, (rest - mid).astype(BF16).astype(F32)


def put_inner(main, extra, s):
    lane = iota((s.main, LANES), 1)
    row = iota((s.main, LANES), 0)
    out = jnp.zeros((s.main, LANES), F32)
    for p, piece in enumerate(split_three(main)):
        out = jnp.where(lane == float(p), piece, out)
    for j in range(s.extra):
        for p, piece in enumerate(split_three(extra[j])):
            out = jnp.where((lane == float(3 + p)) & (row == float(j)), piece, out)
    return out.astype(BF16)


def get_inner(block, s):
    lane = iota((s.main, LANES), 1)
    row = iota((s.main, LANES), 0)
    main = jnp.sum(jnp.where(lane < 3.0, block, 0.0), axis=1, keepdims=True)
    second = jnp.sum(
        jnp.where((lane >= 3.0) & (lane < 6.0), block, 0.0), axis=1, keepdims=True
    )
    extra = [
        jnp.sum(jnp.where(row[:, :1] == float(j), second, 0.0), axis=0, keepdims=True)
        for j in range(s.extra)
    ]
    return main, extra


def backward_kernel(s, *refs):
    packs = refs[: s.blocks]
    c1, c2, hb, wg, wu, wd = refs[s.blocks : s.blocks + 6]
    outs = refs[s.blocks + 6 : s.blocks + 6 + s.slices]
    wg_v, wu_v, wd_v, rows_ref, extra_ref, tail_ref, sems = refs[s.blocks + 6 + s.slices :]
    chunk = wd_v.shape[2]
    steps = s.depth // chunk
    up, down = [], []
    for c in range(steps):
        at = pl.ds(c * chunk, chunk)
        up.append(
            (
                pltpu.make_async_copy(wg.at[at, :], wg_v.at[c], sems.at[0, c]),
                pltpu.make_async_copy(wu.at[at, :], wu_v.at[c], sems.at[1, c]),
            )
        )
        down.append(pltpu.make_async_copy(wd.at[:, at], wd_v.at[c], sems.at[2, c]))
    for copy in down:
        copy.start()
    for pair in up:
        for copy in pair:
            copy.start()
    gather_packs(packs, rows_ref, extra_ref, tail_ref, s)
    a = None
    for c in range(steps):
        down[c].wait()
        lhs = rows_ref[:, c * chunk : (c + 1) * chunk]
        more = lax.dot_general(lhs, wd_v[c], NT, preferred_element_type=F32)
        a = more if a is None else a + more
    dgp = (a * c1[...]).astype(BF16)
    dup = (a * c2[...]).astype(BF16)
    inner = jnp.sum(a * hb[...], axis=1, keepdims=True)
    for i in range(s.blocks):
        first = s.blocks * s.main + i * s.extra
        outs[i // s.count][i % s.count, :, s.width :] = put_inner(
            inner[i * s.main : (i + 1) * s.main],
            [inner[first + j : first + j + 1] for j in range(s.extra)],
            s,
        )
    tail_ref[...] = jnp.zeros_like(tail_ref)
    for c in range(steps):
        for copy in up[c]:
            copy.wait()
        part = lax.dot_general(dgp, wg_v[c], NT, preferred_element_type=F32) + lax.dot_general(
            dup, wu_v[c], NT, preferred_element_type=F32
        )
        scatter_chunk(part, outs, extra_ref, slice(c * chunk, (c + 1) * chunk), s)
    scatter_tails(outs, extra_ref, tail_ref, s)


def total_of(parts, d):
    total = parts[0][d].astype(F32)
    for part in parts[1:]:
        total = total + part[d].astype(F32)
    return total


def forward_sum_kernel(s, *refs):
    parts = refs[: s.slices]
    own, route_ref, score_ref = refs[s.slices : s.slices + 3]
    y_ref, backs = refs[s.slices + 3], refs[s.slices + 4 :]
    for d in range(1, s.count):
        backs[d - 1][...] = total_of(parts, d).astype(BF16)
    route_row = route_ref[...].astype(F32)
    main, extra = slot_values(route_row, 2.5 * score_ref[...], expert_at(s, 0), s)
    add_gated(y_ref, own, main, extra, total_of(parts, 0), s)
    y_ref[s.folds : s.folds + 1, s.depth : s.depth + s.tok] = route_row.astype(BF16)


def forward_add_kernel(s, distance, back, base, route_ref, score_ref, y_ref):
    route_row = route_ref[...].astype(F32)
    main, extra = slot_values(route_row, 2.5 * score_ref[...], expert_at(s, distance), s)
    add_gated(y_ref, base, main, extra, back[...].astype(F32), s)


def tokens_of(packs, route_row, rows_ref, extra_ref, tail_ref, s):
    extra_ref[...] = jnp.zeros_like(extra_ref)
    for d, pack in enumerate(packs):
        rows_ref[d * s.main : (d + 1) * s.main, :] = pack[:, : s.depth]
        tail_ref[...] = pack[:, s.depth : s.width].astype(F32)
        unfold(tail_ref, extra_ref, d * s.extra, s)
    rows_ref[s.count * s.main :, :] = extra_ref[...].astype(BF16)
    col, rank = slot_columns(route_row, s)
    high = rows_ref.shape[0]
    place = jnp.full((s.tok, 1), -1.0, F32)
    for d in range(s.count):
        at = jnp.where(
            rank < float(s.main),
            rank + float(d * s.main),
            rank + float(s.count * s.main + d * s.extra - s.main),
        )
        place = jnp.where(col == expert_at(s, d), at, place)
    table = jnp.where(place == iota((s.tok, high), 1), 1.0, 0.0).astype(BF16)
    return jnp.dot(table, rows_ref[...], preferred_element_type=F32)


def forward_end_kernel(s, *refs):
    packs = refs[: s.count]
    out_ref, rows_ref, extra_ref, tail_ref, row_ref = refs[s.count :]
    row_ref[...] = packs[0][:, s.depth : s.depth + LANES].astype(F32)
    route_row = row_ref[s.folds : s.folds + 1, : s.tok]
    out_ref[...] = tokens_of(packs, route_row, rows_ref, extra_ref, tail_ref, s).astype(BF16)


def backward_sum_kernel(s, *refs):
    parts, outs = refs[: s.slices], refs[s.slices :]
    for d in range(s.count - 1, -1, -1):
        total = total_of(parts, d)
        outs[d][:, : s.width] = total[:, : s.width].astype(BF16)
        main, extra = get_inner(total[:, s.width :], s)
        outs[d][:, s.width :] = put_inner(main, extra, s)


def backward_end_kernel(s, *refs):
    packs = refs[: s.count]
    dy_ref, route_ref, score_ref, out_ref, grad_ref = refs[s.count : s.count + 5]
    rows_ref, extra_ref, tail_ref = refs[s.count + 5 :]
    route_row = route_ref[...].astype(F32)
    rows = tokens_of(packs, route_row, rows_ref, extra_ref, tail_ref, s)
    gate = as_column(2.5 * score_ref[...])
    out_ref[...] = (dy_ref[...].astype(F32) + gate * rows).astype(BF16)
    rank = slot_rows(route_row, s)
    dgate = jnp.zeros((1, s.tok), F32)
    for d in range(s.count):
        hit = route_row == expert_at(s, d)
        main, extra = get_inner(packs[d][:, s.width :].astype(F32), s)
        dgate += jnp.sum(
            jnp.where(hit & (rank == iota((s.main, s.tok), 0)), main, 0.0), axis=0, keepdims=True
        )
        for j in range(s.extra):
            dgate += jnp.where(hit & (rank == float(s.main + j)), extra[j], 0.0)
    grad_ref[...] = 2.5 * dgate


VMEM = pl.BlockSpec(memory_space=pltpu.VMEM)
HBM = pl.BlockSpec(memory_space=pl.ANY)


def call(kernel, name, outs, scratch, ins, *args, mib=16, flops=0):
    shapes = [jax.ShapeDtypeStruct(shape, kind) for shape, kind in outs]
    size = sum(a.size * a.dtype.itemsize for a in args)
    return pl.pallas_call(
        kernel,
        out_shape=shapes,
        in_specs=ins,
        out_specs=[VMEM] * len(shapes),
        scratch_shapes=scratch,
        compiler_params=pltpu.CompilerParams(vmem_limit_bytes=mib << 20),
        cost_estimate=pl.CostEstimate(flops=flops, bytes_accessed=size, transcendentals=0),
        name=name,
    )(*args)


def tail_scratch(s, rows):
    return [
        pltpu.VMEM((rows, s.depth), F32),
        pltpu.VMEM((s.main, LANES * s.extra), F32),
    ]


def pack(s, routes, tokens):
    return call(
        functools.partial(pack_kernel, s),
        "pack",
        [((s.main, s.width), BF16)] * s.count,
        tail_scratch(s, 16),
        [VMEM, VMEM],
        routes,
        tokens,
    )


def weight_scratch(s, hidden):
    chunk = chunk_of(s.depth)
    steps = s.depth // chunk
    return [
        pltpu.VMEM((steps, chunk, hidden), BF16),
        pltpu.VMEM((steps, chunk, hidden), BF16),
        pltpu.VMEM((steps, hidden, chunk), BF16),
        pltpu.VMEM((s.rows, s.depth), BF16),
        *tail_scratch(s, s.tail_rows),
        pltpu.SemaphoreType.DMA((3, steps)),
    ]


def dispatch(s, packs):
    got = [packs[0]] + [across(packs[d], d, s) for d in range(1, s.count)]
    out = list(got)
    for k in range(1, s.slices):
        out += [beside(b, k, s) for b in got]
    return out


def gather_parts(s, parts):
    return [parts[0]] + [beside(parts[k], -k, s) for k in range(1, s.slices)]


def end_scratch(s):
    low = -(-(s.count * s.extra) // 16) * 16
    return [pltpu.VMEM((s.count * s.main + low, s.depth), BF16), *tail_scratch(s, low)]


def body(
    x_fwd,
    saved_gate,
    saved_up,
    grad_next,
    routes_fwd,
    routes_bwd,
    scores_fwd,
    scores_bwd,
    w_gate,
    w_up,
    w_down,
):
    groups = lax.axis_size("expert")
    tok, depth = x_fwd.shape[1:]
    s = Sizes(saved_gate.shape[2], depth, EXPERTS, groups // EXPERTS, tok)
    hidden = w_gate.shape[2]
    weights = (w_gate[0], w_up[0], w_down[0])
    flops = 6 * s.rows * depth * hidden
    route_a = routes_fwd.reshape(1, tok)
    route_b = routes_bwd.reshape(1, tok)
    score_a = scores_fwd.reshape(1, tok)
    score_b = scores_bwd.reshape(1, tok)

    sent_a = pack(s, route_a, x_fwd[0])
    rows_a = dispatch(s, sent_a)
    upstream = from_behind(grad_next, "section", -1)[0]

    parts_a = call(
        functools.partial(forward_kernel, s),
        "forward",
        [((s.count, s.main, s.width), BF16)] * s.slices,
        weight_scratch(s, hidden),
        [VMEM] * s.blocks + [HBM] * 3,
        *rows_a,
        *weights,
        mib=32,
        flops=flops,
    )
    parts_a = gather_parts(s, parts_a)
    sums = call(
        functools.partial(forward_sum_kernel, s),
        "forward_sum",
        [((s.main, s.width), BF16)] * s.count,
        [],
        [VMEM] * (s.slices + 3),
        *parts_a,
        sent_a[0],
        route_a,
        score_a,
    )
    moved = [from_behind(sums[0], "section", 1)]
    for d in range(1, s.count):
        back = across(sums[d], -d, s)
        y = call(
            functools.partial(forward_add_kernel, s, d),
            "forward_add",
            [((s.main, s.width), BF16)],
            [],
            [VMEM] * 4,
            back,
            sent_a[d],
            route_a,
            score_a,
        )[0]
        moved.append(from_behind(y, "section", 1))
    next_input = call(
        functools.partial(forward_end_kernel, s),
        "forward_end",
        [((tok, depth), BF16)],
        end_scratch(s) + [pltpu.VMEM((s.main, LANES), F32)],
        [VMEM] * s.count,
        *moved,
    )[0]

    sent_b = pack(s, route_b, upstream)
    rows_b = dispatch(s, sent_b)
    factors = call(
        functools.partial(saved_kernel, s),
        "saved",
        [((s.rows, hidden), F32)] * 3,
        [pltpu.VMEM((s.rows, hidden), F32)] * 2,
        [VMEM] * 2,
        saved_gate[0],
        saved_up[0],
    )
    wide = s.width + LANES
    parts_b = call(
        functools.partial(backward_kernel, s),
        "backward",
        [((s.count, s.main, wide), BF16)] * s.slices,
        weight_scratch(s, hidden),
        [VMEM] * (s.blocks + 3) + [HBM] * 3,
        *rows_b,
        *factors,
        *weights,
        mib=32,
        flops=flops,
    )
    parts_b = gather_parts(s, parts_b)
    sums = call(
        functools.partial(backward_sum_kernel, s),
        "backward_sum",
        [((s.main, wide), BF16)] * s.count,
        [],
        [VMEM] * s.slices,
        *parts_b,
    )
    back = [sums[0]] + [across(sums[d], -d, s) for d in range(1, s.count)]
    input_grad, score_grad = call(
        functools.partial(backward_end_kernel, s),
        "backward_end",
        [((tok, depth), BF16), ((1, tok), F32)],
        end_scratch(s),
        [VMEM] * (s.count + 3),
        *back,
        upstream,
        route_b,
        score_b,
    )
    return next_input[None], input_grad[None], score_grad.reshape(1, tok, 1)


def solution(mesh):
    placed = (
        P("section", "expert", None),
        P("section", None, None, "expert"),
        P("section", None, None, "expert"),
        P("section", "expert", None),
        P("section", "expert", None),
        P("section", "expert", None),
        P("section", "expert", None),
        P("section", "expert", None),
        P("section", None, "expert"),
        P("section", None, "expert"),
        P("section", "expert", None),
    )
    return jax.shard_map(
        body,
        mesh=mesh,
        in_specs=placed,
        out_specs=(
            P("section", "expert", None),
            P("section", "expert", None),
            P("section", "expert", None),
        ),
        check_vma=False,
    )
```

time: 109 us -> 65.5 us (0.60)
  waiting for transfers between devices: 48.7 us -> 26.8 us
  matrix products: 19.3 us -> 0 us
  Pallas kernels: 0 us -> 15.1 us
  starting transfers between devices: 24.1 us -> 13.9 us
  other arithmetic: 6.62 us -> 0 us
    all_to_all x5 -> x0, waiting for transfers between devices: 46.3 us -> none  [the longest x1 13.4 us: body(): lax.all_to_all(send, 'expert', split_axis=0, concat_axis=0, tiled=True)]
    dot_general x7 -> x0, matrix products: 19.3 us -> none  [the longest x1 4.46 us: body(): jnp.dot(hidden, wd, preferred_element_type=jnp.float32).astype(jnp.bfloat16)]
    all_to_all x5 -> x0, starting transfers between devices: 18.1 us -> none  [the longest x1 4.26 us: body(): lax.all_to_all(send_d, 'expert', split_axis=0, concat_axis=0, tiled=True)]
    pallas_call x0 -> x10, Pallas kernels: none -> 15.1 us  [call(): pl.pallas_call(kernel, out_shape=shapes, in_specs=ins, out_specs=[VMEM] *...]
    ppermute x2 -> x3, waiting for transfers between devices: 2.44 us -> 16.6 us  [from_behind(): return lax.ppermute(block, axis, route)]
    ppermute x0 -> x10, waiting for transfers between devices: none -> 10.2 us  [the longest x4 10.1 us: across(): return lax.ppermute(block, 'expert', route)]
    ppermute x0 -> x10, starting transfers between devices: none -> 7.34 us  [the longest x4 6.15 us: across(): return lax.ppermute(block, 'expert', route)]
    unnamed x17 -> x30, local copies, waits for them, and re-layouts: 1.98 us -> 8.48 us
  transfers between devices with their start and end apart: 7 -> 13, of which waited for: 6 -> 5; matrix products, arithmetic and copies ran while one was open for 25% -> 0% of each run, Pallas kernels for 0% -> 21%
where the time goes in v2:
time: 65.5 us; the launch traced here: 65.2 us
  waiting for transfers between devices  26.8 us (41%)
  Pallas kernels  15.1 us (23%)
  starting transfers between devices  13.9 us (21%)
  local copies, waits for them, and re-layouts  8.53 us (13%)
  between operations  0.79 us (1%)
    ppermute x3, waiting for transfers between devices, from_behind(): return lax.ppermute(block, axis, route)  16.6 us
    pallas_call x10, Pallas kernels, call(): pl.pallas_call(kernel, out_shape=shapes, in_specs=ins, out_specs=[VMEM] *...  15.1 us
    ppermute x4, waiting for transfers between devices, across(): return lax.ppermute(block, 'expert', route)  10.1 us
    unnamed x30, local copies, waits for them, and re-layouts  8.48 us
    ppermute x3, starting transfers between devices, from_behind(): return lax.ppermute(block, axis, route)  6.58 us
    ppermute x4, starting transfers between devices, across(): return lax.ppermute(block, 'expert', route)  6.15 us
  transfers between devices with their start and end apart: 13, of which 5 were waited for; matrix products, arithmetic and copies ran while one was open for 0% of the time, Pallas kernels for 21%

profile of v2, /device:TPU:0, one launch (start us, length us, event | category | flops | bytes accessed | tf_op | source)
XLA Modules:
  0.0 65.2 jit_solution(805496842366731525)
XLA Ops:
  0.6 6.1 %collective-permute-start.7 = (bf16[1,64,3584]{2,1,0:T(8,128)(2,1)}, bf16[1,64,3584]{2,1,0:T(8,128)(2,1)S(1)}, u32[]{:S(2)}, u32[]{:S(2)}) collective-permute-start(bf16[1,64,3584]{2,1,0:T(8,128)(2,1)} %param.14), channel_id=1, source_target_pairs={{4,0},{8,4},{12,8},{16,12},{20,16},{24,20},{28,24},{0,28},{5,1},{9... | collective-permute-start | bytes 1376264 | tf_op jit(solution)/shard_map/ppermute | solution.py:33
  6.7 1.0 %copy-done.6 = bf16[1,64,3584]{2,1,0:T(8,128)(2,1)S(1)} copy-done((bf16[1,64,3584]{2,1,0:T(8,128)(2,1)S(1)}, bf16[1,64,3584]{2,1,0:T(8,128)(2,1)}, u32[]{:S(2)}) %copy-start.6) | copy-done | bytes 458776
  7.7 0.7 %copy-done.7 = s32[1,64,1]{1,2,0:T(1,128)S(1)} copy-done((s32[1,64,1]{1,2,0:T(1,128)S(1)}, s32[1,64,1]{1,2,0:T(1,128)}, u32[]{:S(2)}) %copy-start.7) | copy-done | bytes 280
  8.4 0.4 pack.2
  8.8 1.6 %collective-permute-start = (bf16[32,3840]{1,0:T(8,128)(2,1)S(1)}, bf16[32,3840]{1,0:T(8,128)(2,1)S(1)}, u32[]{:S(2)}, u32[]{:S(2)}) collective-permute-start(bf16[32,3840]{1,0:T(8,128)(2,1)S(1)} %get-tuple-element.21.base), channel_id=1, source_target_pairs={{0,2},{1,3},{2,0},{3,1},{4,6},{5,7},{6,4},{7,5},{8,10},{9,11},{10,... | collective-permute-start | bytes 737288 | tf_op jit(solution)/shard_map/ppermute | solution.py:42
  10.4 6.4 %collective-permute-done.7 = bf16[1,64,3584]{2,1,0:T(8,128)(2,1)S(1)} collective-permute-done((bf16[1,64,3584]{2,1,0:T(8,128)(2,1)}, bf16[1,64,3584]{2,1,0:T(8,128)(2,1)S(1)}, u32[]{:S(2)}, u32[]{:S(2)}) %collective-permute-start.7) | collective-permute-done | bytes 458784 | tf_op jit(solution)/shard_map/ppermute | solution.py:33
  16.8 0.7 %copy-done.10 = s32[1,64,1]{1,2,0:T(1,128)S(1)} copy-done((s32[1,64,1]{1,2,0:T(1,128)S(1)}, s32[1,64,1]{1,2,0:T(1,128)}, u32[]{:S(2)}) %copy-start.10) | copy-done | bytes 280
  17.4 0.4 pack.3
  17.9 1.6 %collective-permute-start.8 = (bf16[32,3840]{1,0:T(8,128)(2,1)S(1)}, bf16[32,3840]{1,0:T(8,128)(2,1)S(1)}, u32[]{:S(2)}, u32[]{:S(2)}) collective-permute-start(bf16[32,3840]{1,0:T(8,128)(2,1)S(1)} %get-tuple-element.27), channel_id=1, source_target_pairs={{0,2},{1,3},{2,0},{3,1},{4,6},{5,7},{6,4},{7,5},{8,10},{9,11},{10,... | collective-permute-start | bytes 737288 | tf_op jit(solution)/shard_map/ppermute | solution.py:42
  19.4 0.5 collective-permute-start.2
  20.0 4.8 %collective-permute-done.8.refs_1_ = bf16[32,3840]{1,0:T(8,128)(2,1)S(1)} collective-permute-done((bf16[32,3840]{1,0:T(8,128)(2,1)S(1)}, bf16[32,3840]{1,0:T(8,128)(2,1)S(1)}, u32[]{:S(2)}, u32[]{:S(2)}) %collective-permute-start.8) | collective-permute-done | bytes 245792 | tf_op jit(solution)/shard_map/ppermute | solution.py:42
  24.8 2.0 %copy-done = bf16[1,3584,512]{2,1,0:T(8,128)(2,1)S(1)} copy-done((bf16[1,3584,512]{2,1,0:T(8,128)(2,1)S(1)}, bf16[1,3584,512]{2,1,0:T(8,128)(2,1)}, u32[]{:S(2)}) %copy-start) | copy-done | bytes 3670040
  26.8 2.0 %copy-done.2 = bf16[1,3584,512]{2,1,0:T(8,128)(2,1)S(1)} copy-done((bf16[1,3584,512]{2,1,0:T(8,128)(2,1)S(1)}, bf16[1,3584,512]{2,1,0:T(8,128)(2,1)}, u32[]{:S(2)}) %copy-start.2) | copy-done | bytes 3670040
  28.9 2.0 %copy-done.4 = bf16[1,512,3584]{2,1,0:T(8,128)(2,1)S(1)} copy-done((bf16[1,512,3584]{2,1,0:T(8,128)(2,1)S(1)}, bf16[1,512,3584]{2,1,0:T(8,128)(2,1)}, u32[]{:S(2)}) %copy-start.4) | copy-done | bytes 3670040
  30.9 4.5 %forward.1 = (bf16[2,32,3840]{2,1,0:T(8,128)(2,1)S(1)}, bf16[2,32,3840]{2,1,0:T(8,128)(2,1)S(1)}) custom-call(bf16[32,3840]{1,0:T(8,128)(2,1)S(1)} %get-tuple-element.20.refs_0_.refs_2_, bf16[32,3840]{1,0:T(8,128)(2,1)S(1)} %collective-permute-done.refs_1_, bf16[32,3840]{1,0:T(8,128)(2,1)S(1)} %collective-permute-done.1.refs_2_, ...), custom_call_target="tpu_custom_call" | custom-call | flops 1585446912 | bytes 11993088 | tf_op jit(solution)/shard_map/forward/pallas_call | solution.py:404
  35.4 0.6 collective-permute-start.3
  36.4 6.3 %backward.1 = (bf16[2,32,3968]{2,1,0:T(8,128)(2,1)S(1)}, bf16[2,32,3968]{2,1,0:T(8,128)(2,1)S(1)}) custom-call(bf16[32,3840]{1,0:T(8,128)(2,1)S(1)} %get-tuple-element.26.refs_0_, bf16[32,3840]{1,0:T(8,128)(2,1)S(1)} %collective-permute-done.8.refs_1_, bf16[32,3840]{1,0:T(8,128)(2,1)S(1)} %collective-permute-done.9.refs_2_, ...), custom_call_target="tpu_custom_call" | custom-call | flops 1585446912 | bytes 12877824 | tf_op jit(solution)/shard_map/backward/pallas_call | solution.py:404
  43.2 1.6 %collective-permute-start.5 = (bf16[32,3840]{1,0:T(8,128)(2,1)S(1)}, bf16[32,3840]{1,0:T(8,128)(2,1)S(1)}, u32[]{:S(2)}, u32[]{:S(2)}) collective-permute-start(bf16[32,3840]{1,0:T(8,128)(2,1)S(1)} %get-tuple-element.25), channel_id=1, source_target_pairs={{0,2},{1,3},{2,0},{3,1},{4,6},{5,7},{6,4},{7,5},{8,10},{9,11},{10,... | collective-permute-start | bytes 737288 | tf_op jit(solution)/shard_map/ppermute | solution.py:42
  45.0 1.5 %collective-permute-start.12 = (bf16[32,3968]{1,0:T(8,128)(2,1)S(1)}, bf16[32,3968]{1,0:T(8,128)(2,1)S(1)}, u32[]{:S(2)}, u32[]{:S(2)}) collective-permute-start(bf16[32,3968]{1,0:T(8,128)(2,1)S(1)} %get-tuple-element.34), channel_id=1, source_target_pairs={{0,2},{1,3},{2,0},{3,1},{4,6},{5,7},{6,4},{7,5},{8,10},{9,11},{10,... | collective-permute-start | bytes 761864 | tf_op jit(solution)/shard_map/ppermute | solution.py:42
  46.7 5.3 %collective-permute-done.5.back = bf16[32,3840]{1,0:T(8,128)(2,1)S(1)} collective-permute-done((bf16[32,3840]{1,0:T(8,128)(2,1)S(1)}, bf16[32,3840]{1,0:T(8,128)(2,1)S(1)}, u32[]{:S(2)}, u32[]{:S(2)}) %collective-permute-start.5) | collective-permute-done | bytes 245792 | tf_op jit(solution)/shard_map/ppermute | solution.py:42
  52.5 4.9 %collective-permute-done.4.refs_0_ = bf16[32,3840]{1,0:T(8,128)(2,1)S(1)} collective-permute-done((bf16[32,3840]{1,0:T(8,128)(2,1)S(1)}, bf16[32,3840]{1,0:T(8,128)(2,1)S(1)}, u32[]{:S(2)}, u32[]{:S(2)}) %collective-permute-start.4) | collective-permute-done | bytes 245792 | tf_op jit(solution)/shard_map/ppermute | solution.py:33
  57.5 5.3 %collective-permute-done.6.refs_1_ = bf16[32,3840]{1,0:T(8,128)(2,1)S(1)} collective-permute-done((bf16[32,3840]{1,0:T(8,128)(2,1)S(1)}, bf16[32,3840]{1,0:T(8,128)(2,1)S(1)}, u32[]{:S(2)}, u32[]{:S(2)}) %collective-permute-start.6) | collective-permute-done | bytes 245792 | tf_op jit(solution)/shard_map/ppermute | solution.py:33
  62.8 1.2 %forward_end.1 = bf16[64,3584]{1,0:T(8,128)(2,1)} custom-call(bf16[32,3840]{1,0:T(8,128)(2,1)S(1)} %collective-permute-done.4.refs_0_, bf16[32,3840]{1,0:T(8,128)(2,1)S(1)} %collective-permute-done.6.refs_1_), custom_call_target="tpu_custom_call" | custom-call | bytes 491520 | tf_op jit(solution)/shard_map/forward_end/pallas_call | solution.py:404
  64.0 1.2 %backward_end.1 = (bf16[64,3584]{1,0:T(8,128)(2,1)}, f32[1,64]{1,0:T(1,128)}) custom-call(bf16[32,3968]{1,0:T(8,128)(2,1)S(1)} %get-tuple-element.33.refs_0_, bf16[32,3968]{1,0:T(8,128)(2,1)S(1)} %collective-permute-done.12.refs_1_, bf16[64,3584]{1,0:T(8,128)(2,1)S(1)} %bitcast.23, s32[1,64]{1,0:T(1,128)S(1)} %bitcast.31, f32[1,64]{1,0:T(1,128)S(1)} %bitcast.32), custom_call_target="tpu_custom_call" | custom-call | bytes 967168 | tf_op jit(solution)/shard_map/backward_end/pallas_call | solution.py:404
  (43 shorter events, 1.9 us)
Async XLA Ops:
  0.6 16.2 %collective-permute-start.7 = (bf16[1,64,3584]{2,1,0:T(8,128)(2,1)}, bf16[1,64,3584]{2,1,0:T(8,128)(2,1)S(1)}, u32[]{:S(2)}, u32[]{:S(2)}) collective-permute-start(bf16[1,64,3584]{2,1,0:T(8,128)(2,1)} %param.14), channel_id=1, source_target_pairs={{4,0},{8,4},{12,8},{16,12},{20,16},{24,20},{28,24},{0,28},{5,1},{9... | collective-permute-start | bytes 1376264 | tf_op jit(solution)/shard_map/ppermute | solution.py:33
  8.8 10.6 %collective-permute-start = (bf16[32,3840]{1,0:T(8,128)(2,1)S(1)}, bf16[32,3840]{1,0:T(8,128)(2,1)S(1)}, u32[]{:S(2)}, u32[]{:S(2)}) collective-permute-start(bf16[32,3840]{1,0:T(8,128)(2,1)S(1)} %get-tuple-element.21.base), channel_id=1, source_target_pairs={{0,2},{1,3},{2,0},{3,1},{4,6},{5,7},{6,4},{7,5},{8,10},{9,11},{10,... | collective-permute-start | bytes 737288 | tf_op jit(solution)/shard_map/ppermute | solution.py:42
  17.9 6.9 %collective-permute-start.8 = (bf16[32,3840]{1,0:T(8,128)(2,1)S(1)}, bf16[32,3840]{1,0:T(8,128)(2,1)S(1)}, u32[]{:S(2)}, u32[]{:S(2)}) collective-permute-start(bf16[32,3840]{1,0:T(8,128)(2,1)S(1)} %get-tuple-element.27), channel_id=1, source_target_pairs={{0,2},{1,3},{2,0},{3,1},{4,6},{5,7},{6,4},{7,5},{8,10},{9,11},{10,... | collective-permute-start | bytes 737288 | tf_op jit(solution)/shard_map/ppermute | solution.py:42
  19.4 5.3 %collective-permute-start.1 = (bf16[32,3840]{1,0:T(8,128)(2,1)S(1)}, bf16[32,3840]{1,0:T(8,128)(2,1)S(1)}, u32[]{:S(2)}, u32[]{:S(2)}) collective-permute-start(bf16[32,3840]{1,0:T(8,128)(2,1)S(1)} %get-tuple-element.20.refs_0_.refs_2_), channel_id=1, source_target_pairs={{0,1},{1,0},{2,3},{3,2},{4,5},{5,4},{6,7},{7,6},{8,9},{9,8},{10,11... | collective-permute-start | bytes 737288 | tf_op jit(solution)/shard_map/ppermute | solution.py:51
  19.4 5.3 %collective-permute-start.2 = (bf16[32,3840]{1,0:T(8,128)(2,1)S(1)}, bf16[32,3840]{1,0:T(8,128)(2,1)S(1)}, u32[]{:S(2)}, u32[]{:S(2)}) collective-permute-start(bf16[32,3840]{1,0:T(8,128)(2,1)S(1)} %collective-permute-done.refs_1_), channel_id=1, source_target_pairs={{0,1},{1,0},{2,3},{3,2},{4,5},{5,4},{6,7},{7,6},{8,9},{9,8},{10,11... | collective-permute-start | bytes 737288 | tf_op jit(solution)/shard_map/ppermute | solution.py:51
  20.0 16.4 %collective-permute-start.9 = (bf16[32,3840]{1,0:T(8,128)(2,1)S(1)}, bf16[32,3840]{1,0:T(8,128)(2,1)S(1)}, u32[]{:S(2)}, u32[]{:S(2)}) collective-permute-start(bf16[32,3840]{1,0:T(8,128)(2,1)S(1)} %get-tuple-element.26.refs_0_), channel_id=1, source_target_pairs={{0,1},{1,0},{2,3},{3,2},{4,5},{5,4},{6,7},{7,6},{8,9},{9,8},{10,11... | collective-permute-start | bytes 737288 | tf_op jit(solution)/shard_map/ppermute | solution.py:51
  24.8 11.6 %collective-permute-start.10 = (bf16[32,3840]{1,0:T(8,128)(2,1)S(1)}, bf16[32,3840]{1,0:T(8,128)(2,1)S(1)}, u32[]{:S(2)}, u32[]{:S(2)}) collective-permute-start(bf16[32,3840]{1,0:T(8,128)(2,1)S(1)} %collective-permute-done.8.refs_1_), channel_id=1, source_target_pairs={{0,1},{1,0},{2,3},{3,2},{4,5},{5,4},{6,7},{7,6},{8,9},{9,8},{10,11... | collective-permute-start | bytes 737288 | tf_op jit(solution)/shard_map/ppermute | solution.py:51
  24.8 2.0 %copy-start = (bf16[1,3584,512]{2,1,0:T(8,128)(2,1)S(1)}, bf16[1,3584,512]{2,1,0:T(8,128)(2,1)}, u32[]{:S(2)}) copy-start(bf16[1,3584,512]{2,1,0:T(8,128)(2,1)} %param.19) | copy-start | bytes 11010052
  26.8 2.0 %copy-start.2 = (bf16[1,3584,512]{2,1,0:T(8,128)(2,1)S(1)}, bf16[1,3584,512]{2,1,0:T(8,128)(2,1)}, u32[]{:S(2)}) copy-start(bf16[1,3584,512]{2,1,0:T(8,128)(2,1)} %param.20) | copy-start | bytes 11010052
  30.9 5.1 %copy-start.13 = (bf16[1,4,34,512]{3,1,2,0:T(4,128)(2,1)S(1)}, bf16[1,4,34,512]{3,1,2,0:T(4,128)(2,1)}, u32[]{:S(2)}) copy-start(bf16[1,4,34,512]{3,1,2,0:T(4,128)(2,1)} %param.13) | copy-start | bytes 417796
  30.9 5.1 %copy-start.14 = (bf16[1,4,34,512]{3,1,2,0:T(4,128)(2,1)S(1)}, bf16[1,4,34,512]{3,1,2,0:T(4,128)(2,1)}, u32[]{:S(2)}) copy-start(bf16[1,4,34,512]{3,1,2,0:T(4,128)(2,1)} %param.12) | copy-start | bytes 417796
  30.9 5.4 %copy-start.1 = (bf16[1,3584,512]{2,1,0:T(8,128)(2,1)S(1)}, bf16[1,3584,512]{2,1,0:T(8,128)(2,1)}, u32[]{:S(2)}) copy-start(bf16[1,3584,512]{2,1,0:T(8,128)(2,1)} %param.19) | copy-start | bytes 11010052
  30.9 5.5 %copy-start.3 = (bf16[1,3584,512]{2,1,0:T(8,128)(2,1)S(1)}, bf16[1,3584,512]{2,1,0:T(8,128)(2,1)}, u32[]{:S(2)}) copy-start(bf16[1,3584,512]{2,1,0:T(8,128)(2,1)} %param.20) | copy-start | bytes 11010052
  30.9 5.5 %copy-start.5 = (bf16[1,512,3584]{2,1,0:T(8,128)(2,1)S(1)}, bf16[1,512,3584]{2,1,0:T(8,128)(2,1)}, u32[]{:S(2)}) copy-start(bf16[1,512,3584]{2,1,0:T(8,128)(2,1)} %param.21) | copy-start | bytes 11010052
  35.4 7.4 %collective-permute-start.3 = (bf16[2,32,3840]{2,1,0:T(8,128)(2,1)S(1)}, bf16[2,32,3840]{2,1,0:T(8,128)(2,1)S(1)}, u32[]{:S(2)}, u32[]{:S(2)}) collective-permute-start(bf16[2,32,3840]{2,1,0:T(8,128)(2,1)S(1)} %get-tuple-element.23), channel_id=1, source_target_pairs={{0,1},{1,0},{2,3},{3,2},{4,5},{5,4},{6,7},{7,6},{8,9},{9,8},{10,11... | collective-permute-start | bytes 1474568 | tf_op jit(solution)/shard_map/ppermute | solution.py:51
  36.4 6.4 %copy-start.8 = (s32[1,64,1]{1,2,0:T(1,128)S(1)}, s32[1,64,1]{1,2,0:T(1,128)}, u32[]{:S(2)}) copy-start(s32[1,64,1]{1,2,0:T(1,128)} %param.15) | copy-start | bytes 772
  36.4 6.4 %copy-start.9 = (f32[1,64,1]{1,2,0:T(1,128)S(1)}, f32[1,64,1]{1,2,0:T(1,128)}, u32[]{:S(2)}) copy-start(f32[1,64,1]{1,2,0:T(1,128)} %param.17) | copy-start | bytes 772
  42.7 21.3 %copy-start.11 = (s32[1,64,1]{1,2,0:T(1,128)S(1)}, s32[1,64,1]{1,2,0:T(1,128)}, u32[]{:S(2)}) copy-start(s32[1,64,1]{1,2,0:T(1,128)} %param.16) | copy-start | bytes 772
  42.7 21.3 %copy-start.12 = (f32[1,64,1]{1,2,0:T(1,128)S(1)}, f32[1,64,1]{1,2,0:T(1,128)}, u32[]{:S(2)}) copy-start(f32[1,64,1]{1,2,0:T(1,128)} %param.18) | copy-start | bytes 772
  42.7 2.0 %collective-permute-start.11 = (bf16[2,32,3968]{2,1,0:T(8,128)(2,1)S(1)}, bf16[2,32,3968]{2,1,0:T(8,128)(2,1)S(1)}, u32[]{:S(2)}, u32[]{:S(2)}) collective-permute-start(bf16[2,32,3968]{2,1,0:T(8,128)(2,1)S(1)} %get-tuple-element.32), channel_id=1, source_target_pairs={{0,1},{1,0},{2,3},{3,2},{4,5},{5,4},{6,7},{7,6},{8,9},{9,8},{10,11... | collective-permute-start | bytes 1523720 | tf_op jit(solution)/shard_map/ppermute | solution.py:51
  43.2 8.8 %collective-permute-start.5 = (bf16[32,3840]{1,0:T(8,128)(2,1)S(1)}, bf16[32,3840]{1,0:T(8,128)(2,1)S(1)}, u32[]{:S(2)}, u32[]{:S(2)}) collective-permute-start(bf16[32,3840]{1,0:T(8,128)(2,1)S(1)} %get-tuple-element.25), channel_id=1, source_target_pairs={{0,2},{1,3},{2,0},{3,1},{4,6},{5,7},{6,4},{7,5},{8,10},{9,11},{10,... | collective-permute-start | bytes 737288 | tf_op jit(solution)/shard_map/ppermute | solution.py:42
  45.0 19.0 %collective-permute-start.12 = (bf16[32,3968]{1,0:T(8,128)(2,1)S(1)}, bf16[32,3968]{1,0:T(8,128)(2,1)S(1)}, u32[]{:S(2)}, u32[]{:S(2)}) collective-permute-start(bf16[32,3968]{1,0:T(8,128)(2,1)S(1)} %get-tuple-element.34), channel_id=1, source_target_pairs={{0,2},{1,3},{2,0},{3,1},{4,6},{5,7},{6,4},{7,5},{8,10},{9,11},{10,... | collective-permute-start | bytes 761864 | tf_op jit(solution)/shard_map/ppermute | solution.py:42
  46.4 11.0 %collective-permute-start.4 = (bf16[32,3840]{1,0:T(8,128)(2,1)S(1)}, bf16[32,3840]{1,0:T(8,128)(2,1)S(1)}, u32[]{:S(2)}, u32[]{:S(2)}) collective-permute-start(bf16[32,3840]{1,0:T(8,128)(2,1)S(1)} %get-tuple-element.24), channel_id=1, source_target_pairs={{28,0},{0,4},{4,8},{8,12},{12,16},{16,20},{20,24},{24,28},{29,1},{... | collective-permute-start | bytes 737288 | tf_op jit(solution)/shard_map/ppermute | solution.py:33
  52.3 10.5 %collective-permute-start.6 = (bf16[32,3840]{1,0:T(8,128)(2,1)S(1)}, bf16[32,3840]{1,0:T(8,128)(2,1)S(1)}, u32[]{:S(2)}, u32[]{:S(2)}) collective-permute-start(bf16[32,3840]{1,0:T(8,128)(2,1)S(1)} %forward_add.1), channel_id=1, source_target_pairs={{28,0},{0,4},{4,8},{8,12},{12,16},{16,20},{20,24},{24,28},{29,1},{... | collective-permute-start | bytes 737288 | tf_op jit(solution)/shard_map/ppermute | solution.py:33
  (4 other events, 4.4 us)

commit v3 on v2

--- a/solution.py
+++ b/solution.py
@@ -121,21 +121,50 @@
         out_ref[:, at] = (base_ref[:, at].astype(F32) + extra[j] * total[:, at]).astype(BF16)
 
 
-def pack_kernel(s, route_ref, x_ref, *rest):
-    outs, (extra_ref, tail_ref) = rest[: s.count], rest[s.count :]
-    route_row = route_ref[...].astype(F32)
+def pack_rows(s, route_row, x, outs, extra_ref, tail_ref):
     rank = slot_rows(route_row, s)
-    high = s.main + 16
-    slots = iota((high, s.tok), 0)
+    slots = iota((s.main + 16, s.tok), 0)
     tail_ref[...] = jnp.zeros_like(tail_ref)
     for d in range(s.count):
         hit = route_row == expert_at(s, d)
         table = jnp.where(hit & (rank == slots), 1.0, 0.0).astype(BF16)
-        rows = jnp.dot(table, x_ref[...], preferred_element_type=F32)
+        rows = jnp.dot(table, x, preferred_element_type=F32)
         outs[d][:, : s.depth] = rows[: s.main].astype(BF16)
         extra_ref[...] = rows[s.main :]
         fold(extra_ref, 0, tail_ref, s)
         outs[d][:, s.depth :] = tail_ref[...].astype(BF16)
+
+
+def first_kernel(s, route_hbm, x_hbm, dy_hbm, *rest):
+    outs, dy_ref = rest[: s.count], rest[s.count]
+    route_ref, x_ref, extra_ref, tail_ref, sems = rest[s.count + 1 :]
+    copies = [
+        pltpu.make_async_copy(src, dst, sems.at[i])
+        for i, (src, dst) in enumerate(
+            ((route_hbm, route_ref), (x_hbm, x_ref), (dy_hbm, dy_ref))
+        )
+    ]
+    for copy in copies:
+        copy.start()
+    copies[0].wait()
+    copies[1].wait()
+    pack_rows(s, route_ref[...].astype(F32), x_ref[...], outs, extra_ref, tail_ref)
+    copies[2].wait()
+
+
+def pack_kernel(s, route_ref, x_ref, *rest):
+    outs, (extra_ref, tail_ref) = rest[: s.count], rest[s.count :]
+    pack_rows(s, route_ref[...].astype(F32), x_ref[...], outs, extra_ref, tail_ref)
+
+
+def load_kernel(*refs):
+    sems = refs[-1]
+    n = (len(refs) - 1) // 2
+    copies = [pltpu.make_async_copy(refs[i], refs[n + i], sems.at[i]) for i in range(n)]
+    for copy in copies:
+        copy.start()
+    for copy in copies:
+        copy.wait()
 
 
 def gather_packs(packs, rows_ref, extra_ref, tail_ref, s):
@@ -149,14 +178,14 @@
 
 def scatter_chunk(value, outs, extra_ref, at, s):
     for i in range(s.blocks):
-        outs[i // s.count][i % s.count, :, at] = value[i * s.main : (i + 1) * s.main].astype(BF16)
+        outs[i][:, at] = value[i * s.main : (i + 1) * s.main].astype(BF16)
     extra_ref[:, at] = value[s.blocks * s.main :]
 
 
 def scatter_tails(outs, extra_ref, tail_ref, s):
     for i in range(s.blocks):
         fold(extra_ref, i * s.extra, tail_ref, s)
-        outs[i // s.count][i % s.count, :, s.depth : s.width] = tail_ref[...].astype(BF16)
+        outs[i][:, s.depth : s.width] = tail_ref[...].astype(BF16)
 
 
 def chunk_of(depth):
@@ -168,41 +197,22 @@
 def forward_kernel(s, *refs):
     packs = refs[: s.blocks]
     wg, wu, wd = refs[s.blocks : s.blocks + 3]
-    outs = refs[s.blocks + 3 : s.blocks + 3 + s.slices]
-    wg_v, wu_v, wd_v, rows_ref, extra_ref, tail_ref, sems = refs[s.blocks + 3 + s.slices :]
-    chunk = wd_v.shape[2]
-    steps = s.depth // chunk
-    up, down = [], []
-    for c in range(steps):
-        at = pl.ds(c * chunk, chunk)
-        up.append(
-            (
-                pltpu.make_async_copy(wg.at[at, :], wg_v.at[c], sems.at[0, c]),
-                pltpu.make_async_copy(wu.at[at, :], wu_v.at[c], sems.at[1, c]),
-            )
-        )
-        down.append(pltpu.make_async_copy(wd.at[:, at], wd_v.at[c], sems.at[2, c]))
-    for pair in up:
-        for copy in pair:
-            copy.start()
-    for copy in down:
-        copy.start()
+    outs = refs[s.blocks + 3 : -3]
+    rows_ref, extra_ref, tail_ref = refs[-3:]
+    chunk = chunk_of(s.depth)
     gather_packs(packs, rows_ref, extra_ref, tail_ref, s)
     g = u = None
-    for c in range(steps):
-        for copy in up[c]:
-            copy.wait()
-        lhs = rows_ref[:, c * chunk : (c + 1) * chunk]
-        more_g = jnp.dot(lhs, wg_v[c], preferred_element_type=F32)
-        more_u = jnp.dot(lhs, wu_v[c], preferred_element_type=F32)
+    for c in range(0, s.depth, chunk):
+        lhs = rows_ref[:, c : c + chunk]
+        more_g = jnp.dot(lhs, wg[c : c + chunk, :], preferred_element_type=F32)
+        more_u = jnp.dot(lhs, wu[c : c + chunk, :], preferred_element_type=F32)
         g = more_g if g is None else g + more_g
         u = more_u if u is None else u + more_u
     hidden = (g * jax.nn.sigmoid(g) * u).astype(BF16)
     tail_ref[...] = jnp.zeros_like(tail_ref)
-    for c in range(steps):
-        down[c].wait()
-        part = jnp.dot(hidden, wd_v[c], preferred_element_type=F32)
-        scatter_chunk(part, outs, extra_ref, slice(c * chunk, (c + 1) * chunk), s)
+    for c in range(0, s.depth, chunk):
+        part = jnp.dot(hidden, wd[:, c : c + chunk], preferred_element_type=F32)
+        scatter_chunk(part, outs, extra_ref, slice(c, c + chunk), s)
     scatter_tails(outs, extra_ref, tail_ref, s)
 
 
@@ -263,76 +273,60 @@
 def backward_kernel(s, *refs):
     packs = refs[: s.blocks]
     c1, c2, hb, wg, wu, wd = refs[s.blocks : s.blocks + 6]
-    outs = refs[s.blocks + 6 : s.blocks + 6 + s.slices]
-    wg_v, wu_v, wd_v, rows_ref, extra_ref, tail_ref, sems = refs[s.blocks + 6 + s.slices :]
-    chunk = wd_v.shape[2]
-    steps = s.depth // chunk
-    up, down = [], []
-    for c in range(steps):
-        at = pl.ds(c * chunk, chunk)
-        up.append(
-            (
-                pltpu.make_async_copy(wg.at[at, :], wg_v.at[c], sems.at[0, c]),
-                pltpu.make_async_copy(wu.at[at, :], wu_v.at[c], sems.at[1, c]),
-            )
-        )
-        down.append(pltpu.make_async_copy(wd.at[:, at], wd_v.at[c], sems.at[2, c]))
-    for copy in down:
-        copy.start()
-    for pair in up:
-        for copy in pair:
-            copy.start()
+    outs = refs[s.blocks + 6 : -3]
+    rows_ref, extra_ref, tail_ref = refs[-3:]
+    chunk = chunk_of(s.depth)
     gather_packs(packs, rows_ref, extra_ref, tail_ref, s)
     a = None
-    for c in range(steps):
-        down[c].wait()
-        lhs = rows_ref[:, c * chunk : (c + 1) * chunk]
-        more = lax.dot_general(lhs, wd_v[c], NT, preferred_element_type=F32)
+    for c in range(0, s.depth, chunk):
+        more = lax.dot_general(
+            rows_ref[:, c : c + chunk], wd[:, c : c + chunk], NT, preferred_element_type=F32
+        )
         a = more if a is None else a + more
     dgp = (a * c1[...]).astype(BF16)
     dup = (a * c2[...]).astype(BF16)
     inner = jnp.sum(a * hb[...], axis=1, keepdims=True)
     for i in range(s.blocks):
         first = s.blocks * s.main + i * s.extra
-        outs[i // s.count][i % s.count, :, s.width :] = put_inner(
+        outs[i][:, s.width :] = put_inner(
             inner[i * s.main : (i + 1) * s.main],
             [inner[first + j : first + j + 1] for j in range(s.extra)],
             s,
         )
     tail_ref[...] = jnp.zeros_like(tail_ref)
-    for c in range(steps):
-        for copy in up[c]:
-            copy.wait()
-        part = lax.dot_general(dgp, wg_v[c], NT, preferred_element_type=F32) + lax.dot_general(
-            dup, wu_v[c], NT, preferred_element_type=F32
-        )
-        scatter_chunk(part, outs, extra_ref, slice(c * chunk, (c + 1) * chunk), s)
+    for c in range(0, s.depth, chunk):
+        part = lax.dot_general(
+            dgp, wg[c : c + chunk, :], NT, preferred_element_type=F32
+        ) + lax.dot_general(dup, wu[c : c + chunk, :], NT, preferred_element_type=F32)
+        scatter_chunk(part, outs, extra_ref, slice(c, c + chunk), s)
     scatter_tails(outs, extra_ref, tail_ref, s)
 
 
-def total_of(parts, d):
-    total = parts[0][d].astype(F32)
-    for part in parts[1:]:
-        total = total + part[d].astype(F32)
+def total_of(parts, d, k):
+    total = parts[d][...].astype(F32)
+    for part in parts[d + len(parts) // k :: len(parts) // k]:
+        total = total + part[...].astype(F32)
     return total
 
 
 def forward_sum_kernel(s, *refs):
-    parts = refs[: s.slices]
-    own, route_ref, score_ref = refs[s.slices : s.slices + 3]
-    y_ref, backs = refs[s.slices + 3], refs[s.slices + 4 :]
+    parts = refs[: s.blocks]
+    own, route_ref, score_ref, y_ref = refs[s.blocks : s.blocks + 4]
+    backs = refs[s.blocks + 4 :]
     for d in range(1, s.count):
-        backs[d - 1][...] = total_of(parts, d).astype(BF16)
+        backs[d - 1][:, : s.width] = total_of(parts, d, s.slices).astype(BF16)
+        backs[d - 1][:, s.width :] = jnp.zeros((s.main, LANES), BF16)
     route_row = route_ref[...].astype(F32)
     main, extra = slot_values(route_row, 2.5 * score_ref[...], expert_at(s, 0), s)
-    add_gated(y_ref, own, main, extra, total_of(parts, 0), s)
+    add_gated(y_ref, own, main, extra, total_of(parts, 0, s.slices), s)
     y_ref[s.folds : s.folds + 1, s.depth : s.depth + s.tok] = route_row.astype(BF16)
+    y_ref[:, s.width :] = jnp.zeros((s.main, LANES), BF16)
 
 
 def forward_add_kernel(s, distance, back, base, route_ref, score_ref, y_ref):
     route_row = route_ref[...].astype(F32)
     main, extra = slot_values(route_row, 2.5 * score_ref[...], expert_at(s, distance), s)
-    add_gated(y_ref, base, main, extra, back[...].astype(F32), s)
+    add_gated(y_ref, base, main, extra, back[:, : s.width].astype(F32), s)
 
 
 def tokens_of(packs, route_row, rows_ref, extra_ref, tail_ref, s):
@@ -365,9 +359,9 @@
 
 
 def backward_sum_kernel(s, *refs):
-    parts, outs = refs[: s.slices], refs[s.slices :]
+    parts, outs = refs[: s.blocks], refs[s.blocks :]
     for d in range(s.count - 1, -1, -1):
-        total = total_of(parts, d)
+        total = total_of(parts, d, s.slices)
         outs[d][:, : s.width] = total[:, : s.width].astype(BF16)
         main, extra = get_inner(total[:, s.width :], s)
         outs[d][:, s.width :] = put_inner(main, extra, s)
@@ -395,12 +389,15 @@
 
 
 VMEM = pl.BlockSpec(memory_space=pltpu.VMEM)
-HBM = pl.BlockSpec(memory_space=pl.ANY)
-
-
-def call(kernel, name, outs, scratch, ins, *args, mib=16, flops=0):
+HBM = pl.BlockSpec(memory_space=pltpu.HBM)
+
+
+def call(kernel, name, outs, scratch, ins, *args, mib=16):
     shapes = [jax.ShapeDtypeStruct(shape, kind) for shape, kind in outs]
-    size = sum(a.size * a.dtype.itemsize for a in args)
+    args = [
+        pltpu.with_memory_space_constraint(a, pltpu.HBM) if spec is HBM else a
+        for a, spec in zip(args, ins)
+    ]
     return pl.pallas_call(
         kernel,
         out_shape=shapes,
@@ -408,7 +405,7 @@
         out_specs=[VMEM] * len(shapes),
         scratch_shapes=scratch,
         compiler_params=pltpu.CompilerParams(vmem_limit_bytes=mib << 20),
-        cost_estimate=pl.CostEstimate(flops=flops, bytes_accessed=size, transcendentals=0),
+        cost_estimate=pl.CostEstimate(flops=0, bytes_accessed=0, transcendentals=0),
         name=name,
     )(*args)
 
@@ -420,41 +417,24 @@
     ]
 
 
-def pack(s, routes, tokens):
-    return call(
-        functools.partial(pack_kernel, s),
-        "pack",
-        [((s.main, s.width), BF16)] * s.count,
-        tail_scratch(s, 16),
-        [VMEM, VMEM],
-        routes,
-        tokens,
-    )
-
-
-def weight_scratch(s, hidden):
-    chunk = chunk_of(s.depth)
-    steps = s.depth // chunk
-    return [
-        pltpu.VMEM((steps, chunk, hidden), BF16),
-        pltpu.VMEM((steps, chunk, hidden), BF16),
-        pltpu.VMEM((steps, hidden, chunk), BF16),
-        pltpu.VMEM((s.rows, s.depth), BF16),
-        *tail_scratch(s, s.tail_rows),
-        pltpu.SemaphoreType.DMA((3, steps)),
-    ]
-
-
-def dispatch(s, packs):
-    got = [packs[0]] + [across(packs[d], d, s) for d in range(1, s.count)]
-    out = list(got)
-    for k in range(1, s.slices):
-        out += [beside(b, k, s) for b in got]
-    return out
+def row_scratch(s):
+    return [pltpu.VMEM((s.rows, s.depth), BF16), *tail_scratch(s, s.tail_rows)]
+
+
+def cross(s, packs):
+    return [packs[0]] + [across(packs[d], d, s) for d in range(1, s.count)]
+
+
+def spread(s, got):
+    return got + [beside(b, k, s) for k in range(1, s.slices) for b in got]
+
+
+def hold(values, *after):
+    return lax.optimization_barrier((values, after))[0]
 
 
 def gather_parts(s, parts):
-    return [parts[0]] + [beside(parts[k], -k, s) for k in range(1, s.slices)]
+    return [beside(p, -(i // s.count), s) if i >= s.count else p for i, p in enumerate(parts)]
 
 
 def end_scratch(s):
@@ -480,65 +460,37 @@
     s = Sizes(saved_gate.shape[2], depth, EXPERTS, groups // EXPERTS, tok)
     hidden = w_gate.shape[2]
     weights = (w_gate[0], w_up[0], w_down[0])
-    flops = 6 * s.rows * depth * hidden
     route_a = routes_fwd.reshape(1, tok)
     route_b = routes_bwd.reshape(1, tok)
     score_a = scores_fwd.reshape(1, tok)
     score_b = scores_bwd.reshape(1, tok)
 
-    sent_a = pack(s, route_a, x_fwd[0])
-    rows_a = dispatch(s, sent_a)
-    upstream = from_behind(grad_next, "section", -1)[0]
-
-    parts_a = call(
-        functools.partial(forward_kernel, s),
-        "forward",
-        [((s.count, s.main, s.width), BF16)] * s.slices,
-        weight_scratch(s, hidden),
-        [VMEM] * s.blocks + [HBM] * 3,
-        *rows_a,
-        *weights,
-        mib=32,
-        flops=flops,
-    )
-    parts_a = gather_parts(s, parts_a)
-    sums = call(
-        functools.partial(forward_sum_kernel, s),
-        "forward_sum",
-        [((s.main, s.width), BF16)] * s.count,
-        [],
-        [VMEM] * (s.slices + 3),
-        *parts_a,
-        sent_a[0],
+    packed = [((s.main, s.width), BF16)] * s.count
+    *sent_a, grads = call(
+        functools.partial(first_kernel, s),
+        "first",
+        packed + [((tok, depth), BF16)],
+        [
+            pltpu.VMEM((1, tok), jnp.int32),
+            pltpu.VMEM((tok, depth), BF16),
+            *tail_scratch(s, 16),
+            pltpu.SemaphoreType.DMA((3,)),
+        ],
+        [HBM] * 3,
         route_a,
-        score_a,
-    )
-    moved = [from_behind(sums[0], "section", 1)]
-    for d in range(1, s.count):
-        back = across(sums[d], -d, s)
-        y = call(
-            functools.partial(forward_add_kernel, s, d),
-            "forward_add",
-            [((s.main, s.width), BF16)],
-            [],
-            [VMEM] * 4,
-            back,
-            sent_a[d],
-            route_a,
-            score_a,
-        )[0]
-        moved.append(from_behind(y, "section", 1))
-    next_input = call(
-        functools.partial(forward_end_kernel, s),
-        "forward_end",
-        [((tok, depth), BF16)],
-        end_scratch(s) + [pltpu.VMEM((s.main, LANES), F32)],
-        [VMEM] * s.count,
-        *moved,
-    )[0]
-
-    sent_b = pack(s, route_b, upstream)
-    rows_b = dispatch(s, sent_b)
+        x_fwd[0],
+        grad_next[0],
+    )
+    upstream = from_behind(grads, "section", -1)
+    held = (*weights, route_a, route_b, score_a, score_b)
+    *weights, route_a, route_b, score_a, score_b = call(
+        load_kernel,
+        "load",
+        [(a.shape, a.dtype) for a in held],
+        [pltpu.SemaphoreType.DMA((len(held),))],
+        [HBM] * len(held),
+        *held,
+    )
     factors = call(
         functools.partial(saved_kernel, s),
         "saved",
@@ -548,40 +500,99 @@
         saved_gate[0],
         saved_up[0],
     )
+    got = cross(s, sent_a)
+    got[1:] = hold(got[1:], score_b, factors)
+    rows_a = spread(s, got)
+    sent_b = call(
+        functools.partial(pack_kernel, s),
+        "pack",
+        packed,
+        tail_scratch(s, 16),
+        [VMEM] * 2,
+        route_b,
+        hold(upstream, got[1:]),
+    )
+    got_b = cross(s, sent_b)
+
+    parts_a = call(
+        functools.partial(forward_kernel, s),
+        "forward",
+        [((s.main, s.width), BF16)] * s.blocks,
+        row_scratch(s),
+        [VMEM] * (s.blocks + 3),
+        *hold(rows_a, sent_b),
+        *weights,
+    )
     wide = s.width + LANES
+    got_b[1:] = hold(got_b[1:], parts_a)
+    rows_b = spread(s, got_b)
+    parts_a = hold(gather_parts(s, parts_a), got_b[1:])
+    sums_a = call(
+        functools.partial(forward_sum_kernel, s),
+        "forward_sum",
+        [((s.main, wide), BF16)] * s.count,
+        [],
+        [VMEM] * (s.blocks + 3),
+        *parts_a,
+        sent_a[0],
+        route_a,
+        score_a,
+    )
+    back_a = [across(sums_a[d], -d, s) for d in range(1, s.count)]
+
     parts_b = call(
         functools.partial(backward_kernel, s),
         "backward",
-        [((s.count, s.main, wide), BF16)] * s.slices,
-        weight_scratch(s, hidden),
-        [VMEM] * (s.blocks + 3) + [HBM] * 3,
-        *rows_b,
+        [((s.main, wide), BF16)] * s.blocks,
+        row_scratch(s),
+        [VMEM] * (s.blocks + 6),
+        *hold(rows_b, sums_a),
         *factors,
         *weights,
-        mib=32,
-        flops=flops,
-    )
-    parts_b = gather_parts(s, parts_b)
-    sums = call(
+    )
+    back_a = hold(back_a, parts_b)
+    moved = [from_behind(sums_a[0], "section", 1)]
+    for d in range(1, s.count):
+        y = call(
+            functools.partial(forward_add_kernel, s, d),
+            "forward_add",
+            [((s.main, s.width), BF16)],
+            [],
+            [VMEM] * 4,
+            back_a[d - 1],
+            sent_a[d],
+            route_a,
+            score_a,
+        )[0]
+        moved.append(from_behind(y, "section", 1))
+    sums_b = call(
         functools.partial(backward_sum_kernel, s),
         "backward_sum",
         [((s.main, wide), BF16)] * s.count,
         [],
-        [VMEM] * s.slices,
-        *parts_b,
-    )
-    back = [sums[0]] + [across(sums[d], -d, s) for d in range(1, s.count)]
+        [VMEM] * s.blocks,
+        *hold(gather_parts(s, parts_b), y),
+    )
+    back_b = [sums_b[0]] + [across(sums_b[d], -d, s) for d in range(1, s.count)]
     input_grad, score_grad = call(
         functools.partial(backward_end_kernel, s),
         "backward_end",
         [((tok, depth), BF16), ((1, tok), F32)],
         end_scratch(s),
         [VMEM] * (s.count + 3),
-        *back,
+        *hold(back_b, moved[0]),
         upstream,
         route_b,
         score_b,
     )
+    next_input = call(
+        functools.partial(forward_end_kernel, s),
+        "forward_end",
+        [((tok, depth), BF16)],
+        end_scratch(s) + [pltpu.VMEM((s.main, LANES), F32)],
+        [VMEM] * s.count,
+        *hold(moved, score_grad),
+    )[0]
     return next_input[None], input_grad[None], score_grad.reshape(1, tok, 1)
 
 

time: 65.5 us -> 50 us (0.76)
  waiting for transfers between devices: 26.8 us -> 18.2 us
  local copies, waits for them, and re-layouts: 8.53 us -> 1.03 us
    unnamed x30 -> x0, local copies, waits for them, and re-layouts: 8.48 us -> none
    ppermute x4, waiting for transfers between devices: 10.1 us -> 5.35 us  [across(): return lax.ppermute(block, 'expert', route)]
    ppermute x3, waiting for transfers between devices: 16.6 us -> 12.9 us  [from_behind(): return lax.ppermute(block, axis, route)]
    squeeze x1, local copies, waits for them, and re-layouts: 0.05 us -> 1.03 us  [body(): saved_up[0]]
    pallas_call x10 -> x11, Pallas kernels: 15.1 us -> 15.6 us  [call(): pl.pallas_call(kernel, out_shape=shapes, in_specs=ins, out_specs=[VMEM] *...]
    ppermute x6 -> x8, starting transfers between devices: 1.19 us -> 1.45 us  [beside(): return lax.ppermute(block, 'expert', route)]
  transfers between devices with their start and end apart: 13 -> 15, of which waited for: 5 -> 6; matrix products, arithmetic and copies ran while one was open for 0% -> 2% of each run, Pallas kernels for 21% -> 26%
where the time goes in v3:
time: 50 us; the launch traced here: 49.9 us
  waiting for transfers between devices  18.2 us (36%)
  Pallas kernels  15.6 us (31%)
  starting transfers between devices  14.3 us (29%)
  local copies, waits for them, and re-layouts  1.03 us (2%)
  between operations  0.71 us (1%)
    pallas_call x11, Pallas kernels, call(): pl.pallas_call(kernel, out_shape=shapes, in_specs=ins, out_specs=[VMEM] *...  15.6 us
    ppermute x3, waiting for transfers between devices, from_behind(): return lax.ppermute(block, axis, route)  12.9 us
    ppermute x3, starting transfers between devices, from_behind(): return lax.ppermute(block, axis, route)  6.73 us
    ppermute x4, starting transfers between devices, across(): return lax.ppermute(block, 'expert', route)  6.15 us
    ppermute x4, waiting for transfers between devices, across(): return lax.ppermute(block, 'expert', route)  5.35 us
    ppermute x8, starting transfers between devices, beside(): return lax.ppermute(block, 'expert', route)  1.45 us
    squeeze x1, local copies, waits for them, and re-layouts, body(): saved_up[0]  1.03 us
  transfers between devices with their start and end apart: 15, of which 6 were waited for; matrix products, arithmetic and copies ran while one was open for 2% of the time, Pallas kernels for 26%

profile of v3, /device:TPU:0, one launch (start us, length us, event | category | flops | bytes accessed | tf_op | source)
XLA Modules:
  0.0 49.9 jit_solution(18424518129019007193)
XLA Ops:
  0.6 1.5 %first.1 = (bf16[32,3840]{1,0:T(8,128)(2,1)S(1)}, bf16[32,3840]{1,0:T(8,128)(2,1)S(1)}, bf16[64,3584]{1,0:T(8,128)(2,1)S(1)}) custom-call(s32[1,64]{1,0:T(1,128)} %bitcast.22, bf16[64,3584]{1,0:T(8,128)(2,1)} %bitcast.19, bf16[64,3584]{1,0:T(8,128)(2,1)} %bitcast.20), custom_call_target="tpu_custom_call" | custom-call | tf_op jit(solution)/shard_map/first/pallas_call | solution.py:401
  2.1 6.1 %collective-permute-start.3 = (bf16[64,3584]{1,0:T(8,128)(2,1)S(1)}, bf16[64,3584]{1,0:T(8,128)(2,1)S(1)}, u32[]{:S(2)}, u32[]{:S(2)}) collective-permute-start(bf16[64,3584]{1,0:T(8,128)(2,1)S(1)} %get-tuple-element.64), channel_id=1, source_target_pairs={{4,0},{8,4},{12,8},{16,12},{20,16},{24,20},{28,24},{0,28},{5,1},{9... | collective-permute-start | bytes 1376264 | tf_op jit(solution)/shard_map/ppermute | solution.py:33
  8.2 1.5 %collective-permute-start = (bf16[32,3840]{1,0:T(8,128)(2,1)S(1)}, bf16[32,3840]{1,0:T(8,128)(2,1)S(1)}, u32[]{:S(2)}, u32[]{:S(2)}) collective-permute-start(bf16[32,3840]{1,0:T(8,128)(2,1)S(1)} %get-tuple-element.57.base), channel_id=1, source_target_pairs={{0,2},{1,3},{2,0},{3,1},{4,6},{5,7},{6,4},{7,5},{8,10},{9,11},{10,... | collective-permute-start | bytes 737288 | tf_op jit(solution)/shard_map/ppermute | solution.py:42
  9.7 1.0 %copy_bitcast_fusion = (bf16[4,34,512]{2,1,0:T(8,128)(2,1)S(1)}, bf16[4,34,512]{2,1,0:T(8,128)(2,1)S(1)}) fusion(bf16[1,4,34,512]{3,1,2,0:T(4,128)(2,1)} %param.13, bf16[1,4,34,512]{3,1,2,0:T(4,128)(2,1)} %param.12), kind=kLoop, calls=%fused_computation | loop fusion | bytes 557056 | tf_op jit(solution)/shard_map/squeeze | solution.py:501
  11.0 4.3 %load.1 = (bf16[3584,512]{1,0:T(8,128)(2,1)S(1)}, bf16[3584,512]{1,0:T(8,128)(2,1)S(1)}, bf16[512,3584]{1,0:T(8,128)(2,1)S(1)}, s32[1,64]{1,0:T(1,128)S(1)}, s32...) custom-call(bf16[3584,512]{1,0:T(8,128)(2,1)} %bitcast.16, bf16[3584,512]{1,0:T(8,128)(2,1)} %bitcast.17, ...), custom_call_target="tpu_custom_call" | custom-call | tf_op jit(solution)/shard_map/load/pallas_call | solution.py:401
  15.3 0.3 collective-permute-done.refs_1_
  15.9 2.1 %collective-permute-done.3.x_ref.refs_2_ = bf16[64,3584]{1,0:T(8,128)(2,1)S(1)} collective-permute-done((bf16[64,3584]{1,0:T(8,128)(2,1)S(1)}, bf16[64,3584]{1,0:T(8,128)(2,1)S(1)}, u32[]{:S(2)}, u32[]{:S(2)}) %collective-permute-start.3) | collective-permute-done | bytes 458784 | tf_op jit(solution)/shard_map/ppermute | solution.py:33
  18.0 0.4 pack.1
  18.4 1.6 %collective-permute-start.6 = (bf16[32,3840]{1,0:T(8,128)(2,1)S(1)}, bf16[32,3840]{1,0:T(8,128)(2,1)S(1)}, u32[]{:S(2)}, u32[]{:S(2)}) collective-permute-start(bf16[32,3840]{1,0:T(8,128)(2,1)S(1)} %get-tuple-element.67), channel_id=1, source_target_pairs={{0,2},{1,3},{2,0},{3,1},{4,6},{5,7},{6,4},{7,5},{8,10},{9,11},{10,... | collective-permute-start | bytes 737288 | tf_op jit(solution)/shard_map/ppermute | solution.py:42
  20.0 2.0 %forward.1 = (bf16[32,3840]{1,0:T(8,128)(2,1)S(1)}, bf16[32,3840]{1,0:T(8,128)(2,1)S(1)}, bf16[32,3840]{1,0:T(8,128)(2,1)S(1)}, bf16[32,3840]{1,0:T(8,128)(2,1)S(1)}) custom-call(bf16[32,3840]{1,0:T(8,128)(2,1)S(1)} %get-tuple-element.68.refs_0_.refs_4_, bf16[32,3840]{1,0:T(8,128)(2,1)S(1)} %collective-permute-done.refs_1_, ...), custom_call_target="tpu_custom_call" | custom-call | tf_op jit(solution)/shard_map/forward/pallas_call | solution.py:401
  22.0 0.5 collective-permute-start.5
  22.6 2.7 %collective-permute-done.6.refs_1_ = bf16[32,3840]{1,0:T(8,128)(2,1)S(1)} collective-permute-done((bf16[32,3840]{1,0:T(8,128)(2,1)S(1)}, bf16[32,3840]{1,0:T(8,128)(2,1)S(1)}, u32[]{:S(2)}, u32[]{:S(2)}) %collective-permute-start.6) | collective-permute-done | bytes 245792 | tf_op jit(solution)/shard_map/ppermute | solution.py:42
  25.3 0.4 forward_sum.1
  25.7 1.6 %collective-permute-start.8 = (bf16[32,3968]{1,0:T(8,128)(2,1)S(1)}, bf16[32,3968]{1,0:T(8,128)(2,1)S(1)}, u32[]{:S(2)}, u32[]{:S(2)}) collective-permute-start(bf16[32,3968]{1,0:T(8,128)(2,1)S(1)} %get-tuple-element.87), channel_id=1, source_target_pairs={{0,2},{1,3},{2,0},{3,1},{4,6},{5,7},{6,4},{7,5},{8,10},{9,11},{10,... | collective-permute-start | bytes 761864 | tf_op jit(solution)/shard_map/ppermute | solution.py:42
  27.3 3.9 %backward.1 = (bf16[32,3968]{1,0:T(8,128)(2,1)S(1)}, bf16[32,3968]{1,0:T(8,128)(2,1)S(1)}, bf16[32,3968]{1,0:T(8,128)(2,1)S(1)}, bf16[32,3968]{1,0:T(8,128)(2,1)S(1)}) custom-call(bf16[32,3840]{1,0:T(8,128)(2,1)S(1)} %get-tuple-element.88.refs_0_, bf16[32,3840]{1,0:T(8,128)(2,1)S(1)} %collective-permute-done.6.refs_1_, ...), custom_call_target="tpu_custom_call" | custom-call | tf_op jit(solution)/shard_map/backward/pallas_call | solution.py:401
  31.1 0.3 collective-permute-start.12
  31.7 0.3 collective-permute-start.7
  32.0 2.3 %collective-permute-done.8.back = bf16[32,3968]{1,0:T(8,128)(2,1)S(1)} collective-permute-done((bf16[32,3968]{1,0:T(8,128)(2,1)S(1)}, bf16[32,3968]{1,0:T(8,128)(2,1)S(1)}, u32[]{:S(2)}, u32[]{:S(2)}) %collective-permute-start.8) | collective-permute-done | bytes 253984 | tf_op jit(solution)/shard_map/ppermute | solution.py:42
  34.8 1.6 %collective-permute-start.14 = (bf16[32,3968]{1,0:T(8,128)(2,1)S(1)}, bf16[32,3968]{1,0:T(8,128)(2,1)S(1)}, u32[]{:S(2)}, u32[]{:S(2)}) collective-permute-start(bf16[32,3968]{1,0:T(8,128)(2,1)S(1)} %get-tuple-element.102), channel_id=1, source_target_pairs={{0,2},{1,3},{2,0},{3,1},{4,6},{5,7},{6,4},{7,5},{8,10},{9,11},{10,... | collective-permute-start | bytes 761864 | tf_op jit(solution)/shard_map/ppermute | solution.py:42
  36.4 0.3 collective-permute-start.11
  36.7 7.1 %collective-permute-done.7.refs_0_ = bf16[32,3968]{1,0:T(8,128)(2,1)S(1)} collective-permute-done((bf16[32,3968]{1,0:T(8,128)(2,1)S(1)}, bf16[32,3968]{1,0:T(8,128)(2,1)S(1)}, u32[]{:S(2)}, u32[]{:S(2)}) %collective-permute-start.7) | collective-permute-done | bytes 253984 | tf_op jit(solution)/shard_map/ppermute | solution.py:33
  43.8 1.2 %backward_end.1 = (bf16[64,3584]{1,0:T(8,128)(2,1)}, f32[1,64]{1,0:T(1,128)}) custom-call(bf16[32,3968]{1,0:T(8,128)(2,1)S(1)} %get-tuple-element.103.refs_0_, bf16[32,3968]{1,0:T(8,128)(2,1)S(1)} %collective-permute-done.14.refs_1_, bf16[64,3584]{1,0:T(8,128)(2,1)S(1)} %collective-permute-done.3.x_ref.refs_2_, ...), custom_call_target="tpu_custom_call" | custom-call | tf_op jit(solution)/shard_map/backward_end/pallas_call | solution.py:401
  45.0 3.7 %collective-permute-done.11.refs_1_ = bf16[32,3840]{1,0:T(8,128)(2,1)S(1)} collective-permute-done((bf16[32,3840]{1,0:T(8,128)(2,1)S(1)}, bf16[32,3840]{1,0:T(8,128)(2,1)S(1)}, u32[]{:S(2)}, u32[]{:S(2)}) %collective-permute-start.11) | collective-permute-done | bytes 245792 | tf_op jit(solution)/shard_map/ppermute | solution.py:33
  48.7 1.2 %forward_end.1 = bf16[64,3584]{1,0:T(8,128)(2,1)} custom-call(bf16[32,3968]{1,0:T(8,128)(2,1)S(1)} %collective-permute-done.7.refs_0_, bf16[32,3840]{1,0:T(8,128)(2,1)S(1)} %collective-permute-done.11.refs_1_), custom_call_target="tpu_custom_call" | custom-call | tf_op jit(solution)/shard_map/forward_end/pallas_call | solution.py:401
  (18 shorter events, 1.4 us)
Async XLA Ops:
  2.1 15.8 %collective-permute-start.3 = (bf16[64,3584]{1,0:T(8,128)(2,1)S(1)}, bf16[64,3584]{1,0:T(8,128)(2,1)S(1)}, u32[]{:S(2)}, u32[]{:S(2)}) collective-permute-start(bf16[64,3584]{1,0:T(8,128)(2,1)S(1)} %get-tuple-element.64), channel_id=1, source_target_pairs={{4,0},{8,4},{12,8},{16,12},{20,16},{24,20},{28,24},{0,28},{5,1},{9... | collective-permute-start | bytes 1376264 | tf_op jit(solution)/shard_map/ppermute | solution.py:33
  8.2 7.4 %collective-permute-start = (bf16[32,3840]{1,0:T(8,128)(2,1)S(1)}, bf16[32,3840]{1,0:T(8,128)(2,1)S(1)}, u32[]{:S(2)}, u32[]{:S(2)}) collective-permute-start(bf16[32,3840]{1,0:T(8,128)(2,1)S(1)} %get-tuple-element.57.base), channel_id=1, source_target_pairs={{0,2},{1,3},{2,0},{3,1},{4,6},{5,7},{6,4},{7,5},{8,10},{9,11},{10,... | collective-permute-start | bytes 737288 | tf_op jit(solution)/shard_map/ppermute | solution.py:42
  9.7 10.3 %collective-permute-start.1 = (bf16[32,3840]{1,0:T(8,128)(2,1)S(1)}, bf16[32,3840]{1,0:T(8,128)(2,1)S(1)}, u32[]{:S(2)}, u32[]{:S(2)}) collective-permute-start(bf16[32,3840]{1,0:T(8,128)(2,1)S(1)} %get-tuple-element.68.refs_0_.refs_4_), channel_id=1, source_target_pairs={{0,1},{1,0},{2,3},{3,2},{4,5},{5,4},{6,7},{7,6},{8,9},{9,8},{10,11... | collective-permute-start | bytes 737288 | tf_op jit(solution)/shard_map/ppermute | solution.py:51
  15.6 4.4 %collective-permute-start.2 = (bf16[32,3840]{1,0:T(8,128)(2,1)S(1)}, bf16[32,3840]{1,0:T(8,128)(2,1)S(1)}, u32[]{:S(2)}, u32[]{:S(2)}) collective-permute-start(bf16[32,3840]{1,0:T(8,128)(2,1)S(1)} %collective-permute-done.refs_1_), channel_id=1, source_target_pairs={{0,1},{1,0},{2,3},{3,2},{4,5},{5,4},{6,7},{7,6},{8,9},{9,8},{10,11... | collective-permute-start | bytes 737288 | tf_op jit(solution)/shard_map/ppermute | solution.py:51
  18.4 6.9 %collective-permute-start.6 = (bf16[32,3840]{1,0:T(8,128)(2,1)S(1)}, bf16[32,3840]{1,0:T(8,128)(2,1)S(1)}, u32[]{:S(2)}, u32[]{:S(2)}) collective-permute-start(bf16[32,3840]{1,0:T(8,128)(2,1)S(1)} %get-tuple-element.67), channel_id=1, source_target_pairs={{0,2},{1,3},{2,0},{3,1},{4,6},{5,7},{6,4},{7,5},{8,10},{9,11},{10,... | collective-permute-start | bytes 737288 | tf_op jit(solution)/shard_map/ppermute | solution.py:42
  22.0 3.4 %collective-permute-start.4 = (bf16[32,3840]{1,0:T(8,128)(2,1)S(1)}, bf16[32,3840]{1,0:T(8,128)(2,1)S(1)}, u32[]{:S(2)}, u32[]{:S(2)}) collective-permute-start(bf16[32,3840]{1,0:T(8,128)(2,1)S(1)} %get-tuple-element.77), channel_id=1, source_target_pairs={{0,1},{1,0},{2,3},{3,2},{4,5},{5,4},{6,7},{7,6},{8,9},{9,8},{10,11... | collective-permute-start | bytes 737288 | tf_op jit(solution)/shard_map/ppermute | solution.py:51
  22.0 3.3 %collective-permute-start.5 = (bf16[32,3840]{1,0:T(8,128)(2,1)S(1)}, bf16[32,3840]{1,0:T(8,128)(2,1)S(1)}, u32[]{:S(2)}, u32[]{:S(2)}) collective-permute-start(bf16[32,3840]{1,0:T(8,128)(2,1)S(1)} %get-tuple-element.78), channel_id=1, source_target_pairs={{0,1},{1,0},{2,3},{3,2},{4,5},{5,4},{6,7},{7,6},{8,9},{9,8},{10,11... | collective-permute-start | bytes 737288 | tf_op jit(solution)/shard_map/ppermute | solution.py:51
  22.5 4.7 %collective-permute-start.9 = (bf16[32,3840]{1,0:T(8,128)(2,1)S(1)}, bf16[32,3840]{1,0:T(8,128)(2,1)S(1)}, u32[]{:S(2)}, u32[]{:S(2)}) collective-permute-start(bf16[32,3840]{1,0:T(8,128)(2,1)S(1)} %get-tuple-element.88.refs_0_), channel_id=1, source_target_pairs={{0,1},{1,0},{2,3},{3,2},{4,5},{5,4},{6,7},{7,6},{8,9},{9,8},{10,11... | collective-permute-start | bytes 737288 | tf_op jit(solution)/shard_map/ppermute | solution.py:51
  25.3 1.9 %collective-permute-start.10 = (bf16[32,3840]{1,0:T(8,128)(2,1)S(1)}, bf16[32,3840]{1,0:T(8,128)(2,1)S(1)}, u32[]{:S(2)}, u32[]{:S(2)}) collective-permute-start(bf16[32,3840]{1,0:T(8,128)(2,1)S(1)} %collective-permute-done.6.refs_1_), channel_id=1, source_target_pairs={{0,1},{1,0},{2,3},{3,2},{4,5},{5,4},{6,7},{7,6},{8,9},{9,8},{10,11... | collective-permute-start | bytes 737288 | tf_op jit(solution)/shard_map/ppermute | solution.py:51
  25.7 8.6 %collective-permute-start.8 = (bf16[32,3968]{1,0:T(8,128)(2,1)S(1)}, bf16[32,3968]{1,0:T(8,128)(2,1)S(1)}, u32[]{:S(2)}, u32[]{:S(2)}) collective-permute-start(bf16[32,3968]{1,0:T(8,128)(2,1)S(1)} %get-tuple-element.87), channel_id=1, source_target_pairs={{0,2},{1,3},{2,0},{3,1},{4,6},{5,7},{6,4},{7,5},{8,10},{9,11},{10,... | collective-permute-start | bytes 761864 | tf_op jit(solution)/shard_map/ppermute | solution.py:42
  31.1 3.4 %collective-permute-start.12 = (bf16[32,3968]{1,0:T(8,128)(2,1)S(1)}, bf16[32,3968]{1,0:T(8,128)(2,1)S(1)}, u32[]{:S(2)}, u32[]{:S(2)}) collective-permute-start(bf16[32,3968]{1,0:T(8,128)(2,1)S(1)} %get-tuple-element.94), channel_id=1, source_target_pairs={{0,1},{1,0},{2,3},{3,2},{4,5},{5,4},{6,7},{7,6},{8,9},{9,8},{10,11... | collective-permute-start | bytes 761864 | tf_op jit(solution)/shard_map/ppermute | solution.py:51
  31.4 3.2 %collective-permute-start.13 = (bf16[32,3968]{1,0:T(8,128)(2,1)S(1)}, bf16[32,3968]{1,0:T(8,128)(2,1)S(1)}, u32[]{:S(2)}, u32[]{:S(2)}) collective-permute-start(bf16[32,3968]{1,0:T(8,128)(2,1)S(1)} %get-tuple-element.95), channel_id=1, source_target_pairs={{0,1},{1,0},{2,3},{3,2},{4,5},{5,4},{6,7},{7,6},{8,9},{9,8},{10,11... | collective-permute-start | bytes 761864 | tf_op jit(solution)/shard_map/ppermute | solution.py:51
  31.7 12.1 %collective-permute-start.7 = (bf16[32,3968]{1,0:T(8,128)(2,1)S(1)}, bf16[32,3968]{1,0:T(8,128)(2,1)S(1)}, u32[]{:S(2)}, u32[]{:S(2)}) collective-permute-start(bf16[32,3968]{1,0:T(8,128)(2,1)S(1)} %get-tuple-element.86), channel_id=1, source_target_pairs={{28,0},{0,4},{4,8},{8,12},{12,16},{16,20},{20,24},{24,28},{29,1},{... | collective-permute-start | bytes 761864 | tf_op jit(solution)/shard_map/ppermute | solution.py:33
  34.8 9.0 %collective-permute-start.14 = (bf16[32,3968]{1,0:T(8,128)(2,1)S(1)}, bf16[32,3968]{1,0:T(8,128)(2,1)S(1)}, u32[]{:S(2)}, u32[]{:S(2)}) collective-permute-start(bf16[32,3968]{1,0:T(8,128)(2,1)S(1)} %get-tuple-element.102), channel_id=1, source_target_pairs={{0,2},{1,3},{2,0},{3,1},{4,6},{5,7},{6,4},{7,5},{8,10},{9,11},{10,... | collective-permute-start | bytes 761864 | tf_op jit(solution)/shard_map/ppermute | solution.py:42
  36.4 12.3 %collective-permute-start.11 = (bf16[32,3840]{1,0:T(8,128)(2,1)S(1)}, bf16[32,3840]{1,0:T(8,128)(2,1)S(1)}, u32[]{:S(2)}, u32[]{:S(2)}) collective-permute-start(bf16[32,3840]{1,0:T(8,128)(2,1)S(1)} %forward_add.1), channel_id=1, source_target_pairs={{28,0},{0,4},{4,8},{8,12},{12,16},{16,20},{20,24},{24,28},{29,1},{... | collective-permute-start | bytes 737288 | tf_op jit(solution)/shard_map/ppermute | solution.py:33

commit v4 on v3

--- a/solution.py
+++ b/solution.py
@@ -9,6 +9,8 @@
 
 EXPERTS = 2
 LANES = 128
+HALVES_A = 2
+HALVES_B = 1
 F32 = jnp.float32
 BF16 = jnp.bfloat16
 NT = (((1,), (1,)), ((), ()))
@@ -135,21 +137,17 @@
         outs[d][:, s.depth :] = tail_ref[...].astype(BF16)
 
 
-def first_kernel(s, route_hbm, x_hbm, dy_hbm, *rest):
-    outs, dy_ref = rest[: s.count], rest[s.count]
-    route_ref, x_ref, extra_ref, tail_ref, sems = rest[s.count + 1 :]
+def first_kernel(s, route_hbm, x_hbm, *rest):
+    outs, (route_ref, x_ref, extra_ref, tail_ref, sems) = rest[: s.count], rest[s.count :]
     copies = [
-        pltpu.make_async_copy(src, dst, sems.at[i])
-        for i, (src, dst) in enumerate(
-            ((route_hbm, route_ref), (x_hbm, x_ref), (dy_hbm, dy_ref))
-        )
+        pltpu.make_async_copy(route_hbm, route_ref, sems.at[0]),
+        pltpu.make_async_copy(x_hbm, x_ref, sems.at[1]),
     ]
     for copy in copies:
         copy.start()
-    copies[0].wait()
-    copies[1].wait()
+    for copy in copies:
+        copy.wait()
     pack_rows(s, route_ref[...].astype(F32), x_ref[...], outs, extra_ref, tail_ref)
-    copies[2].wait()
 
 
 def pack_kernel(s, route_ref, x_ref, *rest):
@@ -176,16 +174,26 @@
     rows_ref[s.blocks * s.main :, :] = extra_ref[...].astype(BF16)
 
 
+def put(outs, i, at, value, s):
+    if i < s.count:
+        outs[i][:, at] = value
+        return
+    n = (len(outs) - s.count) // (s.blocks - s.count)
+    rows = s.main // n
+    for h in range(n):
+        outs[s.count + (i - s.count) * n + h][:, at] = value[h * rows : (h + 1) * rows]
+
+
 def scatter_chunk(value, outs, extra_ref, at, s):
     for i in range(s.blocks):
-        outs[i][:, at] = value[i * s.main : (i + 1) * s.main].astype(BF16)
+        put(outs, i, at, value[i * s.main : (i + 1) * s.main].astype(BF16), s)
     extra_ref[:, at] = value[s.blocks * s.main :]
 
 
 def scatter_tails(outs, extra_ref, tail_ref, s):
     for i in range(s.blocks):
         fold(extra_ref, i * s.extra, tail_ref, s)
-        outs[i][:, s.depth : s.width] = tail_ref[...].astype(BF16)
+        put(outs, i, slice(s.depth, s.width), tail_ref[...].astype(BF16), s)
 
 
 def chunk_of(depth):
@@ -288,11 +296,12 @@
     inner = jnp.sum(a * hb[...], axis=1, keepdims=True)
     for i in range(s.blocks):
         first = s.blocks * s.main + i * s.extra
-        outs[i][:, s.width :] = put_inner(
+        pieces = put_inner(
             inner[i * s.main : (i + 1) * s.main],
             [inner[first + j : first + j + 1] for j in range(s.extra)],
             s,
         )
+        put(outs, i, slice(s.width, s.width + LANES), pieces, s)
     tail_ref[...] = jnp.zeros_like(tail_ref)
     for c in range(0, s.depth, chunk):
         part = lax.dot_general(
@@ -302,23 +311,27 @@
     scatter_tails(outs, extra_ref, tail_ref, s)
 
 
-def total_of(parts, d, k):
+def total_of(parts, d, s):
     total = parts[d][...].astype(F32)
-    for part in parts[d + len(parts) // k :: len(parts) // k]:
-        total = total + part[...].astype(F32)
+    n = (len(parts) - s.count) // (s.blocks - s.count)
+    for i in range(s.count + d, s.blocks, s.count):
+        first = s.count + (i - s.count) * n
+        halves = [part[...].astype(F32) for part in parts[first : first + n]]
+        total = total + jnp.concatenate(halves, axis=0)
     return total
 
 
 def forward_sum_kernel(s, *refs):
-    parts = refs[: s.blocks]
-    own, route_ref, score_ref, y_ref = refs[s.blocks : s.blocks + 4]
-    backs = refs[s.blocks + 4 :]
+    n = len(refs) - 3 - s.count
+    parts = refs[:n]
+    own, route_ref, score_ref, y_ref = refs[n : n + 4]
+    backs = refs[n + 4 :]
     for d in range(1, s.count):
-        backs[d - 1][:, : s.width] = total_of(parts, d, s.slices).astype(BF16)
+        backs[d - 1][:, : s.width] = total_of(parts, d, s).astype(BF16)
         backs[d - 1][:, s.width :] = jnp.zeros((s.main, LANES), BF16)
     route_row = route_ref[...].astype(F32)
     main, extra = slot_values(route_row, 2.5 * score_ref[...], expert_at(s, 0), s)
-    add_gated(y_ref, own, main, extra, total_of(parts, 0, s.slices), s)
+    add_gated(y_ref, own, main, extra, total_of(parts, 0, s), s)
     y_ref[s.folds : s.folds + 1, s.depth : s.depth + s.tok] = route_row.astype(BF16)
     y_ref[:, s.width :] = jnp.zeros((s.main, LANES), BF16)
 
@@ -327,6 +340,7 @@
     route_row = route_ref[...].astype(F32)
     main, extra = slot_values(route_row, 2.5 * score_ref[...], expert_at(s, distance), s)
     add_gated(y_ref, base, main, extra, back[:, : s.width].astype(F32), s)
+    y_ref[:, s.width :] = jnp.zeros((s.main, LANES), BF16)
 
 
 def tokens_of(packs, route_row, rows_ref, extra_ref, tail_ref, s):
@@ -359,9 +373,9 @@
 
 
 def backward_sum_kernel(s, *refs):
-    parts, outs = refs[: s.blocks], refs[s.blocks :]
+    parts, outs = refs[: -s.count], refs[-s.count :]
     for d in range(s.count - 1, -1, -1):
-        total = total_of(parts, d, s.slices)
+        total = total_of(parts, d, s)
         outs[d][:, : s.width] = total[:, : s.width].astype(BF16)
         main, extra = get_inner(total[:, s.width :], s)
         outs[d][:, s.width :] = put_inner(main, extra, s)
@@ -417,6 +431,17 @@
     ]
 
 
+def load(*arrays):
+    return call(
+        load_kernel,
+        "load",
+        [(a.shape, a.dtype) for a in arrays],
+        [pltpu.SemaphoreType.DMA((len(arrays),))],
+        [HBM] * len(arrays),
+        *arrays,
+    )
+
+
 def row_scratch(s):
     return [pltpu.VMEM((s.rows, s.depth), BF16), *tail_scratch(s, s.tail_rows)]
 
@@ -426,15 +451,22 @@
 
 
 def spread(s, got):
-    return got + [beside(b, k, s) for k in range(1, s.slices) for b in got]
+    return list(got) + [beside(b, k, s) for k in range(1, s.slices) for b in got]
 
 
 def hold(values, *after):
     return lax.optimization_barrier((values, after))[0]
 
 
+def parts_shape(s, width, halves):
+    kept = [((s.main, width), BF16)] * s.count
+    return kept + [((s.main // halves, width), BF16)] * ((s.blocks - s.count) * halves)
+
+
 def gather_parts(s, parts):
-    return [beside(p, -(i // s.count), s) if i >= s.count else p for i, p in enumerate(parts)]
+    n = (len(parts) - s.count) // (s.blocks - s.count)
+    moved = [beside(p, -(i // n // s.count + 1), s) for i, p in enumerate(parts[s.count :])]
+    return list(parts[: s.count]) + moved
 
 
 def end_scratch(s):
@@ -459,50 +491,56 @@
     tok, depth = x_fwd.shape[1:]
     s = Sizes(saved_gate.shape[2], depth, EXPERTS, groups // EXPERTS, tok)
     hidden = w_gate.shape[2]
-    weights = (w_gate[0], w_up[0], w_down[0])
     route_a = routes_fwd.reshape(1, tok)
     route_b = routes_bwd.reshape(1, tok)
     score_a = scores_fwd.reshape(1, tok)
     score_b = scores_bwd.reshape(1, tok)
 
     packed = [((s.main, s.width), BF16)] * s.count
-    *sent_a, grads = call(
+    sent_a = call(
         functools.partial(first_kernel, s),
         "first",
-        packed + [((tok, depth), BF16)],
+        packed,
         [
             pltpu.VMEM((1, tok), jnp.int32),
             pltpu.VMEM((tok, depth), BF16),
             *tail_scratch(s, 16),
-            pltpu.SemaphoreType.DMA((3,)),
+            pltpu.SemaphoreType.DMA((2,)),
         ],
-        [HBM] * 3,
+        [HBM] * 2,
         route_a,
         x_fwd[0],
-        grad_next[0],
-    )
-    upstream = from_behind(grads, "section", -1)
-    held = (*weights, route_a, route_b, score_a, score_b)
-    *weights, route_a, route_b, score_a, score_b = call(
-        load_kernel,
-        "load",
-        [(a.shape, a.dtype) for a in held],
-        [pltpu.SemaphoreType.DMA((len(held),))],
-        [HBM] * len(held),
-        *held,
-    )
-    factors = call(
-        functools.partial(saved_kernel, s),
-        "saved",
-        [((s.rows, hidden), F32)] * 3,
-        [pltpu.VMEM((s.rows, hidden), F32)] * 2,
-        [VMEM] * 2,
-        saved_gate[0],
-        saved_up[0],
-    )
+    )
+    upstream = from_behind(grad_next, "section", -1)[0]
+    wg, wu, route_a, score_a = load(w_gate[0], w_up[0], route_a, score_a)
     got = cross(s, sent_a)
-    got[1:] = hold(got[1:], score_b, factors)
-    rows_a = spread(s, got)
+    got[1:] = hold(got[1:], score_a)
+    wd, route_b, score_b = load(hold(w_down[0], got[1:]), route_b, score_b)
+    parts_a = call(
+        functools.partial(forward_kernel, s),
+        "forward",
+        parts_shape(s, s.width, HALVES_A),
+        row_scratch(s),
+        [VMEM] * (s.blocks + 3),
+        *spread(s, got),
+        wg,
+        wu,
+        wd,
+    )
+    wide = s.width + LANES
+    sums_a = call(
+        functools.partial(forward_sum_kernel, s),
+        "forward_sum",
+        [((s.main, wide), BF16)] * s.count,
+        [],
+        [VMEM] * (len(parts_a) + 3),
+        *gather_parts(s, parts_a),
+        sent_a[0],
+        route_a,
+        score_a,
+    )
+    back_a = [across(sums_a[d], -d, s) for d in range(1, s.count)]
+    moved = [from_behind(sums_a[0], "section", 1)]
     sent_b = call(
         functools.partial(pack_kernel, s),
         "pack",
@@ -510,53 +548,23 @@
         tail_scratch(s, 16),
         [VMEM] * 2,
         route_b,
-        hold(upstream, got[1:]),
+        hold(upstream, sums_a),
     )
     got_b = cross(s, sent_b)
-
-    parts_a = call(
-        functools.partial(forward_kernel, s),
-        "forward",
-        [((s.main, s.width), BF16)] * s.blocks,
-        row_scratch(s),
-        [VMEM] * (s.blocks + 3),
-        *hold(rows_a, sent_b),
-        *weights,
-    )
-    wide = s.width + LANES
-    got_b[1:] = hold(got_b[1:], parts_a)
-    rows_b = spread(s, got_b)
-    parts_a = hold(gather_parts(s, parts_a), got_b[1:])
-    sums_a = call(
-        functools.partial(forward_sum_kernel, s),
-        "forward_sum",
-        [((s.main, wide), BF16)] * s.count,
-        [],
-        [VMEM] * (s.blocks + 3),
-        *parts_a,
-        sent_a[0],
-        route_a,
-        score_a,
-    )
-    back_a = [across(sums_a[d], -d, s) for d in range(1, s.count)]
-
-    parts_b = call(
-        functools.partial(backward_kernel, s),
-        "backward",
-        [((s.main, wide), BF16)] * s.blocks,
-        row_scratch(s),
-        [VMEM] * (s.blocks + 6),
-        *hold(rows_b, sums_a),
-        *factors,
-        *weights,
-    )
-    back_a = hold(back_a, parts_b)
-    moved = [from_behind(sums_a[0], "section", 1)]
+    factors = call(
+        functools.partial(saved_kernel, s),
+        "saved",
+        [((s.rows, hidden), F32)] * 3,
+        [pltpu.VMEM((s.rows, hidden), F32)] * 2,
+        [VMEM] * 2,
+        *hold((saved_gate[0], saved_up[0]), sent_b),
+    )
+    back_a = hold(back_a, factors)
     for d in range(1, s.count):
         y = call(
             functools.partial(forward_add_kernel, s, d),
             "forward_add",
-            [((s.main, s.width), BF16)],
+            [((s.main, wide), BF16)],
             [],
             [VMEM] * 4,
             back_a[d - 1],
@@ -565,34 +573,56 @@
             score_a,
         )[0]
         moved.append(from_behind(y, "section", 1))
-    sums_b = call(
-        functools.partial(backward_sum_kernel, s),
-        "backward_sum",
-        [((s.main, wide), BF16)] * s.count,
-        [],
-        [VMEM] * s.blocks,
-        *hold(gather_parts(s, parts_b), y),
+    got_b[1:] = hold(got_b[1:], y)
+    def middle(got_b, factors, weights):
+        parts_b = call(
+            functools.partial(backward_kernel, s),
+            "backward",
+            parts_shape(s, wide, HALVES_B),
+            row_scratch(s),
+            [VMEM] * (s.blocks + 6),
+            *spread(s, got_b),
+            *factors,
+                *weights,
+        )
+        sums_b = call(
+            functools.partial(backward_sum_kernel, s),
+            "backward_sum",
+            [((s.main, wide), BF16)] * s.count,
+            [],
+            [VMEM] * len(parts_b),
+            *gather_parts(s, parts_b),
+        )
+        return tuple(sums_b)
+
+    sums_b = lax.cond(
+        route_b[0, 0] < s.count,
+        middle,
+        lambda got_b, factors, weights: tuple(sums_a),
+        tuple(got_b),
+        tuple(factors),
+        (wg, wu, wd),
     )
     back_b = [sums_b[0]] + [across(sums_b[d], -d, s) for d in range(1, s.count)]
+    next_input = call(
+        functools.partial(forward_end_kernel, s),
+        "forward_end",
+        [((tok, depth), BF16)],
+        end_scratch(s) + [pltpu.VMEM((s.main, LANES), F32)],
+        [VMEM] * s.count,
+        *moved,
+    )[0]
     input_grad, score_grad = call(
         functools.partial(backward_end_kernel, s),
         "backward_end",
         [((tok, depth), BF16), ((1, tok), F32)],
         end_scratch(s),
         [VMEM] * (s.count + 3),
-        *hold(back_b, moved[0]),
+        *hold(back_b, next_input),
         upstream,
         route_b,
         score_b,
     )
-    next_input = call(
-        functools.partial(forward_end_kernel, s),
-        "forward_end",
-        [((tok, depth), BF16)],
-        end_scratch(s) + [pltpu.VMEM((s.main, LANES), F32)],
-        [VMEM] * s.count,
-        *hold(moved, score_grad),
-    )[0]
     return next_input[None], input_grad[None], score_grad.reshape(1, tok, 1)
 
 

time: 50 us -> 51.8 us (1.036)
  waiting for transfers between devices: 18.2 us -> 20.6 us
  Pallas kernels: 15.6 us -> 17.1 us
  starting transfers between devices: 14.3 us -> 13.1 us
  local copies, waits for them, and re-layouts: 1.03 us -> 0.07 us
    ppermute x3, waiting for transfers between devices: 12.9 us -> 0.01 us  [from_behind(): return lax.ppermute(block, axis, route)]
    ppermute x4, waiting for transfers between devices: 5.35 us -> 16.8 us  [across(): return lax.ppermute(block, 'expert', route)]
    ppermute x8 -> x10, waiting for transfers between devices: 0.02 us -> 3.73 us  [beside(): return lax.ppermute(block, 'expert', route)]
    ppermute x3, starting transfers between devices: 6.73 us -> 4.68 us  [from_behind(): return lax.ppermute(block, axis, route)]
    pallas_call x11 -> x12, Pallas kernels: 15.6 us -> 17.1 us  [call(): pl.pallas_call(kernel, out_shape=shapes, in_specs=ins, out_specs=[VMEM] *...]
    ppermute x8 -> x10, starting transfers between devices: 1.45 us -> 2.73 us  [beside(): return lax.ppermute(block, 'expert', route)]
    squeeze x1, local copies, waits for them, and re-layouts: 1.03 us -> 0.05 us  [body(): saved_up[0]]
  transfers between devices with their start and end apart: 15 -> 17, of which waited for: 6 -> 11; matrix products, arithmetic and copies ran while one was open for 2% -> 0% of each run, Pallas kernels for 26% -> 28%
where the time goes in v4:
time: 51.8 us; the launch traced here: 51.6 us
  waiting for transfers between devices  20.6 us (40%)
  Pallas kernels  17.1 us (33%)
  starting transfers between devices  13.1 us (25%)
  between operations  0.79 us (2%)
    pallas_call x12, Pallas kernels, call(): pl.pallas_call(kernel, out_shape=shapes, in_specs=ins, out_specs=[VMEM] *...  17.1 us
    ppermute x4, waiting for transfers between devices, across(): return lax.ppermute(block, 'expert', route)  16.8 us
    ppermute x4, starting transfers between devices, across(): return lax.ppermute(block, 'expert', route)  5.67 us
    ppermute x3, starting transfers between devices, from_behind(): return lax.ppermute(block, axis, route)  4.68 us
    ppermute x10, waiting for transfers between devices, beside(): return lax.ppermute(block, 'expert', route)  3.73 us
    ppermute x10, starting transfers between devices, beside(): return lax.ppermute(block, 'expert', route)  2.73 us
  transfers between devices with their start and end apart: 17, of which 11 were waited for; matrix products, arithmetic and copies ran while one was open for 0% of the time, Pallas kernels for 28%

profile of v4, /device:TPU:0, one launch (start us, length us, event | category | flops | bytes accessed | tf_op | source)
XLA Modules:
  0.0 51.6 jit_solution(10004404344501209862)
XLA Ops:
  0.6 1.5 %first.1 = (bf16[32,3840]{1,0:T(8,128)(2,1)S(1)}, bf16[32,3840]{1,0:T(8,128)(2,1)S(1)}) custom-call(s32[1,64]{1,0:T(1,128)} %bitcast.26, bf16[64,3584]{1,0:T(8,128)(2,1)} %bitcast.24), custom_call_target="tpu_custom_call" | custom-call | tf_op jit(solution)/shard_map/first/pallas_call | solution.py:415
  2.1 3.0 %collective-permute-start.4 = (bf16[32,3840]{1,0:T(8,128)(2,1)S(1)}, bf16[32,3840]{1,0:T(8,128)(2,1)S(1)}, u32[]{:S(2)}, u32[]{:S(2)}) collective-permute-start(bf16[32,3840]{1,0:T(8,128)(2,1)S(1)} %get-tuple-element.71.base), channel_id=1, source_target_pairs={{0,2},{1,3},{2,0},{3,1},{4,6},{5,7},{6,4},{7,5},{8,10},{9,11},{10,... | collective-permute-start | bytes 737288 | tf_op jit(solution)/shard_map/ppermute | solution.py:44
  5.1 4.6 %collective-permute-start.13 = (bf16[1,64,3584]{2,1,0:T(8,128)(2,1)}, bf16[1,64,3584]{2,1,0:T(8,128)(2,1)S(1)}, u32[]{:S(2)}, u32[]{:S(2)}) collective-permute-start(bf16[1,64,3584]{2,1,0:T(8,128)(2,1)} %param.16), channel_id=1, source_target_pairs={{4,0},{8,4},{12,8},{16,12},{20,16},{24,20},{28,24},{0,28},{5,1},{9... | collective-permute-start | bytes 1376264 | tf_op jit(solution)/shard_map/ppermute | solution.py:35
  9.7 3.2 %load.2 = (bf16[3584,512]{1,0:T(8,128)(2,1)S(1)}, bf16[3584,512]{1,0:T(8,128)(2,1)S(1)}, s32[1,64]{1,0:T(1,128)S(1)}, f32[1,64]{1,0:T(1,128)S(1)}) custom-call(bf16[3584,512]{1,0:T(8,128)(2,1)} %bitcast.21, bf16[3584,512]{1,0:T(8,128)(2,1)} %bitcast.22, s32[1,64]{1,0:T(1,128)} %bitcast.27, f32[1,64]{1,0:T(1,128)} %bitcast.28), custom_call_target="tpu_custom_call" | custom-call | tf_op jit(solution)/shard_map/load/pallas_call | solution.py:415
  12.9 0.6 %collective-permute-start.6 = (bf16[32,3840]{1,0:T(8,128)(2,1)S(1)}, bf16[32,3840]{1,0:T(8,128)(2,1)S(1)}, u32[]{:S(2)}, u32[]{:S(2)}) collective-permute-start(bf16[32,3840]{1,0:T(8,128)(2,1)S(1)} %collective-permute-done.4.refs_1_), channel_id=1, source_target_pairs={{0,1},{1,0},{2,3},{3,2},{4,5},{5,4},{6,7},{7,6},{8,9},{9,8},{10,11... | collective-permute-start | bytes 737288 | tf_op jit(solution)/shard_map/ppermute | solution.py:53
  13.5 2.1 %load.3 = (bf16[512,3584]{1,0:T(8,128)(2,1)S(1)}, s32[1,64]{1,0:T(1,128)S(1)}, f32[1,64]{1,0:T(1,128)S(1)}) custom-call(bf16[512,3584]{1,0:T(8,128)(2,1)} %bitcast.23, s32[1,64]{1,0:T(1,128)} %bitcast.29, f32[1,64]{1,0:T(1,128)} %bitcast.30), custom_call_target="tpu_custom_call" | custom-call | tf_op jit(solution)/shard_map/load/pallas_call | solution.py:415
  15.6 2.0 %forward.1 = (bf16[32,3840]{1,0:T(8,128)(2,1)S(1)}, bf16[32,3840]{1,0:T(8,128)(2,1)S(1)}, bf16[16,3840]{1,0:T(8,128)(2,1)S(1)}, bf16[16,3840]{1,0:T(8,128)(2,1)S...) custom-call(bf16[32,3840]{1,0:T(8,128)(2,1)S(1)} %get-tuple-element.70.refs_0_.refs_6_, ...), custom_call_target="tpu_custom_call" | custom-call | tf_op jit(solution)/shard_map/forward/pallas_call | solution.py:415
  17.7 0.5 collective-permute-start.7
  18.3 0.4 collective-permute-start.9
  19.7 0.9 %forward_sum.1 = (bf16[32,3968]{1,0:T(8,128)(2,1)}, bf16[32,3968]{1,0:T(8,128)(2,1)S(1)}) custom-call(bf16[32,3840]{1,0:T(8,128)(2,1)S(1)} %get-tuple-element.78.refs_0_, bf16[32,3840]{1,0:T(8,128)(2,1)S(1)} %get-tuple-element.79.refs_1_, bf16[16,3840]{1,0:T(8,128)(2,1)S(1)} %collective-permute-done.7.refs_2_, ...), custom_call_target="tpu_custom_call" | custom-call | tf_op jit(solution)/shard_map/forward_sum/pallas_call | solution.py:415
  20.6 0.5 collective-permute-start.12
  21.1 0.4 pack.1
  21.6 1.6 %collective-permute-start.15 = (bf16[32,3840]{1,0:T(8,128)(2,1)S(1)}, bf16[32,3840]{1,0:T(8,128)(2,1)S(1)}, u32[]{:S(2)}, u32[]{:S(2)}) collective-permute-start(bf16[32,3840]{1,0:T(8,128)(2,1)S(1)} %get-tuple-element.90), channel_id=1, source_target_pairs={{0,2},{1,3},{2,0},{3,1},{4,6},{5,7},{6,4},{7,5},{8,10},{9,11},{10,... | collective-permute-start | bytes 737288 | tf_op jit(solution)/shard_map/ppermute | solution.py:44
  23.6 6.0 %collective-permute-done.12.back = bf16[32,3968]{1,0:T(8,128)(2,1)S(1)} collective-permute-done((bf16[32,3968]{1,0:T(8,128)(2,1)S(1)}, bf16[32,3968]{1,0:T(8,128)(2,1)S(1)}, u32[]{:S(2)}, u32[]{:S(2)}) %collective-permute-start.12) | collective-permute-done | bytes 253984 | tf_op jit(solution)/shard_map/ppermute | solution.py:44
  29.9 4.4 %collective-permute-done.15 = bf16[32,3840]{1,0:T(8,128)(2,1)S(1)} collective-permute-done((bf16[32,3840]{1,0:T(8,128)(2,1)S(1)}, bf16[32,3840]{1,0:T(8,128)(2,1)S(1)}, u32[]{:S(2)}, u32[]{:S(2)}) %collective-permute-start.15) | collective-permute-done | bytes 245792 | tf_op jit(solution)/shard_map/ppermute | solution.py:44
  34.3 7.9 %conditional.1 = ((bf16[32,3968]{1,0:T(8,128)(2,1)S(1)}, bf16[32,3968]{1,0:T(8,128)(2,1)S(1)})) conditional(s32[]{:T(128)} %bitcast.12, (bf16[32,3968]{1,0:T(8,128)(2,1)}, bf16[32,3968]{1,0:T(8,128)(2,1)S(1)}) %forward_sum.1, (bf16[32,3840]{1,0:T(8,128)(2,1)S(1)}, bf16[32,3840]{1,0:T(8,128)(2,1)S(1)}, f32[144,512]{1,0:T(8,128)S(1)}, ...), branch_computations={%region_0.0_spmd, %region_1.0_spmd} | conditional | bytes 3997864 | solution.py:598
  34.3 0.5 collective-permute-start.1
  34.8 1.0 %collective-permute-done.refs_2_ = bf16[32,3840]{1,0:T(8,128)(2,1)S(1)} collective-permute-done((bf16[32,3840]{1,0:T(8,128)(2,1)S(1)}, bf16[32,3840]{1,0:T(8,128)(2,1)S(1)}, u32[]{:S(2)}, u32[]{:S(2)}) %collective-permute-start) | collective-permute-done | bytes 245792 | tf_op jit(solution)/shard_map/cond/branch_1_fun/ppermute | solution.py:53
  36.1 3.9 %backward.1 = (bf16[32,3968]{1,0:T(8,128)(2,1)S(1)}, bf16[32,3968]{1,0:T(8,128)(2,1)S(1)}, bf16[32,3968]{1,0:T(8,128)(2,1)S(1)}, bf16[32,3968]{1,0:T(8,128)(2,1)S(1)}) custom-call(bf16[32,3840]{1,0:T(8,128)(2,1)S(1)} %get-tuple-element.20.refs_0_, bf16[32,3840]{1,0:T(8,128)(2,1)S(1)} %get-tuple-element.21.refs_1_, ...), custom_call_target="tpu_custom_call" | custom-call | tf_op jit(solution)/shard_map/cond/branch_1_fun/backward/pallas_call | solution.py:415
  40.6 1.0 %collective-permute-done.2.refs_2_ = bf16[32,3968]{1,0:T(8,128)(2,1)S(1)} collective-permute-done((bf16[32,3968]{1,0:T(8,128)(2,1)S(1)}, bf16[32,3968]{1,0:T(8,128)(2,1)S(1)}, u32[]{:S(2)}, u32[]{:S(2)}) %collective-permute-start.2) | collective-permute-done | bytes 253984 | tf_op jit(solution)/shard_map/cond/branch_1_fun/ppermute | solution.py:53
  42.2 0.6 %collective-permute-start.16 = (bf16[32,3968]{1,0:T(8,128)(2,1)S(1)}, bf16[32,3968]{1,0:T(8,128)(2,1)S(1)}, u32[]{:S(2)}, u32[]{:S(2)}) collective-permute-start(bf16[32,3968]{1,0:T(8,128)(2,1)S(1)} %get-tuple-element.99), channel_id=1, source_target_pairs={{0,2},{1,3},{2,0},{3,1},{4,6},{5,7},{6,4},{7,5},{8,10},{9,11},{10,... | collective-permute-start | bytes 761864 | tf_op jit(solution)/shard_map/ppermute | solution.py:44
  42.8 1.2 %forward_end.1 = bf16[64,3584]{1,0:T(8,128)(2,1)} custom-call(bf16[32,3968]{1,0:T(8,128)(2,1)S(1)} %collective-permute-done.11.refs_0_, bf16[32,3968]{1,0:T(8,128)(2,1)S(1)} %collective-permute-done.14.refs_1_), custom_call_target="tpu_custom_call" | custom-call | tf_op jit(solution)/shard_map/forward_end/pallas_call | solution.py:415
  43.9 6.5 %collective-permute-done.16.refs_1_ = bf16[32,3968]{1,0:T(8,128)(2,1)S(1)} collective-permute-done((bf16[32,3968]{1,0:T(8,128)(2,1)S(1)}, bf16[32,3968]{1,0:T(8,128)(2,1)S(1)}, u32[]{:S(2)}, u32[]{:S(2)}) %collective-permute-start.16) | collective-permute-done | bytes 253984 | tf_op jit(solution)/shard_map/ppermute | solution.py:44
  50.4 1.2 %backward_end.1 = (bf16[64,3584]{1,0:T(8,128)(2,1)}, f32[1,64]{1,0:T(1,128)}) custom-call(bf16[32,3968]{1,0:T(8,128)(2,1)S(1)} %get-tuple-element.100.refs_0_, bf16[32,3968]{1,0:T(8,128)(2,1)S(1)} %collective-permute-done.16.refs_1_, bf16[64,3584]{1,0:T(8,128)(2,1)S(1)} %bitcast.19, s32[1,64]{1,0:T(1,128)S(1)} %get-tuple-element.87.route_ref.refs_3_, ...), custom_call_target="tpu_custom_call" | custom-call | tf_op jit(solution)/shard_map/backward_end/pallas_call | solution.py:415
  (28 shorter events, 3.4 us)
Async XLA Ops:
  2.1 10.8 %collective-permute-start.4 = (bf16[32,3840]{1,0:T(8,128)(2,1)S(1)}, bf16[32,3840]{1,0:T(8,128)(2,1)S(1)}, u32[]{:S(2)}, u32[]{:S(2)}) collective-permute-start(bf16[32,3840]{1,0:T(8,128)(2,1)S(1)} %get-tuple-element.71.base), channel_id=1, source_target_pairs={{0,2},{1,3},{2,0},{3,1},{4,6},{5,7},{6,4},{7,5},{8,10},{9,11},{10,... | collective-permute-start | bytes 737288 | tf_op jit(solution)/shard_map/ppermute | solution.py:44
  5.1 16.0 %collective-permute-start.13 = (bf16[1,64,3584]{2,1,0:T(8,128)(2,1)}, bf16[1,64,3584]{2,1,0:T(8,128)(2,1)S(1)}, u32[]{:S(2)}, u32[]{:S(2)}) collective-permute-start(bf16[1,64,3584]{2,1,0:T(8,128)(2,1)} %param.16), channel_id=1, source_target_pairs={{4,0},{8,4},{12,8},{16,12},{20,16},{24,20},{28,24},{0,28},{5,1},{9... | collective-permute-start | bytes 1376264 | tf_op jit(solution)/shard_map/ppermute | solution.py:35
  9.7 5.9 %collective-permute-start.5 = (bf16[32,3840]{1,0:T(8,128)(2,1)S(1)}, bf16[32,3840]{1,0:T(8,128)(2,1)S(1)}, u32[]{:S(2)}, u32[]{:S(2)}) collective-permute-start(bf16[32,3840]{1,0:T(8,128)(2,1)S(1)} %get-tuple-element.70.refs_0_.refs_6_), channel_id=1, source_target_pairs={{0,1},{1,0},{2,3},{3,2},{4,5},{5,4},{6,7},{7,6},{8,9},{9,8},{10,11... | collective-permute-start | bytes 737288 | tf_op jit(solution)/shard_map/ppermute | solution.py:53
  12.9 2.7 %collective-permute-start.6 = (bf16[32,3840]{1,0:T(8,128)(2,1)S(1)}, bf16[32,3840]{1,0:T(8,128)(2,1)S(1)}, u32[]{:S(2)}, u32[]{:S(2)}) collective-permute-start(bf16[32,3840]{1,0:T(8,128)(2,1)S(1)} %collective-permute-done.4.refs_1_), channel_id=1, source_target_pairs={{0,1},{1,0},{2,3},{3,2},{4,5},{5,4},{6,7},{7,6},{8,9},{9,8},{10,11... | collective-permute-start | bytes 737288 | tf_op jit(solution)/shard_map/ppermute | solution.py:53
  15.6 7.6 %copy-start = (bf16[1,4,34,512]{3,1,2,0:T(4,128)(2,1)S(1)}, bf16[1,4,34,512]{3,1,2,0:T(4,128)(2,1)}, u32[]{:S(2)}) copy-start(bf16[1,4,34,512]{3,1,2,0:T(4,128)(2,1)} %param.15) | copy-start | bytes 417796
  15.6 7.6 %copy-start.1 = (bf16[1,4,34,512]{3,1,2,0:T(4,128)(2,1)S(1)}, bf16[1,4,34,512]{3,1,2,0:T(4,128)(2,1)}, u32[]{:S(2)}) copy-start(bf16[1,4,34,512]{3,1,2,0:T(4,128)(2,1)} %param.14) | copy-start | bytes 417796
  17.6 1.4 %collective-permute-start.10 = (bf16[16,3840]{1,0:T(8,128)(2,1)S(1)}, bf16[16,3840]{1,0:T(8,128)(2,1)S(1)}, u32[]{:S(2)}, u32[]{:S(2)}) collective-permute-start(bf16[16,3840]{1,0:T(8,128)(2,1)S(1)} %get-tuple-element.83), channel_id=1, source_target_pairs={{0,1},{1,0},{2,3},{3,2},{4,5},{5,4},{6,7},{7,6},{8,9},{9,8},{10,11... | collective-permute-start | bytes 368648 | tf_op jit(solution)/shard_map/ppermute | solution.py:53
  17.7 1.5 %collective-permute-start.7 = (bf16[16,3840]{1,0:T(8,128)(2,1)S(1)}, bf16[16,3840]{1,0:T(8,128)(2,1)S(1)}, u32[]{:S(2)}, u32[]{:S(2)}) collective-permute-start(bf16[16,3840]{1,0:T(8,128)(2,1)S(1)} %get-tuple-element.80), channel_id=1, source_target_pairs={{0,1},{1,0},{2,3},{3,2},{4,5},{5,4},{6,7},{7,6},{8,9},{9,8},{10,11... | collective-permute-start | bytes 368648 | tf_op jit(solution)/shard_map/ppermute | solution.py:53
  18.2 1.3 %collective-permute-start.8 = (bf16[16,3840]{1,0:T(8,128)(2,1)S(1)}, bf16[16,3840]{1,0:T(8,128)(2,1)S(1)}, u32[]{:S(2)}, u32[]{:S(2)}) collective-permute-start(bf16[16,3840]{1,0:T(8,128)(2,1)S(1)} %get-tuple-element.81), channel_id=1, source_target_pairs={{0,1},{1,0},{2,3},{3,2},{4,5},{5,4},{6,7},{7,6},{8,9},{9,8},{10,11... | collective-permute-start | bytes 368648 | tf_op jit(solution)/shard_map/ppermute | solution.py:53
  18.3 1.4 %collective-permute-start.9 = (bf16[16,3840]{1,0:T(8,128)(2,1)S(1)}, bf16[16,3840]{1,0:T(8,128)(2,1)S(1)}, u32[]{:S(2)}, u32[]{:S(2)}) collective-permute-start(bf16[16,3840]{1,0:T(8,128)(2,1)S(1)} %get-tuple-element.82), channel_id=1, source_target_pairs={{0,1},{1,0},{2,3},{3,2},{4,5},{5,4},{6,7},{7,6},{8,9},{9,8},{10,11... | collective-permute-start | bytes 368648 | tf_op jit(solution)/shard_map/ppermute | solution.py:53
  20.6 8.9 %collective-permute-start.12 = (bf16[32,3968]{1,0:T(8,128)(2,1)S(1)}, bf16[32,3968]{1,0:T(8,128)(2,1)S(1)}, u32[]{:S(2)}, u32[]{:S(2)}) collective-permute-start(bf16[32,3968]{1,0:T(8,128)(2,1)S(1)} %get-tuple-element.86), channel_id=1, source_target_pairs={{0,2},{1,3},{2,0},{3,1},{4,6},{5,7},{6,4},{7,5},{8,10},{9,11},{10,... | collective-permute-start | bytes 761864 | tf_op jit(solution)/shard_map/ppermute | solution.py:44
  21.6 12.7 %collective-permute-start.15 = (bf16[32,3840]{1,0:T(8,128)(2,1)S(1)}, bf16[32,3840]{1,0:T(8,128)(2,1)S(1)}, u32[]{:S(2)}, u32[]{:S(2)}) collective-permute-start(bf16[32,3840]{1,0:T(8,128)(2,1)S(1)} %get-tuple-element.90), channel_id=1, source_target_pairs={{0,2},{1,3},{2,0},{3,1},{4,6},{5,7},{6,4},{7,5},{8,10},{9,11},{10,... | collective-permute-start | bytes 737288 | tf_op jit(solution)/shard_map/ppermute | solution.py:44
  23.3 19.5 %collective-permute-start.11 = (bf16[32,3968]{1,0:T(8,128)(2,1)}, bf16[32,3968]{1,0:T(8,128)(2,1)S(1)}, u32[]{:S(2)}, u32[]{:S(2)}) collective-permute-start(bf16[32,3968]{1,0:T(8,128)(2,1)} %get-tuple-element.85), channel_id=1, source_target_pairs={{28,0},{0,4},{4,8},{8,12},{12,16},{16,20},{20,24},{24,28},{29,1},{... | collective-permute-start | bytes 761864 | tf_op jit(solution)/shard_map/ppermute | solution.py:35
  29.8 12.9 %collective-permute-start.14 = (bf16[32,3968]{1,0:T(8,128)(2,1)S(1)}, bf16[32,3968]{1,0:T(8,128)(2,1)S(1)}, u32[]{:S(2)}, u32[]{:S(2)}) collective-permute-start(bf16[32,3968]{1,0:T(8,128)(2,1)S(1)} %forward_add.1), channel_id=1, source_target_pairs={{28,0},{0,4},{4,8},{8,12},{12,16},{16,20},{20,24},{24,28},{29,1},{... | collective-permute-start | bytes 761864 | tf_op jit(solution)/shard_map/ppermute | solution.py:35
  34.3 1.5 %collective-permute-start = (bf16[32,3840]{1,0:T(8,128)(2,1)S(1)}, bf16[32,3840]{1,0:T(8,128)(2,1)S(1)}, u32[]{:S(2)}, u32[]{:S(2)}) collective-permute-start(bf16[32,3840]{1,0:T(8,128)(2,1)S(1)} %get-tuple-element.20.refs_0_), channel_id=1, source_target_pairs={{0,1},{1,0},{2,3},{3,2},{4,5},{5,4},{6,7},{7,6},{8,9},{9,8},{10,11... | collective-permute-start | bytes 737288 | tf_op jit(solution)/shard_map/cond/branch_1_fun/ppermute | solution.py:53
  34.3 1.9 %collective-permute-start.1 = (bf16[32,3840]{1,0:T(8,128)(2,1)S(1)}, bf16[32,3840]{1,0:T(8,128)(2,1)S(1)}, u32[]{:S(2)}, u32[]{:S(2)}) collective-permute-start(bf16[32,3840]{1,0:T(8,128)(2,1)S(1)} %get-tuple-element.21.refs_1_), channel_id=1, source_target_pairs={{0,1},{1,0},{2,3},{3,2},{4,5},{5,4},{6,7},{7,6},{8,9},{9,8},{10,11... | collective-permute-start | bytes 737288 | tf_op jit(solution)/shard_map/cond/branch_1_fun/ppermute | solution.py:53
  40.0 1.6 %collective-permute-start.2 = (bf16[32,3968]{1,0:T(8,128)(2,1)S(1)}, bf16[32,3968]{1,0:T(8,128)(2,1)S(1)}, u32[]{:S(2)}, u32[]{:S(2)}) collective-permute-start(bf16[32,3968]{1,0:T(8,128)(2,1)S(1)} %get-tuple-element.30), channel_id=1, source_target_pairs={{0,1},{1,0},{2,3},{3,2},{4,5},{5,4},{6,7},{7,6},{8,9},{9,8},{10,11... | collective-permute-start | bytes 761864 | tf_op jit(solution)/shard_map/cond/branch_1_fun/ppermute | solution.py:53
  40.2 1.7 %collective-permute-start.3 = (bf16[32,3968]{1,0:T(8,128)(2,1)S(1)}, bf16[32,3968]{1,0:T(8,128)(2,1)S(1)}, u32[]{:S(2)}, u32[]{:S(2)}) collective-permute-start(bf16[32,3968]{1,0:T(8,128)(2,1)S(1)} %get-tuple-element.31), channel_id=1, source_target_pairs={{0,1},{1,0},{2,3},{3,2},{4,5},{5,4},{6,7},{7,6},{8,9},{9,8},{10,11... | collective-permute-start | bytes 761864 | tf_op jit(solution)/shard_map/cond/branch_1_fun/ppermute | solution.py:53
  42.2 8.3 %collective-permute-start.16 = (bf16[32,3968]{1,0:T(8,128)(2,1)S(1)}, bf16[32,3968]{1,0:T(8,128)(2,1)S(1)}, u32[]{:S(2)}, u32[]{:S(2)}) collective-permute-start(bf16[32,3968]{1,0:T(8,128)(2,1)S(1)} %get-tuple-element.99), channel_id=1, source_target_pairs={{0,2},{1,3},{2,0},{3,1},{4,6},{5,7},{6,4},{7,5},{8,10},{9,11},{10,... | collective-permute-start | bytes 761864 | tf_op jit(solution)/shard_map/ppermute | solution.py:44

commit v5 on v3

--- a/solution.py
+++ b/solution.py
@@ -9,6 +9,7 @@
 
 EXPERTS = 2
 LANES = 128
+PIECES = 2
 F32 = jnp.float32
 BF16 = jnp.bfloat16
 NT = (((1,), (1,)), ((), ()))
@@ -113,12 +114,44 @@
     return main, extra
 
 
-def add_gated(out_ref, base_ref, main, extra, total, s):
+def add_gated(out_ref, base, main, extra, total, s):
     d = s.depth
-    out_ref[:, :d] = (base_ref[:, :d].astype(F32) + main * total[:, :d]).astype(BF16)
+    out_ref[:, :d] = (read(base, 0, d).astype(F32) + main * total[:, :d]).astype(BF16)
     for j in range(s.extra):
         at = slice(d + j * LANES, d + (j + 1) * LANES)
-        out_ref[:, at] = (base_ref[:, at].astype(F32) + extra[j] * total[:, at]).astype(BF16)
+        value = read(base, at.start, at.stop).astype(F32) + extra[j] * total[:, at]
+        out_ref[:, at] = value.astype(BF16)
+
+
+def read(pieces, low, high):
+    found, at = [], 0
+    for piece in pieces:
+        width = piece.shape[1]
+        a, b = max(low, at), min(high, at + width)
+        if a < b:
+            found.append(piece[:, a - at : b - at])
+        at += width
+    return found[0] if len(found) == 1 else jnp.concatenate(found, axis=1)
+
+
+def write(pieces, low, value):
+    at = 0
+    for piece in pieces:
+        width = piece.shape[1]
+        a, b = max(low, at), min(low + value.shape[1], at + width)
+        if a < b:
+            piece[:, a - at : b - at] = value[:, a - low : b - low]
+        at += width
+
+
+def grouped(refs, s, pieces):
+    one = 1 + (s.count - 1) * pieces
+    packs = []
+    for first in range(0, len(refs), one):
+        packs.append(refs[first : first + 1])
+        for at in range(first + 1, first + one, pieces):
+            packs.append(refs[at : at + pieces])
+    return packs
 
 
 def pack_rows(s, route_row, x, outs, extra_ref, tail_ref):
@@ -129,31 +162,28 @@
         hit = route_row == expert_at(s, d)
         table = jnp.where(hit & (rank == slots), 1.0, 0.0).astype(BF16)
         rows = jnp.dot(table, x, preferred_element_type=F32)
-        outs[d][:, : s.depth] = rows[: s.main].astype(BF16)
+        write(outs[d], 0, rows[: s.main].astype(BF16))
         extra_ref[...] = rows[s.main :]
         fold(extra_ref, 0, tail_ref, s)
-        outs[d][:, s.depth :] = tail_ref[...].astype(BF16)
-
-
-def first_kernel(s, route_hbm, x_hbm, dy_hbm, *rest):
-    outs, dy_ref = rest[: s.count], rest[s.count]
-    route_ref, x_ref, extra_ref, tail_ref, sems = rest[s.count + 1 :]
+        write(outs[d], s.depth, tail_ref[...].astype(BF16))
+
+
+def first_kernel(s, route_hbm, x_hbm, *rest):
+    outs = grouped(rest[:-5], s, PIECES)
+    route_ref, x_ref, extra_ref, tail_ref, sems = rest[-5:]
     copies = [
-        pltpu.make_async_copy(src, dst, sems.at[i])
-        for i, (src, dst) in enumerate(
-            ((route_hbm, route_ref), (x_hbm, x_ref), (dy_hbm, dy_ref))
-        )
+        pltpu.make_async_copy(route_hbm, route_ref, sems.at[0]),
+        pltpu.make_async_copy(x_hbm, x_ref, sems.at[1]),
     ]
     for copy in copies:
         copy.start()
-    copies[0].wait()
-    copies[1].wait()
+    for copy in copies:
+        copy.wait()
     pack_rows(s, route_ref[...].astype(F32), x_ref[...], outs, extra_ref, tail_ref)
-    copies[2].wait()
 
 
 def pack_kernel(s, route_ref, x_ref, *rest):
-    outs, (extra_ref, tail_ref) = rest[: s.count], rest[s.count :]
+    outs, (extra_ref, tail_ref) = grouped(rest[:-2], s, 1), rest[-2:]
     pack_rows(s, route_ref[...].astype(F32), x_ref[...], outs, extra_ref, tail_ref)
 
 
@@ -170,8 +200,8 @@
 def gather_packs(packs, rows_ref, extra_ref, tail_ref, s):
     extra_ref[...] = jnp.zeros_like(extra_ref)
     for i, pack in enumerate(packs):
-        rows_ref[i * s.main : (i + 1) * s.main, :] = pack[:, : s.depth]
-        tail_ref[...] = pack[:, s.depth : s.width].astype(F32)
+        rows_ref[i * s.main : (i + 1) * s.main, :] = read(pack, 0, s.depth)
+        tail_ref[...] = read(pack, s.depth, s.width).astype(F32)
         unfold(tail_ref, extra_ref, i * s.extra, s)
     rows_ref[s.blocks * s.main :, :] = extra_ref[...].astype(BF16)
 
@@ -195,9 +225,10 @@
 
 
 def forward_kernel(s, *refs):
-    packs = refs[: s.blocks]
-    wg, wu, wd = refs[s.blocks : s.blocks + 3]
-    outs = refs[s.blocks + 3 : -3]
+    n = len(refs) - s.blocks - 6
+    packs = grouped(refs[:n], s, PIECES)
+    wg, wu, wd = refs[n : n + 3]
+    outs = refs[n + 3 : -3]
     rows_ref, extra_ref, tail_ref = refs[-3:]
     chunk = chunk_of(s.depth)
     gather_packs(packs, rows_ref, extra_ref, tail_ref, s)
@@ -271,7 +302,7 @@
 
 
 def backward_kernel(s, *refs):
-    packs = refs[: s.blocks]
+    packs = grouped(refs[: s.blocks], s, 1)
     c1, c2, hb, wg, wu, wd = refs[s.blocks : s.blocks + 6]
     outs = refs[s.blocks + 6 : -3]
     rows_ref, extra_ref, tail_ref = refs[-3:]
@@ -302,31 +333,33 @@
     scatter_tails(outs, extra_ref, tail_ref, s)
 
 
-def total_of(parts, d, k):
+def total_of(parts, d, s):
     total = parts[d][...].astype(F32)
-    for part in parts[d + len(parts) // k :: len(parts) // k]:
+    for part in parts[s.count + d :: s.count]:
         total = total + part[...].astype(F32)
     return total
 
 
 def forward_sum_kernel(s, *refs):
-    parts = refs[: s.blocks]
-    own, route_ref, score_ref, y_ref = refs[s.blocks : s.blocks + 4]
-    backs = refs[s.blocks + 4 :]
+    n = len(refs) - 3 - s.count
+    parts = refs[:n]
+    own, route_ref, score_ref, y_ref = refs[n : n + 4]
+    backs = refs[n + 4 :]
     for d in range(1, s.count):
-        backs[d - 1][:, : s.width] = total_of(parts, d, s.slices).astype(BF16)
-        backs[d - 1][:, s.width :] = jnp.zeros((s.main, LANES), BF16)
+        backs[d - 1][...] = total_of(parts, d, s).astype(BF16)
     route_row = route_ref[...].astype(F32)
     main, extra = slot_values(route_row, 2.5 * score_ref[...], expert_at(s, 0), s)
-    add_gated(y_ref, own, main, extra, total_of(parts, 0, s.slices), s)
+    add_gated(y_ref, [own], main, extra, total_of(parts, 0, s), s)
     y_ref[s.folds : s.folds + 1, s.depth : s.depth + s.tok] = route_row.astype(BF16)
-    y_ref[:, s.width :] = jnp.zeros((s.main, LANES), BF16)
-
-
-def forward_add_kernel(s, distance, back, base, route_ref, score_ref, y_ref):
+    y_ref[:, s.width :] = jnp.zeros((s.main, 2 * LANES), BF16)
+
+
+def forward_add_kernel(s, distance, back, *rest):
+    base, (route_ref, score_ref, y_ref) = rest[:-3], rest[-3:]
     route_row = route_ref[...].astype(F32)
     main, extra = slot_values(route_row, 2.5 * score_ref[...], expert_at(s, distance), s)
-    add_gated(y_ref, base, main, extra, back[:, : s.width].astype(F32), s)
+    add_gated(y_ref, base, main, extra, back[...].astype(F32), s)
+    y_ref[:, s.width :] = jnp.zeros((s.main, LANES), BF16)
 
 
 def tokens_of(packs, route_row, rows_ref, extra_ref, tail_ref, s):
@@ -359,9 +392,9 @@
 
 
 def backward_sum_kernel(s, *refs):
-    parts, outs = refs[: s.blocks], refs[s.blocks :]
+    parts, outs = refs[: -s.count], refs[-s.count :]
     for d in range(s.count - 1, -1, -1):
-        total = total_of(parts, d, s.slices)
+        total = total_of(parts, d, s)
         outs[d][:, : s.width] = total[:, : s.width].astype(BF16)
         main, extra = get_inner(total[:, s.width :], s)
         outs[d][:, s.width :] = put_inner(main, extra, s)
@@ -417,16 +450,27 @@
     ]
 
 
+def load(*arrays):
+    return call(
+        load_kernel,
+        "load",
+        [(a.shape, a.dtype) for a in arrays],
+        [pltpu.SemaphoreType.DMA((len(arrays),))],
+        [HBM] * len(arrays),
+        *arrays,
+    )
+
+
 def row_scratch(s):
     return [pltpu.VMEM((s.rows, s.depth), BF16), *tail_scratch(s, s.tail_rows)]
 
 
-def cross(s, packs):
-    return [packs[0]] + [across(packs[d], d, s) for d in range(1, s.count)]
+def cross(s, packs, pieces):
+    return [packs[0]] + [across(p, 1 + i // pieces, s) for i, p in enumerate(packs[1:])]
 
 
 def spread(s, got):
-    return got + [beside(b, k, s) for k in range(1, s.slices) for b in got]
+    return list(got) + [beside(b, k, s) for k in range(1, s.slices) for b in got]
 
 
 def hold(values, *after):
@@ -435,6 +479,12 @@
 
 def gather_parts(s, parts):
     return [beside(p, -(i // s.count), s) if i >= s.count else p for i, p in enumerate(parts)]
+
+
+def step(routes, run, *args):
+    like = jax.eval_shape(run, *args)
+    skip = lambda *_: jax.tree.map(lambda a: jnp.zeros(a.shape, a.dtype), like)
+    return lax.cond(routes[0, 0] < EXPERTS, run, skip, *args)
 
 
 def end_scratch(s):
@@ -459,37 +509,29 @@
     tok, depth = x_fwd.shape[1:]
     s = Sizes(saved_gate.shape[2], depth, EXPERTS, groups // EXPERTS, tok)
     hidden = w_gate.shape[2]
-    weights = (w_gate[0], w_up[0], w_down[0])
     route_a = routes_fwd.reshape(1, tok)
     route_b = routes_bwd.reshape(1, tok)
     score_a = scores_fwd.reshape(1, tok)
     score_b = scores_bwd.reshape(1, tok)
 
     packed = [((s.main, s.width), BF16)] * s.count
-    *sent_a, grads = call(
+    sent_a = call(
         functools.partial(first_kernel, s),
         "first",
-        packed + [((tok, depth), BF16)],
+        packed[:1] + [((s.main, s.width // PIECES), BF16)] * (PIECES * (s.count - 1)),
         [
             pltpu.VMEM((1, tok), jnp.int32),
             pltpu.VMEM((tok, depth), BF16),
             *tail_scratch(s, 16),
-            pltpu.SemaphoreType.DMA((3,)),
+            pltpu.SemaphoreType.DMA((2,)),
         ],
-        [HBM] * 3,
+        [HBM] * 2,
         route_a,
         x_fwd[0],
-        grad_next[0],
-    )
-    upstream = from_behind(grads, "section", -1)
-    held = (*weights, route_a, route_b, score_a, score_b)
-    *weights, route_a, route_b, score_a, score_b = call(
-        load_kernel,
-        "load",
-        [(a.shape, a.dtype) for a in held],
-        [pltpu.SemaphoreType.DMA((len(held),))],
-        [HBM] * len(held),
-        *held,
+    )
+    upstream = from_behind(grad_next, "section", -1)[0]
+    wg, wu, wd, route_a, route_b, score_a, score_b = load(
+        w_gate[0], w_up[0], w_down[0], route_a, route_b, score_a, score_b
     )
     factors = call(
         functools.partial(saved_kernel, s),
@@ -500,8 +542,34 @@
         saved_gate[0],
         saved_up[0],
     )
-    got = cross(s, sent_a)
-    got[1:] = hold(got[1:], score_b, factors)
+    wide = s.width + LANES
+
+    def forward(rows, *weights):
+        parts = call(
+            functools.partial(forward_kernel, s),
+            "forward",
+            [((s.main, s.width), BF16)] * s.blocks,
+            row_scratch(s),
+            [VMEM] * (len(rows) + 3),
+            *rows,
+            *weights,
+        )
+        return tuple(gather_parts(s, parts))
+
+    def backward(got, *rest):
+        parts = call(
+            functools.partial(backward_kernel, s),
+            "backward",
+            [((s.main, wide), BF16)] * s.blocks,
+            row_scratch(s),
+            [VMEM] * (s.blocks + 6),
+            *spread(s, got),
+            *rest,
+        )
+        return tuple(gather_parts(s, parts))
+
+    got = cross(s, sent_a, PIECES)
+    got[1:] = hold(got[1:], score_a, factors)
     rows_a = spread(s, got)
     sent_b = call(
         functools.partial(pack_kernel, s),
@@ -512,25 +580,12 @@
         route_b,
         hold(upstream, got[1:]),
     )
-    got_b = cross(s, sent_b)
-
-    parts_a = call(
-        functools.partial(forward_kernel, s),
-        "forward",
-        [((s.main, s.width), BF16)] * s.blocks,
-        row_scratch(s),
-        [VMEM] * (s.blocks + 3),
-        *hold(rows_a, sent_b),
-        *weights,
-    )
-    wide = s.width + LANES
-    got_b[1:] = hold(got_b[1:], parts_a)
-    rows_b = spread(s, got_b)
-    parts_a = hold(gather_parts(s, parts_a), got_b[1:])
+    got_b = cross(s, sent_b, 1)
+    parts_a = step(route_a, forward, hold(rows_a, sent_b), wg, wu, wd)
     sums_a = call(
         functools.partial(forward_sum_kernel, s),
         "forward_sum",
-        [((s.main, wide), BF16)] * s.count,
+        [((s.main, wide + LANES), BF16)] + [((s.main, s.width), BF16)] * (s.count - 1),
         [],
         [VMEM] * (s.blocks + 3),
         *parts_a,
@@ -539,28 +594,19 @@
         score_a,
     )
     back_a = [across(sums_a[d], -d, s) for d in range(1, s.count)]
-
-    parts_b = call(
-        functools.partial(backward_kernel, s),
-        "backward",
-        [((s.main, wide), BF16)] * s.blocks,
-        row_scratch(s),
-        [VMEM] * (s.blocks + 6),
-        *hold(rows_b, sums_a),
-        *factors,
-        *weights,
-    )
+    moved = [from_behind(sums_a[0], "section", 1)]
+    got_b[1:] = hold(got_b[1:], sums_a)
+    parts_b = step(route_b, backward, got_b, *factors, wg, wu, wd)
     back_a = hold(back_a, parts_b)
-    moved = [from_behind(sums_a[0], "section", 1)]
     for d in range(1, s.count):
         y = call(
             functools.partial(forward_add_kernel, s, d),
             "forward_add",
-            [((s.main, s.width), BF16)],
+            [((s.main, wide), BF16)],
             [],
-            [VMEM] * 4,
+            [VMEM] * (3 + PIECES),
             back_a[d - 1],
-            sent_a[d],
+            *sent_a[1 + (d - 1) * PIECES : 1 + d * PIECES],
             route_a,
             score_a,
         )[0]
@@ -571,28 +617,28 @@
         [((s.main, wide), BF16)] * s.count,
         [],
         [VMEM] * s.blocks,
-        *hold(gather_parts(s, parts_b), y),
+        *hold(parts_b, y),
     )
     back_b = [sums_b[0]] + [across(sums_b[d], -d, s) for d in range(1, s.count)]
+    next_input = call(
+        functools.partial(forward_end_kernel, s),
+        "forward_end",
+        [((tok, depth), BF16)],
+        end_scratch(s) + [pltpu.VMEM((s.main, LANES), F32)],
+        [VMEM] * s.count,
+        *moved,
+    )[0]
     input_grad, score_grad = call(
         functools.partial(backward_end_kernel, s),
         "backward_end",
         [((tok, depth), BF16), ((1, tok), F32)],
         end_scratch(s),
         [VMEM] * (s.count + 3),
-        *hold(back_b, moved[0]),
+        *hold(back_b, next_input),
         upstream,
         route_b,
         score_b,
     )
-    next_input = call(
-        functools.partial(forward_end_kernel, s),
-        "forward_end",
-        [((tok, depth), BF16)],
-        end_scratch(s) + [pltpu.VMEM((s.main, LANES), F32)],
-        [VMEM] * s.count,
-        *hold(moved, score_grad),
-    )[0]
     return next_input[None], input_grad[None], score_grad.reshape(1, tok, 1)
 
 

time: 50 us -> 60 us (1.20)
  Pallas kernels: 15.6 us -> 31.1 us
  waiting for transfers between devices: 18.2 us -> 12.6 us
    pallas_call x11, Pallas kernels: 15.6 us -> 31.1 us  [call(): pl.pallas_call(kernel, out_shape=shapes, in_specs=ins, out_specs=[VMEM] *...]
    ppermute x4 -> x5, waiting for transfers between devices: 5.35 us -> 0.01 us  [across(): return lax.ppermute(block, 'expert', route)]
    ppermute x3, waiting for transfers between devices: 12.9 us -> 8.23 us  [from_behind(): return lax.ppermute(block, axis, route)]
    ppermute x8 -> x9, waiting for transfers between devices: 0.02 us -> 4.35 us  [beside(): return lax.ppermute(block, 'expert', route)]
    ppermute x8 -> x9, starting transfers between devices: 1.45 us -> 2.37 us  [beside(): return lax.ppermute(block, 'expert', route)]
    ppermute x3, starting transfers between devices: 6.73 us -> 6.12 us  [from_behind(): return lax.ppermute(block, axis, route)]
    ppermute x4 -> x5, starting transfers between devices: 6.15 us -> 5.72 us  [across(): return lax.ppermute(block, 'expert', route)]
  transfers between devices with their start and end apart: 15 -> 17, of which waited for: 6 -> 7; matrix products, arithmetic and copies ran while one was open for 2% -> 2% of each run, Pallas kernels for 26% -> 50%
where the time goes in v5:
time: 60 us; the launch traced here: 59.8 us
  Pallas kernels  31.1 us (52%)
  starting transfers between devices  14.2 us (24%)
  waiting for transfers between devices  12.6 us (21%)
  local copies, waits for them, and re-layouts  1.03 us (2%)
  between operations  0.81 us (1%)
    pallas_call x11, Pallas kernels, call(): pl.pallas_call(kernel, out_shape=shapes, in_specs=ins, out_specs=[VMEM] *...  31.1 us
    ppermute x3, waiting for transfers between devices, from_behind(): return lax.ppermute(block, axis, route)  8.23 us
    ppermute x3, starting transfers between devices, from_behind(): return lax.ppermute(block, axis, route)  6.12 us
    ppermute x5, starting transfers between devices, across(): return lax.ppermute(block, 'expert', route)  5.72 us
    ppermute x9, waiting for transfers between devices, beside(): return lax.ppermute(block, 'expert', route)  4.35 us
    ppermute x9, starting transfers between devices, beside(): return lax.ppermute(block, 'expert', route)  2.37 us
  transfers between devices with their start and end apart: 17, of which 7 were waited for; matrix products, arithmetic and copies ran while one was open for 2% of the time, Pallas kernels for 50%

profile of v5, /device:TPU:0, one launch (start us, length us, event | category | flops | bytes accessed | tf_op | source)
XLA Modules:
  0.0 59.8 jit_solution(6477706892016884072)
XLA Ops:
  0.6 6.1 %collective-permute-start.11 = (bf16[1,64,3584]{2,1,0:T(8,128)(2,1)}, bf16[1,64,3584]{2,1,0:T(8,128)(2,1)S(1)}, u32[]{:S(2)}, u32[]{:S(2)}) collective-permute-start(bf16[1,64,3584]{2,1,0:T(8,128)(2,1)} %param.18), channel_id=1, source_target_pairs={{4,0},{8,4},{12,8},{16,12},{20,16},{24,20},{28,24},{0,28},{5,1},{9... | collective-permute-start | bytes 1376264 | tf_op jit(solution)/shard_map/ppermute | solution.py:34
  6.7 1.5 %first.1 = (bf16[32,3840]{1,0:T(8,128)(2,1)S(1)}, bf16[32,1920]{1,0:T(8,128)(2,1)S(1)}, bf16[32,1920]{1,0:T(8,128)(2,1)S(1)}) custom-call(s32[1,64]{1,0:T(1,128)} %bitcast.29, bf16[64,3584]{1,0:T(8,128)(2,1)} %bitcast.27), custom_call_target="tpu_custom_call" | custom-call | tf_op jit(solution)/shard_map/first/pallas_call | solution.py:434
  8.2 1.6 %collective-permute-start.6 = (bf16[32,1920]{1,0:T(8,128)(2,1)S(1)}, bf16[32,1920]{1,0:T(8,128)(2,1)S(1)}, u32[]{:S(2)}, u32[]{:S(2)}) collective-permute-start(bf16[32,1920]{1,0:T(8,128)(2,1)S(1)} %get-tuple-element.110.rest_0_), channel_id=1, source_target_pairs={{0,2},{1,3},{2,0},{3,1},{4,6},{5,7},{6,4},{7,5},{8,10},{9,11},{10,... | collective-permute-start | bytes 368648 | tf_op jit(solution)/shard_map/ppermute | solution.py:43
  9.8 0.5 collective-permute-start.7
  10.3 1.0 %copy_bitcast_fusion = (bf16[4,34,512]{2,1,0:T(8,128)(2,1)S(1)}, bf16[4,34,512]{2,1,0:T(8,128)(2,1)S(1)}) fusion(bf16[1,4,34,512]{3,1,2,0:T(4,128)(2,1)} %param.17, bf16[1,4,34,512]{3,1,2,0:T(4,128)(2,1)} %param.16), kind=kLoop, calls=%fused_computation | loop fusion | bytes 557056 | tf_op jit(solution)/shard_map/squeeze | solution.py:543
  11.6 8.4 %load.1 = (bf16[3584,512]{1,0:T(8,128)(2,1)}, bf16[3584,512]{1,0:T(8,128)(2,1)}, bf16[512,3584]{1,0:T(8,128)(2,1)}, s32[1,64]{1,0:T(1,128)S(1)}, s32[1,64]{1,0:T...) custom-call(bf16[3584,512]{1,0:T(8,128)(2,1)} %bitcast.24, bf16[3584,512]{1,0:T(8,128)(2,1)} %bitcast.25, ...), custom_call_target="tpu_custom_call" | custom-call | tf_op jit(solution)/shard_map/load/pallas_call | solution.py:434
  20.0 0.6 collective-permute-start.10
  20.7 1.1 %pack.1 = (bf16[32,3840]{1,0:T(8,128)(2,1)}, bf16[32,3840]{1,0:T(8,128)(2,1)S(1)}) custom-call(s32[1,64]{1,0:T(1,128)S(1)} %get-tuple-element.118.route_ref.refs_3_, bf16[64,3584]{1,0:T(8,128)(2,1)S(1)} %bitcast.20), custom_call_target="tpu_custom_call" | custom-call | tf_op jit(solution)/shard_map/pack/pallas_call | solution.py:434
  21.8 1.5 %collective-permute-start.14 = (bf16[32,3840]{1,0:T(8,128)(2,1)S(1)}, bf16[32,3840]{1,0:T(8,128)(2,1)S(1)}, u32[]{:S(2)}, u32[]{:S(2)}) collective-permute-start(bf16[32,3840]{1,0:T(8,128)(2,1)S(1)} %get-tuple-element.121), channel_id=1, source_target_pairs={{0,2},{1,3},{2,0},{3,1},{4,6},{5,7},{6,4},{7,5},{8,10},{9,11},{10,... | collective-permute-start | bytes 737288 | tf_op jit(solution)/shard_map/ppermute | solution.py:43
  23.3 8.3 %conditional.2 = (bf16[32,3840]{1,0:T(8,128)(2,1)S(1)}, bf16[32,3840]{1,0:T(8,128)(2,1)S(1)}, bf16[32,3840]{1,0:T(8,128)(2,1)}, bf16[32,3840]{1,0:T(8,128)(2,1)}) conditional(s32[]{:T(128)} %bitcast.7, () %tuple.31, (bf16[32,3840]{1,0:T(8,128)(2,1)S(1)}, bf16[32,1920]{1,0:T(8,128)(2,1)S(1)}, bf16[32,1920]{1,0:T(8,128)(2,1)S(1)}, ...), branch_computations={%region_0.0_spmd, %region_1.0_spmd} | conditional | bytes 1966192 | solution.py:487
  23.3 6.2 %forward.1 = (bf16[32,3840]{1,0:T(8,128)(2,1)S(1)}, bf16[32,3840]{1,0:T(8,128)(2,1)S(1)}, bf16[32,3840]{1,0:T(8,128)(2,1)S(1)}, bf16[32,3840]{1,0:T(8,128)(2,1)S(1)}) custom-call(bf16[32,3840]{1,0:T(8,128)(2,1)S(1)} %get-tuple-element.34.refs_0_, bf16[32,1920]{1,0:T(8,128)(2,1)S(1)} %get-tuple-element.35.refs_1_, ...), custom_call_target="tpu_custom_call" | custom-call | tf_op jit(solution)/shard_map/cond/branch_1_fun/forward/pallas_call | solution.py:434
  30.1 1.1 %collective-permute-done = bf16[32,3840]{1,0:T(8,128)(2,1)} collective-permute-done((bf16[32,3840]{1,0:T(8,128)(2,1)S(1)}, bf16[32,3840]{1,0:T(8,128)(2,1)}, u32[]{:S(2)}, u32[]{:S(2)}) %collective-permute-start) | collective-permute-done | bytes 245792 | tf_op jit(solution)/shard_map/cond/branch_1_fun/ppermute | solution.py:52
  31.5 1.4 %forward_sum.1 = (bf16[32,4096]{1,0:T(8,128)(2,1)S(1)}, bf16[32,3840]{1,0:T(8,128)(2,1)S(1)}) custom-call(bf16[32,3840]{1,0:T(8,128)(2,1)S(1)} %get-tuple-element.131.refs_0_, bf16[32,3840]{1,0:T(8,128)(2,1)S(1)} %get-tuple-element.132.refs_1_, bf16[32,3840]{1,0:T(8,128)(2,1)} %get-tuple-element.133.refs_2_, bf16[32,3840]{1,0:T(8,128)(2,1)} %get-tuple-element.134.refs_3_, ...), custom_call_target="tpu_custom_call" | custom-call | tf_op jit(solution)/shard_map/forward_sum/pallas_call | solution.py:434
  32.9 0.6 %collective-permute-start.13 = (bf16[32,3840]{1,0:T(8,128)(2,1)S(1)}, bf16[32,3840]{1,0:T(8,128)(2,1)S(1)}, u32[]{:S(2)}, u32[]{:S(2)}) collective-permute-start(bf16[32,3840]{1,0:T(8,128)(2,1)S(1)} %get-tuple-element.136), channel_id=1, source_target_pairs={{0,2},{1,3},{2,0},{3,1},{4,6},{5,7},{6,4},{7,5},{8,10},{9,11},{10,... | collective-permute-start | bytes 737288 | tf_op jit(solution)/shard_map/ppermute | solution.py:43
  33.6 12.3 %conditional.3 = (bf16[32,3968]{1,0:T(8,128)(2,1)S(1)}, bf16[32,3968]{1,0:T(8,128)(2,1)S(1)}, bf16[32,3968]{1,0:T(8,128)(2,1)}, bf16[32,3968]{1,0:T(8,128)(2,1)}) conditional(s32[]{:T(128)} %bitcast.12, () %tuple.36, (bf16[32,3840]{1,0:T(8,128)(2,1)}, bf16[32,3840]{1,0:T(8,128)(2,1)S(1)}, f32[144,512]{1,0:T(8,128)S(1)}, f32[144,512]{1,0:T(8,128)S(1)}, ...), branch_computations={%region_2.0_spmd, %region_3.0_spmd} | conditional | bytes 4980956 | solution.py:487
  33.8 0.5 collective-permute-start.3
  34.2 1.2 %collective-permute-done.2.refs_2_ = bf16[32,3840]{1,0:T(8,128)(2,1)S(1)} collective-permute-done((bf16[32,3840]{1,0:T(8,128)(2,1)}, bf16[32,3840]{1,0:T(8,128)(2,1)S(1)}, u32[]{:S(2)}, u32[]{:S(2)}) %collective-permute-start.2) | collective-permute-done | bytes 245792 | tf_op jit(solution)/shard_map/cond/branch_1_fun/ppermute | solution.py:52
  35.6 8.3 %backward.1 = (bf16[32,3968]{1,0:T(8,128)(2,1)S(1)}, bf16[32,3968]{1,0:T(8,128)(2,1)S(1)}, bf16[32,3968]{1,0:T(8,128)(2,1)S(1)}, bf16[32,3968]{1,0:T(8,128)(2,1)S(1)}) custom-call(bf16[32,3840]{1,0:T(8,128)(2,1)} %get-tuple-element.47.refs_0_, bf16[32,3840]{1,0:T(8,128)(2,1)} %copy-done, bf16[32,3840]{1,0:T(8,128)(2,1)S(1)} %collective-permute-done.2.refs_2_, ...), custom_call_target="tpu_custom_call" | custom-call | tf_op jit(solution)/shard_map/cond/branch_1_fun/backward/pallas_call | solution.py:434
  44.4 1.1 %collective-permute-done.4 = bf16[32,3968]{1,0:T(8,128)(2,1)} collective-permute-done((bf16[32,3968]{1,0:T(8,128)(2,1)S(1)}, bf16[32,3968]{1,0:T(8,128)(2,1)}, u32[]{:S(2)}, u32[]{:S(2)}) %collective-permute-start.4) | collective-permute-done | bytes 253984 | tf_op jit(solution)/shard_map/cond/branch_1_fun/ppermute | solution.py:52
  46.3 1.4 %backward_sum.1 = (bf16[32,3968]{1,0:T(8,128)(2,1)S(1)}, bf16[32,3968]{1,0:T(8,128)(2,1)S(1)}) custom-call(bf16[32,3968]{1,0:T(8,128)(2,1)S(1)} %get-tuple-element.143.refs_0_, bf16[32,3968]{1,0:T(8,128)(2,1)S(1)} %get-tuple-element.144.refs_1_, bf16[32,3968]{1,0:T(8,128)(2,1)} %get-tuple-element.145.refs_2_, bf16[32,3968]{1,0:T(8,128)(2,1)} %get-tuple-element.146.refs_3_), custom_call_target="tpu_custom_call" | custom-call | tf_op jit(solution)/shard_map/backward_sum/pallas_call | solution.py:434
  47.7 1.5 %collective-permute-start.16 = (bf16[32,3968]{1,0:T(8,128)(2,1)S(1)}, bf16[32,3968]{1,0:T(8,128)(2,1)S(1)}, u32[]{:S(2)}, u32[]{:S(2)}) collective-permute-start(bf16[32,3968]{1,0:T(8,128)(2,1)S(1)} %get-tuple-element.148), channel_id=1, source_target_pairs={{0,2},{1,3},{2,0},{3,1},{4,6},{5,7},{6,4},{7,5},{8,10},{9,11},{10,... | collective-permute-start | bytes 761864 | tf_op jit(solution)/shard_map/ppermute | solution.py:43
  49.2 8.2 %collective-permute-done.15.refs_1_ = bf16[32,3968]{1,0:T(8,128)(2,1)S(1)} collective-permute-done((bf16[32,3968]{1,0:T(8,128)(2,1)S(1)}, bf16[32,3968]{1,0:T(8,128)(2,1)S(1)}, u32[]{:S(2)}, u32[]{:S(2)}) %collective-permute-start.15) | collective-permute-done | bytes 253984 | tf_op jit(solution)/shard_map/ppermute | solution.py:34
  57.4 1.2 %forward_end.1 = bf16[64,3584]{1,0:T(8,128)(2,1)} custom-call(bf16[32,4096]{1,0:T(8,128)(2,1)S(1)} %collective-permute-done.12.refs_0_, bf16[32,3968]{1,0:T(8,128)(2,1)S(1)} %collective-permute-done.15.refs_1_), custom_call_target="tpu_custom_call" | custom-call | tf_op jit(solution)/shard_map/forward_end/pallas_call | solution.py:434
  58.6 1.2 %backward_end.1 = (bf16[64,3584]{1,0:T(8,128)(2,1)}, f32[1,64]{1,0:T(1,128)}) custom-call(bf16[32,3968]{1,0:T(8,128)(2,1)S(1)} %get-tuple-element.149.refs_0_, bf16[32,3968]{1,0:T(8,128)(2,1)S(1)} %collective-permute-done.16.refs_1_, bf16[64,3584]{1,0:T(8,128)(2,1)S(1)} %bitcast.21, s32[1,64]{1,0:T(1,128)S(1)} %get-tuple-element.118.route_ref.refs_3_, ...), custom_call_target="tpu_custom_call" | custom-call | tf_op jit(solution)/shard_map/backward_end/pallas_call | solution.py:434
  (26 shorter events, 2.8 us)
Async XLA Ops:
  0.6 20.1 %collective-permute-start.11 = (bf16[1,64,3584]{2,1,0:T(8,128)(2,1)}, bf16[1,64,3584]{2,1,0:T(8,128)(2,1)S(1)}, u32[]{:S(2)}, u32[]{:S(2)}) collective-permute-start(bf16[1,64,3584]{2,1,0:T(8,128)(2,1)} %param.18), channel_id=1, source_target_pairs={{4,0},{8,4},{12,8},{16,12},{20,16},{24,20},{28,24},{0,28},{5,1},{9... | collective-permute-start | bytes 1376264 | tf_op jit(solution)/shard_map/ppermute | solution.py:34
  8.2 11.8 %collective-permute-start.6 = (bf16[32,1920]{1,0:T(8,128)(2,1)S(1)}, bf16[32,1920]{1,0:T(8,128)(2,1)S(1)}, u32[]{:S(2)}, u32[]{:S(2)}) collective-permute-start(bf16[32,1920]{1,0:T(8,128)(2,1)S(1)} %get-tuple-element.110.rest_0_), channel_id=1, source_target_pairs={{0,2},{1,3},{2,0},{3,1},{4,6},{5,7},{6,4},{7,5},{8,10},{9,11},{10,... | collective-permute-start | bytes 368648 | tf_op jit(solution)/shard_map/ppermute | solution.py:43
  9.8 10.3 %collective-permute-start.7 = (bf16[32,1920]{1,0:T(8,128)(2,1)S(1)}, bf16[32,1920]{1,0:T(8,128)(2,1)S(1)}, u32[]{:S(2)}, u32[]{:S(2)}) collective-permute-start(bf16[32,1920]{1,0:T(8,128)(2,1)S(1)} %get-tuple-element.111.rest_1_), channel_id=1, source_target_pairs={{0,2},{1,3},{2,0},{3,1},{4,6},{5,7},{6,4},{7,5},{8,10},{9,11},{10,... | collective-permute-start | bytes 368648 | tf_op jit(solution)/shard_map/ppermute | solution.py:43
  10.3 13.0 %collective-permute-start.8 = (bf16[32,3840]{1,0:T(8,128)(2,1)S(1)}, bf16[32,3840]{1,0:T(8,128)(2,1)S(1)}, u32[]{:S(2)}, u32[]{:S(2)}) collective-permute-start(bf16[32,3840]{1,0:T(8,128)(2,1)S(1)} %get-tuple-element.122.refs_4_), channel_id=1, source_target_pairs={{0,1},{1,0},{2,3},{3,2},{4,5},{5,4},{6,7},{7,6},{8,9},{9,8},{10,11... | collective-permute-start | bytes 737288 | tf_op jit(solution)/shard_map/ppermute | solution.py:52
  20.0 3.2 %collective-permute-start.10 = (bf16[32,1920]{1,0:T(8,128)(2,1)S(1)}, bf16[32,1920]{1,0:T(8,128)(2,1)S(1)}, u32[]{:S(2)}, u32[]{:S(2)}) collective-permute-start(bf16[32,1920]{1,0:T(8,128)(2,1)S(1)} %collective-permute-done.7), channel_id=1, source_target_pairs={{0,1},{1,0},{2,3},{3,2},{4,5},{5,4},{6,7},{7,6},{8,9},{9,8},{10,11... | collective-permute-start | bytes 368648 | tf_op jit(solution)/shard_map/ppermute | solution.py:52
  20.6 2.7 %collective-permute-start.9 = (bf16[32,1920]{1,0:T(8,128)(2,1)S(1)}, bf16[32,1920]{1,0:T(8,128)(2,1)S(1)}, u32[]{:S(2)}, u32[]{:S(2)}) collective-permute-start(bf16[32,1920]{1,0:T(8,128)(2,1)S(1)} %collective-permute-done.6), channel_id=1, source_target_pairs={{0,1},{1,0},{2,3},{3,2},{4,5},{5,4},{6,7},{7,6},{8,9},{9,8},{10,11... | collective-permute-start | bytes 368648 | tf_op jit(solution)/shard_map/ppermute | solution.py:52
  21.8 11.8 %collective-permute-start.14 = (bf16[32,3840]{1,0:T(8,128)(2,1)S(1)}, bf16[32,3840]{1,0:T(8,128)(2,1)S(1)}, u32[]{:S(2)}, u32[]{:S(2)}) collective-permute-start(bf16[32,3840]{1,0:T(8,128)(2,1)S(1)} %get-tuple-element.121), channel_id=1, source_target_pairs={{0,2},{1,3},{2,0},{3,1},{4,6},{5,7},{6,4},{7,5},{8,10},{9,11},{10,... | collective-permute-start | bytes 737288 | tf_op jit(solution)/shard_map/ppermute | solution.py:43
  29.5 1.7 %collective-permute-start = (bf16[32,3840]{1,0:T(8,128)(2,1)S(1)}, bf16[32,3840]{1,0:T(8,128)(2,1)}, u32[]{:S(2)}, u32[]{:S(2)}) collective-permute-start(bf16[32,3840]{1,0:T(8,128)(2,1)S(1)} %get-tuple-element.45), channel_id=1, source_target_pairs={{0,1},{1,0},{2,3},{3,2},{4,5},{5,4},{6,7},{7,6},{8,9},{9,8},{10,11... | collective-permute-start | bytes 737288 | tf_op jit(solution)/shard_map/cond/branch_1_fun/ppermute | solution.py:52
  29.7 1.8 %collective-permute-start.1 = (bf16[32,3840]{1,0:T(8,128)(2,1)S(1)}, bf16[32,3840]{1,0:T(8,128)(2,1)}, u32[]{:S(2)}, u32[]{:S(2)}) collective-permute-start(bf16[32,3840]{1,0:T(8,128)(2,1)S(1)} %get-tuple-element.46), channel_id=1, source_target_pairs={{0,1},{1,0},{2,3},{3,2},{4,5},{5,4},{6,7},{7,6},{8,9},{9,8},{10,11... | collective-permute-start | bytes 737288 | tf_op jit(solution)/shard_map/cond/branch_1_fun/ppermute | solution.py:52
  32.9 13.0 %collective-permute-start.13 = (bf16[32,3840]{1,0:T(8,128)(2,1)S(1)}, bf16[32,3840]{1,0:T(8,128)(2,1)S(1)}, u32[]{:S(2)}, u32[]{:S(2)}) collective-permute-start(bf16[32,3840]{1,0:T(8,128)(2,1)S(1)} %get-tuple-element.136), channel_id=1, source_target_pairs={{0,2},{1,3},{2,0},{3,1},{4,6},{5,7},{6,4},{7,5},{8,10},{9,11},{10,... | collective-permute-start | bytes 737288 | tf_op jit(solution)/shard_map/ppermute | solution.py:43
  33.6 15.6 %collective-permute-start.12 = (bf16[32,4096]{1,0:T(8,128)(2,1)S(1)}, bf16[32,4096]{1,0:T(8,128)(2,1)S(1)}, u32[]{:S(2)}, u32[]{:S(2)}) collective-permute-start(bf16[32,4096]{1,0:T(8,128)(2,1)S(1)} %get-tuple-element.135), channel_id=1, source_target_pairs={{28,0},{0,4},{4,8},{8,12},{12,16},{16,20},{20,24},{24,28},{29,1},{... | collective-permute-start | bytes 786440 | tf_op jit(solution)/shard_map/ppermute | solution.py:34
  33.7 1.9 %copy-start = (bf16[32,3840]{1,0:T(8,128)(2,1)}, bf16[32,3840]{1,0:T(8,128)(2,1)S(1)}, u32[]{:S(2)}) copy-start(bf16[32,3840]{1,0:T(8,128)(2,1)S(1)} %get-tuple-element.48.refs_1_) | copy-start | bytes 737284 | tf_op jit(solution)/shard_map/cond
  33.7 1.8 %collective-permute-start.2 = (bf16[32,3840]{1,0:T(8,128)(2,1)}, bf16[32,3840]{1,0:T(8,128)(2,1)S(1)}, u32[]{:S(2)}, u32[]{:S(2)}) collective-permute-start(bf16[32,3840]{1,0:T(8,128)(2,1)} %get-tuple-element.47.refs_0_), channel_id=1, source_target_pairs={{0,1},{1,0},{2,3},{3,2},{4,5},{5,4},{6,7},{7,6},{8,9},{9,8},{10,11... | collective-permute-start | bytes 737288 | tf_op jit(solution)/shard_map/cond/branch_1_fun/ppermute | solution.py:52
  33.8 1.9 %collective-permute-start.3 = (bf16[32,3840]{1,0:T(8,128)(2,1)S(1)}, bf16[32,3840]{1,0:T(8,128)(2,1)S(1)}, u32[]{:S(2)}, u32[]{:S(2)}) collective-permute-start(bf16[32,3840]{1,0:T(8,128)(2,1)S(1)} %get-tuple-element.48.refs_1_), channel_id=1, source_target_pairs={{0,1},{1,0},{2,3},{3,2},{4,5},{5,4},{6,7},{7,6},{8,9},{9,8},{10,11... | collective-permute-start | bytes 737288 | tf_op jit(solution)/shard_map/cond/branch_1_fun/ppermute | solution.py:52
  43.9 1.7 %collective-permute-start.4 = (bf16[32,3968]{1,0:T(8,128)(2,1)S(1)}, bf16[32,3968]{1,0:T(8,128)(2,1)}, u32[]{:S(2)}, u32[]{:S(2)}) collective-permute-start(bf16[32,3968]{1,0:T(8,128)(2,1)S(1)} %get-tuple-element.57), channel_id=1, source_target_pairs={{0,1},{1,0},{2,3},{3,2},{4,5},{5,4},{6,7},{7,6},{8,9},{9,8},{10,11... | collective-permute-start | bytes 761864 | tf_op jit(solution)/shard_map/cond/branch_1_fun/ppermute | solution.py:52
  44.1 1.9 %collective-permute-start.5 = (bf16[32,3968]{1,0:T(8,128)(2,1)S(1)}, bf16[32,3968]{1,0:T(8,128)(2,1)}, u32[]{:S(2)}, u32[]{:S(2)}) collective-permute-start(bf16[32,3968]{1,0:T(8,128)(2,1)S(1)} %get-tuple-element.58), channel_id=1, source_target_pairs={{0,1},{1,0},{2,3},{3,2},{4,5},{5,4},{6,7},{7,6},{8,9},{9,8},{10,11... | collective-permute-start | bytes 761864 | tf_op jit(solution)/shard_map/cond/branch_1_fun/ppermute | solution.py:52
  46.2 11.2 %collective-permute-start.15 = (bf16[32,3968]{1,0:T(8,128)(2,1)S(1)}, bf16[32,3968]{1,0:T(8,128)(2,1)S(1)}, u32[]{:S(2)}, u32[]{:S(2)}) collective-permute-start(bf16[32,3968]{1,0:T(8,128)(2,1)S(1)} %forward_add.1), channel_id=1, source_target_pairs={{28,0},{0,4},{4,8},{8,12},{12,16},{16,20},{20,24},{24,28},{29,1},{... | collective-permute-start | bytes 761864 | tf_op jit(solution)/shard_map/ppermute | solution.py:34
  47.7 10.9 %collective-permute-start.16 = (bf16[32,3968]{1,0:T(8,128)(2,1)S(1)}, bf16[32,3968]{1,0:T(8,128)(2,1)S(1)}, u32[]{:S(2)}, u32[]{:S(2)}) collective-permute-start(bf16[32,3968]{1,0:T(8,128)(2,1)S(1)} %get-tuple-element.148), channel_id=1, source_target_pairs={{0,2},{1,3},{2,0},{3,1},{4,6},{5,7},{6,4},{7,5},{8,10},{9,11},{10,... | collective-permute-start | bytes 761864 | tf_op jit(solution)/shard_map/ppermute | solution.py:43

commit v6 on v5

--- a/solution.py
+++ b/solution.py
@@ -21,7 +21,8 @@
         self.main = cap // 16 * 16
         self.extra = cap - self.main
         self.folds = depth // LANES
-        assert self.folds < self.main and depth % LANES == 0
+        assert self.folds + 4 <= self.main and depth % LANES == 0
+        assert max(cap, tok) <= LANES
         self.width = depth + LANES * self.extra
         self.blocks = count * slices
         self.tail_rows = -(-(self.blocks * self.extra) // 16) * 16
@@ -32,6 +33,20 @@
     devices = range(lax.axis_size(axis))
     route = [((i - distance) % len(devices), i) for i in devices]
     return lax.ppermute(block, axis, route)
+
+
+def to_next(block, distance, s):
+    sections, own = lax.axis_size("section"), s.count * s.slices
+    route = [
+        (
+            l * own + e * s.slices + j,
+            (l + 1) % sections * own + (e + distance) % s.count * s.slices + j,
+        )
+        for l in range(sections)
+        for e in range(s.count)
+        for j in range(s.slices)
+    ]
+    return lax.ppermute(block, ("section", "expert"), route)
 
 
 def across(block, distance, s):
@@ -101,14 +116,22 @@
             ]
 
 
-def slot_values(route_row, value_row, expert, s):
-    rank = slot_rows(route_row, s)
-    hit = route_row == expert
-    main = jnp.sum(
-        jnp.where(hit & (rank == iota((s.main, s.tok), 0)), value_row, 0.0), axis=1, keepdims=True
-    )
+def put_scores(route_row, score_row, expert, tail_ref, s):
+    col, rank = slot_columns(route_row, s)
+    hit = (col == expert) & (rank == iota((s.tok, LANES), 1))
+    row = jnp.sum(jnp.where(hit, as_column(score_row), 0.0), axis=0, keepdims=True)
+    for p, piece in enumerate(split_three(row)):
+        at = s.folds + 1 + p
+        tail_ref[at : at + 1, :LANES] = piece
+
+
+def get_gates(tail, s):
+    at = s.folds + 1
+    row = 2.5 * (tail[at : at + 1] + tail[at + 1 : at + 2] + tail[at + 2 : at + 3])
+    lane = iota((s.main, LANES), 1)
+    main = jnp.sum(jnp.where(lane == iota((s.main, LANES), 0), row, 0.0), axis=1, keepdims=True)
     extra = [
-        jnp.sum(jnp.where(hit & (rank == float(s.main + j)), value_row, 0.0), axis=1, keepdims=True)
+        jnp.sum(jnp.where(lane[:1] == float(s.main + j), row, 0.0), axis=1, keepdims=True)
         for j in range(s.extra)
     ]
     return main, extra
@@ -154,7 +177,7 @@
     return packs
 
 
-def pack_rows(s, route_row, x, outs, extra_ref, tail_ref):
+def pack_rows(s, route_row, x, outs, extra_ref, tail_ref, score_row=None):
     rank = slot_rows(route_row, s)
     slots = iota((s.main + 16, s.tok), 0)
     tail_ref[...] = jnp.zeros_like(tail_ref)
@@ -165,21 +188,26 @@
         write(outs[d], 0, rows[: s.main].astype(BF16))
         extra_ref[...] = rows[s.main :]
         fold(extra_ref, 0, tail_ref, s)
+        if score_row is not None:
+            put_scores(route_row, score_row, expert_at(s, d), tail_ref, s)
         write(outs[d], s.depth, tail_ref[...].astype(BF16))
 
 
-def first_kernel(s, route_hbm, x_hbm, *rest):
-    outs = grouped(rest[:-5], s, PIECES)
-    route_ref, x_ref, extra_ref, tail_ref, sems = rest[-5:]
+def first_kernel(s, route_hbm, score_hbm, x_hbm, *rest):
+    outs = grouped(rest[:-6], s, PIECES)
+    route_ref, score_ref, x_ref, extra_ref, tail_ref, sems = rest[-6:]
     copies = [
-        pltpu.make_async_copy(route_hbm, route_ref, sems.at[0]),
-        pltpu.make_async_copy(x_hbm, x_ref, sems.at[1]),
+        pltpu.make_async_copy(src, dst, sems.at[i])
+        for i, (src, dst) in enumerate(
+            ((route_hbm, route_ref), (score_hbm, score_ref), (x_hbm, x_ref))
+        )
     ]
     for copy in copies:
         copy.start()
     for copy in copies:
         copy.wait()
-    pack_rows(s, route_ref[...].astype(F32), x_ref[...], outs, extra_ref, tail_ref)
+    route_row = route_ref[...].astype(F32)
+    pack_rows(s, route_row, x_ref[...], outs, extra_ref, tail_ref, score_ref[...])
 
 
 def pack_kernel(s, route_ref, x_ref, *rest):
@@ -206,16 +234,26 @@
     rows_ref[s.blocks * s.main :, :] = extra_ref[...].astype(BF16)
 
 
+def put(outs, i, at, value, s):
+    if i < s.count:
+        outs[i][:, at] = value
+        return
+    n = (len(outs) - s.count) // (s.blocks - s.count)
+    rows = s.main // n
+    for h in range(n):
+        outs[s.count + (i - s.count) * n + h][:, at] = value[h * rows : (h + 1) * rows]
+
+
 def scatter_chunk(value, outs, extra_ref, at, s):
     for i in range(s.blocks):
-        outs[i][:, at] = value[i * s.main : (i + 1) * s.main].astype(BF16)
+        put(outs, i, at, value[i * s.main : (i + 1) * s.main].astype(BF16), s)
     extra_ref[:, at] = value[s.blocks * s.main :]
 
 
 def scatter_tails(outs, extra_ref, tail_ref, s):
     for i in range(s.blocks):
         fold(extra_ref, i * s.extra, tail_ref, s)
-        outs[i][:, s.depth : s.width] = tail_ref[...].astype(BF16)
+        put(outs, i, slice(s.depth, s.width), tail_ref[...].astype(BF16), s)
 
 
 def chunk_of(depth):
@@ -225,7 +263,7 @@
 
 
 def forward_kernel(s, *refs):
-    n = len(refs) - s.blocks - 6
+    n = s.slices * (1 + (s.count - 1) * PIECES)
     packs = grouped(refs[:n], s, PIECES)
     wg, wu, wd = refs[n : n + 3]
     outs = refs[n + 3 : -3]
@@ -335,31 +373,27 @@
 
 def total_of(parts, d, s):
     total = parts[d][...].astype(F32)
-    for part in parts[s.count + d :: s.count]:
-        total = total + part[...].astype(F32)
+    n = (len(parts) - s.count) // (s.blocks - s.count)
+    for i in range(s.count + d, s.blocks, s.count):
+        first = s.count + (i - s.count) * n
+        found = [part[...].astype(F32) for part in parts[first : first + n]]
+        total = total + (found[0] if n == 1 else jnp.concatenate(found, axis=0))
     return total
 
 
 def forward_sum_kernel(s, *refs):
-    n = len(refs) - 3 - s.count
-    parts = refs[:n]
-    own, route_ref, score_ref, y_ref = refs[n : n + 4]
-    backs = refs[n + 4 :]
-    for d in range(1, s.count):
-        backs[d - 1][...] = total_of(parts, d, s).astype(BF16)
-    route_row = route_ref[...].astype(F32)
-    main, extra = slot_values(route_row, 2.5 * score_ref[...], expert_at(s, 0), s)
-    add_gated(y_ref, [own], main, extra, total_of(parts, 0, s), s)
-    y_ref[s.folds : s.folds + 1, s.depth : s.depth + s.tok] = route_row.astype(BF16)
-    y_ref[:, s.width :] = jnp.zeros((s.main, 2 * LANES), BF16)
-
-
-def forward_add_kernel(s, distance, back, *rest):
-    base, (route_ref, score_ref, y_ref) = rest[:-3], rest[-3:]
-    route_row = route_ref[...].astype(F32)
-    main, extra = slot_values(route_row, 2.5 * score_ref[...], expert_at(s, distance), s)
-    add_gated(y_ref, base, main, extra, back[...].astype(F32), s)
-    y_ref[:, s.width :] = jnp.zeros((s.main, LANES), BF16)
+    n = s.count + (s.blocks - s.count) * PIECES
+    parts, bases = refs[:n], grouped(refs[n : n + 1 + (s.count - 1) * PIECES], s, PIECES)
+    route_ref, outs = refs[-1 - s.count], refs[-s.count :]
+    for d in range(s.count - 1, -1, -1):
+        tail = read(bases[d], s.depth, s.depth + LANES).astype(F32)
+        main, extra = get_gates(tail, s)
+        add_gated(outs[d], bases[d], main, extra, total_of(parts, d, s), s)
+        spare = outs[d].shape[1] - s.width
+        if spare:
+            outs[d][:, s.width :] = jnp.zeros((s.main, spare), BF16)
+    at = s.folds
+    outs[0][at : at + 1, s.depth : s.depth + s.tok] = route_ref[...].astype(F32).astype(BF16)
 
 
 def tokens_of(packs, route_row, rows_ref, extra_ref, tail_ref, s):
@@ -477,8 +511,15 @@
     return lax.optimization_barrier((values, after))[0]
 
 
+def parts_shape(s, width, pieces):
+    kept = [((s.main, width), BF16)] * s.count
+    return kept + [((s.main // pieces, width), BF16)] * ((s.blocks - s.count) * pieces)
+
+
 def gather_parts(s, parts):
-    return [beside(p, -(i // s.count), s) if i >= s.count else p for i, p in enumerate(parts)]
+    n = (len(parts) - s.count) // (s.blocks - s.count)
+    moved = [beside(p, -(i // n // s.count + 1), s) for i, p in enumerate(parts[s.count :])]
+    return list(parts[: s.count]) + moved
 
 
 def step(routes, run, *args):
@@ -521,17 +562,19 @@
         packed[:1] + [((s.main, s.width // PIECES), BF16)] * (PIECES * (s.count - 1)),
         [
             pltpu.VMEM((1, tok), jnp.int32),
+            pltpu.VMEM((1, tok), F32),
             pltpu.VMEM((tok, depth), BF16),
             *tail_scratch(s, 16),
-            pltpu.SemaphoreType.DMA((2,)),
+            pltpu.SemaphoreType.DMA((3,)),
         ],
-        [HBM] * 2,
+        [HBM] * 3,
         route_a,
+        score_a,
         x_fwd[0],
     )
     upstream = from_behind(grad_next, "section", -1)[0]
-    wg, wu, wd, route_a, route_b, score_a, score_b = load(
-        w_gate[0], w_up[0], w_down[0], route_a, route_b, score_a, score_b
+    wg, wu, wd, route_a, route_b, score_b = load(
+        w_gate[0], w_up[0], w_down[0], route_a, route_b, score_b
     )
     factors = call(
         functools.partial(saved_kernel, s),
@@ -543,18 +586,6 @@
         saved_up[0],
     )
     wide = s.width + LANES
-
-    def forward(rows, *weights):
-        parts = call(
-            functools.partial(forward_kernel, s),
-            "forward",
-            [((s.main, s.width), BF16)] * s.blocks,
-            row_scratch(s),
-            [VMEM] * (len(rows) + 3),
-            *rows,
-            *weights,
-        )
-        return tuple(gather_parts(s, parts))
 
     def backward(got, *rest):
         parts = call(
@@ -566,10 +597,18 @@
             *spread(s, got),
             *rest,
         )
-        return tuple(gather_parts(s, parts))
+        sums = call(
+            functools.partial(backward_sum_kernel, s),
+            "backward_sum",
+            [((s.main, wide), BF16)] * s.count,
+            [],
+            [VMEM] * s.blocks,
+            *gather_parts(s, parts),
+        )
+        return tuple(sums)
 
     got = cross(s, sent_a, PIECES)
-    got[1:] = hold(got[1:], score_a, factors)
+    got[1:] = hold(got[1:], route_a, factors)
     rows_a = spread(s, got)
     sent_b = call(
         functools.partial(pack_kernel, s),
@@ -581,44 +620,31 @@
         hold(upstream, got[1:]),
     )
     got_b = cross(s, sent_b, 1)
-    parts_a = step(route_a, forward, hold(rows_a, sent_b), wg, wu, wd)
+    parts_a = call(
+        functools.partial(forward_kernel, s),
+        "forward",
+        parts_shape(s, s.width, PIECES),
+        row_scratch(s),
+        [VMEM] * (len(rows_a) + 3),
+        *hold(rows_a, sent_b),
+        wg,
+        wu,
+        wd,
+    )
+    parts_a = gather_parts(s, parts_a)
     sums_a = call(
         functools.partial(forward_sum_kernel, s),
         "forward_sum",
-        [((s.main, wide + LANES), BF16)] + [((s.main, s.width), BF16)] * (s.count - 1),
-        [],
-        [VMEM] * (s.blocks + 3),
-        *parts_a,
-        sent_a[0],
-        route_a,
-        score_a,
-    )
-    back_a = [across(sums_a[d], -d, s) for d in range(1, s.count)]
-    moved = [from_behind(sums_a[0], "section", 1)]
-    got_b[1:] = hold(got_b[1:], sums_a)
-    parts_b = step(route_b, backward, got_b, *factors, wg, wu, wd)
-    back_a = hold(back_a, parts_b)
-    for d in range(1, s.count):
-        y = call(
-            functools.partial(forward_add_kernel, s, d),
-            "forward_add",
-            [((s.main, wide), BF16)],
-            [],
-            [VMEM] * (3 + PIECES),
-            back_a[d - 1],
-            *sent_a[1 + (d - 1) * PIECES : 1 + d * PIECES],
-            route_a,
-            score_a,
-        )[0]
-        moved.append(from_behind(y, "section", 1))
-    sums_b = call(
-        functools.partial(backward_sum_kernel, s),
-        "backward_sum",
         [((s.main, wide), BF16)] * s.count,
         [],
-        [VMEM] * s.blocks,
-        *hold(parts_b, y),
-    )
+        [VMEM] * (len(parts_a) + len(got) + 1),
+        *parts_a,
+        *got,
+        route_a,
+    )
+    moved = [to_next(y, -d, s) for d, y in enumerate(sums_a)]
+    got_b[1:] = hold(got_b[1:], sums_a)
+    sums_b = step(route_b, backward, got_b, *factors, wg, wu, wd)
     back_b = [sums_b[0]] + [across(sums_b[d], -d, s) for d in range(1, s.count)]
     next_input = call(
         functools.partial(forward_end_kernel, s),

time: 60 us -> 45 us (0.75)
  the two profiles are of different devices: /device:TPU:0 before, /device:TPU:7 now
where the time goes in v6:
time: 45 us; the launch traced here: 44.9 us
  waiting for transfers between devices  15.9 us (35%)
  Pallas kernels  15.4 us (34%)
  starting transfers between devices  11.8 us (26%)
  local copies, waits for them, and re-layouts  1.03 us (2%)
  between operations  0.74 us (2%)
    pallas_call x10, Pallas kernels, call(): pl.pallas_call(kernel, out_shape=shapes, in_specs=ins, out_specs=[VMEM] *...  15.4 us
    ppermute x4, waiting for transfers between devices, across(): return lax.ppermute(block, 'expert', route)  9.25 us
    ppermute x11, starting transfers between devices, beside(): return lax.ppermute(block, 'expert', route)  5.88 us
    ppermute x11, waiting for transfers between devices, beside(): return lax.ppermute(block, 'expert', route)  4.1 us
    ppermute x2, starting transfers between devices, to_next(): return lax.ppermute(block, ('section', 'expert'), route)  3.44 us
    ppermute x4, starting transfers between devices, across(): return lax.ppermute(block, 'expert', route)  2.17 us
    ppermute x1, waiting for transfers between devices, from_behind(): return lax.ppermute(block, axis, route)  1.53 us
    ppermute x2, waiting for transfers between devices, to_next(): return lax.ppermute(block, ('section', 'expert'), route)  1.05 us
  transfers between devices with their start and end apart: 18, of which 11 were waited for; matrix products, arithmetic and copies ran while one was open for 2% of the time, Pallas kernels for 32%

profile of v6, /device:TPU:7, one launch (start us, length us, event | category | flops | bytes accessed | tf_op | source)
XLA Modules:
  0.0 44.9 jit_solution(7557657824235719635)
XLA Ops:
  0.9 1.5 %first.1 = (bf16[32,3840]{1,0:T(8,128)(2,1)S(1)}, bf16[32,1920]{1,0:T(8,128)(2,1)S(1)}, bf16[32,1920]{1,0:T(8,128)(2,1)S(1)}) custom-call(s32[1,64]{1,0:T(1,128)} %bitcast.26, f32[1,64]{1,0:T(1,128)} %bitcast.28, bf16[64,3584]{1,0:T(8,128)(2,1)} %bitcast.24), custom_call_target="tpu_custom_call" | custom-call | tf_op jit(solution)/shard_map/first/pallas_call | solution.py:468
  2.6 1.4 %collective-permute-start.5 = (bf16[32,1920]{1,0:T(8,128)(2,1)S(1)}, bf16[32,1920]{1,0:T(8,128)(2,1)S(1)}, u32[]{:S(2)}, u32[]{:S(2)}) collective-permute-start(bf16[32,1920]{1,0:T(8,128)(2,1)S(1)} %get-tuple-element.71), channel_id=1, source_target_pairs={{0,2},{1,3},{2,0},{3,1},{4,6},{5,7},{6,4},{7,5},{8,10},{9,11},{10,... | collective-permute-start | bytes 368648 | tf_op jit(solution)/shard_map/ppermute | solution.py:58
  4.0 1.5 %collective-permute-start.6 = (bf16[32,3840]{1,0:T(8,128)(2,1)S(1)}, bf16[32,3840]{1,0:T(8,128)(2,1)S(1)}, u32[]{:S(2)}, u32[]{:S(2)}) collective-permute-start(bf16[32,3840]{1,0:T(8,128)(2,1)S(1)} %get-tuple-element.82.refs_0_.refs_6_), channel_id=1, source_target_pairs={{0,1},{1,0},{2,3},{3,2},{4,5},{5,4},{6,7},{7,6},{8,9},{9,8},{10,11... | collective-permute-start | bytes 737288 | tf_op jit(solution)/shard_map/ppermute | solution.py:67
  5.5 1.0 %copy_bitcast_fusion = (bf16[4,34,512]{2,1,0:T(8,128)(2,1)S(1)}, bf16[4,34,512]{2,1,0:T(8,128)(2,1)S(1)}) fusion(bf16[1,4,34,512]{3,1,2,0:T(4,128)(2,1)} %param.15, bf16[1,4,34,512]{3,1,2,0:T(4,128)(2,1)} %param.14), kind=kLoop, calls=%fused_computation | loop fusion | bytes 557056 | tf_op jit(solution)/shard_map/squeeze | solution.py:586
  6.8 4.3 %load.1 = (bf16[3584,512]{1,0:T(8,128)(2,1)S(1)}, bf16[3584,512]{1,0:T(8,128)(2,1)S(1)}, bf16[512,3584]{1,0:T(8,128)(2,1)S(1)}, s32[1,64]{1,0:T(1,128)S(1)}, s32[1,64]{1,0:T(1,128)S(1)}, /*index=5*/f32[1,64]{1,0:T(1,128)S(1)}) custom-call(bf16[3584,512]{1,0:T(8,128)(2,1)} %bitcast.21, bf16[3584,512]{1,0:T(8,128)(2,1)} %bitcast.22, ...), custom_call_target="tpu_custom_call" | custom-call | tf_op jit(solution)/shard_map/load/pallas_call | solution.py:468
  11.2 0.5 %collective-permute-start.8 = (bf16[32,1920]{1,0:T(8,128)(2,1)S(1)}, bf16[32,1920]{1,0:T(8,128)(2,1)S(1)}, u32[]{:S(2)}, u32[]{:S(2)}) collective-permute-start(bf16[32,1920]{1,0:T(8,128)(2,1)S(1)} %collective-permute-done.5.refs_2_.refs_8_), channel_id=1, source_target_pairs={{0,1},{1,0},{2,3},{3,2},{4,5},{5,4},{6,7},{7,6},{8,9},{9,8},{10,11... | collective-permute-start | bytes 368648 | tf_op jit(solution)/shard_map/ppermute | solution.py:67
  11.6 1.5 %collective-permute-done.9 = bf16[1,64,3584]{2,1,0:T(8,128)(2,1)S(1)} collective-permute-done((bf16[1,64,3584]{2,1,0:T(8,128)(2,1)}, bf16[1,64,3584]{2,1,0:T(8,128)(2,1)S(1)}, u32[]{:S(2)}, u32[]{:S(2)}) %collective-permute-start.9) | collective-permute-done | bytes 458784 | tf_op jit(solution)/shard_map/ppermute | solution.py:35
  13.2 0.5 %pack.1 = (bf16[32,3840]{1,0:T(8,128)(2,1)S(1)}, bf16[32,3840]{1,0:T(8,128)(2,1)S(1)}) custom-call(s32[1,64]{1,0:T(1,128)S(1)} %get-tuple-element.78.route_ref.refs_3_, bf16[64,3584]{1,0:T(8,128)(2,1)S(1)} %bitcast.18), custom_call_target="tpu_custom_call" | custom-call | tf_op jit(solution)/shard_map/pack/pallas_call | solution.py:468
  14.0 2.0 %forward.1 = (bf16[32,3840]{1,0:T(8,128)(2,1)S(1)}, bf16[32,3840]{1,0:T(8,128)(2,1)S(1)}, bf16[16,3840]{1,0:T(8,128)(2,1)S(1)}, bf16[16,3840]{1,0:T(8,128)(2,1)S...) custom-call(bf16[32,3840]{1,0:T(8,128)(2,1)S(1)} %get-tuple-element.82.refs_0_.refs_6_, ...), custom_call_target="tpu_custom_call" | custom-call | tf_op jit(solution)/shard_map/forward/pallas_call | solution.py:468
  16.0 1.9 %collective-permute-start.10 = (bf16[16,3840]{1,0:T(8,128)(2,1)S(1)}, bf16[16,3840]{1,0:T(8,128)(2,1)S(1)}, u32[]{:S(2)}, u32[]{:S(2)}) collective-permute-start(bf16[16,3840]{1,0:T(8,128)(2,1)S(1)} %get-tuple-element.93), channel_id=1, source_target_pairs={{0,1},{1,0},{2,3},{3,2},{4,5},{5,4},{6,7},{7,6},{8,9},{9,8},{10,11... | collective-permute-start | bytes 368648 | tf_op jit(solution)/shard_map/ppermute | solution.py:67
  18.0 0.4 collective-permute-start.12
  20.1 0.4 collective-permute-start.14
  20.5 3.0 %collective-permute-start.15 = (bf16[32,3968]{1,0:T(8,128)(2,1)S(1)}, bf16[32,3968]{1,0:T(8,128)(2,1)S(1)}, u32[]{:S(2)}, u32[]{:S(2)}) collective-permute-start(bf16[32,3968]{1,0:T(8,128)(2,1)S(1)} %get-tuple-element.98), channel_id=1, source_target_pairs={{0,6},{1,7},{2,4},{3,5},{4,10},{5,11},{6,8},{7,9},{8,14},{9,15},{1... | collective-permute-start | bytes 761864 | tf_op jit(solution)/shard_map/ppermute | solution.py:49
  23.5 8.3 %conditional.1 = ((bf16[32,3968]{1,0:T(8,128)(2,1)S(1)}, bf16[32,3968]{1,0:T(8,128)(2,1)S(1)})) conditional(s32[]{:T(128)} %bitcast.12, () %tuple.23, (bf16[32,3840]{1,0:T(8,128)(2,1)S(1)}, bf16[32,3840]{1,0:T(8,128)(2,1)S(1)}, f32[144,512]{1,0:T(8,128)S(1)}, f32[144,512]{1,0:T(8,128)S(1)}, f32[144,512]{1,0:T(8,128)S(1)}, ...), branch_computations={%region_0.0_spmd, %region_1.0_spmd} | conditional | bytes 3997864 | solution.py:528
  23.5 0.7 %collective-permute-start = (bf16[32,3840]{1,0:T(8,128)(2,1)S(1)}, bf16[32,3840]{1,0:T(8,128)(2,1)S(1)}, u32[]{:S(2)}, u32[]{:S(2)}) collective-permute-start(bf16[32,3840]{1,0:T(8,128)(2,1)S(1)} %get-tuple-element.16.refs_0_), channel_id=1, source_target_pairs={{0,1},{1,0},{2,3},{3,2},{4,5},{5,4},{6,7},{7,6},{8,9},{9,8},{10,11... | collective-permute-start | bytes 737288 | tf_op jit(solution)/shard_map/cond/branch_1_fun/ppermute | solution.py:67
  24.3 1.1 %collective-permute-done.refs_2_ = bf16[32,3840]{1,0:T(8,128)(2,1)S(1)} collective-permute-done((bf16[32,3840]{1,0:T(8,128)(2,1)S(1)}, bf16[32,3840]{1,0:T(8,128)(2,1)S(1)}, u32[]{:S(2)}, u32[]{:S(2)}) %collective-permute-start) | collective-permute-done | bytes 245792 | tf_op jit(solution)/shard_map/cond/branch_1_fun/ppermute | solution.py:67
  25.4 0.4 collective-permute-done.1.refs_3_
  25.8 3.9 %backward.1 = (bf16[32,3968]{1,0:T(8,128)(2,1)S(1)}, bf16[32,3968]{1,0:T(8,128)(2,1)S(1)}, bf16[32,3968]{1,0:T(8,128)(2,1)S(1)}, bf16[32,3968]{1,0:T(8,128)(2,1)S(1)}) custom-call(bf16[32,3840]{1,0:T(8,128)(2,1)S(1)} %get-tuple-element.16.refs_0_, bf16[32,3840]{1,0:T(8,128)(2,1)S(1)} %get-tuple-element.17.refs_1_, ...), custom_call_target="tpu_custom_call" | custom-call | tf_op jit(solution)/shard_map/cond/branch_1_fun/backward/pallas_call | solution.py:468
  29.7 0.4 collective-permute-start.2
  30.2 1.0 %collective-permute-done.2.refs_2_ = bf16[32,3968]{1,0:T(8,128)(2,1)S(1)} collective-permute-done((bf16[32,3968]{1,0:T(8,128)(2,1)S(1)}, bf16[32,3968]{1,0:T(8,128)(2,1)S(1)}, u32[]{:S(2)}, u32[]{:S(2)}) %collective-permute-start.2) | collective-permute-done | bytes 253984 | tf_op jit(solution)/shard_map/cond/branch_1_fun/ppermute | solution.py:67
  32.2 1.0 %collective-permute-done.14.refs_0_ = bf16[32,3968]{1,0:T(8,128)(2,1)S(1)} collective-permute-done((bf16[32,3968]{1,0:T(8,128)(2,1)S(1)}, bf16[32,3968]{1,0:T(8,128)(2,1)S(1)}, u32[]{:S(2)}, u32[]{:S(2)}) %collective-permute-start.14) | collective-permute-done | bytes 253984 | tf_op jit(solution)/shard_map/ppermute | solution.py:49
  33.2 1.2 %forward_end.1 = bf16[64,3584]{1,0:T(8,128)(2,1)} custom-call(bf16[32,3968]{1,0:T(8,128)(2,1)S(1)} %collective-permute-done.14.refs_0_, bf16[32,3968]{1,0:T(8,128)(2,1)S(1)} %collective-permute-done.15.refs_1_), custom_call_target="tpu_custom_call" | custom-call | tf_op jit(solution)/shard_map/forward_end/pallas_call | solution.py:468
  34.4 9.2 %collective-permute-done.17.refs_1_ = bf16[32,3968]{1,0:T(8,128)(2,1)S(1)} collective-permute-done((bf16[32,3968]{1,0:T(8,128)(2,1)S(1)}, bf16[32,3968]{1,0:T(8,128)(2,1)S(1)}, u32[]{:S(2)}, u32[]{:S(2)}) %collective-permute-start.17) | collective-permute-done | bytes 253984 | tf_op jit(solution)/shard_map/ppermute | solution.py:58
  43.7 1.2 %backward_end.1 = (bf16[64,3584]{1,0:T(8,128)(2,1)}, f32[1,64]{1,0:T(1,128)}) custom-call(bf16[32,3968]{1,0:T(8,128)(2,1)S(1)} %get-tuple-element.102.refs_0_, bf16[32,3968]{1,0:T(8,128)(2,1)S(1)} %collective-permute-done.17.refs_1_, bf16[64,3584]{1,0:T(8,128)(2,1)S(1)} %bitcast.19, s32[1,64]{1,0:T(1,128)S(1)} %get-tuple-element.78.route_ref.refs_3_, ...), custom_call_target="tpu_custom_call" | custom-call | tf_op jit(solution)/shard_map/backward_end/pallas_call | solution.py:468
  (24 shorter events, 3.9 us)
Async XLA Ops:
  0.6 12.5 %collective-permute-start.9 = (bf16[1,64,3584]{2,1,0:T(8,128)(2,1)}, bf16[1,64,3584]{2,1,0:T(8,128)(2,1)S(1)}, u32[]{:S(2)}, u32[]{:S(2)}) collective-permute-start(bf16[1,64,3584]{2,1,0:T(8,128)(2,1)} %param.16), channel_id=1, source_target_pairs={{4,0},{8,4},{12,8},{16,12},{20,16},{24,20},{28,24},{0,28},{5,1},{9... | collective-permute-start | bytes 1376264 | tf_op jit(solution)/shard_map/ppermute | solution.py:35
  2.5 8.6 %collective-permute-start.4 = (bf16[32,1920]{1,0:T(8,128)(2,1)S(1)}, bf16[32,1920]{1,0:T(8,128)(2,1)S(1)}, u32[]{:S(2)}, u32[]{:S(2)}) collective-permute-start(bf16[32,1920]{1,0:T(8,128)(2,1)S(1)} %get-tuple-element.70), channel_id=1, source_target_pairs={{0,2},{1,3},{2,0},{3,1},{4,6},{5,7},{6,4},{7,5},{8,10},{9,11},{10,... | collective-permute-start | bytes 368648 | tf_op jit(solution)/shard_map/ppermute | solution.py:58
  2.6 8.5 %collective-permute-start.5 = (bf16[32,1920]{1,0:T(8,128)(2,1)S(1)}, bf16[32,1920]{1,0:T(8,128)(2,1)S(1)}, u32[]{:S(2)}, u32[]{:S(2)}) collective-permute-start(bf16[32,1920]{1,0:T(8,128)(2,1)S(1)} %get-tuple-element.71), channel_id=1, source_target_pairs={{0,2},{1,3},{2,0},{3,1},{4,6},{5,7},{6,4},{7,5},{8,10},{9,11},{10,... | collective-permute-start | bytes 368648 | tf_op jit(solution)/shard_map/ppermute | solution.py:58
  4.0 10.0 %collective-permute-start.6 = (bf16[32,3840]{1,0:T(8,128)(2,1)S(1)}, bf16[32,3840]{1,0:T(8,128)(2,1)S(1)}, u32[]{:S(2)}, u32[]{:S(2)}) collective-permute-start(bf16[32,3840]{1,0:T(8,128)(2,1)S(1)} %get-tuple-element.82.refs_0_.refs_6_), channel_id=1, source_target_pairs={{0,1},{1,0},{2,3},{3,2},{4,5},{5,4},{6,7},{7,6},{8,9},{9,8},{10,11... | collective-permute-start | bytes 737288 | tf_op jit(solution)/shard_map/ppermute | solution.py:67
  11.1 2.9 %collective-permute-start.7 = (bf16[32,1920]{1,0:T(8,128)(2,1)S(1)}, bf16[32,1920]{1,0:T(8,128)(2,1)S(1)}, u32[]{:S(2)}, u32[]{:S(2)}) collective-permute-start(bf16[32,1920]{1,0:T(8,128)(2,1)S(1)} %collective-permute-done.4.refs_1_.refs_7_), channel_id=1, source_target_pairs={{0,1},{1,0},{2,3},{3,2},{4,5},{5,4},{6,7},{7,6},{8,9},{9,8},{10,11... | collective-permute-start | bytes 368648 | tf_op jit(solution)/shard_map/ppermute | solution.py:67
  11.2 2.8 %collective-permute-start.8 = (bf16[32,1920]{1,0:T(8,128)(2,1)S(1)}, bf16[32,1920]{1,0:T(8,128)(2,1)S(1)}, u32[]{:S(2)}, u32[]{:S(2)}) collective-permute-start(bf16[32,1920]{1,0:T(8,128)(2,1)S(1)} %collective-permute-done.5.refs_2_.refs_8_), channel_id=1, source_target_pairs={{0,1},{1,0},{2,3},{3,2},{4,5},{5,4},{6,7},{7,6},{8,9},{9,8},{10,11... | collective-permute-start | bytes 368648 | tf_op jit(solution)/shard_map/ppermute | solution.py:67
  13.6 9.9 %collective-permute-start.16 = (bf16[32,3840]{1,0:T(8,128)(2,1)S(1)}, bf16[32,3840]{1,0:T(8,128)(2,1)S(1)}, u32[]{:S(2)}, u32[]{:S(2)}) collective-permute-start(bf16[32,3840]{1,0:T(8,128)(2,1)S(1)} %get-tuple-element.81), channel_id=1, source_target_pairs={{0,2},{1,3},{2,0},{3,1},{4,6},{5,7},{6,4},{7,5},{8,10},{9,11},{10,... | collective-permute-start | bytes 737288 | tf_op jit(solution)/shard_map/ppermute | solution.py:58
  16.0 2.9 %collective-permute-start.10 = (bf16[16,3840]{1,0:T(8,128)(2,1)S(1)}, bf16[16,3840]{1,0:T(8,128)(2,1)S(1)}, u32[]{:S(2)}, u32[]{:S(2)}) collective-permute-start(bf16[16,3840]{1,0:T(8,128)(2,1)S(1)} %get-tuple-element.93), channel_id=1, source_target_pairs={{0,1},{1,0},{2,3},{3,2},{4,5},{5,4},{6,7},{7,6},{8,9},{9,8},{10,11... | collective-permute-start | bytes 368648 | tf_op jit(solution)/shard_map/ppermute | solution.py:67
  17.9 1.3 %collective-permute-start.11 = (bf16[16,3840]{1,0:T(8,128)(2,1)S(1)}, bf16[16,3840]{1,0:T(8,128)(2,1)S(1)}, u32[]{:S(2)}, u32[]{:S(2)}) collective-permute-start(bf16[16,3840]{1,0:T(8,128)(2,1)S(1)} %get-tuple-element.94), channel_id=1, source_target_pairs={{0,1},{1,0},{2,3},{3,2},{4,5},{5,4},{6,7},{7,6},{8,9},{9,8},{10,11... | collective-permute-start | bytes 368648 | tf_op jit(solution)/shard_map/ppermute | solution.py:67
  18.0 1.4 %collective-permute-start.12 = (bf16[16,3840]{1,0:T(8,128)(2,1)S(1)}, bf16[16,3840]{1,0:T(8,128)(2,1)S(1)}, u32[]{:S(2)}, u32[]{:S(2)}) collective-permute-start(bf16[16,3840]{1,0:T(8,128)(2,1)S(1)} %get-tuple-element.95), channel_id=1, source_target_pairs={{0,1},{1,0},{2,3},{3,2},{4,5},{5,4},{6,7},{7,6},{8,9},{9,8},{10,11... | collective-permute-start | bytes 368648 | tf_op jit(solution)/shard_map/ppermute | solution.py:67
  18.4 1.3 %collective-permute-start.13 = (bf16[16,3840]{1,0:T(8,128)(2,1)S(1)}, bf16[16,3840]{1,0:T(8,128)(2,1)S(1)}, u32[]{:S(2)}, u32[]{:S(2)}) collective-permute-start(bf16[16,3840]{1,0:T(8,128)(2,1)S(1)} %get-tuple-element.96), channel_id=1, source_target_pairs={{0,1},{1,0},{2,3},{3,2},{4,5},{5,4},{6,7},{7,6},{8,9},{9,8},{10,11... | collective-permute-start | bytes 368648 | tf_op jit(solution)/shard_map/ppermute | solution.py:67
  20.1 13.1 %collective-permute-start.14 = (bf16[32,3968]{1,0:T(8,128)(2,1)S(1)}, bf16[32,3968]{1,0:T(8,128)(2,1)S(1)}, u32[]{:S(2)}, u32[]{:S(2)}) collective-permute-start(bf16[32,3968]{1,0:T(8,128)(2,1)S(1)} %get-tuple-element.97), channel_id=1, source_target_pairs={{0,4},{1,5},{2,6},{3,7},{4,8},{5,9},{6,10},{7,11},{8,12},{9,13},{1... | collective-permute-start | bytes 761864 | tf_op jit(solution)/shard_map/ppermute | solution.py:49
  20.5 12.8 %collective-permute-start.15 = (bf16[32,3968]{1,0:T(8,128)(2,1)S(1)}, bf16[32,3968]{1,0:T(8,128)(2,1)S(1)}, u32[]{:S(2)}, u32[]{:S(2)}) collective-permute-start(bf16[32,3968]{1,0:T(8,128)(2,1)S(1)} %get-tuple-element.98), channel_id=1, source_target_pairs={{0,6},{1,7},{2,4},{3,5},{4,10},{5,11},{6,8},{7,9},{8,14},{9,15},{1... | collective-permute-start | bytes 761864 | tf_op jit(solution)/shard_map/ppermute | solution.py:49
  23.5 1.9 %collective-permute-start = (bf16[32,3840]{1,0:T(8,128)(2,1)S(1)}, bf16[32,3840]{1,0:T(8,128)(2,1)S(1)}, u32[]{:S(2)}, u32[]{:S(2)}) collective-permute-start(bf16[32,3840]{1,0:T(8,128)(2,1)S(1)} %get-tuple-element.16.refs_0_), channel_id=1, source_target_pairs={{0,1},{1,0},{2,3},{3,2},{4,5},{5,4},{6,7},{7,6},{8,9},{9,8},{10,11... | collective-permute-start | bytes 737288 | tf_op jit(solution)/shard_map/cond/branch_1_fun/ppermute | solution.py:67
  24.3 1.5 %collective-permute-start.1 = (bf16[32,3840]{1,0:T(8,128)(2,1)S(1)}, bf16[32,3840]{1,0:T(8,128)(2,1)S(1)}, u32[]{:S(2)}, u32[]{:S(2)}) collective-permute-start(bf16[32,3840]{1,0:T(8,128)(2,1)S(1)} %get-tuple-element.17.refs_1_), channel_id=1, source_target_pairs={{0,1},{1,0},{2,3},{3,2},{4,5},{5,4},{6,7},{7,6},{8,9},{9,8},{10,11... | collective-permute-start | bytes 737288 | tf_op jit(solution)/shard_map/cond/branch_1_fun/ppermute | solution.py:67
  29.7 1.6 %collective-permute-start.2 = (bf16[32,3968]{1,0:T(8,128)(2,1)S(1)}, bf16[32,3968]{1,0:T(8,128)(2,1)S(1)}, u32[]{:S(2)}, u32[]{:S(2)}) collective-permute-start(bf16[32,3968]{1,0:T(8,128)(2,1)S(1)} %get-tuple-element.26), channel_id=1, source_target_pairs={{0,1},{1,0},{2,3},{3,2},{4,5},{5,4},{6,7},{7,6},{8,9},{9,8},{10,11... | collective-permute-start | bytes 761864 | tf_op jit(solution)/shard_map/cond/branch_1_fun/ppermute | solution.py:67
  30.1 1.5 %collective-permute-start.3 = (bf16[32,3968]{1,0:T(8,128)(2,1)S(1)}, bf16[32,3968]{1,0:T(8,128)(2,1)S(1)}, u32[]{:S(2)}, u32[]{:S(2)}) collective-permute-start(bf16[32,3968]{1,0:T(8,128)(2,1)S(1)} %get-tuple-element.27), channel_id=1, source_target_pairs={{0,1},{1,0},{2,3},{3,2},{4,5},{5,4},{6,7},{7,6},{8,9},{9,8},{10,11... | collective-permute-start | bytes 761864 | tf_op jit(solution)/shard_map/cond/branch_1_fun/ppermute | solution.py:67
  31.8 11.8 %collective-permute-start.17 = (bf16[32,3968]{1,0:T(8,128)(2,1)S(1)}, bf16[32,3968]{1,0:T(8,128)(2,1)S(1)}, u32[]{:S(2)}, u32[]{:S(2)}) collective-permute-start(bf16[32,3968]{1,0:T(8,128)(2,1)S(1)} %get-tuple-element.101), channel_id=1, source_target_pairs={{0,2},{1,3},{2,0},{3,1},{4,6},{5,7},{6,4},{7,5},{8,10},{9,11},{10,... | collective-permute-start | bytes 761864 | tf_op jit(solution)/shard_map/ppermute | solution.py:58

commit v7 on v6

--- a/solution.py
+++ b/solution.py
@@ -247,7 +247,7 @@
 def scatter_chunk(value, outs, extra_ref, at, s):
     for i in range(s.blocks):
         put(outs, i, at, value[i * s.main : (i + 1) * s.main].astype(BF16), s)
-    extra_ref[:, at] = value[s.blocks * s.main :]
+    extra_ref[:, at] = value[s.blocks * s.main :].astype(F32)
 
 
 def scatter_tails(outs, extra_ref, tail_ref, s):
@@ -301,9 +301,9 @@
     g = g_ref[...]
     u = u_ref[...]
     sig = jax.nn.sigmoid(g)
-    c1_ref[...] = u * sig * (1.0 + g * (1.0 - sig))
-    c2_ref[...] = g * sig
-    hb_ref[...] = (g * sig * u).astype(BF16).astype(F32)
+    c1_ref[...] = (u * sig * (1.0 + g * (1.0 - sig))).T
+    c2_ref[...] = (g * sig).T
+    hb_ref[...] = (g * sig * u).astype(BF16).astype(F32).T
 
 
 def split_three(value):
@@ -349,12 +349,12 @@
     a = None
     for c in range(0, s.depth, chunk):
         more = lax.dot_general(
-            rows_ref[:, c : c + chunk], wd[:, c : c + chunk], NT, preferred_element_type=F32
+            wd[:, c : c + chunk], rows_ref[:, c : c + chunk], NT, preferred_element_type=F32
         )
         a = more if a is None else a + more
     dgp = (a * c1[...]).astype(BF16)
     dup = (a * c2[...]).astype(BF16)
-    inner = jnp.sum(a * hb[...], axis=1, keepdims=True)
+    inner = as_column(jnp.sum(a * hb[...], axis=0, keepdims=True))
     for i in range(s.blocks):
         first = s.blocks * s.main + i * s.extra
         outs[i][:, s.width :] = put_inner(
@@ -364,10 +364,10 @@
         )
     tail_ref[...] = jnp.zeros_like(tail_ref)
     for c in range(0, s.depth, chunk):
-        part = lax.dot_general(
-            dgp, wg[c : c + chunk, :], NT, preferred_element_type=F32
-        ) + lax.dot_general(dup, wu[c : c + chunk, :], NT, preferred_element_type=F32)
-        scatter_chunk(part, outs, extra_ref, slice(c, c + chunk), s)
+        part = jnp.dot(wg[c : c + chunk, :], dgp, preferred_element_type=F32) + jnp.dot(
+            wu[c : c + chunk, :], dup, preferred_element_type=F32
+        )
+        scatter_chunk(part.astype(BF16).T, outs, extra_ref, slice(c, c + chunk), s)
     scatter_tails(outs, extra_ref, tail_ref, s)
 
 
@@ -579,7 +579,7 @@
     factors = call(
         functools.partial(saved_kernel, s),
         "saved",
-        [((s.rows, hidden), F32)] * 3,
+        [((hidden, s.rows), F32)] * 3,
         [pltpu.VMEM((s.rows, hidden), F32)] * 2,
         [VMEM] * 2,
         saved_gate[0],

time: 45 us -> 45 us (level)
  Pallas kernels: 15.4 us -> 16.6 us
  waiting for transfers between devices: 15.9 us -> 14.7 us
    pallas_call x10, Pallas kernels: 15.4 us -> 16.6 us  [call(): pl.pallas_call(kernel, out_shape=shapes, in_specs=ins, out_specs=[VMEM] *...]
    ppermute x2, waiting for transfers between devices: 1.05 us -> 0.43 us  [to_next(): return lax.ppermute(block, ('section', 'expert'), route)]
  transfers between devices with their start and end apart: 18 -> 18, of which waited for: 11 -> 11; matrix products, arithmetic and copies ran while one was open for 2% -> 2% of each run, Pallas kernels for 32% -> 34%
where the time goes in v7:
time: 45 us; the launch traced here: 44.9 us
  Pallas kernels  16.6 us (37%)
  waiting for transfers between devices  14.7 us (33%)
  starting transfers between devices  11.8 us (26%)
  local copies, waits for them, and re-layouts  1.03 us (2%)
  between operations  0.74 us (2%)
    pallas_call x10, Pallas kernels, call(): pl.pallas_call(kernel, out_shape=shapes, in_specs=ins, out_specs=[VMEM] *...  16.6 us
    ppermute x4, waiting for transfers between devices, across(): return lax.ppermute(block, 'expert', route)  8.86 us
    ppermute x11, starting transfers between devices, beside(): return lax.ppermute(block, 'expert', route)  5.88 us
    ppermute x11, waiting for transfers between devices, beside(): return lax.ppermute(block, 'expert', route)  4.1 us
    ppermute x2, starting transfers between devices, to_next(): return lax.ppermute(block, ('section', 'expert'), route)  3.44 us
    ppermute x4, starting transfers between devices, across(): return lax.ppermute(block, 'expert', route)  2.17 us
    ppermute x1, waiting for transfers between devices, from_behind(): return lax.ppermute(block, axis, route)  1.32 us
    squeeze x1, local copies, waits for them, and re-layouts, body(): saved_up[0]  1.03 us
  transfers between devices with their start and end apart: 18, of which 11 were waited for; matrix products, arithmetic and copies ran while one was open for 2% of the time, Pallas kernels for 34%

profile of v7, /device:TPU:7, one launch (start us, length us, event | category | flops | bytes accessed | tf_op | source)
XLA Modules:
  0.0 44.9 jit_solution(23986429621523995)
XLA Ops:
  0.9 1.5 %first.1 = (bf16[32,3840]{1,0:T(8,128)(2,1)S(1)}, bf16[32,1920]{1,0:T(8,128)(2,1)S(1)}, bf16[32,1920]{1,0:T(8,128)(2,1)S(1)}) custom-call(s32[1,64]{1,0:T(1,128)} %bitcast.26, f32[1,64]{1,0:T(1,128)} %bitcast.28, bf16[64,3584]{1,0:T(8,128)(2,1)} %bitcast.24), custom_call_target="tpu_custom_call" | custom-call | tf_op jit(solution)/shard_map/first/pallas_call | solution.py:468
  2.6 1.4 %collective-permute-start.5 = (bf16[32,1920]{1,0:T(8,128)(2,1)S(1)}, bf16[32,1920]{1,0:T(8,128)(2,1)S(1)}, u32[]{:S(2)}, u32[]{:S(2)}) collective-permute-start(bf16[32,1920]{1,0:T(8,128)(2,1)S(1)} %get-tuple-element.71), channel_id=1, source_target_pairs={{0,2},{1,3},{2,0},{3,1},{4,6},{5,7},{6,4},{7,5},{8,10},{9,11},{10,... | collective-permute-start | bytes 368648 | tf_op jit(solution)/shard_map/ppermute | solution.py:58
  4.0 1.5 %collective-permute-start.6 = (bf16[32,3840]{1,0:T(8,128)(2,1)S(1)}, bf16[32,3840]{1,0:T(8,128)(2,1)S(1)}, u32[]{:S(2)}, u32[]{:S(2)}) collective-permute-start(bf16[32,3840]{1,0:T(8,128)(2,1)S(1)} %get-tuple-element.82.refs_0_.refs_6_), channel_id=1, source_target_pairs={{0,1},{1,0},{2,3},{3,2},{4,5},{5,4},{6,7},{7,6},{8,9},{9,8},{10,11... | collective-permute-start | bytes 737288 | tf_op jit(solution)/shard_map/ppermute | solution.py:67
  5.5 1.0 %copy_bitcast_fusion = (bf16[4,34,512]{2,1,0:T(8,128)(2,1)S(1)}, bf16[4,34,512]{2,1,0:T(8,128)(2,1)S(1)}) fusion(bf16[1,4,34,512]{3,1,2,0:T(4,128)(2,1)} %param.15, bf16[1,4,34,512]{3,1,2,0:T(4,128)(2,1)} %param.14), kind=kLoop, calls=%fused_computation | loop fusion | bytes 557056 | tf_op jit(solution)/shard_map/squeeze | solution.py:586
  6.5 0.5 %saved.1 = (f32[512,144]{1,0:T(8,128)S(1)}, f32[512,144]{1,0:T(8,128)S(1)}, f32[512,144]{1,0:T(8,128)S(1)}) custom-call(bf16[4,34,512]{2,1,0:T(8,128)(2,1)S(1)} %get-tuple-element.108.gate_ref, bf16[4,34,512]{2,1,0:T(8,128)(2,1)S(1)} %get-tuple-element.107.up_ref), custom_call_target="tpu_custom_call" | custom-call | tf_op jit(solution)/shard_map/saved/pallas_call | solution.py:468
  7.0 4.3 %load.1 = (bf16[3584,512]{1,0:T(8,128)(2,1)S(1)}, bf16[3584,512]{1,0:T(8,128)(2,1)S(1)}, bf16[512,3584]{1,0:T(8,128)(2,1)S(1)}, s32[1,64]{1,0:T(1,128)S(1)}, s32[1,64]{1,0:T(1,128)S(1)}, /*index=5*/f32[1,64]{1,0:T(1,128)S(1)}) custom-call(bf16[3584,512]{1,0:T(8,128)(2,1)} %bitcast.21, bf16[3584,512]{1,0:T(8,128)(2,1)} %bitcast.22, ...), custom_call_target="tpu_custom_call" | custom-call | tf_op jit(solution)/shard_map/load/pallas_call | solution.py:468
  11.4 0.5 %collective-permute-start.8 = (bf16[32,1920]{1,0:T(8,128)(2,1)S(1)}, bf16[32,1920]{1,0:T(8,128)(2,1)S(1)}, u32[]{:S(2)}, u32[]{:S(2)}) collective-permute-start(bf16[32,1920]{1,0:T(8,128)(2,1)S(1)} %collective-permute-done.5.refs_2_.refs_8_), channel_id=1, source_target_pairs={{0,1},{1,0},{2,3},{3,2},{4,5},{5,4},{6,7},{7,6},{8,9},{9,8},{10,11... | collective-permute-start | bytes 368648 | tf_op jit(solution)/shard_map/ppermute | solution.py:67
  11.9 1.3 %collective-permute-done.9 = bf16[1,64,3584]{2,1,0:T(8,128)(2,1)S(1)} collective-permute-done((bf16[1,64,3584]{2,1,0:T(8,128)(2,1)}, bf16[1,64,3584]{2,1,0:T(8,128)(2,1)S(1)}, u32[]{:S(2)}, u32[]{:S(2)}) %collective-permute-start.9) | collective-permute-done | bytes 458784 | tf_op jit(solution)/shard_map/ppermute | solution.py:35
  13.2 0.5 %pack.1 = (bf16[32,3840]{1,0:T(8,128)(2,1)S(1)}, bf16[32,3840]{1,0:T(8,128)(2,1)S(1)}) custom-call(s32[1,64]{1,0:T(1,128)S(1)} %get-tuple-element.78.route_ref.refs_3_, bf16[64,3584]{1,0:T(8,128)(2,1)S(1)} %bitcast.18), custom_call_target="tpu_custom_call" | custom-call | tf_op jit(solution)/shard_map/pack/pallas_call | solution.py:468
  14.0 2.0 %forward.1 = (bf16[32,3840]{1,0:T(8,128)(2,1)S(1)}, bf16[32,3840]{1,0:T(8,128)(2,1)S(1)}, bf16[16,3840]{1,0:T(8,128)(2,1)S(1)}, bf16[16,3840]{1,0:T(8,128)(2,1)S...) custom-call(bf16[32,3840]{1,0:T(8,128)(2,1)S(1)} %get-tuple-element.82.refs_0_.refs_6_, ...), custom_call_target="tpu_custom_call" | custom-call | tf_op jit(solution)/shard_map/forward/pallas_call | solution.py:468
  16.0 1.9 %collective-permute-start.10 = (bf16[16,3840]{1,0:T(8,128)(2,1)S(1)}, bf16[16,3840]{1,0:T(8,128)(2,1)S(1)}, u32[]{:S(2)}, u32[]{:S(2)}) collective-permute-start(bf16[16,3840]{1,0:T(8,128)(2,1)S(1)} %get-tuple-element.93), channel_id=1, source_target_pairs={{0,1},{1,0},{2,3},{3,2},{4,5},{5,4},{6,7},{7,6},{8,9},{9,8},{10,11... | collective-permute-start | bytes 368648 | tf_op jit(solution)/shard_map/ppermute | solution.py:67
  18.0 0.4 collective-permute-start.12
  20.1 0.4 collective-permute-start.14
  20.5 3.0 %collective-permute-start.15 = (bf16[32,3968]{1,0:T(8,128)(2,1)S(1)}, bf16[32,3968]{1,0:T(8,128)(2,1)S(1)}, u32[]{:S(2)}, u32[]{:S(2)}) collective-permute-start(bf16[32,3968]{1,0:T(8,128)(2,1)S(1)} %get-tuple-element.98), channel_id=1, source_target_pairs={{0,6},{1,7},{2,4},{3,5},{4,10},{5,11},{6,8},{7,9},{8,14},{9,15},{1... | collective-permute-start | bytes 761864 | tf_op jit(solution)/shard_map/ppermute | solution.py:49
  23.5 9.3 %conditional.1 = ((bf16[32,3968]{1,0:T(8,128)(2,1)S(1)}, bf16[32,3968]{1,0:T(8,128)(2,1)S(1)})) conditional(s32[]{:T(128)} %bitcast.12, () %tuple.23, (bf16[32,3840]{1,0:T(8,128)(2,1)S(1)}, bf16[32,3840]{1,0:T(8,128)(2,1)S(1)}, f32[512,144]{1,0:T(8,128)S(1)}, f32[512,144]{1,0:T(8,128)S(1)}, f32[512,144]{1,0:T(8,128)S(1)}, ...), branch_computations={%region_0.0_spmd, %region_1.0_spmd} | conditional | bytes 3997864 | solution.py:528
  23.5 0.7 %collective-permute-start = (bf16[32,3840]{1,0:T(8,128)(2,1)S(1)}, bf16[32,3840]{1,0:T(8,128)(2,1)S(1)}, u32[]{:S(2)}, u32[]{:S(2)}) collective-permute-start(bf16[32,3840]{1,0:T(8,128)(2,1)S(1)} %get-tuple-element.16.refs_0_), channel_id=1, source_target_pairs={{0,1},{1,0},{2,3},{3,2},{4,5},{5,4},{6,7},{7,6},{8,9},{9,8},{10,11... | collective-permute-start | bytes 737288 | tf_op jit(solution)/shard_map/cond/branch_1_fun/ppermute | solution.py:67
  24.3 1.1 %collective-permute-done.refs_2_ = bf16[32,3840]{1,0:T(8,128)(2,1)S(1)} collective-permute-done((bf16[32,3840]{1,0:T(8,128)(2,1)S(1)}, bf16[32,3840]{1,0:T(8,128)(2,1)S(1)}, u32[]{:S(2)}, u32[]{:S(2)}) %collective-permute-start) | collective-permute-done | bytes 245792 | tf_op jit(solution)/shard_map/cond/branch_1_fun/ppermute | solution.py:67
  25.8 4.9 %backward.1 = (bf16[32,3968]{1,0:T(8,128)(2,1)S(1)}, bf16[32,3968]{1,0:T(8,128)(2,1)S(1)}, bf16[32,3968]{1,0:T(8,128)(2,1)S(1)}, bf16[32,3968]{1,0:T(8,128)(2,1)S(1)}) custom-call(bf16[32,3840]{1,0:T(8,128)(2,1)S(1)} %get-tuple-element.16.refs_0_, bf16[32,3840]{1,0:T(8,128)(2,1)S(1)} %get-tuple-element.17.refs_1_, ...), custom_call_target="tpu_custom_call" | custom-call | tf_op jit(solution)/shard_map/cond/branch_1_fun/backward/pallas_call | solution.py:468
  30.7 0.4 collective-permute-start.2
  31.2 1.0 %collective-permute-done.2.refs_2_ = bf16[32,3968]{1,0:T(8,128)(2,1)S(1)} collective-permute-done((bf16[32,3968]{1,0:T(8,128)(2,1)S(1)}, bf16[32,3968]{1,0:T(8,128)(2,1)S(1)}, u32[]{:S(2)}, u32[]{:S(2)}) %collective-permute-start.2) | collective-permute-done | bytes 253984 | tf_op jit(solution)/shard_map/cond/branch_1_fun/ppermute | solution.py:67
  33.2 0.4 collective-permute-done.14.refs_0_
  33.6 1.2 %forward_end.1 = bf16[64,3584]{1,0:T(8,128)(2,1)} custom-call(bf16[32,3968]{1,0:T(8,128)(2,1)S(1)} %collective-permute-done.14.refs_0_, bf16[32,3968]{1,0:T(8,128)(2,1)S(1)} %collective-permute-done.15.refs_1_), custom_call_target="tpu_custom_call" | custom-call | tf_op jit(solution)/shard_map/forward_end/pallas_call | solution.py:468
  34.8 8.9 %collective-permute-done.17.refs_1_ = bf16[32,3968]{1,0:T(8,128)(2,1)S(1)} collective-permute-done((bf16[32,3968]{1,0:T(8,128)(2,1)S(1)}, bf16[32,3968]{1,0:T(8,128)(2,1)S(1)}, u32[]{:S(2)}, u32[]{:S(2)}) %collective-permute-start.17) | collective-permute-done | bytes 253984 | tf_op jit(solution)/shard_map/ppermute | solution.py:58
  43.7 1.2 %backward_end.1 = (bf16[64,3584]{1,0:T(8,128)(2,1)}, f32[1,64]{1,0:T(1,128)}) custom-call(bf16[32,3968]{1,0:T(8,128)(2,1)S(1)} %get-tuple-element.102.refs_0_, bf16[32,3968]{1,0:T(8,128)(2,1)S(1)} %collective-permute-done.17.refs_1_, bf16[64,3584]{1,0:T(8,128)(2,1)S(1)} %bitcast.19, s32[1,64]{1,0:T(1,128)S(1)} %get-tuple-element.78.route_ref.refs_3_, ...), custom_call_target="tpu_custom_call" | custom-call | tf_op jit(solution)/shard_map/backward_end/pallas_call | solution.py:468
  (24 shorter events, 4.0 us)
Async XLA Ops:
  0.6 12.5 %collective-permute-start.9 = (bf16[1,64,3584]{2,1,0:T(8,128)(2,1)}, bf16[1,64,3584]{2,1,0:T(8,128)(2,1)S(1)}, u32[]{:S(2)}, u32[]{:S(2)}) collective-permute-start(bf16[1,64,3584]{2,1,0:T(8,128)(2,1)} %param.16), channel_id=1, source_target_pairs={{4,0},{8,4},{12,8},{16,12},{20,16},{24,20},{28,24},{0,28},{5,1},{9... | collective-permute-start | bytes 1376264 | tf_op jit(solution)/shard_map/ppermute | solution.py:35
  2.5 8.8 %collective-permute-start.4 = (bf16[32,1920]{1,0:T(8,128)(2,1)S(1)}, bf16[32,1920]{1,0:T(8,128)(2,1)S(1)}, u32[]{:S(2)}, u32[]{:S(2)}) collective-permute-start(bf16[32,1920]{1,0:T(8,128)(2,1)S(1)} %get-tuple-element.70), channel_id=1, source_target_pairs={{0,2},{1,3},{2,0},{3,1},{4,6},{5,7},{6,4},{7,5},{8,10},{9,11},{10,... | collective-permute-start | bytes 368648 | tf_op jit(solution)/shard_map/ppermute | solution.py:58
  2.6 8.7 %collective-permute-start.5 = (bf16[32,1920]{1,0:T(8,128)(2,1)S(1)}, bf16[32,1920]{1,0:T(8,128)(2,1)S(1)}, u32[]{:S(2)}, u32[]{:S(2)}) collective-permute-start(bf16[32,1920]{1,0:T(8,128)(2,1)S(1)} %get-tuple-element.71), channel_id=1, source_target_pairs={{0,2},{1,3},{2,0},{3,1},{4,6},{5,7},{6,4},{7,5},{8,10},{9,11},{10,... | collective-permute-start | bytes 368648 | tf_op jit(solution)/shard_map/ppermute | solution.py:58
  4.0 10.0 %collective-permute-start.6 = (bf16[32,3840]{1,0:T(8,128)(2,1)S(1)}, bf16[32,3840]{1,0:T(8,128)(2,1)S(1)}, u32[]{:S(2)}, u32[]{:S(2)}) collective-permute-start(bf16[32,3840]{1,0:T(8,128)(2,1)S(1)} %get-tuple-element.82.refs_0_.refs_6_), channel_id=1, source_target_pairs={{0,1},{1,0},{2,3},{3,2},{4,5},{5,4},{6,7},{7,6},{8,9},{9,8},{10,11... | collective-permute-start | bytes 737288 | tf_op jit(solution)/shard_map/ppermute | solution.py:67
  11.3 2.7 %collective-permute-start.7 = (bf16[32,1920]{1,0:T(8,128)(2,1)S(1)}, bf16[32,1920]{1,0:T(8,128)(2,1)S(1)}, u32[]{:S(2)}, u32[]{:S(2)}) collective-permute-start(bf16[32,1920]{1,0:T(8,128)(2,1)S(1)} %collective-permute-done.4.refs_1_.refs_7_), channel_id=1, source_target_pairs={{0,1},{1,0},{2,3},{3,2},{4,5},{5,4},{6,7},{7,6},{8,9},{9,8},{10,11... | collective-permute-start | bytes 368648 | tf_op jit(solution)/shard_map/ppermute | solution.py:67
  11.4 2.6 %collective-permute-start.8 = (bf16[32,1920]{1,0:T(8,128)(2,1)S(1)}, bf16[32,1920]{1,0:T(8,128)(2,1)S(1)}, u32[]{:S(2)}, u32[]{:S(2)}) collective-permute-start(bf16[32,1920]{1,0:T(8,128)(2,1)S(1)} %collective-permute-done.5.refs_2_.refs_8_), channel_id=1, source_target_pairs={{0,1},{1,0},{2,3},{3,2},{4,5},{5,4},{6,7},{7,6},{8,9},{9,8},{10,11... | collective-permute-start | bytes 368648 | tf_op jit(solution)/shard_map/ppermute | solution.py:67
  13.6 9.9 %collective-permute-start.16 = (bf16[32,3840]{1,0:T(8,128)(2,1)S(1)}, bf16[32,3840]{1,0:T(8,128)(2,1)S(1)}, u32[]{:S(2)}, u32[]{:S(2)}) collective-permute-start(bf16[32,3840]{1,0:T(8,128)(2,1)S(1)} %get-tuple-element.81), channel_id=1, source_target_pairs={{0,2},{1,3},{2,0},{3,1},{4,6},{5,7},{6,4},{7,5},{8,10},{9,11},{10,... | collective-permute-start | bytes 737288 | tf_op jit(solution)/shard_map/ppermute | solution.py:58
  16.0 2.9 %collective-permute-start.10 = (bf16[16,3840]{1,0:T(8,128)(2,1)S(1)}, bf16[16,3840]{1,0:T(8,128)(2,1)S(1)}, u32[]{:S(2)}, u32[]{:S(2)}) collective-permute-start(bf16[16,3840]{1,0:T(8,128)(2,1)S(1)} %get-tuple-element.93), channel_id=1, source_target_pairs={{0,1},{1,0},{2,3},{3,2},{4,5},{5,4},{6,7},{7,6},{8,9},{9,8},{10,11... | collective-permute-start | bytes 368648 | tf_op jit(solution)/shard_map/ppermute | solution.py:67
  17.9 1.3 %collective-permute-start.11 = (bf16[16,3840]{1,0:T(8,128)(2,1)S(1)}, bf16[16,3840]{1,0:T(8,128)(2,1)S(1)}, u32[]{:S(2)}, u32[]{:S(2)}) collective-permute-start(bf16[16,3840]{1,0:T(8,128)(2,1)S(1)} %get-tuple-element.94), channel_id=1, source_target_pairs={{0,1},{1,0},{2,3},{3,2},{4,5},{5,4},{6,7},{7,6},{8,9},{9,8},{10,11... | collective-permute-start | bytes 368648 | tf_op jit(solution)/shard_map/ppermute | solution.py:67
  18.0 1.4 %collective-permute-start.12 = (bf16[16,3840]{1,0:T(8,128)(2,1)S(1)}, bf16[16,3840]{1,0:T(8,128)(2,1)S(1)}, u32[]{:S(2)}, u32[]{:S(2)}) collective-permute-start(bf16[16,3840]{1,0:T(8,128)(2,1)S(1)} %get-tuple-element.95), channel_id=1, source_target_pairs={{0,1},{1,0},{2,3},{3,2},{4,5},{5,4},{6,7},{7,6},{8,9},{9,8},{10,11... | collective-permute-start | bytes 368648 | tf_op jit(solution)/shard_map/ppermute | solution.py:67
  18.4 1.3 %collective-permute-start.13 = (bf16[16,3840]{1,0:T(8,128)(2,1)S(1)}, bf16[16,3840]{1,0:T(8,128)(2,1)S(1)}, u32[]{:S(2)}, u32[]{:S(2)}) collective-permute-start(bf16[16,3840]{1,0:T(8,128)(2,1)S(1)} %get-tuple-element.96), channel_id=1, source_target_pairs={{0,1},{1,0},{2,3},{3,2},{4,5},{5,4},{6,7},{7,6},{8,9},{9,8},{10,11... | collective-permute-start | bytes 368648 | tf_op jit(solution)/shard_map/ppermute | solution.py:67
  20.1 13.5 %collective-permute-start.14 = (bf16[32,3968]{1,0:T(8,128)(2,1)S(1)}, bf16[32,3968]{1,0:T(8,128)(2,1)S(1)}, u32[]{:S(2)}, u32[]{:S(2)}) collective-permute-start(bf16[32,3968]{1,0:T(8,128)(2,1)S(1)} %get-tuple-element.97), channel_id=1, source_target_pairs={{0,4},{1,5},{2,6},{3,7},{4,8},{5,9},{6,10},{7,11},{8,12},{9,13},{1... | collective-permute-start | bytes 761864 | tf_op jit(solution)/shard_map/ppermute | solution.py:49
  20.5 13.2 %collective-permute-start.15 = (bf16[32,3968]{1,0:T(8,128)(2,1)S(1)}, bf16[32,3968]{1,0:T(8,128)(2,1)S(1)}, u32[]{:S(2)}, u32[]{:S(2)}) collective-permute-start(bf16[32,3968]{1,0:T(8,128)(2,1)S(1)} %get-tuple-element.98), channel_id=1, source_target_pairs={{0,6},{1,7},{2,4},{3,5},{4,10},{5,11},{6,8},{7,9},{8,14},{9,15},{1... | collective-permute-start | bytes 761864 | tf_op jit(solution)/shard_map/ppermute | solution.py:49
  23.5 1.9 %collective-permute-start = (bf16[32,3840]{1,0:T(8,128)(2,1)S(1)}, bf16[32,3840]{1,0:T(8,128)(2,1)S(1)}, u32[]{:S(2)}, u32[]{:S(2)}) collective-permute-start(bf16[32,3840]{1,0:T(8,128)(2,1)S(1)} %get-tuple-element.16.refs_0_), channel_id=1, source_target_pairs={{0,1},{1,0},{2,3},{3,2},{4,5},{5,4},{6,7},{7,6},{8,9},{9,8},{10,11... | collective-permute-start | bytes 737288 | tf_op jit(solution)/shard_map/cond/branch_1_fun/ppermute | solution.py:67
  24.3 1.5 %collective-permute-start.1 = (bf16[32,3840]{1,0:T(8,128)(2,1)S(1)}, bf16[32,3840]{1,0:T(8,128)(2,1)S(1)}, u32[]{:S(2)}, u32[]{:S(2)}) collective-permute-start(bf16[32,3840]{1,0:T(8,128)(2,1)S(1)} %get-tuple-element.17.refs_1_), channel_id=1, source_target_pairs={{0,1},{1,0},{2,3},{3,2},{4,5},{5,4},{6,7},{7,6},{8,9},{9,8},{10,11... | collective-permute-start | bytes 737288 | tf_op jit(solution)/shard_map/cond/branch_1_fun/ppermute | solution.py:67
  30.7 1.6 %collective-permute-start.2 = (bf16[32,3968]{1,0:T(8,128)(2,1)S(1)}, bf16[32,3968]{1,0:T(8,128)(2,1)S(1)}, u32[]{:S(2)}, u32[]{:S(2)}) collective-permute-start(bf16[32,3968]{1,0:T(8,128)(2,1)S(1)} %get-tuple-element.26), channel_id=1, source_target_pairs={{0,1},{1,0},{2,3},{3,2},{4,5},{5,4},{6,7},{7,6},{8,9},{9,8},{10,11... | collective-permute-start | bytes 761864 | tf_op jit(solution)/shard_map/cond/branch_1_fun/ppermute | solution.py:67
  31.1 1.5 %collective-permute-start.3 = (bf16[32,3968]{1,0:T(8,128)(2,1)S(1)}, bf16[32,3968]{1,0:T(8,128)(2,1)S(1)}, u32[]{:S(2)}, u32[]{:S(2)}) collective-permute-start(bf16[32,3968]{1,0:T(8,128)(2,1)S(1)} %get-tuple-element.27), channel_id=1, source_target_pairs={{0,1},{1,0},{2,3},{3,2},{4,5},{5,4},{6,7},{7,6},{8,9},{9,8},{10,11... | collective-permute-start | bytes 761864 | tf_op jit(solution)/shard_map/cond/branch_1_fun/ppermute | solution.py:67
  32.9 10.8 %collective-permute-start.17 = (bf16[32,3968]{1,0:T(8,128)(2,1)S(1)}, bf16[32,3968]{1,0:T(8,128)(2,1)S(1)}, u32[]{:S(2)}, u32[]{:S(2)}) collective-permute-start(bf16[32,3968]{1,0:T(8,128)(2,1)S(1)} %get-tuple-element.101), channel_id=1, source_target_pairs={{0,2},{1,3},{2,0},{3,1},{4,6},{5,7},{6,4},{7,5},{8,10},{9,11},{10,... | collective-permute-start | bytes 761864 | tf_op jit(solution)/shard_map/ppermute | solution.py:58

commit v8 on v6

--- a/solution.py
+++ b/solution.py
@@ -120,21 +120,7 @@
     col, rank = slot_columns(route_row, s)
     hit = (col == expert) & (rank == iota((s.tok, LANES), 1))
     row = jnp.sum(jnp.where(hit, as_column(score_row), 0.0), axis=0, keepdims=True)
-    for p, piece in enumerate(split_three(row)):
-        at = s.folds + 1 + p
-        tail_ref[at : at + 1, :LANES] = piece
-
-
-def get_gates(tail, s):
-    at = s.folds + 1
-    row = 2.5 * (tail[at : at + 1] + tail[at + 1 : at + 2] + tail[at + 2 : at + 3])
-    lane = iota((s.main, LANES), 1)
-    main = jnp.sum(jnp.where(lane == iota((s.main, LANES), 0), row, 0.0), axis=1, keepdims=True)
-    extra = [
-        jnp.sum(jnp.where(lane[:1] == float(s.main + j), row, 0.0), axis=1, keepdims=True)
-        for j in range(s.extra)
-    ]
-    return main, extra
+    put_row(row, tail_ref, s)
 
 
 def add_gated(out_ref, base, main, extra, total, s):
@@ -250,9 +236,13 @@
     extra_ref[:, at] = value[s.blocks * s.main :]
 
 
-def scatter_tails(outs, extra_ref, tail_ref, s):
+def scatter_tails(outs, extra_ref, tail_ref, s, inner=None):
     for i in range(s.blocks):
         fold(extra_ref, i * s.extra, tail_ref, s)
+        if inner is not None:
+            first = s.blocks * s.main + i * s.extra
+            extra = [inner[first + j : first + j + 1] for j in range(s.extra)]
+            put_inner(inner[i * s.main : (i + 1) * s.main], extra, tail_ref, s)
         put(outs, i, slice(s.depth, s.width), tail_ref[...].astype(BF16), s)
 
 
@@ -313,27 +303,30 @@
     return high, mid, (rest - mid).astype(BF16).astype(F32)
 
 
-def put_inner(main, extra, s):
+def put_inner(main, extra, tail_ref, s):
     lane = iota((s.main, LANES), 1)
-    row = iota((s.main, LANES), 0)
-    out = jnp.zeros((s.main, LANES), F32)
-    for p, piece in enumerate(split_three(main)):
-        out = jnp.where(lane == float(p), piece, out)
+    row = jnp.sum(jnp.where(lane == iota((s.main, LANES), 0), main, 0.0), axis=0, keepdims=True)
     for j in range(s.extra):
-        for p, piece in enumerate(split_three(extra[j])):
-            out = jnp.where((lane == float(3 + p)) & (row == float(j)), piece, out)
-    return out.astype(BF16)
-
-
-def get_inner(block, s):
+        row = jnp.where(lane[:1] == float(s.main + j), extra[j], row)
+    put_row(row, tail_ref, s)
+
+
+def put_row(row, tail_ref, s):
+    for p, piece in enumerate(split_three(row)):
+        at = s.folds + 1 + p
+        tail_ref[at : at + 1, :LANES] = piece
+
+
+def get_row(tail, s):
+    at = s.folds + 1
+    return tail[at : at + 1] + tail[at + 1 : at + 2] + tail[at + 2 : at + 3]
+
+
+def get_slots(row, s):
     lane = iota((s.main, LANES), 1)
-    row = iota((s.main, LANES), 0)
-    main = jnp.sum(jnp.where(lane < 3.0, block, 0.0), axis=1, keepdims=True)
-    second = jnp.sum(
-        jnp.where((lane >= 3.0) & (lane < 6.0), block, 0.0), axis=1, keepdims=True
-    )
+    main = jnp.sum(jnp.where(lane == iota((s.main, LANES), 0), row, 0.0), axis=1, keepdims=True)
     extra = [
-        jnp.sum(jnp.where(row[:, :1] == float(j), second, 0.0), axis=0, keepdims=True)
+        jnp.sum(jnp.where(lane[:1] == float(s.main + j), row, 0.0), axis=1, keepdims=True)
         for j in range(s.extra)
     ]
     return main, extra
@@ -355,20 +348,13 @@
     dgp = (a * c1[...]).astype(BF16)
     dup = (a * c2[...]).astype(BF16)
     inner = jnp.sum(a * hb[...], axis=1, keepdims=True)
-    for i in range(s.blocks):
-        first = s.blocks * s.main + i * s.extra
-        outs[i][:, s.width :] = put_inner(
-            inner[i * s.main : (i + 1) * s.main],
-            [inner[first + j : first + j + 1] for j in range(s.extra)],
-            s,
-        )
     tail_ref[...] = jnp.zeros_like(tail_ref)
     for c in range(0, s.depth, chunk):
         part = lax.dot_general(
             dgp, wg[c : c + chunk, :], NT, preferred_element_type=F32
         ) + lax.dot_general(dup, wu[c : c + chunk, :], NT, preferred_element_type=F32)
         scatter_chunk(part, outs, extra_ref, slice(c, c + chunk), s)
-    scatter_tails(outs, extra_ref, tail_ref, s)
+    scatter_tails(outs, extra_ref, tail_ref, s, inner)
 
 
 def total_of(parts, d, s):
@@ -387,7 +373,7 @@
     route_ref, outs = refs[-1 - s.count], refs[-s.count :]
     for d in range(s.count - 1, -1, -1):
         tail = read(bases[d], s.depth, s.depth + LANES).astype(F32)
-        main, extra = get_gates(tail, s)
+        main, extra = get_slots(2.5 * get_row(tail, s), s)
         add_gated(outs[d], bases[d], main, extra, total_of(parts, d, s), s)
         spare = outs[d].shape[1] - s.width
         if spare:
@@ -399,7 +385,7 @@
 def tokens_of(packs, route_row, rows_ref, extra_ref, tail_ref, s):
     extra_ref[...] = jnp.zeros_like(extra_ref)
     for d, pack in enumerate(packs):
-        rows_ref[d * s.main : (d + 1) * s.main, :] = pack[:, : s.depth]
+        rows_ref[d * s.main : (d + 1) * s.main, :] = pack[:, : s.depth].astype(BF16)
         tail_ref[...] = pack[:, s.depth : s.width].astype(F32)
         unfold(tail_ref, extra_ref, d * s.extra, s)
     rows_ref[s.count * s.main :, :] = extra_ref[...].astype(BF16)
@@ -419,25 +405,35 @@
 
 def forward_end_kernel(s, *refs):
     packs = refs[: s.count]
-    out_ref, rows_ref, extra_ref, tail_ref, row_ref = refs[s.count :]
+    out_ref, rows_ref, extra_ref, tail_ref, row_ref = refs[s.count + 1 :]
     row_ref[...] = packs[0][:, s.depth : s.depth + LANES].astype(F32)
     route_row = row_ref[s.folds : s.folds + 1, : s.tok]
     out_ref[...] = tokens_of(packs, route_row, rows_ref, extra_ref, tail_ref, s).astype(BF16)
 
 
 def backward_sum_kernel(s, *refs):
-    parts, outs = refs[: -s.count], refs[-s.count :]
-    for d in range(s.count - 1, -1, -1):
-        total = total_of(parts, d, s)
-        outs[d][:, : s.width] = total[:, : s.width].astype(BF16)
-        main, extra = get_inner(total[:, s.width :], s)
-        outs[d][:, s.width :] = put_inner(main, extra, s)
+    n = s.count - 1
+    parts, outs, tail_ref = refs[: n * s.slices], refs[-1 - n : -1], refs[-1]
+    for d in range(n):
+        total = parts[d][...].astype(F32)
+        for part in parts[n + d :: n]:
+            total = total + part[...].astype(F32)
+        outs[d][:, : s.depth] = total[:, : s.depth].astype(BF16)
+        tail_ref[...] = total[:, s.depth :]
+        put_row(get_row(total[:, s.depth : s.depth + LANES], s), tail_ref, s)
+        outs[d][:, s.depth :] = tail_ref[...].astype(BF16)
 
 
 def backward_end_kernel(s, *refs):
-    packs = refs[: s.count]
-    dy_ref, route_ref, score_ref, out_ref, grad_ref = refs[s.count : s.count + 5]
-    rows_ref, extra_ref, tail_ref = refs[s.count + 5 :]
+    own, packs = refs[: s.slices], refs[s.slices : s.slices + s.count - 1]
+    n = s.slices + s.count - 1
+    dy_ref, route_ref, score_ref, out_ref, grad_ref, token_ref = refs[n : n + 6]
+    rows_ref, extra_ref, tail_ref = refs[n + 6 :]
+    token_ref[...] = jnp.zeros_like(token_ref)
+    total = own[0][...].astype(F32)
+    for part in own[1:]:
+        total = total + part[...].astype(F32)
+    packs = [total, *packs]
     route_row = route_ref[...].astype(F32)
     rows = tokens_of(packs, route_row, rows_ref, extra_ref, tail_ref, s)
     gate = as_column(2.5 * score_ref[...])
@@ -446,7 +442,8 @@
     dgate = jnp.zeros((1, s.tok), F32)
     for d in range(s.count):
         hit = route_row == expert_at(s, d)
-        main, extra = get_inner(packs[d][:, s.width :].astype(F32), s)
+        tail = packs[d][:, s.depth : s.depth + LANES].astype(F32)
+        main, extra = get_slots(get_row(tail, s), s)
         dgate += jnp.sum(
             jnp.where(hit & (rank == iota((s.main, s.tok), 0)), main, 0.0), axis=0, keepdims=True
         )
@@ -588,24 +585,27 @@
     wide = s.width + LANES
 
     def backward(got, *rest):
+        rows = spread(s, got)
         parts = call(
             functools.partial(backward_kernel, s),
             "backward",
-            [((s.main, wide), BF16)] * s.blocks,
+            packed * s.slices,
             row_scratch(s),
             [VMEM] * (s.blocks + 6),
-            *spread(s, got),
+            *rows,
             *rest,
         )
+        others = [p for i, p in enumerate(parts) if i % s.count]
+        others = [beside(p, -(i // (s.count - 1)), s) if i >= s.count - 1 else p for i, p in enumerate(others)]
         sums = call(
             functools.partial(backward_sum_kernel, s),
             "backward_sum",
-            [((s.main, wide), BF16)] * s.count,
-            [],
-            [VMEM] * s.blocks,
-            *gather_parts(s, parts),
+            packed[1:],
+            [pltpu.VMEM((s.main, LANES * s.extra), F32)],
+            [VMEM] * len(others),
+            *others,
         )
-        return tuple(sums)
+        return tuple(parts[:: s.count]), tuple(sums)
 
     got = cross(s, sent_a, PIECES)
     got[1:] = hold(got[1:], route_a, factors)
@@ -644,27 +644,30 @@
     )
     moved = [to_next(y, -d, s) for d, y in enumerate(sums_a)]
     got_b[1:] = hold(got_b[1:], sums_a)
-    sums_b = step(route_b, backward, got_b, *factors, wg, wu, wd)
-    back_b = [sums_b[0]] + [across(sums_b[d], -d, s) for d in range(1, s.count)]
+    own_b, sums_b = step(route_b, backward, got_b, *factors, wg, wu, wd)
+    back_b = [across(y, -1 - d, s) for d, y in enumerate(sums_b)]
+    own_b = [beside(p, -k, s) if k else p for k, p in enumerate(own_b)]
+    input_grad, score_grad, token = call(
+        functools.partial(backward_end_kernel, s),
+        "backward_end",
+        [((tok, depth), BF16), ((1, tok), F32), ((8, LANES), F32)],
+        end_scratch(s),
+        [VMEM] * (s.blocks // s.count + s.count - 1 + 3),
+        *own_b,
+        *back_b,
+        upstream,
+        route_b,
+        score_b,
+    )
     next_input = call(
         functools.partial(forward_end_kernel, s),
         "forward_end",
         [((tok, depth), BF16)],
         end_scratch(s) + [pltpu.VMEM((s.main, LANES), F32)],
-        [VMEM] * s.count,
+        [VMEM] * (s.count + 1),
         *moved,
+        token,
     )[0]
-    input_grad, score_grad = call(
-        functools.partial(backward_end_kernel, s),
-        "backward_end",
-        [((tok, depth), BF16), ((1, tok), F32)],
-        end_scratch(s),
-        [VMEM] * (s.count + 3),
-        *hold(back_b, next_input),
-        upstream,
-        route_b,
-        score_b,
-    )
     return next_input[None], input_grad[None], score_grad.reshape(1, tok, 1)
 
 

time: 45 us -> 46.1 us (1.024)
  the two profiles are of different devices: /device:TPU:7 before, /device:TPU:5 now
where the time goes in v8:
time: 46.1 us; the launch traced here: 45.9 us
  waiting for transfers between devices  16.3 us (35%)
  Pallas kernels  15.2 us (33%)
  starting transfers between devices  12.6 us (27%)
  local copies, waits for them, and re-layouts  1.03 us (2%)
  between operations  0.75 us (2%)
    pallas_call x10, Pallas kernels, call(): pl.pallas_call(kernel, out_shape=shapes, in_specs=ins, out_specs=[VMEM] *...  15.2 us
    ppermute x4, waiting for transfers between devices, across(): return lax.ppermute(block, 'expert', route)  10.4 us
    ppermute x11, starting transfers between devices, beside(): return lax.ppermute(block, 'expert', route)  5.97 us
    ppermute x4, starting transfers between devices, across(): return lax.ppermute(block, 'expert', route)  4.03 us
    ppermute x11, waiting for transfers between devices, beside(): return lax.ppermute(block, 'expert', route)  3.86 us
    ppermute x2, starting transfers between devices, to_next(): return lax.ppermute(block, ('section', 'expert'), route)  2.52 us
    ppermute x1, waiting for transfers between devices, from_behind(): return lax.ppermute(block, axis, route)  1.99 us
    squeeze x1, local copies, waits for them, and re-layouts, body(): saved_up[0]  1.03 us
  transfers between devices with their start and end apart: 18, of which 9 were waited for; matrix products, arithmetic and copies ran while one was open for 2% of the time, Pallas kernels for 31%

profile of v8, /device:TPU:5, one launch (start us, length us, event | category | flops | bytes accessed | tf_op | source)
XLA Modules:
  0.0 45.9 jit_solution(5492218765448197680)
XLA Ops:
  0.7 1.5 %first.1 = (bf16[32,3840]{1,0:T(8,128)(2,1)S(1)}, bf16[32,1920]{1,0:T(8,128)(2,1)S(1)}, bf16[32,1920]{1,0:T(8,128)(2,1)S(1)}) custom-call(s32[1,64]{1,0:T(1,128)} %bitcast.26, f32[1,64]{1,0:T(1,128)} %bitcast.28, bf16[64,3584]{1,0:T(8,128)(2,1)} %bitcast.24), custom_call_target="tpu_custom_call" | custom-call | tf_op jit(solution)/shard_map/first/pallas_call | solution.py:465
  2.2 1.5 %collective-permute-start.3 = (bf16[32,1920]{1,0:T(8,128)(2,1)S(1)}, bf16[32,1920]{1,0:T(8,128)(2,1)S(1)}, u32[]{:S(2)}, u32[]{:S(2)}) collective-permute-start(bf16[32,1920]{1,0:T(8,128)(2,1)S(1)} %get-tuple-element.70), channel_id=1, source_target_pairs={{0,2},{1,3},{2,0},{3,1},{4,6},{5,7},{6,4},{7,5},{8,10},{9,11},{10,... | collective-permute-start | bytes 368648 | tf_op jit(solution)/shard_map/ppermute | solution.py:58
  3.8 1.2 %collective-permute-start.5 = (bf16[32,3840]{1,0:T(8,128)(2,1)S(1)}, bf16[32,3840]{1,0:T(8,128)(2,1)S(1)}, u32[]{:S(2)}, u32[]{:S(2)}) collective-permute-start(bf16[32,3840]{1,0:T(8,128)(2,1)S(1)} %get-tuple-element.82.refs_0_.refs_6_), channel_id=1, source_target_pairs={{0,1},{1,0},{2,3},{3,2},{4,5},{5,4},{6,7},{7,6},{8,9},{9,8},{10,11... | collective-permute-start | bytes 737288 | tf_op jit(solution)/shard_map/ppermute | solution.py:67
  5.0 1.0 %copy_bitcast_fusion = (bf16[4,34,512]{2,1,0:T(8,128)(2,1)S(1)}, bf16[4,34,512]{2,1,0:T(8,128)(2,1)S(1)}) fusion(bf16[1,4,34,512]{3,1,2,0:T(4,128)(2,1)} %param.15, bf16[1,4,34,512]{3,1,2,0:T(4,128)(2,1)} %param.14), kind=kLoop, calls=%fused_computation | loop fusion | bytes 557056 | tf_op jit(solution)/shard_map/squeeze | solution.py:583
  6.3 4.3 %load.1 = (bf16[3584,512]{1,0:T(8,128)(2,1)S(1)}, bf16[3584,512]{1,0:T(8,128)(2,1)S(1)}, bf16[512,3584]{1,0:T(8,128)(2,1)S(1)}, s32[1,64]{1,0:T(1,128)S(1)}, s32[1,64]{1,0:T(1,128)S(1)}, /*index=5*/f32[1,64]{1,0:T(1,128)S(1)}) custom-call(bf16[3584,512]{1,0:T(8,128)(2,1)} %bitcast.21, bf16[3584,512]{1,0:T(8,128)(2,1)} %bitcast.22, ...), custom_call_target="tpu_custom_call" | custom-call | tf_op jit(solution)/shard_map/load/pallas_call | solution.py:465
  10.7 0.5 %collective-permute-start.7 = (bf16[32,1920]{1,0:T(8,128)(2,1)S(1)}, bf16[32,1920]{1,0:T(8,128)(2,1)S(1)}, u32[]{:S(2)}, u32[]{:S(2)}) collective-permute-start(bf16[32,1920]{1,0:T(8,128)(2,1)S(1)} %collective-permute-done.4.refs_2_.refs_8_), channel_id=1, source_target_pairs={{0,1},{1,0},{2,3},{3,2},{4,5},{5,4},{6,7},{7,6},{8,9},{9,8},{10,11... | collective-permute-start | bytes 368648 | tf_op jit(solution)/shard_map/ppermute | solution.py:67
  11.2 2.0 %collective-permute-done.8 = bf16[1,64,3584]{2,1,0:T(8,128)(2,1)S(1)} collective-permute-done((bf16[1,64,3584]{2,1,0:T(8,128)(2,1)}, bf16[1,64,3584]{2,1,0:T(8,128)(2,1)S(1)}, u32[]{:S(2)}, u32[]{:S(2)}) %collective-permute-start.8) | collective-permute-done | bytes 458784 | tf_op jit(solution)/shard_map/ppermute | solution.py:35
  13.2 0.4 pack.1
  13.6 1.3 %collective-permute-start.15 = (bf16[32,3840]{1,0:T(8,128)(2,1)S(1)}, bf16[32,3840]{1,0:T(8,128)(2,1)S(1)}, u32[]{:S(2)}, u32[]{:S(2)}) collective-permute-start(bf16[32,3840]{1,0:T(8,128)(2,1)S(1)} %get-tuple-element.81), channel_id=1, source_target_pairs={{0,2},{1,3},{2,0},{3,1},{4,6},{5,7},{6,4},{7,5},{8,10},{9,11},{10,... | collective-permute-start | bytes 737288 | tf_op jit(solution)/shard_map/ppermute | solution.py:58
  14.9 2.0 %forward.1 = (bf16[32,3840]{1,0:T(8,128)(2,1)S(1)}, bf16[32,3840]{1,0:T(8,128)(2,1)S(1)}, bf16[16,3840]{1,0:T(8,128)(2,1)S(1)}, bf16[16,3840]{1,0:T(8,128)(2,1)S...) custom-call(bf16[32,3840]{1,0:T(8,128)(2,1)S(1)} %get-tuple-element.82.refs_0_.refs_6_, ...), custom_call_target="tpu_custom_call" | custom-call | tf_op jit(solution)/shard_map/forward/pallas_call | solution.py:465
  16.9 1.9 %collective-permute-start.10 = (bf16[16,3840]{1,0:T(8,128)(2,1)S(1)}, bf16[16,3840]{1,0:T(8,128)(2,1)S(1)}, u32[]{:S(2)}, u32[]{:S(2)}) collective-permute-start(bf16[16,3840]{1,0:T(8,128)(2,1)S(1)} %get-tuple-element.94), channel_id=1, source_target_pairs={{0,1},{1,0},{2,3},{3,2},{4,5},{5,4},{6,7},{7,6},{8,9},{9,8},{10,11... | collective-permute-start | bytes 368648 | tf_op jit(solution)/shard_map/ppermute | solution.py:67
  18.9 0.4 collective-permute-start.12
  21.4 2.1 %collective-permute-start.14 = (bf16[32,3968]{1,0:T(8,128)(2,1)S(1)}, bf16[32,3968]{1,0:T(8,128)(2,1)S(1)}, u32[]{:S(2)}, u32[]{:S(2)}) collective-permute-start(bf16[32,3968]{1,0:T(8,128)(2,1)S(1)} %get-tuple-element.98), channel_id=1, source_target_pairs={{0,6},{1,7},{2,4},{3,5},{4,10},{5,11},{6,8},{7,9},{8,14},{9,15},{1... | collective-permute-start | bytes 761864 | tf_op jit(solution)/shard_map/ppermute | solution.py:49
  23.6 7.9 %conditional.1 = (bf16[32,3840]{1,0:T(8,128)(2,1)S(1)}, bf16[32,3840]{1,0:T(8,128)(2,1)S(1)}, bf16[32,3840]{1,0:T(8,128)(2,1)S(1)}) conditional(s32[]{:T(128)} %bitcast.11, () %tuple.23, (bf16[32,3840]{1,0:T(8,128)(2,1)S(1)}, bf16[32,3840]{1,0:T(8,128)(2,1)S(1)}, f32[144,512]{1,0:T(8,128)S(1)}, f32[144,512]{1,0:T(8,128)S(1)}, ...), branch_computations={%region_0.0_spmd, %region_1.0_spmd} | conditional | bytes 2949264 | solution.py:525
  23.6 0.8 %collective-permute-start = (bf16[32,3840]{1,0:T(8,128)(2,1)S(1)}, bf16[32,3840]{1,0:T(8,128)(2,1)S(1)}, u32[]{:S(2)}, u32[]{:S(2)}) collective-permute-start(bf16[32,3840]{1,0:T(8,128)(2,1)S(1)} %get-tuple-element.16.refs_0_), channel_id=1, source_target_pairs={{0,1},{1,0},{2,3},{3,2},{4,5},{5,4},{6,7},{7,6},{8,9},{9,8},{10,11... | collective-permute-start | bytes 737288 | tf_op jit(solution)/shard_map/cond/branch_1_fun/ppermute | solution.py:67
  24.5 1.1 %collective-permute-done.refs_2_ = bf16[32,3840]{1,0:T(8,128)(2,1)S(1)} collective-permute-done((bf16[32,3840]{1,0:T(8,128)(2,1)S(1)}, bf16[32,3840]{1,0:T(8,128)(2,1)S(1)}, u32[]{:S(2)}, u32[]{:S(2)}) %collective-permute-start) | collective-permute-done | bytes 245792 | tf_op jit(solution)/shard_map/cond/branch_1_fun/ppermute | solution.py:67
  25.9 3.9 %backward.1 = (bf16[32,3840]{1,0:T(8,128)(2,1)S(1)}, bf16[32,3840]{1,0:T(8,128)(2,1)S(1)}, bf16[32,3840]{1,0:T(8,128)(2,1)S(1)}, bf16[32,3840]{1,0:T(8,128)(2,1)S(1)}) custom-call(bf16[32,3840]{1,0:T(8,128)(2,1)S(1)} %get-tuple-element.16.refs_0_, bf16[32,3840]{1,0:T(8,128)(2,1)S(1)} %get-tuple-element.17.refs_1_, ...), custom_call_target="tpu_custom_call" | custom-call | tf_op jit(solution)/shard_map/cond/branch_1_fun/backward/pallas_call | solution.py:465
  29.8 0.4 collective-permute-start.2
  30.2 1.2 %collective-permute-done.2.refs_1_ = bf16[32,3840]{1,0:T(8,128)(2,1)S(1)} collective-permute-done((bf16[32,3840]{1,0:T(8,128)(2,1)S(1)}, bf16[32,3840]{1,0:T(8,128)(2,1)S(1)}, u32[]{:S(2)}, u32[]{:S(2)}) %collective-permute-start.2) | collective-permute-done | bytes 245792 | tf_op jit(solution)/shard_map/cond/branch_1_fun/ppermute | solution.py:67
  31.5 0.4 collective-permute-start.16
  31.9 1.2 %collective-permute-start.17 = (bf16[32,3840]{1,0:T(8,128)(2,1)S(1)}, bf16[32,3840]{1,0:T(8,128)(2,1)S(1)}, u32[]{:S(2)}, u32[]{:S(2)}) collective-permute-start(bf16[32,3840]{1,0:T(8,128)(2,1)S(1)} %get-tuple-element.102), channel_id=1, source_target_pairs={{0,2},{1,3},{2,0},{3,1},{4,6},{5,7},{6,4},{7,5},{8,10},{9,11},{10,... | collective-permute-start | bytes 737288 | tf_op jit(solution)/shard_map/ppermute | solution.py:58
  33.1 10.4 %collective-permute-done.17.refs_2_ = bf16[32,3840]{1,0:T(8,128)(2,1)S(1)} collective-permute-done((bf16[32,3840]{1,0:T(8,128)(2,1)S(1)}, bf16[32,3840]{1,0:T(8,128)(2,1)S(1)}, u32[]{:S(2)}, u32[]{:S(2)}) %collective-permute-start.17) | collective-permute-done | bytes 245792 | tf_op jit(solution)/shard_map/ppermute | solution.py:58
  43.5 1.2 %backward_end.1 = (bf16[64,3584]{1,0:T(8,128)(2,1)}, f32[1,64]{1,0:T(1,128)}, f32[8,128]{1,0:T(8,128)S(1)}) custom-call(bf16[32,3840]{1,0:T(8,128)(2,1)S(1)} %get-tuple-element.100.refs_0_, bf16[32,3840]{1,0:T(8,128)(2,1)S(1)} %collective-permute-done.16.refs_1_, bf16[32,3840]{1,0:T(8,128)(2,1)S(1)} %collective-permute-done.17.refs_2_, ...), custom_call_target="tpu_custom_call" | custom-call | tf_op jit(solution)/shard_map/backward_end/pallas_call | solution.py:465
  44.7 1.2 %forward_end.1 = bf16[64,3584]{1,0:T(8,128)(2,1)} custom-call(bf16[32,3968]{1,0:T(8,128)(2,1)S(1)} %collective-permute-done.13.refs_0_, bf16[32,3968]{1,0:T(8,128)(2,1)S(1)} %collective-permute-done.14.refs_1_, f32[8,128]{1,0:T(8,128)S(1)} %get-tuple-element.104.refs_2_), custom_call_target="tpu_custom_call" | custom-call | tf_op jit(solution)/shard_map/forward_end/pallas_call | solution.py:465
  (24 shorter events, 3.2 us)
Async XLA Ops:
  0.6 12.5 %collective-permute-start.8 = (bf16[1,64,3584]{2,1,0:T(8,128)(2,1)}, bf16[1,64,3584]{2,1,0:T(8,128)(2,1)S(1)}, u32[]{:S(2)}, u32[]{:S(2)}) collective-permute-start(bf16[1,64,3584]{2,1,0:T(8,128)(2,1)} %param.16), channel_id=1, source_target_pairs={{4,0},{8,4},{12,8},{16,12},{20,16},{24,20},{28,24},{0,28},{5,1},{9... | collective-permute-start | bytes 1376264 | tf_op jit(solution)/shard_map/ppermute | solution.py:35
  2.2 8.3 %collective-permute-start.3 = (bf16[32,1920]{1,0:T(8,128)(2,1)S(1)}, bf16[32,1920]{1,0:T(8,128)(2,1)S(1)}, u32[]{:S(2)}, u32[]{:S(2)}) collective-permute-start(bf16[32,1920]{1,0:T(8,128)(2,1)S(1)} %get-tuple-element.70), channel_id=1, source_target_pairs={{0,2},{1,3},{2,0},{3,1},{4,6},{5,7},{6,4},{7,5},{8,10},{9,11},{10,... | collective-permute-start | bytes 368648 | tf_op jit(solution)/shard_map/ppermute | solution.py:58
  3.7 6.9 %collective-permute-start.4 = (bf16[32,1920]{1,0:T(8,128)(2,1)S(1)}, bf16[32,1920]{1,0:T(8,128)(2,1)S(1)}, u32[]{:S(2)}, u32[]{:S(2)}) collective-permute-start(bf16[32,1920]{1,0:T(8,128)(2,1)S(1)} %get-tuple-element.71), channel_id=1, source_target_pairs={{0,2},{1,3},{2,0},{3,1},{4,6},{5,7},{6,4},{7,5},{8,10},{9,11},{10,... | collective-permute-start | bytes 368648 | tf_op jit(solution)/shard_map/ppermute | solution.py:58
  3.8 11.1 %collective-permute-start.5 = (bf16[32,3840]{1,0:T(8,128)(2,1)S(1)}, bf16[32,3840]{1,0:T(8,128)(2,1)S(1)}, u32[]{:S(2)}, u32[]{:S(2)}) collective-permute-start(bf16[32,3840]{1,0:T(8,128)(2,1)S(1)} %get-tuple-element.82.refs_0_.refs_6_), channel_id=1, source_target_pairs={{0,1},{1,0},{2,3},{3,2},{4,5},{5,4},{6,7},{7,6},{8,9},{9,8},{10,11... | collective-permute-start | bytes 737288 | tf_op jit(solution)/shard_map/ppermute | solution.py:67
  10.6 4.3 %collective-permute-start.6 = (bf16[32,1920]{1,0:T(8,128)(2,1)S(1)}, bf16[32,1920]{1,0:T(8,128)(2,1)S(1)}, u32[]{:S(2)}, u32[]{:S(2)}) collective-permute-start(bf16[32,1920]{1,0:T(8,128)(2,1)S(1)} %collective-permute-done.3.refs_1_.refs_7_), channel_id=1, source_target_pairs={{0,1},{1,0},{2,3},{3,2},{4,5},{5,4},{6,7},{7,6},{8,9},{9,8},{10,11... | collective-permute-start | bytes 368648 | tf_op jit(solution)/shard_map/ppermute | solution.py:67
  10.7 4.2 %collective-permute-start.7 = (bf16[32,1920]{1,0:T(8,128)(2,1)S(1)}, bf16[32,1920]{1,0:T(8,128)(2,1)S(1)}, u32[]{:S(2)}, u32[]{:S(2)}) collective-permute-start(bf16[32,1920]{1,0:T(8,128)(2,1)S(1)} %collective-permute-done.4.refs_2_.refs_8_), channel_id=1, source_target_pairs={{0,1},{1,0},{2,3},{3,2},{4,5},{5,4},{6,7},{7,6},{8,9},{9,8},{10,11... | collective-permute-start | bytes 368648 | tf_op jit(solution)/shard_map/ppermute | solution.py:67
  13.6 10.0 %collective-permute-start.15 = (bf16[32,3840]{1,0:T(8,128)(2,1)S(1)}, bf16[32,3840]{1,0:T(8,128)(2,1)S(1)}, u32[]{:S(2)}, u32[]{:S(2)}) collective-permute-start(bf16[32,3840]{1,0:T(8,128)(2,1)S(1)} %get-tuple-element.81), channel_id=1, source_target_pairs={{0,2},{1,3},{2,0},{3,1},{4,6},{5,7},{6,4},{7,5},{8,10},{9,11},{10,... | collective-permute-start | bytes 737288 | tf_op jit(solution)/shard_map/ppermute | solution.py:58
  16.9 2.9 %collective-permute-start.10 = (bf16[16,3840]{1,0:T(8,128)(2,1)S(1)}, bf16[16,3840]{1,0:T(8,128)(2,1)S(1)}, u32[]{:S(2)}, u32[]{:S(2)}) collective-permute-start(bf16[16,3840]{1,0:T(8,128)(2,1)S(1)} %get-tuple-element.94), channel_id=1, source_target_pairs={{0,1},{1,0},{2,3},{3,2},{4,5},{5,4},{6,7},{7,6},{8,9},{9,8},{10,11... | collective-permute-start | bytes 368648 | tf_op jit(solution)/shard_map/ppermute | solution.py:67
  18.8 1.3 %collective-permute-start.11 = (bf16[16,3840]{1,0:T(8,128)(2,1)S(1)}, bf16[16,3840]{1,0:T(8,128)(2,1)S(1)}, u32[]{:S(2)}, u32[]{:S(2)}) collective-permute-start(bf16[16,3840]{1,0:T(8,128)(2,1)S(1)} %get-tuple-element.95), channel_id=1, source_target_pairs={{0,1},{1,0},{2,3},{3,2},{4,5},{5,4},{6,7},{7,6},{8,9},{9,8},{10,11... | collective-permute-start | bytes 368648 | tf_op jit(solution)/shard_map/ppermute | solution.py:67
  18.9 1.4 %collective-permute-start.12 = (bf16[16,3840]{1,0:T(8,128)(2,1)S(1)}, bf16[16,3840]{1,0:T(8,128)(2,1)S(1)}, u32[]{:S(2)}, u32[]{:S(2)}) collective-permute-start(bf16[16,3840]{1,0:T(8,128)(2,1)S(1)} %get-tuple-element.96), channel_id=1, source_target_pairs={{0,1},{1,0},{2,3},{3,2},{4,5},{5,4},{6,7},{7,6},{8,9},{9,8},{10,11... | collective-permute-start | bytes 368648 | tf_op jit(solution)/shard_map/ppermute | solution.py:67
  19.3 1.3 %collective-permute-start.9 = (bf16[16,3840]{1,0:T(8,128)(2,1)S(1)}, bf16[16,3840]{1,0:T(8,128)(2,1)S(1)}, u32[]{:S(2)}, u32[]{:S(2)}) collective-permute-start(bf16[16,3840]{1,0:T(8,128)(2,1)S(1)} %get-tuple-element.93), channel_id=1, source_target_pairs={{0,1},{1,0},{2,3},{3,2},{4,5},{5,4},{6,7},{7,6},{8,9},{9,8},{10,11... | collective-permute-start | bytes 368648 | tf_op jit(solution)/shard_map/ppermute | solution.py:67
  21.0 23.7 %collective-permute-start.13 = (bf16[32,3968]{1,0:T(8,128)(2,1)S(1)}, bf16[32,3968]{1,0:T(8,128)(2,1)S(1)}, u32[]{:S(2)}, u32[]{:S(2)}) collective-permute-start(bf16[32,3968]{1,0:T(8,128)(2,1)S(1)} %get-tuple-element.97), channel_id=1, source_target_pairs={{0,4},{1,5},{2,6},{3,7},{4,8},{5,9},{6,10},{7,11},{8,12},{9,13},{1... | collective-permute-start | bytes 761864 | tf_op jit(solution)/shard_map/ppermute | solution.py:49
  21.4 23.3 %collective-permute-start.14 = (bf16[32,3968]{1,0:T(8,128)(2,1)S(1)}, bf16[32,3968]{1,0:T(8,128)(2,1)S(1)}, u32[]{:S(2)}, u32[]{:S(2)}) collective-permute-start(bf16[32,3968]{1,0:T(8,128)(2,1)S(1)} %get-tuple-element.98), channel_id=1, source_target_pairs={{0,6},{1,7},{2,4},{3,5},{4,10},{5,11},{6,8},{7,9},{8,14},{9,15},{1... | collective-permute-start | bytes 761864 | tf_op jit(solution)/shard_map/ppermute | solution.py:49
  23.6 1.9 %collective-permute-start = (bf16[32,3840]{1,0:T(8,128)(2,1)S(1)}, bf16[32,3840]{1,0:T(8,128)(2,1)S(1)}, u32[]{:S(2)}, u32[]{:S(2)}) collective-permute-start(bf16[32,3840]{1,0:T(8,128)(2,1)S(1)} %get-tuple-element.16.refs_0_), channel_id=1, source_target_pairs={{0,1},{1,0},{2,3},{3,2},{4,5},{5,4},{6,7},{7,6},{8,9},{9,8},{10,11... | collective-permute-start | bytes 737288 | tf_op jit(solution)/shard_map/cond/branch_1_fun/ppermute | solution.py:67
  24.4 1.5 %collective-permute-start.1 = (bf16[32,3840]{1,0:T(8,128)(2,1)S(1)}, bf16[32,3840]{1,0:T(8,128)(2,1)S(1)}, u32[]{:S(2)}, u32[]{:S(2)}) collective-permute-start(bf16[32,3840]{1,0:T(8,128)(2,1)S(1)} %get-tuple-element.17.refs_1_), channel_id=1, source_target_pairs={{0,1},{1,0},{2,3},{3,2},{4,5},{5,4},{6,7},{7,6},{8,9},{9,8},{10,11... | collective-permute-start | bytes 737288 | tf_op jit(solution)/shard_map/cond/branch_1_fun/ppermute | solution.py:67
  29.8 1.6 %collective-permute-start.2 = (bf16[32,3840]{1,0:T(8,128)(2,1)S(1)}, bf16[32,3840]{1,0:T(8,128)(2,1)S(1)}, u32[]{:S(2)}, u32[]{:S(2)}) collective-permute-start(bf16[32,3840]{1,0:T(8,128)(2,1)S(1)} %get-tuple-element.27), channel_id=1, source_target_pairs={{0,1},{1,0},{2,3},{3,2},{4,5},{5,4},{6,7},{7,6},{8,9},{9,8},{10,11... | collective-permute-start | bytes 737288 | tf_op jit(solution)/shard_map/cond/branch_1_fun/ppermute | solution.py:67
  31.5 1.6 %collective-permute-start.16 = (bf16[32,3840]{1,0:T(8,128)(2,1)S(1)}, bf16[32,3840]{1,0:T(8,128)(2,1)S(1)}, u32[]{:S(2)}, u32[]{:S(2)}) collective-permute-start(bf16[32,3840]{1,0:T(8,128)(2,1)S(1)} %get-tuple-element.101), channel_id=1, source_target_pairs={{0,1},{1,0},{2,3},{3,2},{4,5},{5,4},{6,7},{7,6},{8,9},{9,8},{10,11... | collective-permute-start | bytes 737288 | tf_op jit(solution)/shard_map/ppermute | solution.py:67
  31.9 11.6 %collective-permute-start.17 = (bf16[32,3840]{1,0:T(8,128)(2,1)S(1)}, bf16[32,3840]{1,0:T(8,128)(2,1)S(1)}, u32[]{:S(2)}, u32[]{:S(2)}) collective-permute-start(bf16[32,3840]{1,0:T(8,128)(2,1)S(1)} %get-tuple-element.102), channel_id=1, source_target_pairs={{0,2},{1,3},{2,0},{3,1},{4,6},{5,7},{6,4},{7,5},{8,10},{9,11},{10,... | collective-permute-start | bytes 737288 | tf_op jit(solution)/shard_map/ppermute | solution.py:58

commit v9 on v8

--- a/solution.py
+++ b/solution.py
@@ -405,7 +405,8 @@
 
 def forward_end_kernel(s, *refs):
     packs = refs[: s.count]
-    out_ref, rows_ref, extra_ref, tail_ref, row_ref = refs[s.count + 1 :]
+    out_ref, token_ref, rows_ref, extra_ref, tail_ref, row_ref = refs[s.count :]
+    token_ref[...] = jnp.zeros_like(token_ref)
     row_ref[...] = packs[0][:, s.depth : s.depth + LANES].astype(F32)
     route_row = row_ref[s.folds : s.folds + 1, : s.tok]
     out_ref[...] = tokens_of(packs, route_row, rows_ref, extra_ref, tail_ref, s).astype(BF16)
@@ -427,9 +428,8 @@
 def backward_end_kernel(s, *refs):
     own, packs = refs[: s.slices], refs[s.slices : s.slices + s.count - 1]
     n = s.slices + s.count - 1
-    dy_ref, route_ref, score_ref, out_ref, grad_ref, token_ref = refs[n : n + 6]
+    dy_ref, route_ref, score_ref, _, out_ref, grad_ref = refs[n : n + 6]
     rows_ref, extra_ref, tail_ref = refs[n + 6 :]
-    token_ref[...] = jnp.zeros_like(token_ref)
     total = own[0][...].astype(F32)
     for part in own[1:]:
         total = total + part[...].astype(F32)
@@ -635,7 +635,7 @@
     sums_a = call(
         functools.partial(forward_sum_kernel, s),
         "forward_sum",
-        [((s.main, wide), BF16)] * s.count,
+        packed[:1] + [((s.main, wide), BF16)] * (s.count - 1),
         [],
         [VMEM] * (len(parts_a) + len(got) + 1),
         *parts_a,
@@ -647,27 +647,27 @@
     own_b, sums_b = step(route_b, backward, got_b, *factors, wg, wu, wd)
     back_b = [across(y, -1 - d, s) for d, y in enumerate(sums_b)]
     own_b = [beside(p, -k, s) if k else p for k, p in enumerate(own_b)]
-    input_grad, score_grad, token = call(
+    next_input, token = call(
+        functools.partial(forward_end_kernel, s),
+        "forward_end",
+        [((tok, depth), BF16), ((8, LANES), F32)],
+        end_scratch(s) + [pltpu.VMEM((s.main, LANES), F32)],
+        [VMEM] * s.count,
+        *moved,
+    )
+    input_grad, score_grad = call(
         functools.partial(backward_end_kernel, s),
         "backward_end",
-        [((tok, depth), BF16), ((1, tok), F32), ((8, LANES), F32)],
+        [((tok, depth), BF16), ((1, tok), F32)],
         end_scratch(s),
-        [VMEM] * (s.blocks // s.count + s.count - 1 + 3),
+        [VMEM] * (s.slices + s.count - 1 + 4),
         *own_b,
         *back_b,
         upstream,
         route_b,
         score_b,
-    )
-    next_input = call(
-        functools.partial(forward_end_kernel, s),
-        "forward_end",
-        [((tok, depth), BF16)],
-        end_scratch(s) + [pltpu.VMEM((s.main, LANES), F32)],
-        [VMEM] * (s.count + 1),
-        *moved,
         token,
-    )[0]
+    )
     return next_input[None], input_grad[None], score_grad.reshape(1, tok, 1)
 
 

time: 46.1 us -> 46.7 us (1.013)
  the two profiles are of different devices: /device:TPU:5 before, /device:TPU:30 now
where the time goes in v9:
time: 46.7 us; the launch traced here: 46.5 us
  waiting for transfers between devices  22 us (47%)
  Pallas kernels  15.9 us (34%)
  starting transfers between devices  6.78 us (15%)
  local copies, waits for them, and re-layouts  1.03 us (2%)
  between operations  0.74 us (2%)
    pallas_call x10, Pallas kernels, call(): pl.pallas_call(kernel, out_shape=shapes, in_specs=ins, out_specs=[VMEM] *...  15.9 us
    ppermute x4, waiting for transfers between devices, across(): return lax.ppermute(block, 'expert', route)  13.4 us
    ppermute x1, waiting for transfers between devices, from_behind(): return lax.ppermute(block, axis, route)  4.79 us
    ppermute x11, waiting for transfers between devices, beside(): return lax.ppermute(block, 'expert', route)  3.87 us
    ppermute x4, starting transfers between devices, across(): return lax.ppermute(block, 'expert', route)  2.69 us
    ppermute x11, starting transfers between devices, beside(): return lax.ppermute(block, 'expert', route)  2.62 us
    squeeze x1, local copies, waits for them, and re-layouts, body(): saved_up[0]  1.03 us
  transfers between devices with their start and end apart: 18, of which 11 were waited for; matrix products, arithmetic and copies ran while one was open for 2% of the time, Pallas kernels for 32%

profile of v9, /device:TPU:30, one launch (start us, length us, event | category | flops | bytes accessed | tf_op | source)
XLA Modules:
  0.0 46.5 jit_solution(6627624083230151438)
XLA Ops:
  0.6 0.6 %collective-permute-start.8 = (bf16[1,64,3584]{2,1,0:T(8,128)(2,1)}, bf16[1,64,3584]{2,1,0:T(8,128)(2,1)S(1)}, u32[]{:S(2)}, u32[]{:S(2)}) collective-permute-start(bf16[1,64,3584]{2,1,0:T(8,128)(2,1)} %param.16), channel_id=1, source_target_pairs={{4,0},{8,4},{12,8},{16,12},{20,16},{24,20},{28,24},{0,28},{5,1},{9... | collective-permute-start | bytes 1376264 | tf_op jit(solution)/shard_map/ppermute | solution.py:35
  1.2 1.5 %first.1 = (bf16[32,3840]{1,0:T(8,128)(2,1)S(1)}, bf16[32,1920]{1,0:T(8,128)(2,1)S(1)}, bf16[32,1920]{1,0:T(8,128)(2,1)S(1)}) custom-call(s32[1,64]{1,0:T(1,128)} %bitcast.25, f32[1,64]{1,0:T(1,128)} %bitcast.27, bf16[64,3584]{1,0:T(8,128)(2,1)} %bitcast.24), custom_call_target="tpu_custom_call" | custom-call | tf_op jit(solution)/shard_map/first/pallas_call | solution.py:465
  2.7 0.6 %collective-permute-start.3 = (bf16[32,1920]{1,0:T(8,128)(2,1)S(1)}, bf16[32,1920]{1,0:T(8,128)(2,1)S(1)}, u32[]{:S(2)}, u32[]{:S(2)}) collective-permute-start(bf16[32,1920]{1,0:T(8,128)(2,1)S(1)} %get-tuple-element.71), channel_id=1, source_target_pairs={{0,2},{1,3},{2,0},{3,1},{4,6},{5,7},{6,4},{7,5},{8,10},{9,11},{10,... | collective-permute-start | bytes 368648 | tf_op jit(solution)/shard_map/ppermute | solution.py:58
  3.3 1.5 %collective-permute-start.4 = (bf16[32,1920]{1,0:T(8,128)(2,1)S(1)}, bf16[32,1920]{1,0:T(8,128)(2,1)S(1)}, u32[]{:S(2)}, u32[]{:S(2)}) collective-permute-start(bf16[32,1920]{1,0:T(8,128)(2,1)S(1)} %get-tuple-element.72), channel_id=1, source_target_pairs={{0,2},{1,3},{2,0},{3,1},{4,6},{5,7},{6,4},{7,5},{8,10},{9,11},{10,... | collective-permute-start | bytes 368648 | tf_op jit(solution)/shard_map/ppermute | solution.py:58
  4.8 1.0 %copy_bitcast_fusion = (bf16[4,34,512]{2,1,0:T(8,128)(2,1)S(1)}, bf16[4,34,512]{2,1,0:T(8,128)(2,1)S(1)}) fusion(bf16[1,4,34,512]{3,1,2,0:T(4,128)(2,1)} %param.15, bf16[1,4,34,512]{3,1,2,0:T(4,128)(2,1)} %param.14), kind=kLoop, calls=%fused_computation | loop fusion | bytes 557056 | tf_op jit(solution)/shard_map/squeeze | solution.py:583
  6.1 4.3 %load.1 = (bf16[3584,512]{1,0:T(8,128)(2,1)S(1)}, bf16[3584,512]{1,0:T(8,128)(2,1)S(1)}, bf16[512,3584]{1,0:T(8,128)(2,1)S(1)}, s32[1,64]{1,0:T(1,128)S(1)}, s32[1,64]{1,0:T(1,128)S(1)}, /*index=5*/f32[1,64]{1,0:T(1,128)S(1)}) custom-call(bf16[3584,512]{1,0:T(8,128)(2,1)} %bitcast.21, bf16[3584,512]{1,0:T(8,128)(2,1)} %bitcast.22, ...), custom_call_target="tpu_custom_call" | custom-call | tf_op jit(solution)/shard_map/load/pallas_call | solution.py:465
  10.4 0.6 %collective-permute-start.6 = (bf16[32,1920]{1,0:T(8,128)(2,1)S(1)}, bf16[32,1920]{1,0:T(8,128)(2,1)S(1)}, u32[]{:S(2)}, u32[]{:S(2)}) collective-permute-start(bf16[32,1920]{1,0:T(8,128)(2,1)S(1)} %collective-permute-done.3.refs_1_.refs_7_), channel_id=1, source_target_pairs={{0,1},{1,0},{2,3},{3,2},{4,5},{5,4},{6,7},{7,6},{8,9},{9,8},{10,11... | collective-permute-start | bytes 368648 | tf_op jit(solution)/shard_map/ppermute | solution.py:67
  11.1 4.8 %collective-permute-done.8 = bf16[1,64,3584]{2,1,0:T(8,128)(2,1)S(1)} collective-permute-done((bf16[1,64,3584]{2,1,0:T(8,128)(2,1)}, bf16[1,64,3584]{2,1,0:T(8,128)(2,1)S(1)}, u32[]{:S(2)}, u32[]{:S(2)}) %collective-permute-start.8) | collective-permute-done | bytes 458784 | tf_op jit(solution)/shard_map/ppermute | solution.py:35
  15.8 0.4 pack.1
  16.3 0.6 %collective-permute-start.15 = (bf16[32,3840]{1,0:T(8,128)(2,1)S(1)}, bf16[32,3840]{1,0:T(8,128)(2,1)S(1)}, u32[]{:S(2)}, u32[]{:S(2)}) collective-permute-start(bf16[32,3840]{1,0:T(8,128)(2,1)S(1)} %get-tuple-element.82), channel_id=1, source_target_pairs={{0,2},{1,3},{2,0},{3,1},{4,6},{5,7},{6,4},{7,5},{8,10},{9,11},{10,... | collective-permute-start | bytes 737288 | tf_op jit(solution)/shard_map/ppermute | solution.py:58
  16.9 2.0 %forward.1 = (bf16[32,3840]{1,0:T(8,128)(2,1)S(1)}, bf16[32,3840]{1,0:T(8,128)(2,1)S(1)}, bf16[16,3840]{1,0:T(8,128)(2,1)S(1)}, bf16[16,3840]{1,0:T(8,128)(2,1)S...) custom-call(bf16[32,3840]{1,0:T(8,128)(2,1)S(1)} %get-tuple-element.83.refs_0_.refs_6_, ...), custom_call_target="tpu_custom_call" | custom-call | tf_op jit(solution)/shard_map/forward/pallas_call | solution.py:465
  19.0 0.5 %collective-permute-start.10 = (bf16[16,3840]{1,0:T(8,128)(2,1)S(1)}, bf16[16,3840]{1,0:T(8,128)(2,1)S(1)}, u32[]{:S(2)}, u32[]{:S(2)}) collective-permute-start(bf16[16,3840]{1,0:T(8,128)(2,1)S(1)} %get-tuple-element.95), channel_id=1, source_target_pairs={{0,1},{1,0},{2,3},{3,2},{4,5},{5,4},{6,7},{7,6},{8,9},{9,8},{10,11... | collective-permute-start | bytes 368648 | tf_op jit(solution)/shard_map/ppermute | solution.py:67
  19.6 0.4 collective-permute-start.12
  21.4 0.6 %collective-permute-start.14 = (bf16[32,3968]{1,0:T(8,128)(2,1)S(1)}, bf16[32,3968]{1,0:T(8,128)(2,1)S(1)}, u32[]{:S(2)}, u32[]{:S(2)}) collective-permute-start(bf16[32,3968]{1,0:T(8,128)(2,1)S(1)} %get-tuple-element.99), channel_id=1, source_target_pairs={{0,6},{1,7},{2,4},{3,5},{4,10},{5,11},{6,8},{7,9},{8,14},{9,15},{1... | collective-permute-start | bytes 761864 | tf_op jit(solution)/shard_map/ppermute | solution.py:49
  22.3 6.3 %collective-permute-done.15 = bf16[32,3840]{1,0:T(8,128)(2,1)S(1)} collective-permute-done((bf16[32,3840]{1,0:T(8,128)(2,1)S(1)}, bf16[32,3840]{1,0:T(8,128)(2,1)S(1)}, u32[]{:S(2)}, u32[]{:S(2)}) %collective-permute-start.15) | collective-permute-done | bytes 245792 | tf_op jit(solution)/shard_map/ppermute | solution.py:58
  28.6 8.1 %conditional.1 = (bf16[32,3840]{1,0:T(8,128)(2,1)S(1)}, bf16[32,3840]{1,0:T(8,128)(2,1)S(1)}, bf16[32,3840]{1,0:T(8,128)(2,1)}) conditional(s32[]{:T(128)} %bitcast.12, () %tuple.23, (bf16[32,3840]{1,0:T(8,128)(2,1)S(1)}, bf16[32,3840]{1,0:T(8,128)(2,1)S(1)}, f32[144,512]{1,0:T(8,128)S(1)}, f32[144,512]{1,0:T(8,128)S(1)}, f32[144,512]{1,0:T(8,128)S(1)}, ...), branch_computations={%region_0.0_spmd, %region_1.0_spmd} | conditional | bytes 2949264 | solution.py:525
  28.6 0.5 %collective-permute-start.1 = (bf16[32,3840]{1,0:T(8,128)(2,1)S(1)}, bf16[32,3840]{1,0:T(8,128)(2,1)S(1)}, u32[]{:S(2)}, u32[]{:S(2)}) collective-permute-start(bf16[32,3840]{1,0:T(8,128)(2,1)S(1)} %get-tuple-element.17.refs_1_), channel_id=1, source_target_pairs={{0,1},{1,0},{2,3},{3,2},{4,5},{5,4},{6,7},{7,6},{8,9},{9,8},{10,11... | collective-permute-start | bytes 737288 | tf_op jit(solution)/shard_map/cond/branch_1_fun/ppermute | solution.py:67
  29.1 1.0 %collective-permute-done.refs_2_ = bf16[32,3840]{1,0:T(8,128)(2,1)S(1)} collective-permute-done((bf16[32,3840]{1,0:T(8,128)(2,1)S(1)}, bf16[32,3840]{1,0:T(8,128)(2,1)S(1)}, u32[]{:S(2)}, u32[]{:S(2)}) %collective-permute-start) | collective-permute-done | bytes 245792 | tf_op jit(solution)/shard_map/cond/branch_1_fun/ppermute | solution.py:67
  30.5 3.9 %backward.1 = (bf16[32,3840]{1,0:T(8,128)(2,1)S(1)}, bf16[32,3840]{1,0:T(8,128)(2,1)S(1)}, bf16[32,3840]{1,0:T(8,128)(2,1)S(1)}, bf16[32,3840]{1,0:T(8,128)(2,1)S(1)}) custom-call(bf16[32,3840]{1,0:T(8,128)(2,1)S(1)} %get-tuple-element.16.refs_0_, bf16[32,3840]{1,0:T(8,128)(2,1)S(1)} %get-tuple-element.17.refs_1_, ...), custom_call_target="tpu_custom_call" | custom-call | tf_op jit(solution)/shard_map/cond/branch_1_fun/backward/pallas_call | solution.py:465
  34.6 1.4 %collective-permute-done.2.refs_1_ = bf16[32,3840]{1,0:T(8,128)(2,1)S(1)} collective-permute-done((bf16[32,3840]{1,0:T(8,128)(2,1)S(1)}, bf16[32,3840]{1,0:T(8,128)(2,1)S(1)}, u32[]{:S(2)}, u32[]{:S(2)}) %collective-permute-start.2) | collective-permute-done | bytes 245792 | tf_op jit(solution)/shard_map/cond/branch_1_fun/ppermute | solution.py:67
  35.9 0.8 %backward_sum.1 = bf16[32,3840]{1,0:T(8,128)(2,1)} custom-call(bf16[32,3840]{1,0:T(8,128)(2,1)S(1)} %get-tuple-element.26.refs_0_, bf16[32,3840]{1,0:T(8,128)(2,1)S(1)} %collective-permute-done.2.refs_1_), custom_call_target="tpu_custom_call" | custom-call | tf_op jit(solution)/shard_map/cond/branch_1_fun/backward_sum/pallas_call | solution.py:465
  36.9 1.2 %forward_end.1 = (bf16[64,3584]{1,0:T(8,128)(2,1)}, f32[8,128]{1,0:T(8,128)S(1)}) custom-call(bf16[32,3840]{1,0:T(8,128)(2,1)S(1)} %collective-permute-done.13.refs_0_, bf16[32,3968]{1,0:T(8,128)(2,1)S(1)} %collective-permute-done.14.refs_1_), custom_call_target="tpu_custom_call" | custom-call | tf_op jit(solution)/shard_map/forward_end/pallas_call | solution.py:465
  38.3 7.1 %collective-permute-done.17.refs_2_ = bf16[32,3840]{1,0:T(8,128)(2,1)S(1)} collective-permute-done((bf16[32,3840]{1,0:T(8,128)(2,1)}, bf16[32,3840]{1,0:T(8,128)(2,1)S(1)}, u32[]{:S(2)}, u32[]{:S(2)}) %collective-permute-start.17) | collective-permute-done | bytes 245792 | tf_op jit(solution)/shard_map/ppermute | solution.py:58
  45.3 1.2 %backward_end.1 = (bf16[64,3584]{1,0:T(8,128)(2,1)}, f32[1,64]{1,0:T(1,128)}) custom-call(bf16[32,3840]{1,0:T(8,128)(2,1)S(1)} %get-tuple-element.102.refs_0_, bf16[32,3840]{1,0:T(8,128)(2,1)S(1)} %collective-permute-done.16.refs_1_, bf16[32,3840]{1,0:T(8,128)(2,1)S(1)} %collective-permute-done.17.refs_2_, bf16[64,3584]{1,0:T(8,128)(2,1)S(1)} %bitcast.19, ...), custom_call_target="tpu_custom_call" | custom-call | tf_op jit(solution)/shard_map/backward_end/pallas_call | solution.py:465
  (24 shorter events, 3.0 us)
Async XLA Ops:
  0.6 15.2 %collective-permute-start.8 = (bf16[1,64,3584]{2,1,0:T(8,128)(2,1)}, bf16[1,64,3584]{2,1,0:T(8,128)(2,1)S(1)}, u32[]{:S(2)}, u32[]{:S(2)}) collective-permute-start(bf16[1,64,3584]{2,1,0:T(8,128)(2,1)} %param.16), channel_id=1, source_target_pairs={{4,0},{8,4},{12,8},{16,12},{20,16},{24,20},{28,24},{0,28},{5,1},{9... | collective-permute-start | bytes 1376264 | tf_op jit(solution)/shard_map/ppermute | solution.py:35
  2.7 7.7 %collective-permute-start.3 = (bf16[32,1920]{1,0:T(8,128)(2,1)S(1)}, bf16[32,1920]{1,0:T(8,128)(2,1)S(1)}, u32[]{:S(2)}, u32[]{:S(2)}) collective-permute-start(bf16[32,1920]{1,0:T(8,128)(2,1)S(1)} %get-tuple-element.71), channel_id=1, source_target_pairs={{0,2},{1,3},{2,0},{3,1},{4,6},{5,7},{6,4},{7,5},{8,10},{9,11},{10,... | collective-permute-start | bytes 368648 | tf_op jit(solution)/shard_map/ppermute | solution.py:58
  3.3 7.1 %collective-permute-start.4 = (bf16[32,1920]{1,0:T(8,128)(2,1)S(1)}, bf16[32,1920]{1,0:T(8,128)(2,1)S(1)}, u32[]{:S(2)}, u32[]{:S(2)}) collective-permute-start(bf16[32,1920]{1,0:T(8,128)(2,1)S(1)} %get-tuple-element.72), channel_id=1, source_target_pairs={{0,2},{1,3},{2,0},{3,1},{4,6},{5,7},{6,4},{7,5},{8,10},{9,11},{10,... | collective-permute-start | bytes 368648 | tf_op jit(solution)/shard_map/ppermute | solution.py:58
  4.8 12.1 %collective-permute-start.5 = (bf16[32,3840]{1,0:T(8,128)(2,1)S(1)}, bf16[32,3840]{1,0:T(8,128)(2,1)S(1)}, u32[]{:S(2)}, u32[]{:S(2)}) collective-permute-start(bf16[32,3840]{1,0:T(8,128)(2,1)S(1)} %get-tuple-element.83.refs_0_.refs_6_), channel_id=1, source_target_pairs={{0,1},{1,0},{2,3},{3,2},{4,5},{5,4},{6,7},{7,6},{8,9},{9,8},{10,11... | collective-permute-start | bytes 737288 | tf_op jit(solution)/shard_map/ppermute | solution.py:67
  10.4 6.5 %collective-permute-start.6 = (bf16[32,1920]{1,0:T(8,128)(2,1)S(1)}, bf16[32,1920]{1,0:T(8,128)(2,1)S(1)}, u32[]{:S(2)}, u32[]{:S(2)}) collective-permute-start(bf16[32,1920]{1,0:T(8,128)(2,1)S(1)} %collective-permute-done.3.refs_1_.refs_7_), channel_id=1, source_target_pairs={{0,1},{1,0},{2,3},{3,2},{4,5},{5,4},{6,7},{7,6},{8,9},{9,8},{10,11... | collective-permute-start | bytes 368648 | tf_op jit(solution)/shard_map/ppermute | solution.py:67
  11.0 5.9 %collective-permute-start.7 = (bf16[32,1920]{1,0:T(8,128)(2,1)S(1)}, bf16[32,1920]{1,0:T(8,128)(2,1)S(1)}, u32[]{:S(2)}, u32[]{:S(2)}) collective-permute-start(bf16[32,1920]{1,0:T(8,128)(2,1)S(1)} %collective-permute-done.4.refs_2_.refs_8_), channel_id=1, source_target_pairs={{0,1},{1,0},{2,3},{3,2},{4,5},{5,4},{6,7},{7,6},{8,9},{9,8},{10,11... | collective-permute-start | bytes 368648 | tf_op jit(solution)/shard_map/ppermute | solution.py:67
  16.3 12.3 %collective-permute-start.15 = (bf16[32,3840]{1,0:T(8,128)(2,1)S(1)}, bf16[32,3840]{1,0:T(8,128)(2,1)S(1)}, u32[]{:S(2)}, u32[]{:S(2)}) collective-permute-start(bf16[32,3840]{1,0:T(8,128)(2,1)S(1)} %get-tuple-element.82), channel_id=1, source_target_pairs={{0,2},{1,3},{2,0},{3,1},{4,6},{5,7},{6,4},{7,5},{8,10},{9,11},{10,... | collective-permute-start | bytes 737288 | tf_op jit(solution)/shard_map/ppermute | solution.py:58
  18.9 1.4 %collective-permute-start.9 = (bf16[16,3840]{1,0:T(8,128)(2,1)S(1)}, bf16[16,3840]{1,0:T(8,128)(2,1)S(1)}, u32[]{:S(2)}, u32[]{:S(2)}) collective-permute-start(bf16[16,3840]{1,0:T(8,128)(2,1)S(1)} %get-tuple-element.94), channel_id=1, source_target_pairs={{0,1},{1,0},{2,3},{3,2},{4,5},{5,4},{6,7},{7,6},{8,9},{9,8},{10,11... | collective-permute-start | bytes 368648 | tf_op jit(solution)/shard_map/ppermute | solution.py:67
  19.0 1.5 %collective-permute-start.10 = (bf16[16,3840]{1,0:T(8,128)(2,1)S(1)}, bf16[16,3840]{1,0:T(8,128)(2,1)S(1)}, u32[]{:S(2)}, u32[]{:S(2)}) collective-permute-start(bf16[16,3840]{1,0:T(8,128)(2,1)S(1)} %get-tuple-element.95), channel_id=1, source_target_pairs={{0,1},{1,0},{2,3},{3,2},{4,5},{5,4},{6,7},{7,6},{8,9},{9,8},{10,11... | collective-permute-start | bytes 368648 | tf_op jit(solution)/shard_map/ppermute | solution.py:67
  19.5 1.3 %collective-permute-start.11 = (bf16[16,3840]{1,0:T(8,128)(2,1)S(1)}, bf16[16,3840]{1,0:T(8,128)(2,1)S(1)}, u32[]{:S(2)}, u32[]{:S(2)}) collective-permute-start(bf16[16,3840]{1,0:T(8,128)(2,1)S(1)} %get-tuple-element.96), channel_id=1, source_target_pairs={{0,1},{1,0},{2,3},{3,2},{4,5},{5,4},{6,7},{7,6},{8,9},{9,8},{10,11... | collective-permute-start | bytes 368648 | tf_op jit(solution)/shard_map/ppermute | solution.py:67
  19.6 1.4 %collective-permute-start.12 = (bf16[16,3840]{1,0:T(8,128)(2,1)S(1)}, bf16[16,3840]{1,0:T(8,128)(2,1)S(1)}, u32[]{:S(2)}, u32[]{:S(2)}) collective-permute-start(bf16[16,3840]{1,0:T(8,128)(2,1)S(1)} %get-tuple-element.97), channel_id=1, source_target_pairs={{0,1},{1,0},{2,3},{3,2},{4,5},{5,4},{6,7},{7,6},{8,9},{9,8},{10,11... | collective-permute-start | bytes 368648 | tf_op jit(solution)/shard_map/ppermute | solution.py:67
  21.4 15.6 %collective-permute-start.14 = (bf16[32,3968]{1,0:T(8,128)(2,1)S(1)}, bf16[32,3968]{1,0:T(8,128)(2,1)S(1)}, u32[]{:S(2)}, u32[]{:S(2)}) collective-permute-start(bf16[32,3968]{1,0:T(8,128)(2,1)S(1)} %get-tuple-element.99), channel_id=1, source_target_pairs={{0,6},{1,7},{2,4},{3,5},{4,10},{5,11},{6,8},{7,9},{8,14},{9,15},{1... | collective-permute-start | bytes 761864 | tf_op jit(solution)/shard_map/ppermute | solution.py:49
  22.0 14.9 %collective-permute-start.13 = (bf16[32,3840]{1,0:T(8,128)(2,1)S(1)}, bf16[32,3840]{1,0:T(8,128)(2,1)S(1)}, u32[]{:S(2)}, u32[]{:S(2)}) collective-permute-start(bf16[32,3840]{1,0:T(8,128)(2,1)S(1)} %get-tuple-element.98), channel_id=1, source_target_pairs={{0,4},{1,5},{2,6},{3,7},{4,8},{5,9},{6,10},{7,11},{8,12},{9,13},{1... | collective-permute-start | bytes 737288 | tf_op jit(solution)/shard_map/ppermute | solution.py:49
  28.6 1.5 %collective-permute-start = (bf16[32,3840]{1,0:T(8,128)(2,1)S(1)}, bf16[32,3840]{1,0:T(8,128)(2,1)S(1)}, u32[]{:S(2)}, u32[]{:S(2)}) collective-permute-start(bf16[32,3840]{1,0:T(8,128)(2,1)S(1)} %get-tuple-element.16.refs_0_), channel_id=1, source_target_pairs={{0,1},{1,0},{2,3},{3,2},{4,5},{5,4},{6,7},{7,6},{8,9},{9,8},{10,11... | collective-permute-start | bytes 737288 | tf_op jit(solution)/shard_map/cond/branch_1_fun/ppermute | solution.py:67
  28.6 1.9 %collective-permute-start.1 = (bf16[32,3840]{1,0:T(8,128)(2,1)S(1)}, bf16[32,3840]{1,0:T(8,128)(2,1)S(1)}, u32[]{:S(2)}, u32[]{:S(2)}) collective-permute-start(bf16[32,3840]{1,0:T(8,128)(2,1)S(1)} %get-tuple-element.17.refs_1_), channel_id=1, source_target_pairs={{0,1},{1,0},{2,3},{3,2},{4,5},{5,4},{6,7},{7,6},{8,9},{9,8},{10,11... | collective-permute-start | bytes 737288 | tf_op jit(solution)/shard_map/cond/branch_1_fun/ppermute | solution.py:67
  34.4 1.6 %collective-permute-start.2 = (bf16[32,3840]{1,0:T(8,128)(2,1)S(1)}, bf16[32,3840]{1,0:T(8,128)(2,1)S(1)}, u32[]{:S(2)}, u32[]{:S(2)}) collective-permute-start(bf16[32,3840]{1,0:T(8,128)(2,1)S(1)} %get-tuple-element.27), channel_id=1, source_target_pairs={{0,1},{1,0},{2,3},{3,2},{4,5},{5,4},{6,7},{7,6},{8,9},{9,8},{10,11... | collective-permute-start | bytes 737288 | tf_op jit(solution)/shard_map/cond/branch_1_fun/ppermute | solution.py:67
  36.8 1.5 %collective-permute-start.16 = (bf16[32,3840]{1,0:T(8,128)(2,1)S(1)}, bf16[32,3840]{1,0:T(8,128)(2,1)S(1)}, u32[]{:S(2)}, u32[]{:S(2)}) collective-permute-start(bf16[32,3840]{1,0:T(8,128)(2,1)S(1)} %get-tuple-element.103), channel_id=1, source_target_pairs={{0,1},{1,0},{2,3},{3,2},{4,5},{5,4},{6,7},{7,6},{8,9},{9,8},{10,11... | collective-permute-start | bytes 737288 | tf_op jit(solution)/shard_map/ppermute | solution.py:67
  36.9 8.4 %collective-permute-start.17 = (bf16[32,3840]{1,0:T(8,128)(2,1)}, bf16[32,3840]{1,0:T(8,128)(2,1)S(1)}, u32[]{:S(2)}, u32[]{:S(2)}) collective-permute-start(bf16[32,3840]{1,0:T(8,128)(2,1)} %get-tuple-element.104), channel_id=1, source_target_pairs={{0,2},{1,3},{2,0},{3,1},{4,6},{5,7},{6,4},{7,5},{8,10},{9,11},{10,... | collective-permute-start | bytes 737288 | tf_op jit(solution)/shard_map/ppermute | solution.py:58

commit v10 on v9

--- a/solution.py
+++ b/solution.py
@@ -456,8 +456,8 @@
 HBM = pl.BlockSpec(memory_space=pltpu.HBM)
 
 
-def call(kernel, name, outs, scratch, ins, *args, mib=16):
-    shapes = [jax.ShapeDtypeStruct(shape, kind) for shape, kind in outs]
+def call(kernel, name, outs, scratch, ins, *args, mib=16, place=jax.ShapeDtypeStruct):
+    shapes = [place(shape, kind) for shape, kind in outs]
     args = [
         pltpu.with_memory_space_constraint(a, pltpu.HBM) if spec is HBM else a
         for a, spec in zip(args, ins)
@@ -604,6 +604,7 @@
             [pltpu.VMEM((s.main, LANES * s.extra), F32)],
             [VMEM] * len(others),
             *others,
+            place=pltpu.VMEM,
         )
         return tuple(parts[:: s.count]), tuple(sums)
 
@@ -635,7 +636,7 @@
     sums_a = call(
         functools.partial(forward_sum_kernel, s),
         "forward_sum",
-        packed[:1] + [((s.main, wide), BF16)] * (s.count - 1),
+        [((s.main, wide), BF16)] * s.count,
         [],
         [VMEM] * (len(parts_a) + len(got) + 1),
         *parts_a,

time: 46.7 us -> 44.9 us (0.961)
  the two profiles are of different devices: /device:TPU:30 before, /device:TPU:5 now
where the time goes in v10:
time: 44.9 us; the launch traced here: 44.7 us
  Pallas kernels  15.3 us (34%)
  waiting for transfers between devices  15.1 us (34%)
  starting transfers between devices  12.6 us (28%)
  local copies, waits for them, and re-layouts  1.03 us (2%)
  between operations  0.76 us (2%)
    pallas_call x10, Pallas kernels, call(): pl.pallas_call(kernel, out_shape=shapes, in_specs=ins, out_specs=[VMEM] *...  15.3 us
    ppermute x4, waiting for transfers between devices, across(): return lax.ppermute(block, 'expert', route)  8.11 us
    ppermute x11, starting transfers between devices, beside(): return lax.ppermute(block, 'expert', route)  5.94 us
    ppermute x4, starting transfers between devices, across(): return lax.ppermute(block, 'expert', route)  4.04 us
    ppermute x11, waiting for transfers between devices, beside(): return lax.ppermute(block, 'expert', route)  3.87 us
    ppermute x2, starting transfers between devices, to_next(): return lax.ppermute(block, ('section', 'expert'), route)  2.53 us
    ppermute x1, waiting for transfers between devices, from_behind(): return lax.ppermute(block, axis, route)  1.99 us
    ppermute x2, waiting for transfers between devices, to_next(): return lax.ppermute(block, ('section', 'expert'), route)  1.12 us
  transfers between devices with their start and end apart: 18, of which 10 were waited for; matrix products, arithmetic and copies ran while one was open for 2% of the time, Pallas kernels for 31%

profile of v10, /device:TPU:5, one launch (start us, length us, event | category | flops | bytes accessed | tf_op | source)
XLA Modules:
  0.0 44.7 jit_solution(5349212082122563858)
XLA Ops:
  0.7 1.5 %first.1 = (bf16[32,3840]{1,0:T(8,128)(2,1)S(1)}, bf16[32,1920]{1,0:T(8,128)(2,1)S(1)}, bf16[32,1920]{1,0:T(8,128)(2,1)S(1)}) custom-call(s32[1,64]{1,0:T(1,128)} %bitcast.25, f32[1,64]{1,0:T(1,128)} %bitcast.27, bf16[64,3584]{1,0:T(8,128)(2,1)} %bitcast.24), custom_call_target="tpu_custom_call" | custom-call | tf_op jit(solution)/shard_map/first/pallas_call | solution.py:465
  2.2 1.5 %collective-permute-start.3 = (bf16[32,1920]{1,0:T(8,128)(2,1)S(1)}, bf16[32,1920]{1,0:T(8,128)(2,1)S(1)}, u32[]{:S(2)}, u32[]{:S(2)}) collective-permute-start(bf16[32,1920]{1,0:T(8,128)(2,1)S(1)} %get-tuple-element.71), channel_id=1, source_target_pairs={{0,2},{1,3},{2,0},{3,1},{4,6},{5,7},{6,4},{7,5},{8,10},{9,11},{10,... | collective-permute-start | bytes 368648 | tf_op jit(solution)/shard_map/ppermute | solution.py:58
  3.8 1.2 %collective-permute-start.5 = (bf16[32,3840]{1,0:T(8,128)(2,1)S(1)}, bf16[32,3840]{1,0:T(8,128)(2,1)S(1)}, u32[]{:S(2)}, u32[]{:S(2)}) collective-permute-start(bf16[32,3840]{1,0:T(8,128)(2,1)S(1)} %get-tuple-element.83.refs_0_.refs_6_), channel_id=1, source_target_pairs={{0,1},{1,0},{2,3},{3,2},{4,5},{5,4},{6,7},{7,6},{8,9},{9,8},{10,11... | collective-permute-start | bytes 737288 | tf_op jit(solution)/shard_map/ppermute | solution.py:67
  5.0 1.0 %copy_bitcast_fusion = (bf16[4,34,512]{2,1,0:T(8,128)(2,1)S(1)}, bf16[4,34,512]{2,1,0:T(8,128)(2,1)S(1)}) fusion(bf16[1,4,34,512]{3,1,2,0:T(4,128)(2,1)} %param.15, bf16[1,4,34,512]{3,1,2,0:T(4,128)(2,1)} %param.14), kind=kLoop, calls=%fused_computation | loop fusion | bytes 557056 | tf_op jit(solution)/shard_map/squeeze | solution.py:583
  6.3 4.3 %load.1 = (bf16[3584,512]{1,0:T(8,128)(2,1)S(1)}, bf16[3584,512]{1,0:T(8,128)(2,1)S(1)}, bf16[512,3584]{1,0:T(8,128)(2,1)S(1)}, s32[1,64]{1,0:T(1,128)S(1)}, s32[1,64]{1,0:T(1,128)S(1)}, /*index=5*/f32[1,64]{1,0:T(1,128)S(1)}) custom-call(bf16[3584,512]{1,0:T(8,128)(2,1)} %bitcast.21, bf16[3584,512]{1,0:T(8,128)(2,1)} %bitcast.22, ...), custom_call_target="tpu_custom_call" | custom-call | tf_op jit(solution)/shard_map/load/pallas_call | solution.py:465
  10.7 0.5 %collective-permute-start.7 = (bf16[32,1920]{1,0:T(8,128)(2,1)S(1)}, bf16[32,1920]{1,0:T(8,128)(2,1)S(1)}, u32[]{:S(2)}, u32[]{:S(2)}) collective-permute-start(bf16[32,1920]{1,0:T(8,128)(2,1)S(1)} %collective-permute-done.4.refs_2_.refs_8_), channel_id=1, source_target_pairs={{0,1},{1,0},{2,3},{3,2},{4,5},{5,4},{6,7},{7,6},{8,9},{9,8},{10,11... | collective-permute-start | bytes 368648 | tf_op jit(solution)/shard_map/ppermute | solution.py:67
  11.2 2.0 %collective-permute-done.8 = bf16[1,64,3584]{2,1,0:T(8,128)(2,1)S(1)} collective-permute-done((bf16[1,64,3584]{2,1,0:T(8,128)(2,1)}, bf16[1,64,3584]{2,1,0:T(8,128)(2,1)S(1)}, u32[]{:S(2)}, u32[]{:S(2)}) %collective-permute-start.8) | collective-permute-done | bytes 458784 | tf_op jit(solution)/shard_map/ppermute | solution.py:35
  13.2 0.4 pack.1
  13.6 1.3 %collective-permute-start.15 = (bf16[32,3840]{1,0:T(8,128)(2,1)S(1)}, bf16[32,3840]{1,0:T(8,128)(2,1)S(1)}, u32[]{:S(2)}, u32[]{:S(2)}) collective-permute-start(bf16[32,3840]{1,0:T(8,128)(2,1)S(1)} %get-tuple-element.82), channel_id=1, source_target_pairs={{0,2},{1,3},{2,0},{3,1},{4,6},{5,7},{6,4},{7,5},{8,10},{9,11},{10,... | collective-permute-start | bytes 737288 | tf_op jit(solution)/shard_map/ppermute | solution.py:58
  14.9 2.0 %forward.1 = (bf16[32,3840]{1,0:T(8,128)(2,1)S(1)}, bf16[32,3840]{1,0:T(8,128)(2,1)S(1)}, bf16[16,3840]{1,0:T(8,128)(2,1)S(1)}, bf16[16,3840]{1,0:T(8,128)(2,1)S...) custom-call(bf16[32,3840]{1,0:T(8,128)(2,1)S(1)} %get-tuple-element.83.refs_0_.refs_6_, ...), custom_call_target="tpu_custom_call" | custom-call | tf_op jit(solution)/shard_map/forward/pallas_call | solution.py:465
  16.9 1.9 %collective-permute-start.9 = (bf16[16,3840]{1,0:T(8,128)(2,1)S(1)}, bf16[16,3840]{1,0:T(8,128)(2,1)S(1)}, u32[]{:S(2)}, u32[]{:S(2)}) collective-permute-start(bf16[16,3840]{1,0:T(8,128)(2,1)S(1)} %get-tuple-element.94), channel_id=1, source_target_pairs={{0,1},{1,0},{2,3},{3,2},{4,5},{5,4},{6,7},{7,6},{8,9},{9,8},{10,11... | collective-permute-start | bytes 368648 | tf_op jit(solution)/shard_map/ppermute | solution.py:67
  18.9 0.4 collective-permute-start.11
  21.4 2.1 %collective-permute-start.14 = (bf16[32,3968]{1,0:T(8,128)(2,1)S(1)}, bf16[32,3968]{1,0:T(8,128)(2,1)S(1)}, u32[]{:S(2)}, u32[]{:S(2)}) collective-permute-start(bf16[32,3968]{1,0:T(8,128)(2,1)S(1)} %get-tuple-element.99), channel_id=1, source_target_pairs={{0,6},{1,7},{2,4},{3,5},{4,10},{5,11},{6,8},{7,9},{8,14},{9,15},{1... | collective-permute-start | bytes 761864 | tf_op jit(solution)/shard_map/ppermute | solution.py:49
  23.6 7.9 %conditional.1 = (bf16[32,3840]{1,0:T(8,128)(2,1)S(1)}, bf16[32,3840]{1,0:T(8,128)(2,1)S(1)}, bf16[32,3840]{1,0:T(8,128)(2,1)S(1)}) conditional(s32[]{:T(128)} %bitcast.12, () %tuple.23, (bf16[32,3840]{1,0:T(8,128)(2,1)S(1)}, bf16[32,3840]{1,0:T(8,128)(2,1)S(1)}, f32[144,512]{1,0:T(8,128)S(1)}, f32[144,512]{1,0:T(8,128)S(1)}, ...), branch_computations={%region_0.0_spmd, %region_1.0_spmd} | conditional | bytes 2949264 | solution.py:525
  23.6 0.8 %collective-permute-start = (bf16[32,3840]{1,0:T(8,128)(2,1)S(1)}, bf16[32,3840]{1,0:T(8,128)(2,1)S(1)}, u32[]{:S(2)}, u32[]{:S(2)}) collective-permute-start(bf16[32,3840]{1,0:T(8,128)(2,1)S(1)} %get-tuple-element.16.refs_0_), channel_id=1, source_target_pairs={{0,1},{1,0},{2,3},{3,2},{4,5},{5,4},{6,7},{7,6},{8,9},{9,8},{10,11... | collective-permute-start | bytes 737288 | tf_op jit(solution)/shard_map/cond/branch_1_fun/ppermute | solution.py:67
  24.5 1.1 %collective-permute-done.refs_2_ = bf16[32,3840]{1,0:T(8,128)(2,1)S(1)} collective-permute-done((bf16[32,3840]{1,0:T(8,128)(2,1)S(1)}, bf16[32,3840]{1,0:T(8,128)(2,1)S(1)}, u32[]{:S(2)}, u32[]{:S(2)}) %collective-permute-start) | collective-permute-done | bytes 245792 | tf_op jit(solution)/shard_map/cond/branch_1_fun/ppermute | solution.py:67
  25.9 3.9 %backward.1 = (bf16[32,3840]{1,0:T(8,128)(2,1)S(1)}, bf16[32,3840]{1,0:T(8,128)(2,1)S(1)}, bf16[32,3840]{1,0:T(8,128)(2,1)S(1)}, bf16[32,3840]{1,0:T(8,128)(2,1)S(1)}) custom-call(bf16[32,3840]{1,0:T(8,128)(2,1)S(1)} %get-tuple-element.16.refs_0_, bf16[32,3840]{1,0:T(8,128)(2,1)S(1)} %get-tuple-element.17.refs_1_, ...), custom_call_target="tpu_custom_call" | custom-call | tf_op jit(solution)/shard_map/cond/branch_1_fun/backward/pallas_call | solution.py:465
  29.8 0.4 collective-permute-start.2
  30.2 1.2 %collective-permute-done.2.refs_1_ = bf16[32,3840]{1,0:T(8,128)(2,1)S(1)} collective-permute-done((bf16[32,3840]{1,0:T(8,128)(2,1)S(1)}, bf16[32,3840]{1,0:T(8,128)(2,1)S(1)}, u32[]{:S(2)}, u32[]{:S(2)}) %collective-permute-start.2) | collective-permute-done | bytes 245792 | tf_op jit(solution)/shard_map/cond/branch_1_fun/ppermute | solution.py:67
  31.9 1.2 %collective-permute-start.17 = (bf16[32,3840]{1,0:T(8,128)(2,1)S(1)}, bf16[32,3840]{1,0:T(8,128)(2,1)S(1)}, u32[]{:S(2)}, u32[]{:S(2)}) collective-permute-start(bf16[32,3840]{1,0:T(8,128)(2,1)S(1)} %get-tuple-element.104), channel_id=1, source_target_pairs={{0,2},{1,3},{2,0},{3,1},{4,6},{5,7},{6,4},{7,5},{8,10},{9,11},{10,... | collective-permute-start | bytes 737288 | tf_op jit(solution)/shard_map/ppermute | solution.py:58
  33.1 1.1 %collective-permute-done.13.refs_0_ = bf16[32,3968]{1,0:T(8,128)(2,1)S(1)} collective-permute-done((bf16[32,3968]{1,0:T(8,128)(2,1)S(1)}, bf16[32,3968]{1,0:T(8,128)(2,1)S(1)}, u32[]{:S(2)}, u32[]{:S(2)}) %collective-permute-start.13) | collective-permute-done | bytes 253984 | tf_op jit(solution)/shard_map/ppermute | solution.py:49
  34.2 1.2 %forward_end.1 = (bf16[64,3584]{1,0:T(8,128)(2,1)}, f32[8,128]{1,0:T(8,128)S(1)}) custom-call(bf16[32,3968]{1,0:T(8,128)(2,1)S(1)} %collective-permute-done.13.refs_0_, bf16[32,3968]{1,0:T(8,128)(2,1)S(1)} %collective-permute-done.14.refs_1_), custom_call_target="tpu_custom_call" | custom-call | tf_op jit(solution)/shard_map/forward_end/pallas_call | solution.py:465
  35.4 8.1 %collective-permute-done.17.refs_2_ = bf16[32,3840]{1,0:T(8,128)(2,1)S(1)} collective-permute-done((bf16[32,3840]{1,0:T(8,128)(2,1)S(1)}, bf16[32,3840]{1,0:T(8,128)(2,1)S(1)}, u32[]{:S(2)}, u32[]{:S(2)}) %collective-permute-start.17) | collective-permute-done | bytes 245792 | tf_op jit(solution)/shard_map/ppermute | solution.py:58
  43.5 1.2 %backward_end.1 = (bf16[64,3584]{1,0:T(8,128)(2,1)}, f32[1,64]{1,0:T(1,128)}) custom-call(bf16[32,3840]{1,0:T(8,128)(2,1)S(1)} %get-tuple-element.102.refs_0_, bf16[32,3840]{1,0:T(8,128)(2,1)S(1)} %collective-permute-done.16.refs_1_, bf16[32,3840]{1,0:T(8,128)(2,1)S(1)} %collective-permute-done.17.refs_2_, bf16[64,3584]{1,0:T(8,128)(2,1)S(1)} %bitcast.19, ...), custom_call_target="tpu_custom_call" | custom-call | tf_op jit(solution)/shard_map/backward_end/pallas_call | solution.py:465
  (24 shorter events, 3.6 us)
Async XLA Ops:
  0.6 12.5 %collective-permute-start.8 = (bf16[1,64,3584]{2,1,0:T(8,128)(2,1)}, bf16[1,64,3584]{2,1,0:T(8,128)(2,1)S(1)}, u32[]{:S(2)}, u32[]{:S(2)}) collective-permute-start(bf16[1,64,3584]{2,1,0:T(8,128)(2,1)} %param.16), channel_id=1, source_target_pairs={{4,0},{8,4},{12,8},{16,12},{20,16},{24,20},{28,24},{0,28},{5,1},{9... | collective-permute-start | bytes 1376264 | tf_op jit(solution)/shard_map/ppermute | solution.py:35
  2.2 8.4 %collective-permute-start.3 = (bf16[32,1920]{1,0:T(8,128)(2,1)S(1)}, bf16[32,1920]{1,0:T(8,128)(2,1)S(1)}, u32[]{:S(2)}, u32[]{:S(2)}) collective-permute-start(bf16[32,1920]{1,0:T(8,128)(2,1)S(1)} %get-tuple-element.71), channel_id=1, source_target_pairs={{0,2},{1,3},{2,0},{3,1},{4,6},{5,7},{6,4},{7,5},{8,10},{9,11},{10,... | collective-permute-start | bytes 368648 | tf_op jit(solution)/shard_map/ppermute | solution.py:58
  3.7 6.9 %collective-permute-start.4 = (bf16[32,1920]{1,0:T(8,128)(2,1)S(1)}, bf16[32,1920]{1,0:T(8,128)(2,1)S(1)}, u32[]{:S(2)}, u32[]{:S(2)}) collective-permute-start(bf16[32,1920]{1,0:T(8,128)(2,1)S(1)} %get-tuple-element.72), channel_id=1, source_target_pairs={{0,2},{1,3},{2,0},{3,1},{4,6},{5,7},{6,4},{7,5},{8,10},{9,11},{10,... | collective-permute-start | bytes 368648 | tf_op jit(solution)/shard_map/ppermute | solution.py:58
  3.8 11.1 %collective-permute-start.5 = (bf16[32,3840]{1,0:T(8,128)(2,1)S(1)}, bf16[32,3840]{1,0:T(8,128)(2,1)S(1)}, u32[]{:S(2)}, u32[]{:S(2)}) collective-permute-start(bf16[32,3840]{1,0:T(8,128)(2,1)S(1)} %get-tuple-element.83.refs_0_.refs_6_), channel_id=1, source_target_pairs={{0,1},{1,0},{2,3},{3,2},{4,5},{5,4},{6,7},{7,6},{8,9},{9,8},{10,11... | collective-permute-start | bytes 737288 | tf_op jit(solution)/shard_map/ppermute | solution.py:67
  10.6 4.3 %collective-permute-start.6 = (bf16[32,1920]{1,0:T(8,128)(2,1)S(1)}, bf16[32,1920]{1,0:T(8,128)(2,1)S(1)}, u32[]{:S(2)}, u32[]{:S(2)}) collective-permute-start(bf16[32,1920]{1,0:T(8,128)(2,1)S(1)} %collective-permute-done.3.refs_1_.refs_7_), channel_id=1, source_target_pairs={{0,1},{1,0},{2,3},{3,2},{4,5},{5,4},{6,7},{7,6},{8,9},{9,8},{10,11... | collective-permute-start | bytes 368648 | tf_op jit(solution)/shard_map/ppermute | solution.py:67
  10.7 4.2 %collective-permute-start.7 = (bf16[32,1920]{1,0:T(8,128)(2,1)S(1)}, bf16[32,1920]{1,0:T(8,128)(2,1)S(1)}, u32[]{:S(2)}, u32[]{:S(2)}) collective-permute-start(bf16[32,1920]{1,0:T(8,128)(2,1)S(1)} %collective-permute-done.4.refs_2_.refs_8_), channel_id=1, source_target_pairs={{0,1},{1,0},{2,3},{3,2},{4,5},{5,4},{6,7},{7,6},{8,9},{9,8},{10,11... | collective-permute-start | bytes 368648 | tf_op jit(solution)/shard_map/ppermute | solution.py:67
  13.6 10.0 %collective-permute-start.15 = (bf16[32,3840]{1,0:T(8,128)(2,1)S(1)}, bf16[32,3840]{1,0:T(8,128)(2,1)S(1)}, u32[]{:S(2)}, u32[]{:S(2)}) collective-permute-start(bf16[32,3840]{1,0:T(8,128)(2,1)S(1)} %get-tuple-element.82), channel_id=1, source_target_pairs={{0,2},{1,3},{2,0},{3,1},{4,6},{5,7},{6,4},{7,5},{8,10},{9,11},{10,... | collective-permute-start | bytes 737288 | tf_op jit(solution)/shard_map/ppermute | solution.py:58
  16.9 2.8 %collective-permute-start.9 = (bf16[16,3840]{1,0:T(8,128)(2,1)S(1)}, bf16[16,3840]{1,0:T(8,128)(2,1)S(1)}, u32[]{:S(2)}, u32[]{:S(2)}) collective-permute-start(bf16[16,3840]{1,0:T(8,128)(2,1)S(1)} %get-tuple-element.94), channel_id=1, source_target_pairs={{0,1},{1,0},{2,3},{3,2},{4,5},{5,4},{6,7},{7,6},{8,9},{9,8},{10,11... | collective-permute-start | bytes 368648 | tf_op jit(solution)/shard_map/ppermute | solution.py:67
  18.8 1.3 %collective-permute-start.10 = (bf16[16,3840]{1,0:T(8,128)(2,1)S(1)}, bf16[16,3840]{1,0:T(8,128)(2,1)S(1)}, u32[]{:S(2)}, u32[]{:S(2)}) collective-permute-start(bf16[16,3840]{1,0:T(8,128)(2,1)S(1)} %get-tuple-element.95), channel_id=1, source_target_pairs={{0,1},{1,0},{2,3},{3,2},{4,5},{5,4},{6,7},{7,6},{8,9},{9,8},{10,11... | collective-permute-start | bytes 368648 | tf_op jit(solution)/shard_map/ppermute | solution.py:67
  18.9 1.4 %collective-permute-start.11 = (bf16[16,3840]{1,0:T(8,128)(2,1)S(1)}, bf16[16,3840]{1,0:T(8,128)(2,1)S(1)}, u32[]{:S(2)}, u32[]{:S(2)}) collective-permute-start(bf16[16,3840]{1,0:T(8,128)(2,1)S(1)} %get-tuple-element.96), channel_id=1, source_target_pairs={{0,1},{1,0},{2,3},{3,2},{4,5},{5,4},{6,7},{7,6},{8,9},{9,8},{10,11... | collective-permute-start | bytes 368648 | tf_op jit(solution)/shard_map/ppermute | solution.py:67
  19.3 1.3 %collective-permute-start.12 = (bf16[16,3840]{1,0:T(8,128)(2,1)S(1)}, bf16[16,3840]{1,0:T(8,128)(2,1)S(1)}, u32[]{:S(2)}, u32[]{:S(2)}) collective-permute-start(bf16[16,3840]{1,0:T(8,128)(2,1)S(1)} %get-tuple-element.97), channel_id=1, source_target_pairs={{0,1},{1,0},{2,3},{3,2},{4,5},{5,4},{6,7},{7,6},{8,9},{9,8},{10,11... | collective-permute-start | bytes 368648 | tf_op jit(solution)/shard_map/ppermute | solution.py:67
  21.0 13.2 %collective-permute-start.13 = (bf16[32,3968]{1,0:T(8,128)(2,1)S(1)}, bf16[32,3968]{1,0:T(8,128)(2,1)S(1)}, u32[]{:S(2)}, u32[]{:S(2)}) collective-permute-start(bf16[32,3968]{1,0:T(8,128)(2,1)S(1)} %get-tuple-element.98), channel_id=1, source_target_pairs={{0,4},{1,5},{2,6},{3,7},{4,8},{5,9},{6,10},{7,11},{8,12},{9,13},{1... | collective-permute-start | bytes 761864 | tf_op jit(solution)/shard_map/ppermute | solution.py:49
  21.4 12.8 %collective-permute-start.14 = (bf16[32,3968]{1,0:T(8,128)(2,1)S(1)}, bf16[32,3968]{1,0:T(8,128)(2,1)S(1)}, u32[]{:S(2)}, u32[]{:S(2)}) collective-permute-start(bf16[32,3968]{1,0:T(8,128)(2,1)S(1)} %get-tuple-element.99), channel_id=1, source_target_pairs={{0,6},{1,7},{2,4},{3,5},{4,10},{5,11},{6,8},{7,9},{8,14},{9,15},{1... | collective-permute-start | bytes 761864 | tf_op jit(solution)/shard_map/ppermute | solution.py:49
  23.6 1.9 %collective-permute-start = (bf16[32,3840]{1,0:T(8,128)(2,1)S(1)}, bf16[32,3840]{1,0:T(8,128)(2,1)S(1)}, u32[]{:S(2)}, u32[]{:S(2)}) collective-permute-start(bf16[32,3840]{1,0:T(8,128)(2,1)S(1)} %get-tuple-element.16.refs_0_), channel_id=1, source_target_pairs={{0,1},{1,0},{2,3},{3,2},{4,5},{5,4},{6,7},{7,6},{8,9},{9,8},{10,11... | collective-permute-start | bytes 737288 | tf_op jit(solution)/shard_map/cond/branch_1_fun/ppermute | solution.py:67
  24.4 1.5 %collective-permute-start.1 = (bf16[32,3840]{1,0:T(8,128)(2,1)S(1)}, bf16[32,3840]{1,0:T(8,128)(2,1)S(1)}, u32[]{:S(2)}, u32[]{:S(2)}) collective-permute-start(bf16[32,3840]{1,0:T(8,128)(2,1)S(1)} %get-tuple-element.17.refs_1_), channel_id=1, source_target_pairs={{0,1},{1,0},{2,3},{3,2},{4,5},{5,4},{6,7},{7,6},{8,9},{9,8},{10,11... | collective-permute-start | bytes 737288 | tf_op jit(solution)/shard_map/cond/branch_1_fun/ppermute | solution.py:67
  29.8 1.6 %collective-permute-start.2 = (bf16[32,3840]{1,0:T(8,128)(2,1)S(1)}, bf16[32,3840]{1,0:T(8,128)(2,1)S(1)}, u32[]{:S(2)}, u32[]{:S(2)}) collective-permute-start(bf16[32,3840]{1,0:T(8,128)(2,1)S(1)} %get-tuple-element.27), channel_id=1, source_target_pairs={{0,1},{1,0},{2,3},{3,2},{4,5},{5,4},{6,7},{7,6},{8,9},{9,8},{10,11... | collective-permute-start | bytes 737288 | tf_op jit(solution)/shard_map/cond/branch_1_fun/ppermute | solution.py:67
  31.5 3.9 %collective-permute-start.16 = (bf16[32,3840]{1,0:T(8,128)(2,1)S(1)}, bf16[32,3840]{1,0:T(8,128)(2,1)S(1)}, u32[]{:S(2)}, u32[]{:S(2)}) collective-permute-start(bf16[32,3840]{1,0:T(8,128)(2,1)S(1)} %get-tuple-element.103), channel_id=1, source_target_pairs={{0,1},{1,0},{2,3},{3,2},{4,5},{5,4},{6,7},{7,6},{8,9},{9,8},{10,11... | collective-permute-start | bytes 737288 | tf_op jit(solution)/shard_map/ppermute | solution.py:67
  31.9 11.6 %collective-permute-start.17 = (bf16[32,3840]{1,0:T(8,128)(2,1)S(1)}, bf16[32,3840]{1,0:T(8,128)(2,1)S(1)}, u32[]{:S(2)}, u32[]{:S(2)}) collective-permute-start(bf16[32,3840]{1,0:T(8,128)(2,1)S(1)} %get-tuple-element.104), channel_id=1, source_target_pairs={{0,2},{1,3},{2,0},{3,1},{4,6},{5,7},{6,4},{7,5},{8,10},{9,11},{10,... | collective-permute-start | bytes 737288 | tf_op jit(solution)/shard_map/ppermute | solution.py:58

commit v11 on v10

--- a/solution.py
+++ b/solution.py
@@ -35,12 +35,18 @@
     return lax.ppermute(block, axis, route)
 
 
-def to_next(block, distance, s):
+def turn_of(i, last, s):
+    return s.count - 1 - i if last else i
+
+
+def to_next(block, i, s):
     sections, own = lax.axis_size("section"), s.count * s.slices
     route = [
         (
             l * own + e * s.slices + j,
-            (l + 1) % sections * own + (e + distance) % s.count * s.slices + j,
+            (l + 1) % sections * own
+            + (e - turn_of(i, l == sections - 1, s)) % s.count * s.slices
+            + j,
         )
         for l in range(sections)
         for e in range(s.count)
@@ -371,15 +377,23 @@
     n = s.count + (s.blocks - s.count) * PIECES
     parts, bases = refs[:n], grouped(refs[n : n + 1 + (s.count - 1) * PIECES], s, PIECES)
     route_ref, outs = refs[-1 - s.count], refs[-s.count :]
-    for d in range(s.count - 1, -1, -1):
-        tail = read(bases[d], s.depth, s.depth + LANES).astype(F32)
-        main, extra = get_slots(2.5 * get_row(tail, s), s)
-        add_gated(outs[d], bases[d], main, extra, total_of(parts, d, s), s)
-        spare = outs[d].shape[1] - s.width
-        if spare:
-            outs[d][:, s.width :] = jnp.zeros((s.main, spare), BF16)
     at = s.folds
-    outs[0][at : at + 1, s.depth : s.depth + s.tok] = route_ref[...].astype(F32).astype(BF16)
+
+    def fill(last):
+        for i in range(s.count):
+            d = turn_of(i, last, s)
+            tail = read(bases[d], s.depth, s.depth + LANES).astype(F32)
+            main, extra = get_slots(2.5 * get_row(tail, s), s)
+            add_gated(outs[i], bases[d], main, extra, total_of(parts, d, s), s)
+            spare = outs[i].shape[1] - s.width
+            outs[i][:, s.width :] = jnp.zeros((s.main, spare), BF16)
+            if d == 0:
+                row = route_ref[...].astype(F32).astype(BF16)
+                outs[i][at : at + 1, s.depth : s.depth + s.tok] = row
+
+    last = lax.axis_index("section") == lax.axis_size("section") - 1
+    pl.when(last)(functools.partial(fill, True))
+    pl.when(jnp.logical_not(last))(functools.partial(fill, False))
 
 
 def tokens_of(packs, route_row, rows_ref, extra_ref, tail_ref, s):
@@ -407,9 +421,16 @@
     packs = refs[: s.count]
     out_ref, token_ref, rows_ref, extra_ref, tail_ref, row_ref = refs[s.count :]
     token_ref[...] = jnp.zeros_like(token_ref)
-    row_ref[...] = packs[0][:, s.depth : s.depth + LANES].astype(F32)
-    route_row = row_ref[s.folds : s.folds + 1, : s.tok]
-    out_ref[...] = tokens_of(packs, route_row, rows_ref, extra_ref, tail_ref, s).astype(BF16)
+
+    def fill(last):
+        mine = [packs[turn_of(d, last, s)] for d in range(s.count)]
+        row_ref[...] = mine[0][:, s.depth : s.depth + LANES].astype(F32)
+        route_row = row_ref[s.folds : s.folds + 1, : s.tok]
+        out_ref[...] = tokens_of(mine, route_row, rows_ref, extra_ref, tail_ref, s).astype(BF16)
+
+    first = lax.axis_index("section") == 0
+    pl.when(first)(functools.partial(fill, True))
+    pl.when(jnp.logical_not(first))(functools.partial(fill, False))
 
 
 def backward_sum_kernel(s, *refs):
@@ -643,7 +664,7 @@
         *got,
         route_a,
     )
-    moved = [to_next(y, -d, s) for d, y in enumerate(sums_a)]
+    moved = [to_next(y, i, s) for i, y in enumerate(sums_a)]
     got_b[1:] = hold(got_b[1:], sums_a)
     own_b, sums_b = step(route_b, backward, got_b, *factors, wg, wu, wd)
     back_b = [across(y, -1 - d, s) for d, y in enumerate(sums_b)]

time: 44.9 us -> 43.3 us (0.964)
  the two profiles are of different devices: /device:TPU:5 before, /device:TPU:0 now
where the time goes in v11:
time: 43.3 us; the launch traced here: 43.2 us
  Pallas kernels  15.3 us (35%)
  starting transfers between devices  14.7 us (34%)
  waiting for transfers between devices  11.4 us (26%)
  local copies, waits for them, and re-layouts  1.03 us (2%)
  between operations  0.74 us (2%)
    pallas_call x10, Pallas kernels, call(): pl.pallas_call(kernel, out_shape=shapes, in_specs=ins, out_specs=[VMEM] *...  15.3 us
    ppermute x2, waiting for transfers between devices, to_next(): return lax.ppermute(block, ('section', 'expert'), route)  6.26 us
    ppermute x1, starting transfers between devices, from_behind(): return lax.ppermute(block, axis, route)  6.06 us
    ppermute x4, starting transfers between devices, across(): return lax.ppermute(block, 'expert', route)  5.09 us
    ppermute x11, waiting for transfers between devices, beside(): return lax.ppermute(block, 'expert', route)  3.72 us
    ppermute x11, starting transfers between devices, beside(): return lax.ppermute(block, 'expert', route)  2.68 us
    ppermute x4, waiting for transfers between devices, across(): return lax.ppermute(block, 'expert', route)  1.21 us
    squeeze x1, local copies, waits for them, and re-layouts, body(): saved_up[0]  1.03 us
  transfers between devices with their start and end apart: 18, of which 11 were waited for; matrix products, arithmetic and copies ran while one was open for 2% of the time, Pallas kernels for 33%

profile of v11, /device:TPU:0, one launch (start us, length us, event | category | flops | bytes accessed | tf_op | source)
XLA Modules:
  0.0 43.2 jit_solution(2135559504973703828)
XLA Ops:
  0.6 6.1 %collective-permute-start.8 = (bf16[1,64,3584]{2,1,0:T(8,128)(2,1)}, bf16[1,64,3584]{2,1,0:T(8,128)(2,1)S(1)}, u32[]{:S(2)}, u32[]{:S(2)}) collective-permute-start(bf16[1,64,3584]{2,1,0:T(8,128)(2,1)} %param.16), channel_id=1, source_target_pairs={{4,0},{8,4},{12,8},{16,12},{20,16},{24,20},{28,24},{0,28},{5,1},{9... | collective-permute-start | bytes 1376264 | tf_op jit(solution)/shard_map/ppermute | solution.py:35
  6.7 1.5 %first.1 = (bf16[32,3840]{1,0:T(8,128)(2,1)S(1)}, bf16[32,1920]{1,0:T(8,128)(2,1)S(1)}, bf16[32,1920]{1,0:T(8,128)(2,1)S(1)}) custom-call(s32[1,64]{1,0:T(1,128)} %bitcast.25, f32[1,64]{1,0:T(1,128)} %bitcast.27, bf16[64,3584]{1,0:T(8,128)(2,1)} %bitcast.24), custom_call_target="tpu_custom_call" | custom-call | tf_op jit(solution)/shard_map/first/pallas_call | solution.py:486
  8.2 1.5 %collective-permute-start.3 = (bf16[32,1920]{1,0:T(8,128)(2,1)S(1)}, bf16[32,1920]{1,0:T(8,128)(2,1)S(1)}, u32[]{:S(2)}, u32[]{:S(2)}) collective-permute-start(bf16[32,1920]{1,0:T(8,128)(2,1)S(1)} %get-tuple-element.71), channel_id=1, source_target_pairs={{0,2},{1,3},{2,0},{3,1},{4,6},{5,7},{6,4},{7,5},{8,10},{9,11},{10,... | collective-permute-start | bytes 368648 | tf_op jit(solution)/shard_map/ppermute | solution.py:64
  9.8 0.5 %collective-permute-start.4 = (bf16[32,1920]{1,0:T(8,128)(2,1)S(1)}, bf16[32,1920]{1,0:T(8,128)(2,1)S(1)}, u32[]{:S(2)}, u32[]{:S(2)}) collective-permute-start(bf16[32,1920]{1,0:T(8,128)(2,1)S(1)} %get-tuple-element.72), channel_id=1, source_target_pairs={{0,2},{1,3},{2,0},{3,1},{4,6},{5,7},{6,4},{7,5},{8,10},{9,11},{10,... | collective-permute-start | bytes 368648 | tf_op jit(solution)/shard_map/ppermute | solution.py:64
  10.3 1.0 %copy_bitcast_fusion = (bf16[4,34,512]{2,1,0:T(8,128)(2,1)S(1)}, bf16[4,34,512]{2,1,0:T(8,128)(2,1)S(1)}) fusion(bf16[1,4,34,512]{3,1,2,0:T(4,128)(2,1)} %param.15, bf16[1,4,34,512]{3,1,2,0:T(4,128)(2,1)} %param.14), kind=kLoop, calls=%fused_computation | loop fusion | bytes 557056 | tf_op jit(solution)/shard_map/squeeze | solution.py:604
  11.6 4.3 %load.1 = (bf16[3584,512]{1,0:T(8,128)(2,1)S(1)}, bf16[3584,512]{1,0:T(8,128)(2,1)S(1)}, bf16[512,3584]{1,0:T(8,128)(2,1)S(1)}, s32[1,64]{1,0:T(1,128)S(1)}, s32[1,64]{1,0:T(1,128)S(1)}, /*index=5*/f32[1,64]{1,0:T(1,128)S(1)}) custom-call(bf16[3584,512]{1,0:T(8,128)(2,1)} %bitcast.21, bf16[3584,512]{1,0:T(8,128)(2,1)} %bitcast.22, ...), custom_call_target="tpu_custom_call" | custom-call | tf_op jit(solution)/shard_map/load/pallas_call | solution.py:486
  15.9 0.6 %collective-permute-start.6 = (bf16[32,1920]{1,0:T(8,128)(2,1)S(1)}, bf16[32,1920]{1,0:T(8,128)(2,1)S(1)}, u32[]{:S(2)}, u32[]{:S(2)}) collective-permute-start(bf16[32,1920]{1,0:T(8,128)(2,1)S(1)} %collective-permute-done.3.refs_1_.refs_7_), channel_id=1, source_target_pairs={{0,1},{1,0},{2,3},{3,2},{4,5},{5,4},{6,7},{7,6},{8,9},{9,8},{10,11... | collective-permute-start | bytes 368648 | tf_op jit(solution)/shard_map/ppermute | solution.py:73
  16.8 0.4 %pack.1 = (bf16[32,3840]{1,0:T(8,128)(2,1)S(1)}, bf16[32,3840]{1,0:T(8,128)(2,1)S(1)}) custom-call(s32[1,64]{1,0:T(1,128)S(1)} %get-tuple-element.79.route_ref.refs_4_, bf16[64,3584]{1,0:T(8,128)(2,1)S(1)} %bitcast.18), custom_call_target="tpu_custom_call" | custom-call | tf_op jit(solution)/shard_map/pack/pallas_call | solution.py:486
  17.2 1.6 %collective-permute-start.15 = (bf16[32,3840]{1,0:T(8,128)(2,1)S(1)}, bf16[32,3840]{1,0:T(8,128)(2,1)S(1)}, u32[]{:S(2)}, u32[]{:S(2)}) collective-permute-start(bf16[32,3840]{1,0:T(8,128)(2,1)S(1)} %get-tuple-element.82), channel_id=1, source_target_pairs={{0,2},{1,3},{2,0},{3,1},{4,6},{5,7},{6,4},{7,5},{8,10},{9,11},{10,... | collective-permute-start | bytes 737288 | tf_op jit(solution)/shard_map/ppermute | solution.py:64
  18.8 2.0 %forward.1 = (bf16[32,3840]{1,0:T(8,128)(2,1)S(1)}, bf16[32,3840]{1,0:T(8,128)(2,1)S(1)}, bf16[16,3840]{1,0:T(8,128)(2,1)S(1)}, bf16[16,3840]{1,0:T(8,128)(2,1)S...) custom-call(bf16[32,3840]{1,0:T(8,128)(2,1)S(1)} %get-tuple-element.83.refs_0_.refs_6_, ...), custom_call_target="tpu_custom_call" | custom-call | tf_op jit(solution)/shard_map/forward/pallas_call | solution.py:486
  20.9 0.5 %collective-permute-start.10 = (bf16[16,3840]{1,0:T(8,128)(2,1)S(1)}, bf16[16,3840]{1,0:T(8,128)(2,1)S(1)}, u32[]{:S(2)}, u32[]{:S(2)}) collective-permute-start(bf16[16,3840]{1,0:T(8,128)(2,1)S(1)} %get-tuple-element.95), channel_id=1, source_target_pairs={{0,1},{1,0},{2,3},{3,2},{4,5},{5,4},{6,7},{7,6},{8,9},{9,8},{10,11... | collective-permute-start | bytes 368648 | tf_op jit(solution)/shard_map/ppermute | solution.py:73
  21.5 0.4 collective-permute-start.12
  23.5 0.6 %collective-permute-start.14 = (bf16[32,3968]{1,0:T(8,128)(2,1)S(1)}, bf16[32,3968]{1,0:T(8,128)(2,1)S(1)}, u32[]{:S(2)}, u32[]{:S(2)}) collective-permute-start(bf16[32,3968]{1,0:T(8,128)(2,1)S(1)} %get-tuple-element.99), channel_id=1, source_target_pairs={{0,6},{1,7},{2,4},{3,5},{4,10},{5,11},{6,8},{7,9},{8,14},{9,15},{1... | collective-permute-start | bytes 761864 | tf_op jit(solution)/shard_map/ppermute | solution.py:55
  24.2 1.2 %collective-permute-done.15 = bf16[32,3840]{1,0:T(8,128)(2,1)S(1)} collective-permute-done((bf16[32,3840]{1,0:T(8,128)(2,1)S(1)}, bf16[32,3840]{1,0:T(8,128)(2,1)S(1)}, u32[]{:S(2)}, u32[]{:S(2)}) %collective-permute-start.15) | collective-permute-done | bytes 245792 | tf_op jit(solution)/shard_map/ppermute | solution.py:64
  25.4 7.4 %conditional.1 = (bf16[32,3840]{1,0:T(8,128)(2,1)S(1)}, bf16[32,3840]{1,0:T(8,128)(2,1)S(1)}, bf16[32,3840]{1,0:T(8,128)(2,1)S(1)}) conditional(s32[]{:T(128)} %bitcast.12, () %tuple.23, (bf16[32,3840]{1,0:T(8,128)(2,1)S(1)}, bf16[32,3840]{1,0:T(8,128)(2,1)S(1)}, f32[144,512]{1,0:T(8,128)S(1)}, f32[144,512]{1,0:T(8,128)S(1)}, ...), branch_computations={%region_0.0_spmd, %region_1.0_spmd} | conditional | bytes 2949264 | solution.py:546
  25.4 0.5 %collective-permute-start.1 = (bf16[32,3840]{1,0:T(8,128)(2,1)S(1)}, bf16[32,3840]{1,0:T(8,128)(2,1)S(1)}, u32[]{:S(2)}, u32[]{:S(2)}) collective-permute-start(bf16[32,3840]{1,0:T(8,128)(2,1)S(1)} %get-tuple-element.17.refs_1_), channel_id=1, source_target_pairs={{0,1},{1,0},{2,3},{3,2},{4,5},{5,4},{6,7},{7,6},{8,9},{9,8},{10,11... | collective-permute-start | bytes 737288 | tf_op jit(solution)/shard_map/cond/branch_1_fun/ppermute | solution.py:73
  25.9 1.0 %collective-permute-done.refs_2_ = bf16[32,3840]{1,0:T(8,128)(2,1)S(1)} collective-permute-done((bf16[32,3840]{1,0:T(8,128)(2,1)S(1)}, bf16[32,3840]{1,0:T(8,128)(2,1)S(1)}, u32[]{:S(2)}, u32[]{:S(2)}) %collective-permute-start) | collective-permute-done | bytes 245792 | tf_op jit(solution)/shard_map/cond/branch_1_fun/ppermute | solution.py:73
  27.3 3.9 %backward.1 = (bf16[32,3840]{1,0:T(8,128)(2,1)S(1)}, bf16[32,3840]{1,0:T(8,128)(2,1)S(1)}, bf16[32,3840]{1,0:T(8,128)(2,1)S(1)}, bf16[32,3840]{1,0:T(8,128)(2,1)S(1)}) custom-call(bf16[32,3840]{1,0:T(8,128)(2,1)S(1)} %get-tuple-element.16.refs_0_, bf16[32,3840]{1,0:T(8,128)(2,1)S(1)} %get-tuple-element.17.refs_1_, ...), custom_call_target="tpu_custom_call" | custom-call | tf_op jit(solution)/shard_map/cond/branch_1_fun/backward/pallas_call | solution.py:486
  31.3 1.4 %collective-permute-done.2.refs_1_ = bf16[32,3840]{1,0:T(8,128)(2,1)S(1)} collective-permute-done((bf16[32,3840]{1,0:T(8,128)(2,1)S(1)}, bf16[32,3840]{1,0:T(8,128)(2,1)S(1)}, u32[]{:S(2)}, u32[]{:S(2)}) %collective-permute-start.2) | collective-permute-done | bytes 245792 | tf_op jit(solution)/shard_map/cond/branch_1_fun/ppermute | solution.py:73
  33.0 1.4 %collective-permute-start.17 = (bf16[32,3840]{1,0:T(8,128)(2,1)S(1)}, bf16[32,3840]{1,0:T(8,128)(2,1)S(1)}, u32[]{:S(2)}, u32[]{:S(2)}) collective-permute-start(bf16[32,3840]{1,0:T(8,128)(2,1)S(1)} %get-tuple-element.104), channel_id=1, source_target_pairs={{0,2},{1,3},{2,0},{3,1},{4,6},{5,7},{6,4},{7,5},{8,10},{9,11},{10,... | collective-permute-start | bytes 737288 | tf_op jit(solution)/shard_map/ppermute | solution.py:64
  34.5 1.7 %collective-permute-done.13.refs_0_ = bf16[32,3968]{1,0:T(8,128)(2,1)S(1)} collective-permute-done((bf16[32,3968]{1,0:T(8,128)(2,1)S(1)}, bf16[32,3968]{1,0:T(8,128)(2,1)S(1)}, u32[]{:S(2)}, u32[]{:S(2)}) %collective-permute-start.13) | collective-permute-done | bytes 253984 | tf_op jit(solution)/shard_map/ppermute | solution.py:55
  36.1 4.6 %collective-permute-done.14.refs_1_ = bf16[32,3968]{1,0:T(8,128)(2,1)S(1)} collective-permute-done((bf16[32,3968]{1,0:T(8,128)(2,1)S(1)}, bf16[32,3968]{1,0:T(8,128)(2,1)S(1)}, u32[]{:S(2)}, u32[]{:S(2)}) %collective-permute-start.14) | collective-permute-done | bytes 253984 | tf_op jit(solution)/shard_map/ppermute | solution.py:55
  40.8 1.2 %forward_end.1 = (bf16[64,3584]{1,0:T(8,128)(2,1)}, f32[8,128]{1,0:T(8,128)S(1)}) custom-call(bf16[32,3968]{1,0:T(8,128)(2,1)S(1)} %collective-permute-done.13.refs_0_, bf16[32,3968]{1,0:T(8,128)(2,1)S(1)} %collective-permute-done.14.refs_1_), custom_call_target="tpu_custom_call" | custom-call | tf_op jit(solution)/shard_map/forward_end/pallas_call | solution.py:486
  42.0 1.2 %backward_end.1 = (bf16[64,3584]{1,0:T(8,128)(2,1)}, f32[1,64]{1,0:T(1,128)}) custom-call(bf16[32,3840]{1,0:T(8,128)(2,1)S(1)} %get-tuple-element.102.refs_0_, bf16[32,3840]{1,0:T(8,128)(2,1)S(1)} %collective-permute-done.16.refs_1_, bf16[32,3840]{1,0:T(8,128)(2,1)S(1)} %collective-permute-done.17.refs_2_, bf16[64,3584]{1,0:T(8,128)(2,1)S(1)} %bitcast.19, ...), custom_call_target="tpu_custom_call" | custom-call | tf_op jit(solution)/shard_map/backward_end/pallas_call | solution.py:486
  (24 shorter events, 3.3 us)
Async XLA Ops:
  0.6 16.2 %collective-permute-start.8 = (bf16[1,64,3584]{2,1,0:T(8,128)(2,1)}, bf16[1,64,3584]{2,1,0:T(8,128)(2,1)S(1)}, u32[]{:S(2)}, u32[]{:S(2)}) collective-permute-start(bf16[1,64,3584]{2,1,0:T(8,128)(2,1)} %param.16), channel_id=1, source_target_pairs={{4,0},{8,4},{12,8},{16,12},{20,16},{24,20},{28,24},{0,28},{5,1},{9... | collective-permute-start | bytes 1376264 | tf_op jit(solution)/shard_map/ppermute | solution.py:35
  8.2 7.7 %collective-permute-start.3 = (bf16[32,1920]{1,0:T(8,128)(2,1)S(1)}, bf16[32,1920]{1,0:T(8,128)(2,1)S(1)}, u32[]{:S(2)}, u32[]{:S(2)}) collective-permute-start(bf16[32,1920]{1,0:T(8,128)(2,1)S(1)} %get-tuple-element.71), channel_id=1, source_target_pairs={{0,2},{1,3},{2,0},{3,1},{4,6},{5,7},{6,4},{7,5},{8,10},{9,11},{10,... | collective-permute-start | bytes 368648 | tf_op jit(solution)/shard_map/ppermute | solution.py:64
  9.8 6.1 %collective-permute-start.4 = (bf16[32,1920]{1,0:T(8,128)(2,1)S(1)}, bf16[32,1920]{1,0:T(8,128)(2,1)S(1)}, u32[]{:S(2)}, u32[]{:S(2)}) collective-permute-start(bf16[32,1920]{1,0:T(8,128)(2,1)S(1)} %get-tuple-element.72), channel_id=1, source_target_pairs={{0,2},{1,3},{2,0},{3,1},{4,6},{5,7},{6,4},{7,5},{8,10},{9,11},{10,... | collective-permute-start | bytes 368648 | tf_op jit(solution)/shard_map/ppermute | solution.py:64
  10.3 8.5 %collective-permute-start.5 = (bf16[32,3840]{1,0:T(8,128)(2,1)S(1)}, bf16[32,3840]{1,0:T(8,128)(2,1)S(1)}, u32[]{:S(2)}, u32[]{:S(2)}) collective-permute-start(bf16[32,3840]{1,0:T(8,128)(2,1)S(1)} %get-tuple-element.83.refs_0_.refs_6_), channel_id=1, source_target_pairs={{0,1},{1,0},{2,3},{3,2},{4,5},{5,4},{6,7},{7,6},{8,9},{9,8},{10,11... | collective-permute-start | bytes 737288 | tf_op jit(solution)/shard_map/ppermute | solution.py:73
  15.9 2.9 %collective-permute-start.6 = (bf16[32,1920]{1,0:T(8,128)(2,1)S(1)}, bf16[32,1920]{1,0:T(8,128)(2,1)S(1)}, u32[]{:S(2)}, u32[]{:S(2)}) collective-permute-start(bf16[32,1920]{1,0:T(8,128)(2,1)S(1)} %collective-permute-done.3.refs_1_.refs_7_), channel_id=1, source_target_pairs={{0,1},{1,0},{2,3},{3,2},{4,5},{5,4},{6,7},{7,6},{8,9},{9,8},{10,11... | collective-permute-start | bytes 368648 | tf_op jit(solution)/shard_map/ppermute | solution.py:73
  16.5 2.3 %collective-permute-start.7 = (bf16[32,1920]{1,0:T(8,128)(2,1)S(1)}, bf16[32,1920]{1,0:T(8,128)(2,1)S(1)}, u32[]{:S(2)}, u32[]{:S(2)}) collective-permute-start(bf16[32,1920]{1,0:T(8,128)(2,1)S(1)} %collective-permute-done.4.refs_2_.refs_8_), channel_id=1, source_target_pairs={{0,1},{1,0},{2,3},{3,2},{4,5},{5,4},{6,7},{7,6},{8,9},{9,8},{10,11... | collective-permute-start | bytes 368648 | tf_op jit(solution)/shard_map/ppermute | solution.py:73
  17.2 8.2 %collective-permute-start.15 = (bf16[32,3840]{1,0:T(8,128)(2,1)S(1)}, bf16[32,3840]{1,0:T(8,128)(2,1)S(1)}, u32[]{:S(2)}, u32[]{:S(2)}) collective-permute-start(bf16[32,3840]{1,0:T(8,128)(2,1)S(1)} %get-tuple-element.82), channel_id=1, source_target_pairs={{0,2},{1,3},{2,0},{3,1},{4,6},{5,7},{6,4},{7,5},{8,10},{9,11},{10,... | collective-permute-start | bytes 737288 | tf_op jit(solution)/shard_map/ppermute | solution.py:64
  20.8 1.4 %collective-permute-start.9 = (bf16[16,3840]{1,0:T(8,128)(2,1)S(1)}, bf16[16,3840]{1,0:T(8,128)(2,1)S(1)}, u32[]{:S(2)}, u32[]{:S(2)}) collective-permute-start(bf16[16,3840]{1,0:T(8,128)(2,1)S(1)} %get-tuple-element.94), channel_id=1, source_target_pairs={{0,1},{1,0},{2,3},{3,2},{4,5},{5,4},{6,7},{7,6},{8,9},{9,8},{10,11... | collective-permute-start | bytes 368648 | tf_op jit(solution)/shard_map/ppermute | solution.py:73
  20.9 1.5 %collective-permute-start.10 = (bf16[16,3840]{1,0:T(8,128)(2,1)S(1)}, bf16[16,3840]{1,0:T(8,128)(2,1)S(1)}, u32[]{:S(2)}, u32[]{:S(2)}) collective-permute-start(bf16[16,3840]{1,0:T(8,128)(2,1)S(1)} %get-tuple-element.95), channel_id=1, source_target_pairs={{0,1},{1,0},{2,3},{3,2},{4,5},{5,4},{6,7},{7,6},{8,9},{9,8},{10,11... | collective-permute-start | bytes 368648 | tf_op jit(solution)/shard_map/ppermute | solution.py:73
  21.4 1.3 %collective-permute-start.11 = (bf16[16,3840]{1,0:T(8,128)(2,1)S(1)}, bf16[16,3840]{1,0:T(8,128)(2,1)S(1)}, u32[]{:S(2)}, u32[]{:S(2)}) collective-permute-start(bf16[16,3840]{1,0:T(8,128)(2,1)S(1)} %get-tuple-element.96), channel_id=1, source_target_pairs={{0,1},{1,0},{2,3},{3,2},{4,5},{5,4},{6,7},{7,6},{8,9},{9,8},{10,11... | collective-permute-start | bytes 368648 | tf_op jit(solution)/shard_map/ppermute | solution.py:73
  21.5 1.4 %collective-permute-start.12 = (bf16[16,3840]{1,0:T(8,128)(2,1)S(1)}, bf16[16,3840]{1,0:T(8,128)(2,1)S(1)}, u32[]{:S(2)}, u32[]{:S(2)}) collective-permute-start(bf16[16,3840]{1,0:T(8,128)(2,1)S(1)} %get-tuple-element.97), channel_id=1, source_target_pairs={{0,1},{1,0},{2,3},{3,2},{4,5},{5,4},{6,7},{7,6},{8,9},{9,8},{10,11... | collective-permute-start | bytes 368648 | tf_op jit(solution)/shard_map/ppermute | solution.py:73
  23.3 12.9 %collective-permute-start.13 = (bf16[32,3968]{1,0:T(8,128)(2,1)S(1)}, bf16[32,3968]{1,0:T(8,128)(2,1)S(1)}, u32[]{:S(2)}, u32[]{:S(2)}) collective-permute-start(bf16[32,3968]{1,0:T(8,128)(2,1)S(1)} %get-tuple-element.98), channel_id=1, source_target_pairs={{0,4},{1,5},{2,6},{3,7},{4,8},{5,9},{6,10},{7,11},{8,12},{9,13},{1... | collective-permute-start | bytes 761864 | tf_op jit(solution)/shard_map/ppermute | solution.py:55
  23.5 17.2 %collective-permute-start.14 = (bf16[32,3968]{1,0:T(8,128)(2,1)S(1)}, bf16[32,3968]{1,0:T(8,128)(2,1)S(1)}, u32[]{:S(2)}, u32[]{:S(2)}) collective-permute-start(bf16[32,3968]{1,0:T(8,128)(2,1)S(1)} %get-tuple-element.99), channel_id=1, source_target_pairs={{0,6},{1,7},{2,4},{3,5},{4,10},{5,11},{6,8},{7,9},{8,14},{9,15},{1... | collective-permute-start | bytes 761864 | tf_op jit(solution)/shard_map/ppermute | solution.py:55
  25.4 1.5 %collective-permute-start = (bf16[32,3840]{1,0:T(8,128)(2,1)S(1)}, bf16[32,3840]{1,0:T(8,128)(2,1)S(1)}, u32[]{:S(2)}, u32[]{:S(2)}) collective-permute-start(bf16[32,3840]{1,0:T(8,128)(2,1)S(1)} %get-tuple-element.16.refs_0_), channel_id=1, source_target_pairs={{0,1},{1,0},{2,3},{3,2},{4,5},{5,4},{6,7},{7,6},{8,9},{9,8},{10,11... | collective-permute-start | bytes 737288 | tf_op jit(solution)/shard_map/cond/branch_1_fun/ppermute | solution.py:73
  25.4 1.9 %collective-permute-start.1 = (bf16[32,3840]{1,0:T(8,128)(2,1)S(1)}, bf16[32,3840]{1,0:T(8,128)(2,1)S(1)}, u32[]{:S(2)}, u32[]{:S(2)}) collective-permute-start(bf16[32,3840]{1,0:T(8,128)(2,1)S(1)} %get-tuple-element.17.refs_1_), channel_id=1, source_target_pairs={{0,1},{1,0},{2,3},{3,2},{4,5},{5,4},{6,7},{7,6},{8,9},{9,8},{10,11... | collective-permute-start | bytes 737288 | tf_op jit(solution)/shard_map/cond/branch_1_fun/ppermute | solution.py:73
  31.1 1.6 %collective-permute-start.2 = (bf16[32,3840]{1,0:T(8,128)(2,1)S(1)}, bf16[32,3840]{1,0:T(8,128)(2,1)S(1)}, u32[]{:S(2)}, u32[]{:S(2)}) collective-permute-start(bf16[32,3840]{1,0:T(8,128)(2,1)S(1)} %get-tuple-element.27), channel_id=1, source_target_pairs={{0,1},{1,0},{2,3},{3,2},{4,5},{5,4},{6,7},{7,6},{8,9},{9,8},{10,11... | collective-permute-start | bytes 737288 | tf_op jit(solution)/shard_map/cond/branch_1_fun/ppermute | solution.py:73
  32.8 9.1 %collective-permute-start.16 = (bf16[32,3840]{1,0:T(8,128)(2,1)S(1)}, bf16[32,3840]{1,0:T(8,128)(2,1)S(1)}, u32[]{:S(2)}, u32[]{:S(2)}) collective-permute-start(bf16[32,3840]{1,0:T(8,128)(2,1)S(1)} %get-tuple-element.103), channel_id=1, source_target_pairs={{0,1},{1,0},{2,3},{3,2},{4,5},{5,4},{6,7},{7,6},{8,9},{9,8},{10,11... | collective-permute-start | bytes 737288 | tf_op jit(solution)/shard_map/ppermute | solution.py:73
  33.0 8.9 %collective-permute-start.17 = (bf16[32,3840]{1,0:T(8,128)(2,1)S(1)}, bf16[32,3840]{1,0:T(8,128)(2,1)S(1)}, u32[]{:S(2)}, u32[]{:S(2)}) collective-permute-start(bf16[32,3840]{1,0:T(8,128)(2,1)S(1)} %get-tuple-element.104), channel_id=1, source_target_pairs={{0,2},{1,3},{2,0},{3,1},{4,6},{5,7},{6,4},{7,5},{8,10},{9,11},{10,... | collective-permute-start | bytes 737288 | tf_op jit(solution)/shard_map/ppermute | solution.py:64

commit v12 on v11

--- a/solution.py
+++ b/solution.py
@@ -413,20 +413,37 @@
             rank + float(s.count * s.main + d * s.extra - s.main),
         )
         place = jnp.where(col == expert_at(s, d), at, place)
-    table = jnp.where(place == iota((s.tok, high), 1), 1.0, 0.0).astype(BF16)
-    return jnp.dot(table, rows_ref[...], preferred_element_type=F32)
+    return jnp.where(place == iota((s.tok, high), 1), 1.0, 0.0).astype(BF16)
+
+
+def send_out(value_of, out_hbm, chunks_ref, sems):
+    n, _, width = chunks_ref.shape
+    copies = []
+    for c in range(n):
+        at = slice(c * width, (c + 1) * width)
+        chunks_ref[c] = value_of(at).astype(BF16)
+        to = out_hbm.at[:, pl.ds(c * width, width)]
+        copies.append(pltpu.make_async_copy(chunks_ref.at[c], to, sems.at[c]))
+        copies[-1].start()
+    for copy in copies:
+        copy.wait()
 
 
 def forward_end_kernel(s, *refs):
     packs = refs[: s.count]
-    out_ref, token_ref, rows_ref, extra_ref, tail_ref, row_ref = refs[s.count :]
+    out_ref, token_ref, rows_ref, extra_ref, tail_ref, chunks_ref, sems, row_ref = refs[s.count :]
     token_ref[...] = jnp.zeros_like(token_ref)
 
     def fill(last):
         mine = [packs[turn_of(d, last, s)] for d in range(s.count)]
         row_ref[...] = mine[0][:, s.depth : s.depth + LANES].astype(F32)
         route_row = row_ref[s.folds : s.folds + 1, : s.tok]
-        out_ref[...] = tokens_of(mine, route_row, rows_ref, extra_ref, tail_ref, s).astype(BF16)
+        table = tokens_of(mine, route_row, rows_ref, extra_ref, tail_ref, s)
+
+        def rows(at):
+            return jnp.dot(table, rows_ref[:, at], preferred_element_type=F32)
+
+        send_out(rows, out_ref, chunks_ref, sems)
 
     first = lax.axis_index("section") == 0
     pl.when(first)(functools.partial(fill, True))
@@ -450,15 +467,20 @@
     own, packs = refs[: s.slices], refs[s.slices : s.slices + s.count - 1]
     n = s.slices + s.count - 1
     dy_ref, route_ref, score_ref, _, out_ref, grad_ref = refs[n : n + 6]
-    rows_ref, extra_ref, tail_ref = refs[n + 6 :]
+    rows_ref, extra_ref, tail_ref, chunks_ref, sems = refs[n + 6 :]
     total = own[0][...].astype(F32)
     for part in own[1:]:
         total = total + part[...].astype(F32)
     packs = [total, *packs]
     route_row = route_ref[...].astype(F32)
-    rows = tokens_of(packs, route_row, rows_ref, extra_ref, tail_ref, s)
+    table = tokens_of(packs, route_row, rows_ref, extra_ref, tail_ref, s)
     gate = as_column(2.5 * score_ref[...])
-    out_ref[...] = (dy_ref[...].astype(F32) + gate * rows).astype(BF16)
+
+    def rows(at):
+        moved = jnp.dot(table, rows_ref[:, at], preferred_element_type=F32)
+        return dy_ref[:, at].astype(F32) + gate * moved
+
+    send_out(rows, out_ref, chunks_ref, sems)
     rank = slot_rows(route_row, s)
     dgate = jnp.zeros((1, s.tok), F32)
     for d in range(s.count):
@@ -477,7 +499,7 @@
 HBM = pl.BlockSpec(memory_space=pltpu.HBM)
 
 
-def call(kernel, name, outs, scratch, ins, *args, mib=16, place=jax.ShapeDtypeStruct):
+def call(kernel, name, outs, scratch, ins, *args, mib=16, place=jax.ShapeDtypeStruct, to=()):
     shapes = [place(shape, kind) for shape, kind in outs]
     args = [
         pltpu.with_memory_space_constraint(a, pltpu.HBM) if spec is HBM else a
@@ -487,7 +509,7 @@
         kernel,
         out_shape=shapes,
         in_specs=ins,
-        out_specs=[VMEM] * len(shapes),
+        out_specs=[HBM if i in to else VMEM for i in range(len(shapes))],
         scratch_shapes=scratch,
         compiler_params=pltpu.CompilerParams(vmem_limit_bytes=mib << 20),
         cost_estimate=pl.CostEstimate(flops=0, bytes_accessed=0, transcendentals=0),
@@ -548,7 +570,13 @@
 
 def end_scratch(s):
     low = -(-(s.count * s.extra) // 16) * 16
-    return [pltpu.VMEM((s.count * s.main + low, s.depth), BF16), *tail_scratch(s, low)]
+    chunks = 4 if s.depth % (4 * LANES) == 0 else 1
+    return [
+        pltpu.VMEM((s.count * s.main + low, s.depth), BF16),
+        *tail_scratch(s, low),
+        pltpu.VMEM((chunks, s.tok, s.depth // chunks), BF16),
+        pltpu.SemaphoreType.DMA((chunks,)),
+    ]
 
 
 def body(
@@ -676,6 +704,7 @@
         end_scratch(s) + [pltpu.VMEM((s.main, LANES), F32)],
         [VMEM] * s.count,
         *moved,
+        to=(0,),
     )
     input_grad, score_grad = call(
         functools.partial(backward_end_kernel, s),
@@ -689,6 +718,7 @@
         route_b,
         score_b,
         token,
+        to=(0,),
     )
     return next_input[None], input_grad[None], score_grad.reshape(1, tok, 1)
 

time: 43.3 us -> 43.8 us (1.012)
    pallas_call x10, Pallas kernels: 15.3 us -> 15.7 us  [call(): pl.pallas_call(kernel, out_shape=shapes, in_specs=ins, out_specs=[HBM if...]
  transfers between devices with their start and end apart: 18 -> 18, of which waited for: 11 -> 11; matrix products, arithmetic and copies ran while one was open for 2% -> 2% of each run, Pallas kernels for 33% -> 32%
where the time goes in v12:
time: 43.8 us; the launch traced here: 43.7 us
  Pallas kernels  15.7 us (36%)
  starting transfers between devices  14.7 us (34%)
  waiting for transfers between devices  11.4 us (26%)
  local copies, waits for them, and re-layouts  1.03 us (2%)
  between operations  0.77 us (2%)
    pallas_call x10, Pallas kernels, call(): pl.pallas_call(kernel, out_shape=shapes, in_specs=ins, out_specs=[HBM if...  15.7 us
    ppermute x2, waiting for transfers between devices, to_next(): return lax.ppermute(block, ('section', 'expert'), route)  6.26 us
    ppermute x1, starting transfers between devices, from_behind(): return lax.ppermute(block, axis, route)  6.06 us
    ppermute x4, starting transfers between devices, across(): return lax.ppermute(block, 'expert', route)  5.09 us
    ppermute x11, waiting for transfers between devices, beside(): return lax.ppermute(block, 'expert', route)  3.72 us
    ppermute x11, starting transfers between devices, beside(): return lax.ppermute(block, 'expert', route)  2.68 us
    ppermute x4, waiting for transfers between devices, across(): return lax.ppermute(block, 'expert', route)  1.21 us
    squeeze x1, local copies, waits for them, and re-layouts, body(): saved_up[0]  1.03 us
  transfers between devices with their start and end apart: 18, of which 11 were waited for; matrix products, arithmetic and copies ran while one was open for 2% of the time, Pallas kernels for 32%

profile of v12, /device:TPU:0, one launch (start us, length us, event | category | flops | bytes accessed | tf_op | source)
XLA Modules:
  0.0 43.7 jit_solution(5375781335111187247)
XLA Ops:
  0.6 6.1 %collective-permute-start.8 = (bf16[1,64,3584]{2,1,0:T(8,128)(2,1)}, bf16[1,64,3584]{2,1,0:T(8,128)(2,1)S(1)}, u32[]{:S(2)}, u32[]{:S(2)}) collective-permute-start(bf16[1,64,3584]{2,1,0:T(8,128)(2,1)} %param.16), channel_id=1, source_target_pairs={{4,0},{8,4},{12,8},{16,12},{20,16},{24,20},{28,24},{0,28},{5,1},{9... | collective-permute-start | bytes 1376264 | tf_op jit(solution)/shard_map/ppermute | solution.py:35
  6.7 1.5 %first.1 = (bf16[32,3840]{1,0:T(8,128)(2,1)S(1)}, bf16[32,1920]{1,0:T(8,128)(2,1)S(1)}, bf16[32,1920]{1,0:T(8,128)(2,1)S(1)}) custom-call(s32[1,64]{1,0:T(1,128)} %bitcast.25, f32[1,64]{1,0:T(1,128)} %bitcast.27, bf16[64,3584]{1,0:T(8,128)(2,1)} %bitcast.24), custom_call_target="tpu_custom_call" | custom-call | tf_op jit(solution)/shard_map/first/pallas_call | solution.py:508
  8.2 1.5 %collective-permute-start.3 = (bf16[32,1920]{1,0:T(8,128)(2,1)S(1)}, bf16[32,1920]{1,0:T(8,128)(2,1)S(1)}, u32[]{:S(2)}, u32[]{:S(2)}) collective-permute-start(bf16[32,1920]{1,0:T(8,128)(2,1)S(1)} %get-tuple-element.71), channel_id=1, source_target_pairs={{0,2},{1,3},{2,0},{3,1},{4,6},{5,7},{6,4},{7,5},{8,10},{9,11},{10,... | collective-permute-start | bytes 368648 | tf_op jit(solution)/shard_map/ppermute | solution.py:64
  9.8 0.5 %collective-permute-start.4 = (bf16[32,1920]{1,0:T(8,128)(2,1)S(1)}, bf16[32,1920]{1,0:T(8,128)(2,1)S(1)}, u32[]{:S(2)}, u32[]{:S(2)}) collective-permute-start(bf16[32,1920]{1,0:T(8,128)(2,1)S(1)} %get-tuple-element.72), channel_id=1, source_target_pairs={{0,2},{1,3},{2,0},{3,1},{4,6},{5,7},{6,4},{7,5},{8,10},{9,11},{10,... | collective-permute-start | bytes 368648 | tf_op jit(solution)/shard_map/ppermute | solution.py:64
  10.3 1.0 %copy_bitcast_fusion = (bf16[4,34,512]{2,1,0:T(8,128)(2,1)S(1)}, bf16[4,34,512]{2,1,0:T(8,128)(2,1)S(1)}) fusion(bf16[1,4,34,512]{3,1,2,0:T(4,128)(2,1)} %param.15, bf16[1,4,34,512]{3,1,2,0:T(4,128)(2,1)} %param.14), kind=kLoop, calls=%fused_computation | loop fusion | bytes 557056 | tf_op jit(solution)/shard_map/squeeze | solution.py:632
  11.6 4.3 %load.1 = (bf16[3584,512]{1,0:T(8,128)(2,1)S(1)}, bf16[3584,512]{1,0:T(8,128)(2,1)S(1)}, bf16[512,3584]{1,0:T(8,128)(2,1)S(1)}, s32[1,64]{1,0:T(1,128)S(1)}, s32[1,64]{1,0:T(1,128)S(1)}, /*index=5*/f32[1,64]{1,0:T(1,128)S(1)}) custom-call(bf16[3584,512]{1,0:T(8,128)(2,1)} %bitcast.21, bf16[3584,512]{1,0:T(8,128)(2,1)} %bitcast.22, ...), custom_call_target="tpu_custom_call" | custom-call | tf_op jit(solution)/shard_map/load/pallas_call | solution.py:508
  15.9 0.6 %collective-permute-start.6 = (bf16[32,1920]{1,0:T(8,128)(2,1)S(1)}, bf16[32,1920]{1,0:T(8,128)(2,1)S(1)}, u32[]{:S(2)}, u32[]{:S(2)}) collective-permute-start(bf16[32,1920]{1,0:T(8,128)(2,1)S(1)} %collective-permute-done.3.refs_1_.refs_7_), channel_id=1, source_target_pairs={{0,1},{1,0},{2,3},{3,2},{4,5},{5,4},{6,7},{7,6},{8,9},{9,8},{10,11... | collective-permute-start | bytes 368648 | tf_op jit(solution)/shard_map/ppermute | solution.py:73
  16.8 0.4 %pack.1 = (bf16[32,3840]{1,0:T(8,128)(2,1)S(1)}, bf16[32,3840]{1,0:T(8,128)(2,1)S(1)}) custom-call(s32[1,64]{1,0:T(1,128)S(1)} %get-tuple-element.79.route_ref.refs_4_, bf16[64,3584]{1,0:T(8,128)(2,1)S(1)} %bitcast.18), custom_call_target="tpu_custom_call" | custom-call | tf_op jit(solution)/shard_map/pack/pallas_call | solution.py:508
  17.2 1.6 %collective-permute-start.15 = (bf16[32,3840]{1,0:T(8,128)(2,1)S(1)}, bf16[32,3840]{1,0:T(8,128)(2,1)S(1)}, u32[]{:S(2)}, u32[]{:S(2)}) collective-permute-start(bf16[32,3840]{1,0:T(8,128)(2,1)S(1)} %get-tuple-element.82), channel_id=1, source_target_pairs={{0,2},{1,3},{2,0},{3,1},{4,6},{5,7},{6,4},{7,5},{8,10},{9,11},{10,... | collective-permute-start | bytes 737288 | tf_op jit(solution)/shard_map/ppermute | solution.py:64
  18.8 2.0 %forward.1 = (bf16[32,3840]{1,0:T(8,128)(2,1)S(1)}, bf16[32,3840]{1,0:T(8,128)(2,1)S(1)}, bf16[16,3840]{1,0:T(8,128)(2,1)S(1)}, bf16[16,3840]{1,0:T(8,128)(2,1)S...) custom-call(bf16[32,3840]{1,0:T(8,128)(2,1)S(1)} %get-tuple-element.83.refs_0_.refs_6_, ...), custom_call_target="tpu_custom_call" | custom-call | tf_op jit(solution)/shard_map/forward/pallas_call | solution.py:508
  20.9 0.5 %collective-permute-start.10 = (bf16[16,3840]{1,0:T(8,128)(2,1)S(1)}, bf16[16,3840]{1,0:T(8,128)(2,1)S(1)}, u32[]{:S(2)}, u32[]{:S(2)}) collective-permute-start(bf16[16,3840]{1,0:T(8,128)(2,1)S(1)} %get-tuple-element.95), channel_id=1, source_target_pairs={{0,1},{1,0},{2,3},{3,2},{4,5},{5,4},{6,7},{7,6},{8,9},{9,8},{10,11... | collective-permute-start | bytes 368648 | tf_op jit(solution)/shard_map/ppermute | solution.py:73
  21.5 0.4 collective-permute-start.12
  23.5 0.6 %collective-permute-start.14 = (bf16[32,3968]{1,0:T(8,128)(2,1)S(1)}, bf16[32,3968]{1,0:T(8,128)(2,1)S(1)}, u32[]{:S(2)}, u32[]{:S(2)}) collective-permute-start(bf16[32,3968]{1,0:T(8,128)(2,1)S(1)} %get-tuple-element.99), channel_id=1, source_target_pairs={{0,6},{1,7},{2,4},{3,5},{4,10},{5,11},{6,8},{7,9},{8,14},{9,15},{1... | collective-permute-start | bytes 761864 | tf_op jit(solution)/shard_map/ppermute | solution.py:55
  24.2 1.2 %collective-permute-done.15 = bf16[32,3840]{1,0:T(8,128)(2,1)S(1)} collective-permute-done((bf16[32,3840]{1,0:T(8,128)(2,1)S(1)}, bf16[32,3840]{1,0:T(8,128)(2,1)S(1)}, u32[]{:S(2)}, u32[]{:S(2)}) %collective-permute-start.15) | collective-permute-done | bytes 245792 | tf_op jit(solution)/shard_map/ppermute | solution.py:64
  25.4 7.4 %conditional.1 = (bf16[32,3840]{1,0:T(8,128)(2,1)S(1)}, bf16[32,3840]{1,0:T(8,128)(2,1)S(1)}, bf16[32,3840]{1,0:T(8,128)(2,1)S(1)}) conditional(s32[]{:T(128)} %bitcast.12, () %tuple.23, (bf16[32,3840]{1,0:T(8,128)(2,1)S(1)}, bf16[32,3840]{1,0:T(8,128)(2,1)S(1)}, f32[144,512]{1,0:T(8,128)S(1)}, f32[144,512]{1,0:T(8,128)S(1)}, ...), branch_computations={%region_0.0_spmd, %region_1.0_spmd} | conditional | bytes 2949264 | solution.py:568
  25.4 0.5 %collective-permute-start.1 = (bf16[32,3840]{1,0:T(8,128)(2,1)S(1)}, bf16[32,3840]{1,0:T(8,128)(2,1)S(1)}, u32[]{:S(2)}, u32[]{:S(2)}) collective-permute-start(bf16[32,3840]{1,0:T(8,128)(2,1)S(1)} %get-tuple-element.17.refs_1_), channel_id=1, source_target_pairs={{0,1},{1,0},{2,3},{3,2},{4,5},{5,4},{6,7},{7,6},{8,9},{9,8},{10,11... | collective-permute-start | bytes 737288 | tf_op jit(solution)/shard_map/cond/branch_1_fun/ppermute | solution.py:73
  25.9 1.0 %collective-permute-done.refs_2_ = bf16[32,3840]{1,0:T(8,128)(2,1)S(1)} collective-permute-done((bf16[32,3840]{1,0:T(8,128)(2,1)S(1)}, bf16[32,3840]{1,0:T(8,128)(2,1)S(1)}, u32[]{:S(2)}, u32[]{:S(2)}) %collective-permute-start) | collective-permute-done | bytes 245792 | tf_op jit(solution)/shard_map/cond/branch_1_fun/ppermute | solution.py:73
  27.3 3.9 %backward.1 = (bf16[32,3840]{1,0:T(8,128)(2,1)S(1)}, bf16[32,3840]{1,0:T(8,128)(2,1)S(1)}, bf16[32,3840]{1,0:T(8,128)(2,1)S(1)}, bf16[32,3840]{1,0:T(8,128)(2,1)S(1)}) custom-call(bf16[32,3840]{1,0:T(8,128)(2,1)S(1)} %get-tuple-element.16.refs_0_, bf16[32,3840]{1,0:T(8,128)(2,1)S(1)} %get-tuple-element.17.refs_1_, ...), custom_call_target="tpu_custom_call" | custom-call | tf_op jit(solution)/shard_map/cond/branch_1_fun/backward/pallas_call | solution.py:508
  31.3 1.4 %collective-permute-done.2.refs_1_ = bf16[32,3840]{1,0:T(8,128)(2,1)S(1)} collective-permute-done((bf16[32,3840]{1,0:T(8,128)(2,1)S(1)}, bf16[32,3840]{1,0:T(8,128)(2,1)S(1)}, u32[]{:S(2)}, u32[]{:S(2)}) %collective-permute-start.2) | collective-permute-done | bytes 245792 | tf_op jit(solution)/shard_map/cond/branch_1_fun/ppermute | solution.py:73
  33.0 1.4 %collective-permute-start.17 = (bf16[32,3840]{1,0:T(8,128)(2,1)S(1)}, bf16[32,3840]{1,0:T(8,128)(2,1)S(1)}, u32[]{:S(2)}, u32[]{:S(2)}) collective-permute-start(bf16[32,3840]{1,0:T(8,128)(2,1)S(1)} %get-tuple-element.104), channel_id=1, source_target_pairs={{0,2},{1,3},{2,0},{3,1},{4,6},{5,7},{6,4},{7,5},{8,10},{9,11},{10,... | collective-permute-start | bytes 737288 | tf_op jit(solution)/shard_map/ppermute | solution.py:64
  34.5 1.7 %collective-permute-done.13.refs_0_ = bf16[32,3968]{1,0:T(8,128)(2,1)S(1)} collective-permute-done((bf16[32,3968]{1,0:T(8,128)(2,1)S(1)}, bf16[32,3968]{1,0:T(8,128)(2,1)S(1)}, u32[]{:S(2)}, u32[]{:S(2)}) %collective-permute-start.13) | collective-permute-done | bytes 253984 | tf_op jit(solution)/shard_map/ppermute | solution.py:55
  36.1 4.6 %collective-permute-done.14.refs_1_ = bf16[32,3968]{1,0:T(8,128)(2,1)S(1)} collective-permute-done((bf16[32,3968]{1,0:T(8,128)(2,1)S(1)}, bf16[32,3968]{1,0:T(8,128)(2,1)S(1)}, u32[]{:S(2)}, u32[]{:S(2)}) %collective-permute-start.14) | collective-permute-done | bytes 253984 | tf_op jit(solution)/shard_map/ppermute | solution.py:55
  40.8 1.1 %forward_end.1 = (bf16[64,3584]{1,0:T(8,128)(2,1)}, f32[8,128]{1,0:T(8,128)S(1)}) custom-call(bf16[32,3968]{1,0:T(8,128)(2,1)S(1)} %collective-permute-done.13.refs_0_, bf16[32,3968]{1,0:T(8,128)(2,1)S(1)} %collective-permute-done.14.refs_1_), custom_call_target="tpu_custom_call" | custom-call | tf_op jit(solution)/shard_map/forward_end/pallas_call | solution.py:508
  41.9 1.7 %backward_end.1 = (bf16[64,3584]{1,0:T(8,128)(2,1)}, f32[1,64]{1,0:T(1,128)}) custom-call(bf16[32,3840]{1,0:T(8,128)(2,1)S(1)} %get-tuple-element.102.refs_0_, bf16[32,3840]{1,0:T(8,128)(2,1)S(1)} %collective-permute-done.16.refs_1_, bf16[32,3840]{1,0:T(8,128)(2,1)S(1)} %collective-permute-done.17.refs_2_, bf16[64,3584]{1,0:T(8,128)(2,1)S(1)} %bitcast.19, ...), custom_call_target="tpu_custom_call" | custom-call | tf_op jit(solution)/shard_map/backward_end/pallas_call | solution.py:508
  (24 shorter events, 3.3 us)
Async XLA Ops:
  0.6 16.2 %collective-permute-start.8 = (bf16[1,64,3584]{2,1,0:T(8,128)(2,1)}, bf16[1,64,3584]{2,1,0:T(8,128)(2,1)S(1)}, u32[]{:S(2)}, u32[]{:S(2)}) collective-permute-start(bf16[1,64,3584]{2,1,0:T(8,128)(2,1)} %param.16), channel_id=1, source_target_pairs={{4,0},{8,4},{12,8},{16,12},{20,16},{24,20},{28,24},{0,28},{5,1},{9... | collective-permute-start | bytes 1376264 | tf_op jit(solution)/shard_map/ppermute | solution.py:35
  8.2 7.7 %collective-permute-start.3 = (bf16[32,1920]{1,0:T(8,128)(2,1)S(1)}, bf16[32,1920]{1,0:T(8,128)(2,1)S(1)}, u32[]{:S(2)}, u32[]{:S(2)}) collective-permute-start(bf16[32,1920]{1,0:T(8,128)(2,1)S(1)} %get-tuple-element.71), channel_id=1, source_target_pairs={{0,2},{1,3},{2,0},{3,1},{4,6},{5,7},{6,4},{7,5},{8,10},{9,11},{10,... | collective-permute-start | bytes 368648 | tf_op jit(solution)/shard_map/ppermute | solution.py:64
  9.8 6.1 %collective-permute-start.4 = (bf16[32,1920]{1,0:T(8,128)(2,1)S(1)}, bf16[32,1920]{1,0:T(8,128)(2,1)S(1)}, u32[]{:S(2)}, u32[]{:S(2)}) collective-permute-start(bf16[32,1920]{1,0:T(8,128)(2,1)S(1)} %get-tuple-element.72), channel_id=1, source_target_pairs={{0,2},{1,3},{2,0},{3,1},{4,6},{5,7},{6,4},{7,5},{8,10},{9,11},{10,... | collective-permute-start | bytes 368648 | tf_op jit(solution)/shard_map/ppermute | solution.py:64
  10.3 8.5 %collective-permute-start.5 = (bf16[32,3840]{1,0:T(8,128)(2,1)S(1)}, bf16[32,3840]{1,0:T(8,128)(2,1)S(1)}, u32[]{:S(2)}, u32[]{:S(2)}) collective-permute-start(bf16[32,3840]{1,0:T(8,128)(2,1)S(1)} %get-tuple-element.83.refs_0_.refs_6_), channel_id=1, source_target_pairs={{0,1},{1,0},{2,3},{3,2},{4,5},{5,4},{6,7},{7,6},{8,9},{9,8},{10,11... | collective-permute-start | bytes 737288 | tf_op jit(solution)/shard_map/ppermute | solution.py:73
  15.9 2.9 %collective-permute-start.6 = (bf16[32,1920]{1,0:T(8,128)(2,1)S(1)}, bf16[32,1920]{1,0:T(8,128)(2,1)S(1)}, u32[]{:S(2)}, u32[]{:S(2)}) collective-permute-start(bf16[32,1920]{1,0:T(8,128)(2,1)S(1)} %collective-permute-done.3.refs_1_.refs_7_), channel_id=1, source_target_pairs={{0,1},{1,0},{2,3},{3,2},{4,5},{5,4},{6,7},{7,6},{8,9},{9,8},{10,11... | collective-permute-start | bytes 368648 | tf_op jit(solution)/shard_map/ppermute | solution.py:73
  16.5 2.3 %collective-permute-start.7 = (bf16[32,1920]{1,0:T(8,128)(2,1)S(1)}, bf16[32,1920]{1,0:T(8,128)(2,1)S(1)}, u32[]{:S(2)}, u32[]{:S(2)}) collective-permute-start(bf16[32,1920]{1,0:T(8,128)(2,1)S(1)} %collective-permute-done.4.refs_2_.refs_8_), channel_id=1, source_target_pairs={{0,1},{1,0},{2,3},{3,2},{4,5},{5,4},{6,7},{7,6},{8,9},{9,8},{10,11... | collective-permute-start | bytes 368648 | tf_op jit(solution)/shard_map/ppermute | solution.py:73
  17.2 8.2 %collective-permute-start.15 = (bf16[32,3840]{1,0:T(8,128)(2,1)S(1)}, bf16[32,3840]{1,0:T(8,128)(2,1)S(1)}, u32[]{:S(2)}, u32[]{:S(2)}) collective-permute-start(bf16[32,3840]{1,0:T(8,128)(2,1)S(1)} %get-tuple-element.82), channel_id=1, source_target_pairs={{0,2},{1,3},{2,0},{3,1},{4,6},{5,7},{6,4},{7,5},{8,10},{9,11},{10,... | collective-permute-start | bytes 737288 | tf_op jit(solution)/shard_map/ppermute | solution.py:64
  20.8 1.4 %collective-permute-start.9 = (bf16[16,3840]{1,0:T(8,128)(2,1)S(1)}, bf16[16,3840]{1,0:T(8,128)(2,1)S(1)}, u32[]{:S(2)}, u32[]{:S(2)}) collective-permute-start(bf16[16,3840]{1,0:T(8,128)(2,1)S(1)} %get-tuple-element.94), channel_id=1, source_target_pairs={{0,1},{1,0},{2,3},{3,2},{4,5},{5,4},{6,7},{7,6},{8,9},{9,8},{10,11... | collective-permute-start | bytes 368648 | tf_op jit(solution)/shard_map/ppermute | solution.py:73
  20.9 1.5 %collective-permute-start.10 = (bf16[16,3840]{1,0:T(8,128)(2,1)S(1)}, bf16[16,3840]{1,0:T(8,128)(2,1)S(1)}, u32[]{:S(2)}, u32[]{:S(2)}) collective-permute-start(bf16[16,3840]{1,0:T(8,128)(2,1)S(1)} %get-tuple-element.95), channel_id=1, source_target_pairs={{0,1},{1,0},{2,3},{3,2},{4,5},{5,4},{6,7},{7,6},{8,9},{9,8},{10,11... | collective-permute-start | bytes 368648 | tf_op jit(solution)/shard_map/ppermute | solution.py:73
  21.4 1.3 %collective-permute-start.11 = (bf16[16,3840]{1,0:T(8,128)(2,1)S(1)}, bf16[16,3840]{1,0:T(8,128)(2,1)S(1)}, u32[]{:S(2)}, u32[]{:S(2)}) collective-permute-start(bf16[16,3840]{1,0:T(8,128)(2,1)S(1)} %get-tuple-element.96), channel_id=1, source_target_pairs={{0,1},{1,0},{2,3},{3,2},{4,5},{5,4},{6,7},{7,6},{8,9},{9,8},{10,11... | collective-permute-start | bytes 368648 | tf_op jit(solution)/shard_map/ppermute | solution.py:73
  21.5 1.4 %collective-permute-start.12 = (bf16[16,3840]{1,0:T(8,128)(2,1)S(1)}, bf16[16,3840]{1,0:T(8,128)(2,1)S(1)}, u32[]{:S(2)}, u32[]{:S(2)}) collective-permute-start(bf16[16,3840]{1,0:T(8,128)(2,1)S(1)} %get-tuple-element.97), channel_id=1, source_target_pairs={{0,1},{1,0},{2,3},{3,2},{4,5},{5,4},{6,7},{7,6},{8,9},{9,8},{10,11... | collective-permute-start | bytes 368648 | tf_op jit(solution)/shard_map/ppermute | solution.py:73
  23.3 12.9 %collective-permute-start.13 = (bf16[32,3968]{1,0:T(8,128)(2,1)S(1)}, bf16[32,3968]{1,0:T(8,128)(2,1)S(1)}, u32[]{:S(2)}, u32[]{:S(2)}) collective-permute-start(bf16[32,3968]{1,0:T(8,128)(2,1)S(1)} %get-tuple-element.98), channel_id=1, source_target_pairs={{0,4},{1,5},{2,6},{3,7},{4,8},{5,9},{6,10},{7,11},{8,12},{9,13},{1... | collective-permute-start | bytes 761864 | tf_op jit(solution)/shard_map/ppermute | solution.py:55
  23.5 17.2 %collective-permute-start.14 = (bf16[32,3968]{1,0:T(8,128)(2,1)S(1)}, bf16[32,3968]{1,0:T(8,128)(2,1)S(1)}, u32[]{:S(2)}, u32[]{:S(2)}) collective-permute-start(bf16[32,3968]{1,0:T(8,128)(2,1)S(1)} %get-tuple-element.99), channel_id=1, source_target_pairs={{0,6},{1,7},{2,4},{3,5},{4,10},{5,11},{6,8},{7,9},{8,14},{9,15},{1... | collective-permute-start | bytes 761864 | tf_op jit(solution)/shard_map/ppermute | solution.py:55
  25.4 1.5 %collective-permute-start = (bf16[32,3840]{1,0:T(8,128)(2,1)S(1)}, bf16[32,3840]{1,0:T(8,128)(2,1)S(1)}, u32[]{:S(2)}, u32[]{:S(2)}) collective-permute-start(bf16[32,3840]{1,0:T(8,128)(2,1)S(1)} %get-tuple-element.16.refs_0_), channel_id=1, source_target_pairs={{0,1},{1,0},{2,3},{3,2},{4,5},{5,4},{6,7},{7,6},{8,9},{9,8},{10,11... | collective-permute-start | bytes 737288 | tf_op jit(solution)/shard_map/cond/branch_1_fun/ppermute | solution.py:73
  25.4 1.9 %collective-permute-start.1 = (bf16[32,3840]{1,0:T(8,128)(2,1)S(1)}, bf16[32,3840]{1,0:T(8,128)(2,1)S(1)}, u32[]{:S(2)}, u32[]{:S(2)}) collective-permute-start(bf16[32,3840]{1,0:T(8,128)(2,1)S(1)} %get-tuple-element.17.refs_1_), channel_id=1, source_target_pairs={{0,1},{1,0},{2,3},{3,2},{4,5},{5,4},{6,7},{7,6},{8,9},{9,8},{10,11... | collective-permute-start | bytes 737288 | tf_op jit(solution)/shard_map/cond/branch_1_fun/ppermute | solution.py:73
  31.1 1.6 %collective-permute-start.2 = (bf16[32,3840]{1,0:T(8,128)(2,1)S(1)}, bf16[32,3840]{1,0:T(8,128)(2,1)S(1)}, u32[]{:S(2)}, u32[]{:S(2)}) collective-permute-start(bf16[32,3840]{1,0:T(8,128)(2,1)S(1)} %get-tuple-element.27), channel_id=1, source_target_pairs={{0,1},{1,0},{2,3},{3,2},{4,5},{5,4},{6,7},{7,6},{8,9},{9,8},{10,11... | collective-permute-start | bytes 737288 | tf_op jit(solution)/shard_map/cond/branch_1_fun/ppermute | solution.py:73
  32.8 9.1 %collective-permute-start.16 = (bf16[32,3840]{1,0:T(8,128)(2,1)S(1)}, bf16[32,3840]{1,0:T(8,128)(2,1)S(1)}, u32[]{:S(2)}, u32[]{:S(2)}) collective-permute-start(bf16[32,3840]{1,0:T(8,128)(2,1)S(1)} %get-tuple-element.103), channel_id=1, source_target_pairs={{0,1},{1,0},{2,3},{3,2},{4,5},{5,4},{6,7},{7,6},{8,9},{9,8},{10,11... | collective-permute-start | bytes 737288 | tf_op jit(solution)/shard_map/ppermute | solution.py:73
  33.0 8.9 %collective-permute-start.17 = (bf16[32,3840]{1,0:T(8,128)(2,1)S(1)}, bf16[32,3840]{1,0:T(8,128)(2,1)S(1)}, u32[]{:S(2)}, u32[]{:S(2)}) collective-permute-start(bf16[32,3840]{1,0:T(8,128)(2,1)S(1)} %get-tuple-element.104), channel_id=1, source_target_pairs={{0,2},{1,3},{2,0},{3,1},{4,6},{5,7},{6,4},{7,5},{8,10},{9,11},{10,... | collective-permute-start | bytes 737288 | tf_op jit(solution)/shard_map/ppermute | solution.py:64
